TPU v7x, 32 devices: a whole 2x2x4 slice. The times are simulated.
32 devices in a mesh: groups: 2 (over y), band: 16 (over z, x, core).
Axes of the slice: x: 2, y: 2, z: 4, core: 2. Of those that a mesh axis runs over, the one named last changes fastest.
Arguments:
- saved_preact: bfloat16 [98304, 512], P(('groups', 'band')), parts along dimension 0
- edge_senders: int32 [49152], P('band'), may hold values from 0 to 2175, as said below
- edge_slots: int32 [49152], P('band'), may hold values from 0 to 31, as said below
- mesh_requests: int32 [16, 16, 2], P('band'), may hold values from 0 to 15, as said below
- mesh_cotangent: bfloat16 [512, 512], P(('groups', 'band')), parts along dimension 0, may hold values from -6 to 6
- out_weight: bfloat16 [512, 512], replicated, may hold values from -0.25 to 0.25
- out_bias: float32 [512], replicated, may hold values from -4 to 4
- ln_gain: float32 [512], replicated, may hold values from 0.4 to 1.6
- grid_weight: bfloat16 [512, 512], replicated, may hold values from -0.25 to 0.25
- mesh_weight: bfloat16 [512, 512], replicated, may hold values from -0.25 to 0.25
Outputs:
- grid_adjoint: bfloat16 [65536, 512], P(('groups', 'band')), parts along dimension 0
- mesh_adjoint: bfloat16 [512, 512], P(('groups', 'band')), parts along dimension 0
There are 2 independent parts, one for each index of `groups`. A program takes and returns all parts, laid end to end along the dimension named above; an argument that names none is the same for every part. Nothing has to cross between parts.
Inputs may be any that keep to these rules, and one draw needn't show every extreme that they name: `edge_senders`: within each band's 3072 edges the values never fall and every row of the band's window (2048 own grid nodes, then the first 128 of the next band) is named at least once; the last band names only its own 2048 rows. `edge_slots`: the slot k of an edge of band b names the request mesh_requests[b, k // 2, k % 2] at owner k // 2; some slots are named by no edge, and which ones differs from band to band. `mesh_requests`: entry [b, o, j] is a row among owner o's 16 mesh nodes.
All inputs are finite; a program needn't handle non-finite values.
Results may differ from a plain program's by a relative error of at most 0.0057.
Values may be sent and summed in bfloat16 or wider, within the bound.
No kernel may reach another device: no remote copies, remote signals or barrier semaphores. Data moves between devices by JAX's collectives and lax.ppermute only.
A program may use at most 64 MiB of HBM per device.

v0:
```python
import jax
import jax.numpy as jnp
from jax import lax
from jax.sharding import PartitionSpec as P

G_DEV = 2048
RIM = 128


ln_eps = 1e-05


def from_behind(block, axis, distance):
    devices = range(lax.axis_size(axis))
    route = [(i - distance, i) for i in devices if i - distance in devices]
    return lax.ppermute(block, axis, route)


def edge_backward(preact, cot_rows, out_weight, out_bias, ln_gain, grid_weight):
    pre_float = preact.astype(jnp.float32)
    hidden = jax.nn.silu(pre_float).astype(jnp.bfloat16)
    output = jnp.dot(hidden, out_weight, preferred_element_type=jnp.float32) + out_bias
    centre = output - jnp.mean(output, axis=-1, keepdims=True)
    inv_scale = lax.rsqrt(jnp.mean(centre * centre, axis=-1, keepdims=True) + ln_eps)
    normed = centre * inv_scale
    d_normed = cot_rows.astype(jnp.float32) * ln_gain
    d_output = inv_scale * (
        d_normed
        - jnp.mean(d_normed, axis=-1, keepdims=True)
        - normed * jnp.mean(d_normed * normed, axis=-1, keepdims=True)
    )
    d_output = d_output.astype(jnp.bfloat16)
    contract = (((1,), (1,)), ((), ()))
    d_hidden = lax.dot_general(d_output, out_weight, contract, preferred_element_type=jnp.float32)
    gate_sig = jax.nn.sigmoid(pre_float)
    d_preact = (d_hidden * gate_sig * (1.0 + pre_float * (1.0 - gate_sig))).astype(jnp.bfloat16)
    grid_term = lax.dot_general(d_preact, grid_weight, contract, preferred_element_type=jnp.float32)
    return (grid_term, d_preact)


def on_device(
    saved_preact,
    edge_senders,
    edge_slots,
    mesh_requests,
    mesh_cotangent,
    out_weight,
    out_bias,
    ln_gain,
    grid_weight,
    mesh_weight,
):
    band_count = lax.axis_size("band")
    owned_rows = mesh_cotangent.shape[0]
    requests = mesh_requests[0]
    slot_count = requests.shape[1]
    slot_total = band_count * slot_count
    slot_onehot = (edge_slots[:, None] == jnp.arange(slot_total, dtype=jnp.int32)[None, :]).astype(
        jnp.bfloat16
    )
    every_row = lax.all_gather(mesh_cotangent, "band", axis=0, tiled=True)
    owner_base = (jnp.arange(band_count, dtype=jnp.int32) * owned_rows)[:, None]
    wanted = (requests + owner_base).reshape(slot_total)
    slot_rows = jnp.take(every_row, wanted, axis=0)
    cot_rows = jnp.dot(slot_onehot, slot_rows, preferred_element_type=jnp.float32).astype(
        jnp.bfloat16
    )
    grid_term, d_preact = edge_backward(
        saved_preact, cot_rows, out_weight, out_bias, ln_gain, grid_weight
    )
    window = jax.ops.segment_sum(grid_term, edge_senders, num_segments=G_DEV + RIM)
    carried = from_behind(window[G_DEV:], "band", 1)
    head_rows = window[:RIM] + carried
    grid_adjoint = jnp.concatenate([head_rows, window[RIM:G_DEV]], axis=0).astype(jnp.bfloat16)
    slot_preact = lax.dot_general(
        slot_onehot, d_preact, (((0,), (0,)), ((), ())), preferred_element_type=jnp.float32
    )
    slot_sums = lax.dot_general(
        slot_preact,
        mesh_weight.astype(jnp.float32),
        (((1,), (1,)), ((), ())),
        precision=lax.Precision.HIGHEST,
        preferred_element_type=jnp.float32,
    )
    mesh_whole = jax.ops.segment_sum(slot_sums, wanted, num_segments=band_count * owned_rows)
    mesh_sum = lax.psum_scatter(mesh_whole, "band", scatter_dimension=0, tiled=True)
    return (grid_adjoint, mesh_sum.astype(jnp.bfloat16))


def solution(mesh):
    in_specs = (
        P(("groups", "band"), None),
        P("band"),
        P("band"),
        P("band", None, None),
        P(("groups", "band"), None),
        P(),
        P(),
        P(),
        P(),
        P(),
    )
    out_specs = (P(("groups", "band"), None), P(("groups", "band"), None))
    return jax.shard_map(
        on_device, mesh=mesh, in_specs=in_specs, out_specs=out_specs, check_vma=False
    )
```

profile of v0, /device:TPU:0, one launch (start us, length us, event | category | flops | bytes accessed | tf_op | source)
XLA Modules:
  0.0 117.0 jit_solution(10247802939598212148)
XLA Ops:
  7.3 0.1 add.97
  7.4 0.1 add.93
  7.5 0.8 copy.16
  8.5 24.0 %all_gather.3 = bf16[256,512]{1,0:T(8,128)(2,1)S(1)} all-gather(bf16[16,512]{1,0:T(8,128)(2,1)} %param.14), channel_id=1, replica_groups=mesh['groups'=2,'band'=16] {'band'}, dimensions={0}, use_global_device_ids=true | all-gather | bytes 278528 | tf_op jit(solution)/shard_map/all_gather | solution.py:61
  32.5 4.0 %add_reduce_fusion = (f32[3072]{0:T(1024)S(1)}, f32[3072,512]{0,1:T(8,128)S(1)}) fusion(f32[512]{0:T(512)} %param.16, bf16[512,512]{1,0:T(8,128)(2,1)S(1)} %copy-done, bf16[3072,512]{1,0:T(8,128)(2,1)} %param.10), kind=kOutput, calls=%fused_computation.19 | convolution fusion | flops 1623192576 | bytes 9975808 | tf_op jit(solution)/shard_map/dot_general | solution.py:22
  36.5 2.6 %copy-done.2 = f32[3072,512]{0,1:T(8,128)} copy-done((f32[3072,512]{0,1:T(8,128)}, f32[3072,512]{0,1:T(8,128)S(1)}, u32[]{:S(2)}) %copy-start.2) | copy-done | bytes 6291480
  39.2 1.1 multiply_reduce_fusion.1
  40.3 0.6 gather_fusion
  41.0 4.8 %fusion.7 = (f32[3072]{0:T(1024)S(1)}, f32[3072]{0:T(1024)S(1)}, bf16[3072,512]{0,1:T(8,128)(2,1)S(1)}) fusion(f32[512]{0:T(512)S(1)} %copy-done.8, f32[3072]{0:T(1024)S(1)} %add_rsqrt_fusion, f32[3072]{0:T(1024)S(1)} %broadcast_multiply_fusion.2, f32[3072,512]{0,1:T(8,128)} %copy-done.2, f32[512]{0:T(512)S(1)} %copy-done.6, ...), kind=kOutput, calls=%fused_computation.16 | convolution fusion | flops 114927616 | bytes 9535520 | tf_op jit(solution)/shard_map/dot_general | solution.py:65
  45.9 0.2 copy-done.7
  46.1 5.0 %fusion.6 = bf16[3072,512]{1,0:T(8,128)(2,1)S(1)} fusion(bf16[3072,512]{1,0:T(8,128)(2,1)S(1)} %copy-done.7, bf16[512,512]{1,0:T(8,128)(2,1)S(1)} %copy-done, bf16[3072,512]{0,1:T(8,128)(2,1)S(1)} %get-tuple-element.8, f32[3072,512]{0,1:T(8,128)S(1)} %bitcast.12, f32[3072]{0:T(1024)S(1)} %get-tuple-element.9, f32[3072]{0:T(1024)S(1)} %get-tuple-element.10, ...), kind=kOutput, calls=%fused_computation.12 | convolution fusion | flops 1642070016 | bytes 16306176 | tf_op jit(solution)/shard_map/dot_general | solution.py:34
  51.1 1.7 %copy-done.1 = bf16[3072,512]{1,0:T(8,128)(2,1)} copy-done((bf16[3072,512]{1,0:T(8,128)(2,1)}, bf16[3072,512]{1,0:T(8,128)(2,1)S(1)}, u32[]{:S(2)}) %copy-start.1) | copy-done | bytes 3145752
  52.8 0.6 fusion.19
  53.4 0.6 fusion.32
  53.9 1.6 %scatter_custom_fusion.1 = f32[256,512]{1,0:T(8,128)} fusion(s32[32]{0:T(128)S(1)} %get-tuple-element.4, f32[32,512]{1,0:T(8,128)S(1)} %fusion.32, f32[]{:T(128)} %constant.11.clone.1), kind=kCustom, calls=%fused_computation.37 | custom fusion | flops 16384 | bytes 524292 | tf_op jit(solution)/shard_map/scatter-add | solution.py:85
  55.5 6.4 %fusion.31 = f32[3072,512]{1,0:T(8,128)} fusion(bf16[3072,512]{1,0:T(8,128)(2,1)} %copy-done.1, bf16[512,512]{1,0:T(8,128)(2,1)S(1)} %copy-done.3), kind=kOutput, calls=%fused_computation.57 | convolution fusion | flops 1610612736 | bytes 9961472 | tf_op jit(solution)/shard_map/dot_general | solution.py:37
  61.9 21.6 %scatter_custom_fusion = f32[2176,512]{1,0:T(8,128)} fusion(s32[3072]{0:T(1024)} %param.11, f32[3072,512]{1,0:T(8,128)} %fusion.31, f32[]{:T(128)} %constant.11.clone.1), kind=kCustom, calls=%fused_computation.30 | custom fusion | flops 1572864 | bytes 4456960 | tf_op jit(solution)/shard_map/scatter-add | solution.py:71
  83.5 1.0 slice.16
  84.4 2.3 %collective-permute-start = (f32[128,512]{1,0:T(8,128)S(1)}, f32[128,512]{1,0:T(8,128)S(1)}, u32[]{:S(2)}, u32[]{:S(2)}) collective-permute-start(f32[128,512]{1,0:T(8,128)S(1)} %slice.16), channel_id=1, source_target_pairs={{0,1},{1,2},{2,3},{3,4},{4,5},{5,6},{6,7},{7,8},{8,9},{9,10},{10,1... | collective-permute-start | bytes 786440 | tf_op jit(solution)/shard_map/ppermute | solution.py:16
  86.7 2.4 %slice.22 = bf16[1920,512]{1,0:T(8,128)(2,1)S(1)} slice(f32[2176,512]{1,0:T(8,128)} %scatter_custom_fusion), slice={[128:2048], [0:512]} | slice | bytes 3932160 | tf_op jit(solution)/shard_map/slice | solution.py:74
  89.1 1.0 fusion.20
  90.1 1.5 %pad_maximum_fusion = bf16[2048,512]{1,0:T(8,128)(2,1)} fusion(bf16[1920,512]{1,0:T(8,128)(2,1)S(1)} %slice.22, bf16[128,512]{1,0:T(8,128)(2,1)S(1)} %fusion.20), kind=kLoop, calls=%fused_computation.32 | loop fusion | flops 4194304 | bytes 4194304 | tf_op jit(solution)/shard_map/concatenate | solution.py:74
  91.6 17.2 %reduce-scatter.2.cloned.1.call-done = f32[16,512]{1,0:T(8,128)} async-done(((f32[256,512]{1,0:T(8,128)}), f32[16,512]{1,0:T(8,128)}) %reduce-scatter.2.cloned.1.call-update) | async-done | bytes 32784 | tf_op jit(solution)/shard_map/reduce_scatter | solution.py:86
  108.8 1.4 %convert_element_type.30 = bf16[16,512]{1,0:T(8,128)(2,1)} convert(f32[16,512]{1,0:T(8,128)} %reduce-scatter.2.cloned.1.call-done) | non-fusion elementwise | flops 8192 | bytes 49152 | tf_op jit(solution)/shard_map/convert_element_type | solution.py:87
  (33 shorter events, 0.4 us)
Async XLA Ops:
  7.2 25.3 %copy-start = (bf16[512,512]{1,0:T(8,128)(2,1)S(1)}, bf16[512,512]{1,0:T(8,128)(2,1)}, u32[]{:S(2)}) copy-start(bf16[512,512]{1,0:T(8,128)(2,1)} %param.15) | copy-start | bytes 1572868
  7.2 101.6 %reduce-scatter.2.cloned.1.call-start = ((), (), s32[]{:S(2)}) async-start(), calls=%async_computation.1 | async-start | bytes 557056 | tf_op jit(solution)/shard_map/reduce_scatter | solution.py:86
  32.5 6.7 %copy-start.6 = (f32[512]{0:T(512)S(1)}, f32[512]{0:T(512)}, u32[]{:S(2)}) copy-start(f32[512]{0:T(512)} %param.16) | copy-start | bytes 6148
  36.5 2.7 %copy-start.2 = (f32[3072,512]{0,1:T(8,128)}, f32[3072,512]{0,1:T(8,128)S(1)}, u32[]{:S(2)}) copy-start(f32[3072,512]{0,1:T(8,128)S(1)} %get-tuple-element.7) | copy-start | bytes 18874372
  36.5 4.4 %copy-start.5 = (s32[3072]{0:T(1024)S(1)}, s32[3072]{0:T(1024)}, u32[]{:S(2)}) copy-start(s32[3072]{0:T(1024)} %param.12) | copy-start | bytes 36868
  36.5 4.4 %copy-start.8 = (f32[512]{0:T(512)S(1)}, f32[512]{0:T(512)}, u32[]{:S(2)}) copy-start(f32[512]{0:T(512)} %param.17) | copy-start | bytes 6148
  40.3 5.6 %slice-start = ((s8[6291456]{0:T(1024)(128)(4,1)}), s8[2097152]{0:T(1024)(128)(4,1)S(1)}, s32[]{:S(2)}) async-start(s8[6291456]{0:T(1024)(128)(4,1)} %bitcast.11), calls=%async_computation.2 | async-start | bytes 4194304
  41.0 4.9 %slice-start.1 = ((s8[6291456]{0:T(1024)(128)(4,1)}), s8[4194304]{0:T(1024)(128)(4,1)S(1)}, s32[]{:S(2)}) async-start(s8[6291456]{0:T(1024)(128)(4,1)} %bitcast.11), calls=%async_computation.3 | async-start | bytes 8388608
  41.0 5.1 %copy-start.7 = (bf16[3072,512]{1,0:T(8,128)(2,1)S(1)}, bf16[3072,512]{1,0:T(8,128)(2,1)}, u32[]{:S(2)}) copy-start(bf16[3072,512]{1,0:T(8,128)(2,1)} %param.10) | copy-start | bytes 9437188
  46.1 7.3 %copy-start.4 = (bf16[512,512]{1,0:T(8,128)(2,1)S(1)}, bf16[512,512]{1,0:T(8,128)(2,1)}, u32[]{:S(2)}) copy-start(bf16[512,512]{1,0:T(8,128)(2,1)} %param.19) | copy-start | bytes 1572868
  46.1 9.4 %copy-start.3 = (bf16[512,512]{1,0:T(8,128)(2,1)S(1)}, bf16[512,512]{1,0:T(8,128)(2,1)}, u32[]{:S(2)}) copy-start(bf16[512,512]{1,0:T(8,128)(2,1)} %param.18) | copy-start | bytes 1572868
  51.1 1.7 %copy-start.1 = (bf16[3072,512]{1,0:T(8,128)(2,1)}, bf16[3072,512]{1,0:T(8,128)(2,1)S(1)}, u32[]{:S(2)}) copy-start(bf16[3072,512]{1,0:T(8,128)(2,1)S(1)} %fusion.6) | copy-start | bytes 9437188
  84.4 4.7 %collective-permute-start = (f32[128,512]{1,0:T(8,128)S(1)}, f32[128,512]{1,0:T(8,128)S(1)}, u32[]{:S(2)}, u32[]{:S(2)}) collective-permute-start(f32[128,512]{1,0:T(8,128)S(1)} %slice.16), channel_id=1, source_target_pairs={{0,1},{1,2},{2,3},{3,4},{4,5},{5,6},{6,7},{7,8},{8,9},{9,10},{10,1... | collective-permute-start | bytes 786440 | tf_op jit(solution)/shard_map/ppermute | solution.py:16
Sparse Core Ops, SparseCore 0:
  55.6 53.1 reduce-scatter.1
where the time goes:
time: 117 us
  other arithmetic  28.1 us (24%)
  blocking collectives  24 us (21%)
  matrix products  21.4 us (18%)
  waiting for transfers between devices  17.3 us (15%)
  between operations  14.3 us (12%)
  local copies, waits for them, and re-layouts  9.71 us (8%)
  starting transfers between devices  2.31 us (2%)
    all_gather x1, blocking collectives, on_device(): every_row = lax.all_gather(mesh_cotangent, 'band', axis=0, tiled=True)  24 us
    scatter-add x1, other arithmetic, on_device(): jax.ops.segment_sum(grid_term, edge_senders, num_segments=G_DEV + RIM)  21.6 us
    reduce_scatter x1, waiting for transfers between devices, on_device(): lax.psum_scatter(mesh_whole, 'band', scatter_dimension=0, tiled=True)  17.2 us
    dot_general x1, matrix products, edge_backward(): lax.dot_general(d_preact, grid_weight, contract, preferred_element_type=j...  6.38 us
    unnamed x23, local copies, waits for them, and re-layouts  5.31 us
    dot_general x1, matrix products, edge_backward(): lax.dot_general(d_output, out_weight, contract, preferred_element_type=jn...  4.98 us
    dot_general x1, matrix products, on_device(): jnp.dot(slot_onehot, slot_rows, preferred_element_type=jnp.float32)  4.84 us
    dot_general x1, matrix products, edge_backward(): jnp.dot(hidden, out_weight, preferred_element_type=jnp.float32) + out_bias  4.01 us
  transfers between devices with their start and end apart: 2, of which 1 were waited for; matrix products, arithmetic and copies ran while one was open for 29% of the time, Pallas kernels for 0%

commit v1 on v0

v1 whole, which is shorter than its diff:
```python
import functools

import jax
import jax.numpy as jnp
from jax import lax
from jax.experimental import pallas as pl
from jax.experimental.pallas import tpu as pltpu
from jax.sharding import PartitionSpec as P

G_DEV = 2048
RIM = 128
LANES = 128
EPS = 1e-05

VMEM = pltpu.VMEM
SMEM = pltpu.SMEM
T_CONTRACT = (((1,), (1,)), ((), ()))


def stages_of(count):
    bits = count.bit_length() - 1
    assert count == 1 << bits
    shift, stages = 0, []
    while shift < bits:
        width = min(2, bits - shift)
        stages.append((shift, 1 << width))
        shift += width
    return stages


def swap(block, count, mask):
    return lax.ppermute(block, "band", [(i, i ^ mask) for i in range(count)])


def whole(space=VMEM):
    return pl.BlockSpec(memory_space=space)


def fixed(shape):
    return pl.BlockSpec(shape, lambda i: (0,) * len(shape))


def dot(a, b):
    return jnp.dot(a, b, preferred_element_type=jnp.float32)


def dot_t(a, b):
    return lax.dot_general(a, b, T_CONTRACT, preferred_element_type=jnp.float32)


def before_kernel(pre_ref, weight_ref, bias_ref, normed_ref, q_ref, gate_ref):
    p = pre_ref[...].astype(jnp.float32)
    s = 0.5 * jnp.tanh(0.5 * p) + 0.5
    h = p * s
    weight = weight_ref[...]
    out = dot(h.astype(jnp.bfloat16), weight) + bias_ref[...]
    centre = out - jnp.mean(out, axis=-1, keepdims=True)
    inv = lax.rsqrt(jnp.mean(centre * centre, axis=-1, keepdims=True) + EPS)
    normed = (centre * inv).astype(jnp.bfloat16)
    normed_ref[...] = normed
    q_ref[...] = dot_t(normed, weight).astype(jnp.bfloat16)
    gate_ref[...] = ((s + h * (1.0 - s)) * inv).astype(jnp.bfloat16)


def before(preact, weight, bias, block):
    edges, width = preact.shape
    rows = pl.BlockSpec((block, width), lambda i: (i, 0))
    return pl.pallas_call(
        before_kernel,
        grid=(edges // block,),
        in_specs=[rows, fixed(weight.shape), fixed(bias.shape)],
        out_specs=[rows] * 3,
        out_shape=[jax.ShapeDtypeStruct((edges, width), jnp.bfloat16)] * 3,
        cost_estimate=pl.CostEstimate(
            flops=4 * edges * width * width, bytes_accessed=8 * edges * width, transcendentals=edges * width
        ),
        compiler_params=pltpu.CompilerParams(vmem_limit_bytes=40 << 20),
        name="before",
    )(preact, weight, bias)


def after_kernel(
    parts,
    chunks,
    owned,
    me_ref,
    ids_ref,
    slots_ref,
    normed_ref,
    q_ref,
    gate_ref,
    weight_ref,
    gain_ref,
    *rest,
):
    pieces, d_ref, sums_refs, (s_ref, dnt_ref) = rest[:parts], rest[parts], rest[parts + 1 : -2], rest[-2:]
    slots, width = s_ref.shape
    each = slots // chunks
    me = me_ref[0]
    step = pl.program_id(0)

    @pl.when(step == 0)
    def _():
        piece_rows = pieces[0].shape[0]
        place = lax.broadcasted_iota(jnp.int32, (slots, piece_rows), 0) // 2 * owned
        place = place + ids_ref[...][:, :1].astype(jnp.int32)
        column = lax.broadcasted_iota(jnp.int32, (slots, piece_rows), 1)
        rows = jnp.zeros((slots, width), jnp.float32)
        for k in range(parts):
            pick = (place == column + k * piece_rows).astype(jnp.float32).astype(jnp.bfloat16)
            rows += dot(pick, pieces[k][...])
        rows = rows * gain_ref[...]
        rows = rows - jnp.mean(rows, axis=-1, keepdims=True)
        centred = rows.astype(jnp.bfloat16)
        s_ref[...] = dot_t(centred, weight_ref[...]).astype(jnp.bfloat16)
        dnt_ref[...] = (rows * (1.0 / width)).astype(jnp.bfloat16)
        for k, sums_ref in enumerate(sums_refs):
            sums_ref[:, :width] = jnp.zeros((each, width), jnp.float32)
            sums_ref[:, width:] = ids_ref[k * each : (k + 1) * each, :]

    block = normed_ref.shape[0]
    row = lax.broadcasted_iota(jnp.int32, (slots, block), 0)
    key = ((row // 2) ^ me) * 2 + row % 2
    onehot_t = (key == slots_ref[...]).astype(jnp.float32)
    onehot = onehot_t.T
    g = dot_t(normed_ref[...], dnt_ref[...])
    c = jnp.sum(onehot * g, axis=-1, keepdims=True)
    s_rows = dot(onehot.astype(jnp.bfloat16), s_ref[...])
    d = gate_ref[...].astype(jnp.float32) * (s_rows - c * q_ref[...].astype(jnp.float32))
    d = d.astype(jnp.bfloat16)
    d_ref[...] = d
    sums = dot(onehot_t.astype(jnp.bfloat16), d)
    for k, sums_ref in enumerate(sums_refs):
        sums_ref[:, :width] += sums[k * each : (k + 1) * each]


def after(me, ids, slots, normed, q, gate, weight, gain, pieces, owned, chunks, block):
    edges, width = normed.shape
    slot_total = ids.shape[0]
    rows = pl.BlockSpec((block, width), lambda i: (i, 0))
    return pl.pallas_call(
        functools.partial(after_kernel, len(pieces), chunks, owned),
        grid=(edges // block,),
        in_specs=[
            whole(SMEM),
            fixed(ids.shape),
            pl.BlockSpec((1, block), lambda i: (0, i)),
            rows,
            rows,
            rows,
            fixed(weight.shape),
            fixed(gain.shape),
        ]
        + [fixed(pieces[0].shape)] * len(pieces),
        out_specs=[rows] + [fixed((slot_total // chunks, width + LANES))] * chunks,
        out_shape=[
            jax.ShapeDtypeStruct((edges, width), jnp.bfloat16),
        ]
        + [jax.ShapeDtypeStruct((slot_total // chunks, width + LANES), jnp.float32)] * chunks,
        scratch_shapes=[VMEM((slot_total, width), jnp.bfloat16)] * 2,
        cost_estimate=pl.CostEstimate(
            flops=3 * edges * width * width, bytes_accessed=8 * edges * width, transcendentals=0
        ),
        compiler_params=pltpu.CompilerParams(vmem_limit_bytes=40 << 20),
        name="after",
    )(me, ids, slots, normed, q, gate, weight, gain, *pieces)


def grid_kernel(blocks, starts_ref, senders_ref, d_ref, weight_ref, out_ref, head_ref, rim_ref, total_ref):
    step = pl.program_id(0)
    block = d_ref.shape[0]
    rows, width = out_ref.shape

    @pl.when(step == 0)
    def _():
        total_ref[:8, :] = jnp.zeros((8, width), jnp.float32)
        total_ref[G_DEV : G_DEV + RIM, :] = jnp.zeros((RIM, width), jnp.float32)

    @pl.when(step < blocks)
    def _():
        base = pl.multiple_of(starts_ref[step * block] // 8 * 8, 8)
        row = lax.broadcasted_iota(jnp.int32, (block + 16, block), 0)
        onehot = (row == senders_ref[...] - base).astype(jnp.float32).astype(jnp.bfloat16)
        sums = dot(onehot, d_ref[...])
        total_ref[pl.ds(base, 8), :] += sums[:8]
        total_ref[pl.ds(pl.multiple_of(base + 8, 8), block + 8), :] = sums[8:]

    @pl.when(step == blocks)
    def _():
        head_ref[...] = total_ref[:RIM, :]
        rim_ref[...] = total_ref[G_DEV : G_DEV + RIM, :]

    @pl.when(step >= blocks)
    def _():
        at = pl.multiple_of((step - blocks) * rows, rows)
        out_ref[...] = dot_t(total_ref[pl.ds(at, rows), :].astype(jnp.bfloat16), weight_ref[...]).astype(
            jnp.bfloat16
        )


def grid_rows(senders, d_preact, weight, block):
    edges, width = d_preact.shape
    blocks = edges // block
    row_blocks = G_DEV // block
    return pl.pallas_call(
        functools.partial(grid_kernel, blocks),
        grid=(blocks + row_blocks,),
        in_specs=[
            whole(SMEM),
            pl.BlockSpec((1, block), lambda i: (0, jnp.minimum(i, blocks - 1))),
            pl.BlockSpec((block, width), lambda i: (jnp.minimum(i, blocks - 1), 0)),
            fixed(weight.shape),
        ],
        out_specs=[
            pl.BlockSpec((block, width), lambda i: (jnp.maximum(i - blocks, 0), 0)),
            fixed((RIM, width)),
            fixed((RIM, width)),
        ],
        out_shape=[
            jax.ShapeDtypeStruct((G_DEV, width), jnp.bfloat16),
            jax.ShapeDtypeStruct((RIM, width), jnp.float32),
            jax.ShapeDtypeStruct((RIM, width), jnp.float32),
        ],
        scratch_shapes=[VMEM((G_DEV + RIM + block + 16, width), jnp.float32)],
        cost_estimate=pl.CostEstimate(
            flops=3 * edges * width * width, bytes_accessed=4 * edges * width, transcendentals=0
        ),
        compiler_params=pltpu.CompilerParams(vmem_limit_bytes=40 << 20),
        name="grid_rows",
    )(senders, senders.reshape(1, edges), d_preact, weight)


def head_kernel(grid_in, head_ref, rim_ref, weight_ref, out_ref):
    rows = (head_ref[...] + rim_ref[...]).astype(jnp.bfloat16)
    out_ref[...] = dot_t(rows, weight_ref[...]).astype(jnp.bfloat16)


def head_rows(grid_adjoint, head, rim, weight):
    return pl.pallas_call(
        head_kernel,
        grid=(1,),
        in_specs=[whole(pl.ANY), fixed(head.shape), fixed(rim.shape), fixed(weight.shape)],
        out_specs=fixed(head.shape),
        out_shape=jax.ShapeDtypeStruct(grid_adjoint.shape, grid_adjoint.dtype),
        input_output_aliases={0: 0},
        cost_estimate=pl.CostEstimate(
            flops=2 * head.size * head.shape[1], bytes_accessed=4 * head.size, transcendentals=0
        ),
        name="head_rows",
    )(grid_adjoint, head, rim, weight)


def regroup_kernel(groups, parts, *refs):
    outs = refs[parts:]
    low = groups // len(outs)
    each = refs[0].shape[0] // groups
    for j, out_ref in enumerate(outs):
        for g in range(low):
            for k in range(parts):
                to, at = (g * parts + k) * each, (j * low + g) * each
                out_ref[to : to + each, :] = refs[k][at : at + each, :]


def regroup(arrived, radix, low):
    rows, width = arrived[0].shape
    parts = len(arrived)
    return pl.pallas_call(
        functools.partial(regroup_kernel, radix * low, parts),
        out_shape=[jax.ShapeDtypeStruct((rows * parts // radix, width), arrived[0].dtype)] * radix,
        cost_estimate=pl.CostEstimate(flops=0, bytes_accessed=8 * rows * parts * width, transcendentals=0),
        name="regroup",
    )(*arrived)


def mesh_kernel(parts, *refs):
    pieces, weight_ref, out_ref = refs[:parts], refs[parts], refs[parts + 1]
    owned, width = out_ref.shape
    rows = jnp.concatenate([piece[...] for piece in pieces], axis=0)
    ids = rows[:, width:].T[:owned].astype(jnp.int32)
    pick = (lax.broadcasted_iota(jnp.int32, ids.shape, 0) == ids).astype(jnp.float32)
    total = dot(pick.astype(jnp.bfloat16), rows[:, :width].astype(jnp.bfloat16))
    out_ref[...] = dot_t(total.astype(jnp.bfloat16), weight_ref[...]).astype(jnp.bfloat16)


def mesh_rows(pieces, weight, owned):
    width = weight.shape[0]
    return pl.pallas_call(
        functools.partial(mesh_kernel, len(pieces)),
        out_shape=jax.ShapeDtypeStruct((owned, width), jnp.bfloat16),
        cost_estimate=pl.CostEstimate(
            flops=2 * owned * width * width, bytes_accessed=2 * width * width, transcendentals=0
        ),
        name="mesh_rows",
    )(*pieces, weight)


def on_device(
    saved_preact,
    edge_senders,
    edge_slots,
    mesh_requests,
    mesh_cotangent,
    out_weight,
    out_bias,
    ln_gain,
    grid_weight,
    mesh_weight,
):
    count = lax.axis_size("band")
    me = lax.axis_index("band")
    owned, width = mesh_cotangent.shape
    edges = saved_preact.shape[0]
    caps = mesh_requests.shape[2]
    slot_total = count * caps
    stages = stages_of(count)

    held = [mesh_cotangent]
    for shift, radix in stages:
        block = held[0] if len(held) == 1 else jnp.concatenate(held, axis=0)
        held = [block] + [swap(block, count, j << shift) for j in range(1, radix)]

    normed, q, gate = before(saved_preact, out_weight, out_bias.reshape(1, width), 512)

    by_distance = jnp.arange(count, dtype=jnp.int32) ^ me
    ids = jnp.take(mesh_requests[0], by_distance, axis=0).reshape(slot_total, 1)
    ids = jnp.broadcast_to(ids.astype(jnp.float32), (slot_total, LANES))
    d_preact, *slot_chunks = after(
        me.reshape(1),
        ids,
        edge_slots.reshape(1, edges),
        normed,
        q,
        gate,
        out_weight,
        ln_gain.reshape(1, width),
        held,
        owned,
        stages[-1][1],
        512,
    )

    arrived = None
    for shift, radix in reversed(stages):
        if arrived is None:
            chunks = slot_chunks
        else:
            chunks = regroup(arrived, radix, 1 << shift)
        arrived = [chunks[0]] + [swap(chunks[j], count, j << shift) for j in range(1, radix)]
    grid_adjoint, head, rim = grid_rows(edge_senders, d_preact, grid_weight, 256)
    carried = lax.ppermute(rim, "band", [(i, i + 1) for i in range(count - 1)])
    grid_adjoint = head_rows(grid_adjoint, head, carried, grid_weight)
    mesh_adjoint = mesh_rows(arrived, mesh_weight, owned)
    return (grid_adjoint, mesh_adjoint)


def solution(mesh):
    in_specs = (
        P(("groups", "band"), None),
        P("band"),
        P("band"),
        P("band", None, None),
        P(("groups", "band"), None),
        P(),
        P(),
        P(),
        P(),
        P(),
    )
    out_specs = (P(("groups", "band"), None), P(("groups", "band"), None))
    return jax.shard_map(
        on_device, mesh=mesh, in_specs=in_specs, out_specs=out_specs, check_vma=False
    )
```

time: 117 us -> 71.7 us (0.61)
  other arithmetic: 28.1 us -> 0.1 us
  Pallas kernels: 0 us -> 25.8 us
  blocking collectives: 24 us -> 0 us
  matrix products: 21.4 us -> 0 us
  between operations: 14.3 us -> 0.77 us
  starting transfers between devices: 2.31 us -> 15.8 us
  local copies, waits for them, and re-layouts: 9.71 us -> 15.9 us
  waiting for transfers between devices: 17.3 us -> 12.7 us
    pallas_call x0 -> x6, Pallas kernels: none -> 25.8 us  [the longest x1 8.67 us: grid_rows(): pl.pallas_call(functools.partial(grid_kernel, blocks), grid=(blocks + row...]
    all_gather x1 -> x0, blocking collectives: 24 us -> none  [on_device(): every_row = lax.all_gather(mesh_cotangent, 'band', axis=0, tiled=True)]
    scatter-add x2 -> x0, other arithmetic: 23.1 us -> none  [the longest x1 21.6 us: on_device(): jax.ops.segment_sum(grid_term, edge_senders, num_segments=G_DEV + RIM)]
    dot_general x6 -> x0, matrix products: 21.4 us -> none  [the longest x1 6.38 us: edge_backward(): lax.dot_general(d_preact, grid_weight, contract, preferred_element_type=j...]
    reduce_scatter x1 -> x0, waiting for transfers between devices: 17.2 us -> none  [on_device(): lax.psum_scatter(mesh_whole, 'band', scatter_dimension=0, tiled=True)]
    ppermute x1 -> x13, starting transfers between devices: 2.27 us -> 15.8 us  [the longest x12 14.3 us: swap(): return lax.ppermute(block, 'band', [(i, i ^ mask) for i in range(count)])]
    ppermute x1 -> x13, waiting for transfers between devices: 0.01 us -> 12.7 us  [the longest x12 12.7 us: swap(): return lax.ppermute(block, 'band', [(i, i ^ mask) for i in range(count)])]
    unnamed x23 -> x47, local copies, waits for them, and re-layouts: 5.31 us -> 15.1 us
  transfers between devices with their start and end apart: 2 -> 13, of which waited for: 1 -> 6; matrix products, arithmetic and copies ran while one was open for 29% -> 2% of each run, Pallas kernels for 0% -> 15%
where the time goes in v1:
time: 71.7 us; the launch traced here: 71.1 us
  Pallas kernels  25.8 us (36%)
  local copies, waits for them, and re-layouts  15.9 us (22%)
  starting transfers between devices  15.8 us (22%)
  waiting for transfers between devices  12.7 us (18%)
  between operations  0.77 us (1%)
    unnamed x47, local copies, waits for them, and re-layouts  15.1 us
    ppermute x12, starting transfers between devices, swap(): return lax.ppermute(block, 'band', [(i, i ^ mask) for i in range(count)])  14.3 us
    ppermute x12, waiting for transfers between devices, swap(): return lax.ppermute(block, 'band', [(i, i ^ mask) for i in range(count)])  12.7 us
    pallas_call x1, Pallas kernels, grid_rows(): pl.pallas_call(functools.partial(grid_kernel, blocks), grid=(blocks + row...  8.67 us
    pallas_call x1, Pallas kernels, before(): pl.pallas_call(before_kernel, grid=(edges // block,), in_specs=[rows, fix...  6.78 us
    pallas_call x1, Pallas kernels, after(): pl.pallas_call(functools.partial(after_kernel, len(pieces), chunks, owned...  4.63 us
    pallas_call x1, Pallas kernels, head_rows(): pl.pallas_call(head_kernel, grid=(1,), in_specs=[whole(pl.ANY), fixed(hea...  2.16 us
    pallas_call x1, Pallas kernels, mesh_rows(): pl.pallas_call(functools.partial(mesh_kernel, len(pieces)), out_shape=jax...  2.09 us
  transfers between devices with their start and end apart: 13, of which 6 were waited for; matrix products, arithmetic and copies ran while one was open for 2% of the time, Pallas kernels for 15%

profile of v1, /device:TPU:0, one launch (start us, length us, event | category | flops | bytes accessed | tf_op | source)
XLA Modules:
  0.0 71.1 jit_solution(2198582726232942403)
XLA Ops:
  0.6 3.0 %collective-permute-start.1 = (bf16[16,512]{1,0:T(8,128)(2,1)}, bf16[16,512]{1,0:T(8,128)(2,1)S(1)}, u32[]{:S(2)}, u32[]{:S(2)}) collective-permute-start(bf16[16,512]{1,0:T(8,128)(2,1)} %param.14), channel_id=1, source_target_pairs={{0,2},{1,3},{2,0},{3,1},{4,6},{5,7},{6,4},{7,5},{8,10},{9,11},{10,... | collective-permute-start | bytes 49160 | tf_op jit(solution)/shard_map/ppermute | solution.py:32
  4.6 1.0 %copy-done.4 = bf16[512,512]{1,0:T(8,128)(2,1)S(1)} copy-done((bf16[512,512]{1,0:T(8,128)(2,1)S(1)}, bf16[512,512]{1,0:T(8,128)(2,1)}, u32[]{:S(2)}) %copy-start.4) | copy-done | bytes 524312
  5.7 1.9 %copy-done.11 = bf16[3072,512]{1,0:T(8,128)(2,1)S(1)} copy-done((bf16[3072,512]{1,0:T(8,128)(2,1)S(1)}, bf16[3072,512]{1,0:T(8,128)(2,1)}, u32[]{:S(2)}) %copy-start.11) | copy-done | bytes 3145752
  8.2 6.8 %before.1 = (bf16[3072,512]{1,0:T(8,128)(2,1)S(1)}, bf16[3072,512]{1,0:T(8,128)(2,1)S(1)}, bf16[3072,512]{1,0:T(8,128)(2,1)S(1)}) custom-call(bf16[3072,512]{1,0:T(8,128)(2,1)S(1)} %copy-done.11, bf16[512,512]{1,0:T(8,128)(2,1)S(1)} %copy-done.4, f32[1,512]{1,0:T(1,128)S(1)} %bitcast.11), custom_call_target="tpu_custom_call" | custom-call | flops 3221225472 | bytes 12582912 | tf_op jit(solution)/shard_map/before/pallas_call | solution.py:68
  15.0 1.6 %copy-done = bf16[3072,512]{1,0:T(8,128)(2,1)} copy-done((bf16[3072,512]{1,0:T(8,128)(2,1)}, bf16[3072,512]{1,0:T(8,128)(2,1)S(1)}, u32[]{:S(2)}) %copy-start) | copy-done | bytes 3145752
  16.7 1.7 %copy-done.2 = bf16[3072,512]{1,0:T(8,128)(2,1)} copy-done((bf16[3072,512]{1,0:T(8,128)(2,1)}, bf16[3072,512]{1,0:T(8,128)(2,1)S(1)}, u32[]{:S(2)}) %copy-start.2) | copy-done | bytes 3145752
  19.1 4.1 %collective-permute-start.5 = (bf16[64,512]{1,0:T(8,128)(2,1)S(1)}, bf16[64,512]{1,0:T(8,128)(2,1)S(1)}, u32[]{:S(2)}, u32[]{:S(2)}) collective-permute-start(bf16[64,512]{1,0:T(8,128)(2,1)S(1)} %constant_dynamic-update-slice_fusion.rest_0_), channel_id=1, source_target_pairs={{0,12},{1,13},{2,14},{3,15},{4,8},{5,9},{6,10},{7,11},{8,4},{9,5},... | collective-permute-start | bytes 196616 | tf_op jit(solution)/shard_map/ppermute | solution.py:32
  24.0 1.7 %collective-permute-done.5.rest_3_ = bf16[64,512]{1,0:T(8,128)(2,1)S(1)} collective-permute-done((bf16[64,512]{1,0:T(8,128)(2,1)S(1)}, bf16[64,512]{1,0:T(8,128)(2,1)S(1)}, u32[]{:S(2)}, u32[]{:S(2)}) %collective-permute-start.5) | collective-permute-done | bytes 65568 | tf_op jit(solution)/shard_map/ppermute | solution.py:32
  25.7 3.2 %collective-permute-done.4.rest_2_ = bf16[64,512]{1,0:T(8,128)(2,1)S(1)} collective-permute-done((bf16[64,512]{1,0:T(8,128)(2,1)S(1)}, bf16[64,512]{1,0:T(8,128)(2,1)S(1)}, u32[]{:S(2)}, u32[]{:S(2)}) %collective-permute-start.4) | collective-permute-done | bytes 65568 | tf_op jit(solution)/shard_map/ppermute | solution.py:32
  29.0 1.9 %copy-done.1 = bf16[3072,512]{1,0:T(8,128)(2,1)S(1)} copy-done((bf16[3072,512]{1,0:T(8,128)(2,1)S(1)}, bf16[3072,512]{1,0:T(8,128)(2,1)}, u32[]{:S(2)}) %copy-start.1) | copy-done | bytes 3145752
  30.9 1.9 %copy-done.3 = bf16[3072,512]{1,0:T(8,128)(2,1)S(1)} copy-done((bf16[3072,512]{1,0:T(8,128)(2,1)S(1)}, bf16[3072,512]{1,0:T(8,128)(2,1)}, u32[]{:S(2)}) %copy-start.3) | copy-done | bytes 3145752
  32.8 1.0 %copy-done.5 = bf16[512,512]{1,0:T(8,128)(2,1)S(1)} copy-done((bf16[512,512]{1,0:T(8,128)(2,1)S(1)}, bf16[512,512]{1,0:T(8,128)(2,1)}, u32[]{:S(2)}) %copy-start.5) | copy-done | bytes 524312
  33.9 4.6 %after.1 = (bf16[3072,512]{1,0:T(8,128)(2,1)S(1)}, f32[8,640]{1,0:T(8,128)S(1)}, f32[8,640]{1,0:T(8,128)S(1)}, f32[8,640]{1,0:T(8,128)S(1)}, f32[8,640]{1,0:T(8,128)S(1)}) custom-call(s32[1]{0:T(128)} %bitcast.1.me_ref, f32[32,128]{1,0:T(8,128)S(1)} %broadcast_in_dim.17.ids_ref, s32[1,3072]{1,0:T(1,128)S(1)} %bitcast.8, ...), custom_call_target="tpu_custom_call" | custom-call | flops 2415919104 | bytes 12582912 | tf_op jit(solution)/shard_map/after/pallas_call | solution.py:141
  38.5 8.7 %grid_rows.1 = (bf16[2048,512]{1,0:T(8,128)(2,1)}, f32[128,512]{1,0:T(8,128)S(1)}, f32[128,512]{1,0:T(8,128)S(1)}) custom-call(s32[3072]{0:T(1024)S(1)} %copy-done.12, s32[1,3072]{1,0:T(1,128)S(1)} %bitcast.10, bf16[3072,512]{1,0:T(8,128)(2,1)S(1)} %get-tuple-element.20.d_ref, bf16[512,512]{1,0:T(8,128)(2,1)S(1)} %copy-done.6), custom_call_target="tpu_custom_call" | custom-call | flops 2415919104 | bytes 6291456 | tf_op jit(solution)/shard_map/grid_rows/pallas_call | solution.py:205
  47.9 1.6 %collective-permute-start.6 = (f32[128,512]{1,0:T(8,128)S(1)}, f32[128,512]{1,0:T(8,128)S(1)}, u32[]{:S(2)}, u32[]{:S(2)}) collective-permute-start(f32[128,512]{1,0:T(8,128)S(1)} %get-tuple-element.23), channel_id=1, source_target_pairs={{0,1},{1,2},{2,3},{3,4},{4,5},{5,6},{6,7},{7,8},{8,9},{9,10},{10,1... | collective-permute-start | bytes 786440 | tf_op jit(solution)/shard_map/ppermute | solution.py:350
  49.5 1.5 %collective-permute-start.7 = (f32[8,640]{1,0:T(8,128)S(1)}, f32[8,640]{1,0:T(8,128)S(1)}, u32[]{:S(2)}, u32[]{:S(2)}) collective-permute-start(f32[8,640]{1,0:T(8,128)S(1)} %get-tuple-element.25), channel_id=1, source_target_pairs={{0,4},{1,5},{2,6},{3,7},{4,0},{5,1},{6,2},{7,3},{8,12},{9,13},{10,... | collective-permute-start | bytes 61448 | tf_op jit(solution)/shard_map/ppermute | solution.py:32
  51.0 2.1 %collective-permute-start.8 = (f32[8,640]{1,0:T(8,128)S(1)}, f32[8,640]{1,0:T(8,128)S(1)}, u32[]{:S(2)}, u32[]{:S(2)}) collective-permute-start(f32[8,640]{1,0:T(8,128)S(1)} %get-tuple-element.26), channel_id=1, source_target_pairs={{0,8},{1,9},{2,10},{3,11},{4,12},{5,13},{6,14},{7,15},{8,0},{9,1},... | collective-permute-start | bytes 61448 | tf_op jit(solution)/shard_map/ppermute | solution.py:32
  53.9 2.0 %collective-permute-done.8.refs_2_ = f32[8,640]{1,0:T(8,128)S(1)} collective-permute-done((f32[8,640]{1,0:T(8,128)S(1)}, f32[8,640]{1,0:T(8,128)S(1)}, u32[]{:S(2)}, u32[]{:S(2)}) %collective-permute-start.8) | collective-permute-done | bytes 20512 | tf_op jit(solution)/shard_map/ppermute | solution.py:32
  55.9 2.9 %collective-permute-done.9.refs_3_ = f32[8,640]{1,0:T(8,128)S(1)} collective-permute-done((f32[8,640]{1,0:T(8,128)S(1)}, f32[8,640]{1,0:T(8,128)S(1)}, u32[]{:S(2)}, u32[]{:S(2)}) %collective-permute-start.9) | collective-permute-done | bytes 20512 | tf_op jit(solution)/shard_map/ppermute | solution.py:32
  59.4 1.4 %regroup.1 = (f32[8,640]{1,0:T(8,128)}, f32[8,640]{1,0:T(8,128)}, f32[8,640]{1,0:T(8,128)}, f32[8,640]{1,0:T(8,128)}) custom-call(f32[8,640]{1,0:T(8,128)} %copy-done.8, f32[8,640]{1,0:T(8,128)} %copy-done.18, f32[8,640]{1,0:T(8,128)} %copy-done.19, f32[8,640]{1,0:T(8,128)} %copy-done.20), custom_call_target="tpu_custom_call" | custom-call | bytes 163840 | tf_op jit(solution)/shard_map/regroup/pallas_call | solution.py:267
  61.0 1.2 %collective-permute-start.11 = (f32[8,640]{1,0:T(8,128)}, f32[8,640]{1,0:T(8,128)S(1)}, u32[]{:S(2)}, u32[]{:S(2)}) collective-permute-start(f32[8,640]{1,0:T(8,128)} %get-tuple-element.30), channel_id=1, source_target_pairs={{0,2},{1,3},{2,0},{3,1},{4,6},{5,7},{6,4},{7,5},{8,10},{9,11},{10,... | collective-permute-start | bytes 61448 | tf_op jit(solution)/shard_map/ppermute | solution.py:32
  62.7 2.3 %collective-permute-done.11.refs_2_ = f32[8,640]{1,0:T(8,128)S(1)} collective-permute-done((f32[8,640]{1,0:T(8,128)}, f32[8,640]{1,0:T(8,128)S(1)}, u32[]{:S(2)}, u32[]{:S(2)}) %collective-permute-start.11) | collective-permute-done | bytes 20512 | tf_op jit(solution)/shard_map/ppermute | solution.py:32
  66.2 2.1 %mesh_rows.1 = bf16[16,512]{1,0:T(8,128)(2,1)} custom-call(f32[8,640]{1,0:T(8,128)} %get-tuple-element.28.refs_0_, f32[8,640]{1,0:T(8,128)} %copy-done.15, f32[8,640]{1,0:T(8,128)} %copy-done.16, f32[8,640]{1,0:T(8,128)} %copy-done.17, bf16[512,512]{1,0:T(8,128)(2,1)} %refs_4_.1), custom_call_target="tpu_custom_call" | custom-call | flops 8388608 | bytes 524288 | tf_op jit(solution)/shard_map/mesh_rows/pallas_call | solution.py:287
  69.0 2.2 %head_rows.1 = bf16[2048,512]{1,0:T(8,128)(2,1)} custom-call(bf16[2048,512]{1,0:T(8,128)(2,1)} %get-tuple-element.21.grid_in, f32[128,512]{1,0:T(8,128)} %copy-done.7, f32[128,512]{1,0:T(8,128)} %copy-done.14, bf16[512,512]{1,0:T(8,128)(2,1)} %weight_ref.7), custom_call_target="tpu_custom_call", output_to_operand_aliasing={{}: (0, {})} | custom-call | flops 67108864 | bytes 262144 | tf_op jit(solution)/shard_map/head_rows/pallas_call | solution.py:239
  (64 shorter events, 8.0 us)
Async XLA Ops:
  0.6 18.4 %collective-permute-start.1 = (bf16[16,512]{1,0:T(8,128)(2,1)}, bf16[16,512]{1,0:T(8,128)(2,1)S(1)}, u32[]{:S(2)}, u32[]{:S(2)}) collective-permute-start(bf16[16,512]{1,0:T(8,128)(2,1)} %param.14), channel_id=1, source_target_pairs={{0,2},{1,3},{2,0},{3,1},{4,6},{5,7},{6,4},{7,5},{8,10},{9,11},{10,... | collective-permute-start | bytes 49160 | tf_op jit(solution)/shard_map/ppermute | solution.py:32
  3.6 15.4 %collective-permute-start = (bf16[16,512]{1,0:T(8,128)(2,1)}, bf16[16,512]{1,0:T(8,128)(2,1)S(1)}, u32[]{:S(2)}, u32[]{:S(2)}) collective-permute-start(bf16[16,512]{1,0:T(8,128)(2,1)} %param.14), channel_id=1, source_target_pairs={{0,1},{1,0},{2,3},{3,2},{4,5},{5,4},{6,7},{7,6},{8,9},{9,8},{10,11... | collective-permute-start | bytes 49160 | tf_op jit(solution)/shard_map/ppermute | solution.py:32
  3.6 15.4 %collective-permute-start.2 = (bf16[16,512]{1,0:T(8,128)(2,1)}, bf16[16,512]{1,0:T(8,128)(2,1)S(1)}, u32[]{:S(2)}, u32[]{:S(2)}) collective-permute-start(bf16[16,512]{1,0:T(8,128)(2,1)} %param.14), channel_id=1, source_target_pairs={{0,3},{1,2},{2,1},{3,0},{4,7},{5,6},{6,5},{7,4},{8,11},{9,10},{10,... | collective-permute-start | bytes 49160 | tf_op jit(solution)/shard_map/ppermute | solution.py:32
  5.7 1.9 %copy-start.11 = (bf16[3072,512]{1,0:T(8,128)(2,1)S(1)}, bf16[3072,512]{1,0:T(8,128)(2,1)}, u32[]{:S(2)}) copy-start(bf16[3072,512]{1,0:T(8,128)(2,1)} %pre_ref.1) | copy-start | bytes 9437188
  8.2 10.1 %copy-start.21 = (s32[1,16,2]{1,2,0:T(2,128)S(1)}, s32[1,16,2]{1,2,0:T(2,128)}, u32[]{:S(2)}) copy-start(s32[1,16,2]{1,2,0:T(2,128)} %param.13) | copy-start | bytes 388
  8.2 20.8 %copy-start.9 = (s32[3072]{0:T(1024)S(1)}, s32[3072]{0:T(1024)}, u32[]{:S(2)}) copy-start(s32[3072]{0:T(1024)} %param.12) | copy-start | bytes 36868
  8.2 20.8 %copy-start.10 = (f32[512]{0:T(512)S(1)}, f32[512]{0:T(512)}, u32[]{:S(2)}) copy-start(f32[512]{0:T(512)} %param.17) | copy-start | bytes 6148
  19.1 6.6 %collective-permute-start.5 = (bf16[64,512]{1,0:T(8,128)(2,1)S(1)}, bf16[64,512]{1,0:T(8,128)(2,1)S(1)}, u32[]{:S(2)}, u32[]{:S(2)}) collective-permute-start(bf16[64,512]{1,0:T(8,128)(2,1)S(1)} %constant_dynamic-update-slice_fusion.rest_0_), channel_id=1, source_target_pairs={{0,12},{1,13},{2,14},{3,15},{4,8},{5,9},{6,10},{7,11},{8,4},{9,5},... | collective-permute-start | bytes 196616 | tf_op jit(solution)/shard_map/ppermute | solution.py:32
  23.2 5.8 %collective-permute-start.4 = (bf16[64,512]{1,0:T(8,128)(2,1)S(1)}, bf16[64,512]{1,0:T(8,128)(2,1)S(1)}, u32[]{:S(2)}, u32[]{:S(2)}) collective-permute-start(bf16[64,512]{1,0:T(8,128)(2,1)S(1)} %constant_dynamic-update-slice_fusion.rest_0_), channel_id=1, source_target_pairs={{0,8},{1,9},{2,10},{3,11},{4,12},{5,13},{6,14},{7,15},{8,0},{9,1},... | collective-permute-start | bytes 196616 | tf_op jit(solution)/shard_map/ppermute | solution.py:32
  23.2 5.8 %collective-permute-start.3 = (bf16[64,512]{1,0:T(8,128)(2,1)S(1)}, bf16[64,512]{1,0:T(8,128)(2,1)S(1)}, u32[]{:S(2)}, u32[]{:S(2)}) collective-permute-start(bf16[64,512]{1,0:T(8,128)(2,1)S(1)} %constant_dynamic-update-slice_fusion.rest_0_), channel_id=1, source_target_pairs={{0,4},{1,5},{2,6},{3,7},{4,0},{5,1},{6,2},{7,3},{8,12},{9,13},{10,... | collective-permute-start | bytes 196616 | tf_op jit(solution)/shard_map/ppermute | solution.py:32
  29.0 1.9 %copy-start.1 = (bf16[3072,512]{1,0:T(8,128)(2,1)S(1)}, bf16[3072,512]{1,0:T(8,128)(2,1)}, u32[]{:S(2)}) copy-start(bf16[3072,512]{1,0:T(8,128)(2,1)} %copy-done) | copy-start | bytes 9437188
  33.8 4.7 %copy-start.6 = (bf16[512,512]{1,0:T(8,128)(2,1)S(1)}, bf16[512,512]{1,0:T(8,128)(2,1)}, u32[]{:S(2)}) copy-start(bf16[512,512]{1,0:T(8,128)(2,1)} %weight_ref.7) | copy-start | bytes 1572868
  33.9 4.7 %copy-start.12 = (s32[3072]{0:T(1024)S(1)}, s32[3072]{0:T(1024)}, u32[]{:S(2)}) copy-start(s32[3072]{0:T(1024)} %starts_ref.1) | copy-start | bytes 36868
  38.5 8.7 %copy-start.8 = (f32[8,640]{1,0:T(8,128)}, f32[8,640]{1,0:T(8,128)S(1)}, u32[]{:S(2)}) copy-start(f32[8,640]{1,0:T(8,128)S(1)} %get-tuple-element.24.refs_0_) | copy-start | bytes 61444
  47.9 20.4 %collective-permute-start.6 = (f32[128,512]{1,0:T(8,128)S(1)}, f32[128,512]{1,0:T(8,128)S(1)}, u32[]{:S(2)}, u32[]{:S(2)}) collective-permute-start(f32[128,512]{1,0:T(8,128)S(1)} %get-tuple-element.23), channel_id=1, source_target_pairs={{0,1},{1,2},{2,3},{3,4},{4,5},{5,6},{6,7},{7,8},{8,9},{9,10},{10,1... | collective-permute-start | bytes 786440 | tf_op jit(solution)/shard_map/ppermute | solution.py:350
  49.5 4.5 %collective-permute-start.7 = (f32[8,640]{1,0:T(8,128)S(1)}, f32[8,640]{1,0:T(8,128)S(1)}, u32[]{:S(2)}, u32[]{:S(2)}) collective-permute-start(f32[8,640]{1,0:T(8,128)S(1)} %get-tuple-element.25), channel_id=1, source_target_pairs={{0,4},{1,5},{2,6},{3,7},{4,0},{5,1},{6,2},{7,3},{8,12},{9,13},{10,... | collective-permute-start | bytes 61448 | tf_op jit(solution)/shard_map/ppermute | solution.py:32
  51.0 5.0 %collective-permute-start.8 = (f32[8,640]{1,0:T(8,128)S(1)}, f32[8,640]{1,0:T(8,128)S(1)}, u32[]{:S(2)}, u32[]{:S(2)}) collective-permute-start(f32[8,640]{1,0:T(8,128)S(1)} %get-tuple-element.26), channel_id=1, source_target_pairs={{0,8},{1,9},{2,10},{3,11},{4,12},{5,13},{6,14},{7,15},{8,0},{9,1},... | collective-permute-start | bytes 61448 | tf_op jit(solution)/shard_map/ppermute | solution.py:32
  53.0 5.8 %collective-permute-start.9 = (f32[8,640]{1,0:T(8,128)S(1)}, f32[8,640]{1,0:T(8,128)S(1)}, u32[]{:S(2)}, u32[]{:S(2)}) collective-permute-start(f32[8,640]{1,0:T(8,128)S(1)} %get-tuple-element.27), channel_id=1, source_target_pairs={{0,12},{1,13},{2,14},{3,15},{4,8},{5,9},{6,10},{7,11},{8,4},{9,5},... | collective-permute-start | bytes 61448 | tf_op jit(solution)/shard_map/ppermute | solution.py:32
  53.9 4.9 %copy-start.18 = (f32[8,640]{1,0:T(8,128)}, f32[8,640]{1,0:T(8,128)S(1)}, u32[]{:S(2)}) copy-start(f32[8,640]{1,0:T(8,128)S(1)} %collective-permute-done.7.refs_1_) | copy-start | bytes 61444
  55.9 2.9 %copy-start.19 = (f32[8,640]{1,0:T(8,128)}, f32[8,640]{1,0:T(8,128)S(1)}, u32[]{:S(2)}) copy-start(f32[8,640]{1,0:T(8,128)S(1)} %collective-permute-done.8.refs_2_) | copy-start | bytes 61444
  60.9 1.9 %collective-permute-start.10 = (f32[8,640]{1,0:T(8,128)}, f32[8,640]{1,0:T(8,128)S(1)}, u32[]{:S(2)}, u32[]{:S(2)}) collective-permute-start(f32[8,640]{1,0:T(8,128)} %get-tuple-element.29), channel_id=1, source_target_pairs={{0,1},{1,0},{2,3},{3,2},{4,5},{5,4},{6,7},{7,6},{8,9},{9,8},{10,11... | collective-permute-start | bytes 61448 | tf_op jit(solution)/shard_map/ppermute | solution.py:32
  61.0 4.0 %collective-permute-start.11 = (f32[8,640]{1,0:T(8,128)}, f32[8,640]{1,0:T(8,128)S(1)}, u32[]{:S(2)}, u32[]{:S(2)}) collective-permute-start(f32[8,640]{1,0:T(8,128)} %get-tuple-element.30), channel_id=1, source_target_pairs={{0,2},{1,3},{2,0},{3,1},{4,6},{5,7},{6,4},{7,5},{8,10},{9,11},{10,... | collective-permute-start | bytes 61448 | tf_op jit(solution)/shard_map/ppermute | solution.py:32
  62.1 3.4 %collective-permute-start.12 = (f32[8,640]{1,0:T(8,128)}, f32[8,640]{1,0:T(8,128)S(1)}, u32[]{:S(2)}, u32[]{:S(2)}) collective-permute-start(f32[8,640]{1,0:T(8,128)} %get-tuple-element.31), channel_id=1, source_target_pairs={{0,3},{1,2},{2,1},{3,0},{4,7},{5,6},{6,5},{7,4},{8,11},{9,10},{10,... | collective-permute-start | bytes 61448 | tf_op jit(solution)/shard_map/ppermute | solution.py:32
  62.7 2.8 %copy-start.15 = (f32[8,640]{1,0:T(8,128)}, f32[8,640]{1,0:T(8,128)S(1)}, u32[]{:S(2)}) copy-start(f32[8,640]{1,0:T(8,128)S(1)} %collective-permute-done.10.refs_1_) | copy-start | bytes 61444
  (11 other events, 11.2 us)

commit v2 on v0

v2 whole, which is shorter than its diff:
```python
import functools

import jax
import jax.numpy as jnp
from jax import lax
from jax.experimental import pallas as pl
from jax.experimental.pallas import tpu as pltpu
from jax.sharding import PartitionSpec as P

G_DEV = 2048
RIM = 128
LANES = 128
EPS = 1e-05
MIB = 1 << 20

BF16 = jnp.bfloat16
F32 = jnp.float32
VMEM = pl.BlockSpec(memory_space=pltpu.VMEM)
SMEM = pl.BlockSpec(memory_space=pltpu.SMEM)
HBM = pl.BlockSpec(memory_space=pltpu.HBM)
ANY = pl.BlockSpec(memory_space=pl.ANY)
DMA = pltpu.SemaphoreType.DMA


def gather_stages(count):
    top = count.bit_length() - 1
    assert count == 1 << top and top > 1
    stages = []
    while top > 1:
        low = max(1, top - 2)
        stages.append((low, 1 << (top - low)))
        top = low
    return stages + [(0, 2)]


def return_stages(count):
    top = count.bit_length() - 1
    stages = []
    while top > 0:
        low = max(0, top - 2)
        stages.append((low, 1 << (top - low)))
        top = low
    return stages


def swap(block, count, mask):
    return lax.ppermute(block, "band", [(i, i ^ mask) for i in range(count)])


def like(shape, dtype):
    return jax.ShapeDtypeStruct(shape, dtype)


def in_hbm(x):
    return pltpu.with_memory_space_constraint(x, pltpu.HBM)


def in_vmem(shape, dtype):
    return pltpu.VMEM(shape, dtype)


def dot(a, b):
    return jnp.dot(a, b, preferred_element_type=F32)


def dot_t(a, b):
    return lax.dot_general(a, b, (((1,), (1,)), ((), ())), preferred_element_type=F32)


def split(x):
    high = x.astype(BF16)
    return high, (x - high.astype(F32)).astype(BF16)


def cost(flops, size):
    return pl.CostEstimate(flops=int(flops), bytes_accessed=int(size), transcendentals=0)


def params(limit):
    return pltpu.CompilerParams(vmem_limit_bytes=limit * MIB)


def edge_block(pre, weight, bias):
    p = pre.astype(F32)
    s = 0.5 * jnp.tanh(0.5 * p) + 0.5
    h = p * s
    out = dot(h.astype(BF16), weight) + bias
    centre = out - jnp.mean(out, axis=-1, keepdims=True)
    inv = lax.rsqrt(jnp.mean(centre * centre, axis=-1, keepdims=True) + EPS)
    normed = (centre * inv).astype(BF16)
    q = dot_t(normed, weight).astype(BF16)
    return normed, q, (s + h * (1.0 - s)) * inv


def before_kernel(first, block, copies, pre_hbm, *refs):
    sources, rest = refs[:copies], refs[copies:]
    if copies:
        me_ref, requests_ref, *rest = rest
        targets, (ids_ref, *rest) = rest[:copies], rest[copies:]
        weight_ref, bias_ref = targets[:2]
    else:
        weight_ref, bias_ref, _, *rest = rest
    normed_ref, q_ref, gate_ref, pre_ref, sem, other_sem = rest
    rows = normed_ref.shape[0]
    loads = [
        pltpu.make_async_copy(
            pre_hbm.at[pl.ds(first + at, block)], pre_ref.at[pl.ds(at, block)], sem.at[at // block]
        )
        for at in range(0, rows, block)
    ]
    others = [pltpu.make_async_copy(a, b, other_sem.at[k]) for k, (a, b) in enumerate(zip(sources, targets))] if copies else []
    for copy in others[:2] + loads + others[2:]:
        copy.start()
    for copy in others[:2]:
        copy.wait()
    weight, bias = weight_ref[...], bias_ref[...]
    for k, at in enumerate(range(0, rows, block)):
        loads[k].wait()
        piece = slice(at, at + block)
        normed_ref[piece], q_ref[piece], gate_ref[piece] = edge_block(pre_ref[piece], weight, bias)
    for copy in others[2:]:
        copy.wait()
    if copies:
        slots, caps = ids_ref.shape[0], requests_ref.shape[2]
        row = lax.broadcasted_iota(jnp.int32, ids_ref.shape, 0)
        ids = jnp.zeros(ids_ref.shape, jnp.int32)
        for r in range(slots):
            ids = jnp.where(row == r, requests_ref[0, (r // caps) ^ me_ref[0], r % caps], ids)
        ids_ref[...] = ids.astype(F32)


def before(preact, first, rows, held, sources=(), given=(), me=None, requests=None, block=256):
    width = preact.shape[1]
    copies = len(sources)
    outs = [in_vmem(a.shape, a.dtype) for a in sources]
    if copies:
        outs.append(in_vmem((requests.shape[1] * requests.shape[2], LANES), F32))
    outs += [in_vmem((rows, width), BF16)] * 2 + [in_vmem((rows, width), F32)]
    return pl.pallas_call(
        functools.partial(before_kernel, first, block, copies),
        in_specs=[HBM] * (1 + copies) + ([SMEM, SMEM] if copies else [VMEM, VMEM, ANY]),
        out_specs=[VMEM] * len(outs),
        out_shape=outs,
        scratch_shapes=[pltpu.VMEM((rows, width), BF16), DMA((rows // block,)), DMA((max(copies, 1),))],
        cost_estimate=cost(6 * rows * width * width, 10 * rows * width),
        compiler_params=params(16),
        name="before",
    )(in_hbm(preact), *[in_hbm(a) for a in sources], *((me, requests) if copies else (*given, held)))


def after_kernel(
    halves, parts, chunks, owned, block, me_ref, ids_ref, slots_ref, senders_ref, weight_ref, gain_ref, *refs
):
    edge_refs = [refs[3 * k : 3 * k + 3] for k in range(halves)]
    refs = refs[3 * halves :]
    pieces, d_ref, rim_ref, sums_refs = refs[:parts], refs[parts], refs[parts + 1], refs[parts + 2 :]
    slots = ids_ref.shape[0]
    edges, width = d_ref.shape
    each = slots // chunks
    me = me_ref[0]
    weight = weight_ref[...]

    piece_rows = pieces[0].shape[0]
    row = lax.broadcasted_iota(jnp.int32, (slots, 1), 0)
    far, place, step = row // 2, jnp.zeros_like(row), 1
    for shift, radix in gather_stages(slots // 2):
        place = place + ((far >> shift) & (radix - 1)) * step
        step *= radix
    place = place * owned + ids_ref[...][:, :1].astype(jnp.int32)
    column = lax.broadcasted_iota(jnp.int32, (slots, piece_rows), 1)
    rows = jnp.zeros((slots, width), F32)
    for k in range(parts):
        pick = (place == column + k * piece_rows).astype(F32).astype(BF16)
        rows += dot(pick, pieces[k][...])
    rows = rows * gain_ref[...]
    rows = rows - jnp.mean(rows, axis=-1, keepdims=True)
    high, low = split(rows)
    s_high, s_low = split(dot_t(high, weight) + dot_t(low, weight))
    s_both = jnp.concatenate([s_high, s_low], axis=0)
    mean_rows = (rows * (1.0 / width)).astype(BF16)

    key = ((row // 2) ^ me) * 2 + row % 2
    sums = jnp.zeros((slots, width), F32)
    rim = jnp.zeros((RIM, width), F32)
    rim_row = lax.broadcasted_iota(jnp.int32, (RIM, block), 0) + G_DEV
    for at in range(0, edges, block):
        half = edges // halves
        normed_ref, q_ref, gate_ref = edge_refs[at // half]
        piece = slice(at % half, at % half + block)
        onehot_t = (key == slots_ref[:, at : at + block]).astype(F32)
        onehot = onehot_t.T
        g = dot_t(normed_ref[piece], mean_rows)
        c = jnp.sum(onehot * g, axis=-1, keepdims=True)
        onehot = onehot.astype(BF16)
        s_rows = dot(jnp.concatenate([onehot, onehot], axis=1), s_both)
        d = (gate_ref[piece] * (s_rows - c * q_ref[piece].astype(F32))).astype(BF16)
        d_ref[at : at + block, :] = d
        sums += dot(onehot_t.astype(BF16), d)
        if at + block > G_DEV:
            pick = (rim_row == senders_ref[:, at : at + block]).astype(F32).astype(BF16)
            rim += dot(pick, d)
    rim_ref[...] = rim
    for k, sums_ref in enumerate(sums_refs):
        sums_ref[:, :width] = sums[k * each : (k + 1) * each]
        sums_ref[:, width:] = ids_ref[k * each : (k + 1) * each, :]


def after(me, ids, slots, senders, weight, gain, parts, pieces, owned, chunks, block=512):
    edges, width = slots.shape[1], weight.shape[0]
    slot_total = ids.shape[0]
    return pl.pallas_call(
        functools.partial(after_kernel, len(parts), len(pieces), chunks, owned, block),
        in_specs=[SMEM] + [VMEM] * (5 + 3 * len(parts) + len(pieces)),
        out_specs=[VMEM] * (2 + chunks),
        out_shape=[in_vmem((edges, width), BF16), in_vmem((RIM, width), F32)]
        + [in_vmem((slot_total // chunks, width + LANES), F32)] * chunks,
        cost_estimate=cost(6 * edges * width * width, 8 * edges * width),
        compiler_params=params(16),
        name="after",
    )(me, ids, slots, senders, weight, gain, *[a for part in parts for a in part], *pieces)


def grid_kernel(block, starts_ref, senders_ref, d_ref, weight_ref, out_hbm, head_ref, total_ref, out_ref, sem):
    edges, width = d_ref.shape
    total_ref[:8, :] = jnp.zeros((8, width), F32)
    row = lax.broadcasted_iota(jnp.int32, (block + 16, block), 0)
    for at in range(0, edges, block):
        base = pl.multiple_of(starts_ref[at] // 8 * 8, 8)
        onehot = (row == senders_ref[:, at : at + block] - base).astype(F32).astype(BF16)
        sums = dot(onehot, d_ref[at : at + block, :])
        total_ref[pl.ds(base, 8), :] += sums[:8]
        total_ref[pl.ds(pl.multiple_of(base + 8, 8), block + 8), :] = sums[8:]
    head_ref[...] = total_ref[:RIM, :]
    weight = weight_ref[...]
    copies = []
    for k, at in enumerate(range(RIM, G_DEV, 2 * RIM)):
        size = min(2 * RIM, G_DEV - at)
        out_ref[at : at + size, :] = dot_t(total_ref[at : at + size, :].astype(BF16), weight).astype(BF16)
        copies.append(
            pltpu.make_async_copy(out_ref.at[pl.ds(at, size)], out_hbm.at[pl.ds(at, size)], sem.at[k])
        )
        copies[-1].start()
    for copy in copies:
        copy.wait()


def grid_rows(senders, d_preact, weight, block=256):
    edges, width = d_preact.shape
    return pl.pallas_call(
        functools.partial(grid_kernel, block),
        in_specs=[SMEM] + [VMEM] * 3,
        out_specs=[HBM, VMEM],
        out_shape=[like((G_DEV, width), BF16), in_vmem((RIM, width), F32)],
        scratch_shapes=[
            pltpu.VMEM((G_DEV + RIM + block + 16, width), F32),
            pltpu.VMEM((G_DEV, width), BF16),
            DMA((-(-(G_DEV - RIM) // (2 * RIM)),)),
        ],
        cost_estimate=cost(4 * edges * width * width, 4 * edges * width),
        compiler_params=params(16),
        name="grid_rows",
    )(senders, senders.reshape(1, edges), d_preact, weight)


def head_kernel(grid_in, head_ref, rim_ref, weight_ref, out_hbm, out_ref, sem):
    rows = (head_ref[...] + rim_ref[...]).astype(BF16)
    out_ref[...] = dot_t(rows, weight_ref[...]).astype(BF16)
    copy = pltpu.make_async_copy(out_ref, out_hbm.at[pl.ds(0, RIM)], sem)
    copy.start()
    copy.wait()


def head_rows(grid_adjoint, head, rim, weight):
    return pl.pallas_call(
        head_kernel,
        in_specs=[HBM, VMEM, VMEM, VMEM],
        out_specs=HBM,
        out_shape=like(grid_adjoint.shape, grid_adjoint.dtype),
        scratch_shapes=[pltpu.VMEM(head.shape, BF16), DMA],
        input_output_aliases={0: 0},
        cost_estimate=cost(2 * head.size * head.shape[1], 4 * head.size),
        compiler_params=params(4),
        name="head_rows",
    )(grid_adjoint, head, rim, weight)


def regroup_kernel(groups, parts, *refs):
    outs = refs[parts:]
    low = groups // len(outs)
    each = refs[0].shape[0] // groups
    for j, out_ref in enumerate(outs):
        for g in range(low):
            for k in range(parts):
                to, at = (g * parts + k) * each, (j * low + g) * each
                out_ref[to : to + each, :] = refs[k][at : at + each, :]


def regroup(arrived, radix, low):
    rows, width = arrived[0].shape
    parts = len(arrived)
    return pl.pallas_call(
        functools.partial(regroup_kernel, radix * low, parts),
        in_specs=[VMEM] * parts,
        out_specs=[VMEM] * radix,
        out_shape=[in_vmem((rows * parts // radix, width), arrived[0].dtype)] * radix,
        cost_estimate=cost(0, 8 * rows * parts * width),
        compiler_params=params(8),
        name="regroup",
    )(*arrived)


def mesh_kernel(parts, *refs):
    pieces, weight_ref, out_ref = refs[:parts], refs[parts], refs[parts + 1]
    owned, width = out_ref.shape
    rows = jnp.concatenate([piece[...] for piece in pieces], axis=0)
    ids = rows[:, width:].T[:owned].astype(jnp.int32)
    pick = (lax.broadcasted_iota(jnp.int32, ids.shape, 0) == ids).astype(F32).astype(BF16)
    high, low = split(rows[:, :width])
    high, low = split(dot(pick, high) + dot(pick, low))
    both = dot_t(jnp.concatenate([high, low], axis=0), weight_ref[...])
    out_ref[...] = (both[:owned] + both[owned:]).astype(BF16)


def mesh_rows(pieces, weight, owned):
    width = weight.shape[0]
    return pl.pallas_call(
        functools.partial(mesh_kernel, len(pieces)),
        in_specs=[VMEM] * (len(pieces) + 1),
        out_specs=VMEM,
        out_shape=like((owned, width), BF16),
        cost_estimate=cost(2 * owned * width * width, 2 * width * width),
        compiler_params=params(8),
        name="mesh_rows",
    )(*pieces, weight)


def on_device(
    saved_preact,
    edge_senders,
    edge_slots,
    mesh_requests,
    mesh_cotangent,
    out_weight,
    out_bias,
    ln_gain,
    grid_weight,
    mesh_weight,
):
    count = lax.axis_size("band")
    me = lax.axis_index("band")
    owned, width = mesh_cotangent.shape
    edges = saved_preact.shape[0]
    half = edges // 2

    held, seen = [mesh_cotangent], []
    for shift, radix in gather_stages(count):
        block = held[0] if len(held) == 1 else jnp.concatenate(held, axis=0)
        seen.append(block)
        held = [block] + [swap(block, count, j << shift) for j in range(1, radix)]

    sources = (out_weight, out_bias.reshape(1, width), grid_weight, mesh_weight, ln_gain.reshape(1, width))
    weight, bias, weight_g, weight_m, gain, ids, *first = before(
        saved_preact, 0, half, None, sources, me=me.reshape(1), requests=mesh_requests
    )
    second = before(saved_preact, half, half, seen[1], given=(weight, bias))

    stages = return_stages(count)
    d_preact, rim, *chunks = after(
        me.reshape(1),
        ids,
        edge_slots.reshape(1, edges),
        edge_senders.reshape(1, edges),
        weight,
        gain,
        [first, second],
        held,
        owned,
        stages[0][1],
    )

    arrived = None
    for shift, radix in stages:
        if arrived is not None:
            chunks = regroup(arrived, radix, 1 << shift)
        arrived = [chunks[0]] + [swap(chunks[j], count, j << shift) for j in range(1, radix)]
    carried = lax.ppermute(rim, "band", [(i, i + 1) for i in range(count - 1)])
    grid_adjoint, head = grid_rows(edge_senders, d_preact, weight_g)
    grid_adjoint = head_rows(grid_adjoint, head, carried, weight_g)
    mesh_adjoint = mesh_rows(arrived, weight_m, owned)
    return (grid_adjoint, mesh_adjoint)


def solution(mesh):
    in_specs = (
        P(("groups", "band"), None),
        P("band"),
        P("band"),
        P("band", None, None),
        P(("groups", "band"), None),
        P(),
        P(),
        P(),
        P(),
        P(),
    )
    out_specs = (P(("groups", "band"), None), P(("groups", "band"), None))
    return jax.shard_map(
        on_device, mesh=mesh, in_specs=in_specs, out_specs=out_specs, check_vma=False
    )
```

time: 117 us -> 44.9 us (0.38)
  other arithmetic: 28.1 us -> 0 us
  blocking collectives: 24 us -> 0 us
  Pallas kernels: 0 us -> 21.7 us
  matrix products: 21.4 us -> 0 us
  starting transfers between devices: 2.31 us -> 15.7 us
  between operations: 14.3 us -> 0.96 us
  waiting for transfers between devices: 17.3 us -> 4.43 us
  local copies, waits for them, and re-layouts: 9.71 us -> 1.57 us
    all_gather x1 -> x0, blocking collectives: 24 us -> none  [on_device(): every_row = lax.all_gather(mesh_cotangent, 'band', axis=0, tiled=True)]
    scatter-add x2 -> x0, other arithmetic: 23.1 us -> none  [the longest x1 21.6 us: on_device(): jax.ops.segment_sum(grid_term, edge_senders, num_segments=G_DEV + RIM)]
    pallas_call x0 -> x7, Pallas kernels: none -> 21.7 us  [the longest x2 12 us: before(): pl.pallas_call(functools.partial(before_kernel, first, block, copies), in...]
    dot_general x6 -> x0, matrix products: 21.4 us -> none  [the longest x1 6.38 us: edge_backward(): lax.dot_general(d_preact, grid_weight, contract, preferred_element_type=j...]
    reduce_scatter x1 -> x0, waiting for transfers between devices: 17.2 us -> none  [on_device(): lax.psum_scatter(mesh_whole, 'band', scatter_dimension=0, tiled=True)]
    ppermute x1 -> x12, starting transfers between devices: 2.27 us -> 15.7 us  [the longest x11 14 us: swap(): return lax.ppermute(block, 'band', [(i, i ^ mask) for i in range(count)])]
    ppermute x1 -> x12, waiting for transfers between devices: 0.01 us -> 4.43 us  [the longest x11 4.42 us: swap(): return lax.ppermute(block, 'band', [(i, i ^ mask) for i in range(count)])]
    unnamed x23 -> x9, local copies, waits for them, and re-layouts: 5.31 us -> 1.56 us
  transfers between devices with their start and end apart: 2 -> 12, of which waited for: 1 -> 3; matrix products, arithmetic and copies ran while one was open for 29% -> 3% of each run, Pallas kernels for 0% -> 38%
where the time goes in v2:
time: 44.9 us; the launch traced here: 44.3 us
  Pallas kernels  21.7 us (48%)
  starting transfers between devices  15.7 us (35%)
  waiting for transfers between devices  4.43 us (10%)
  local copies, waits for them, and re-layouts  1.57 us (3%)
  between operations  0.96 us (2%)
    ppermute x11, starting transfers between devices, swap(): return lax.ppermute(block, 'band', [(i, i ^ mask) for i in range(count)])  14 us
    pallas_call x2, Pallas kernels, before(): pl.pallas_call(functools.partial(before_kernel, first, block, copies), in...  12 us
    ppermute x11, waiting for transfers between devices, swap(): return lax.ppermute(block, 'band', [(i, i ^ mask) for i in range(count)])  4.42 us
    pallas_call x1, Pallas kernels, after(): pl.pallas_call(functools.partial(after_kernel, len(parts), len(pieces), c...  3.98 us
    pallas_call x1, Pallas kernels, grid_rows(): pl.pallas_call(functools.partial(grid_kernel, block), in_specs=[SMEM] + [...  3.71 us
    ppermute x1, starting transfers between devices, on_device(): carried = lax.ppermute(rim, 'band', [(i, i + 1) for i in range(count - 1)])  1.73 us
    unnamed x9, local copies, waits for them, and re-layouts  1.56 us
    pallas_call x1, Pallas kernels, mesh_rows(): pl.pallas_call(functools.partial(mesh_kernel, len(pieces)), in_specs=[VME...  1 us
  transfers between devices with their start and end apart: 12, of which 3 were waited for; matrix products, arithmetic and copies ran while one was open for 3% of the time, Pallas kernels for 38%

profile of v2, /device:TPU:0, one launch (start us, length us, event | category | flops | bytes accessed | tf_op | source)
XLA Modules:
  0.0 44.3 jit_solution(4802198292428300640)
XLA Ops:
  0.6 4.1 %collective-permute-start.1 = (bf16[16,512]{1,0:T(8,128)(2,1)}, bf16[16,512]{1,0:T(8,128)(2,1)S(1)}, u32[]{:S(2)}, u32[]{:S(2)}) collective-permute-start(bf16[16,512]{1,0:T(8,128)(2,1)} %param.14), channel_id=1, source_target_pairs={{0,8},{1,9},{2,10},{3,11},{4,12},{5,13},{6,14},{7,15},{8,0},{9,1},... | collective-permute-start | bytes 49160 | tf_op jit(solution)/shard_map/ppermute | solution.py:47
  4.7 1.6 %collective-permute-start = (bf16[16,512]{1,0:T(8,128)(2,1)}, bf16[16,512]{1,0:T(8,128)(2,1)S(1)}, u32[]{:S(2)}, u32[]{:S(2)}) collective-permute-start(bf16[16,512]{1,0:T(8,128)(2,1)} %param.14), channel_id=1, source_target_pairs={{0,4},{1,5},{2,6},{3,7},{4,0},{5,1},{6,2},{7,3},{8,12},{9,13},{10,... | collective-permute-start | bytes 49160 | tf_op jit(solution)/shard_map/ppermute | solution.py:47
  6.3 0.8 %constant_dynamic-update-slice_fusion.8 = (bf16[128,512]{1,0:T(8,128)(2,1)S(1)}, bf16[64,512]{1,0:T(8,128)(2,1)S(1)}) fusion(bf16[16,512]{1,0:T(8,128)(2,1)} %param.14), kind=kLoop, calls=%fused_computation.8 | loop fusion | bytes 49152
  7.1 0.8 %copy.13.refs_6_ = s32[1,16,2]{2,1,0:T(8,128)S(1)} copy(s32[1,16,2]{1,2,0:T(2,128)} %param.13) | data formatting | bytes 256 | tf_op args[3]
  7.9 0.8 %collective-permute-done = bf16[16,512]{1,0:T(8,128)(2,1)S(1)} collective-permute-done((bf16[16,512]{1,0:T(8,128)(2,1)}, bf16[16,512]{1,0:T(8,128)(2,1)S(1)}, u32[]{:S(2)}, u32[]{:S(2)}) %collective-permute-start) | collective-permute-done | bytes 16416 | tf_op jit(solution)/shard_map/ppermute | solution.py:47
  8.7 3.4 %collective-permute-done.2 = bf16[16,512]{1,0:T(8,128)(2,1)S(1)} collective-permute-done((bf16[16,512]{1,0:T(8,128)(2,1)}, bf16[16,512]{1,0:T(8,128)(2,1)S(1)}, u32[]{:S(2)}, u32[]{:S(2)}) %collective-permute-start.2) | collective-permute-done | bytes 16416 | tf_op jit(solution)/shard_map/ppermute | solution.py:47
  12.1 1.5 %collective-permute-start.3 = (bf16[64,512]{1,0:T(8,128)(2,1)S(1)}, bf16[64,512]{1,0:T(8,128)(2,1)S(1)}, u32[]{:S(2)}, u32[]{:S(2)}) collective-permute-start(bf16[64,512]{1,0:T(8,128)(2,1)S(1)} %get-tuple-element.51.refs_2_), channel_id=1, source_target_pairs={{0,2},{1,3},{2,0},{3,1},{4,6},{5,7},{6,4},{7,5},{8,10},{9,11},{10,... | collective-permute-start | bytes 196616 | tf_op jit(solution)/shard_map/ppermute | solution.py:47
  13.6 6.4 %before.2 = (bf16[512,512]{1,0:T(8,128)(2,1)S(1)}, f32[1,512]{1,0:T(1,128)S(1)}, bf16[512,512]{1,0:T(8,128)(2,1)S(1)}, bf16[512,512]{1,0:T(8,128)(2,1)S(1)}, f32...) custom-call(bf16[3072,512]{1,0:T(8,128)(2,1)} %pre_hbm.3, ...), custom_call_target="tpu_custom_call" | custom-call | flops 2415919104 | bytes 7864320 | tf_op jit(solution)/shard_map/before/pallas_call | solution.py:139
  20.0 0.1 collective-permute-start.4
  20.1 0.0 copy-start
  20.1 0.0 copy-start.1
  20.1 5.5 %before.3 = (bf16[1536,512]{1,0:T(8,128)(2,1)S(1)}, bf16[1536,512]{1,0:T(8,128)(2,1)S(1)}, f32[1536,512]{1,0:T(8,128)S(1)}) custom-call(bf16[3072,512]{1,0:T(8,128)(2,1)} %pre_hbm.3, bf16[512,512]{1,0:T(8,128)(2,1)S(1)} %get-tuple-element.27.refs_0_.weight_ref, f32[1,512]{1,0:T(1,128)S(1)} %get-tuple-element.32.refs_1_, ...), custom_call_target="tpu_custom_call" | custom-call | flops 2415919104 | bytes 7864320 | tf_op jit(solution)/shard_map/before/pallas_call | solution.py:139
  25.7 4.0 %after.1 = (bf16[3072,512]{1,0:T(8,128)(2,1)S(1)}, f32[128,512]{1,0:T(8,128)S(1)}, f32[8,640]{1,0:T(8,128)S(1)}, f32[8,640]{1,0:T(8,128)S(1)}, f32[8,640]{1,0:T(8,128)S(1)}, /*index=5*/f32[8,640]{1,0:T(8,128)S(1)}) custom-call(s32[1]{0:T(128)} %bitcast.1.refs_5_.me_ref, f32[32,128]{1,0:T(8,128)S(1)} %get-tuple-element.26.ids_ref, s32[1,3072]{1,0:T(1,128)S(1)} %bitcast.5, ...), custom_call_target="tpu_custom_call" | custom-call | flops 4831838208 | bytes 12582912 | tf_op jit(solution)/shard_map/after/pallas_call | solution.py:211
  29.7 0.1 collective-permute-start.6
  29.8 0.8 %collective-permute-start.7 = (f32[8,640]{1,0:T(8,128)S(1)}, f32[8,640]{1,0:T(8,128)S(1)}, u32[]{:S(2)}, u32[]{:S(2)}) collective-permute-start(f32[8,640]{1,0:T(8,128)S(1)} %get-tuple-element.43), channel_id=1, source_target_pairs={{0,8},{1,9},{2,10},{3,11},{4,12},{5,13},{6,14},{7,15},{8,0},{9,1},... | collective-permute-start | bytes 61448 | tf_op jit(solution)/shard_map/ppermute | solution.py:47
  30.6 3.6 %collective-permute-start.8 = (f32[8,640]{1,0:T(8,128)S(1)}, f32[8,640]{1,0:T(8,128)S(1)}, u32[]{:S(2)}, u32[]{:S(2)}) collective-permute-start(f32[8,640]{1,0:T(8,128)S(1)} %get-tuple-element.44), channel_id=1, source_target_pairs={{0,12},{1,13},{2,14},{3,15},{4,8},{5,9},{6,10},{7,11},{8,4},{9,5},... | collective-permute-start | bytes 61448 | tf_op jit(solution)/shard_map/ppermute | solution.py:47
  34.2 1.7 %collective-permute-start.5 = (f32[128,512]{1,0:T(8,128)S(1)}, f32[128,512]{1,0:T(8,128)S(1)}, u32[]{:S(2)}, u32[]{:S(2)}) collective-permute-start(f32[128,512]{1,0:T(8,128)S(1)} %get-tuple-element.40), channel_id=1, source_target_pairs={{0,1},{1,2},{2,3},{3,4},{4,5},{5,6},{6,7},{7,8},{8,9},{9,10},{10,1... | collective-permute-start | bytes 786440 | tf_op jit(solution)/shard_map/ppermute | solution.py:386
  35.9 0.2 collective-permute-done.8.refs_3_
  36.2 0.9 %collective-permute-start.9 = (f32[8,640]{1,0:T(8,128)S(1)}, f32[8,640]{1,0:T(8,128)S(1)}, u32[]{:S(2)}, u32[]{:S(2)}) collective-permute-start(f32[8,640]{1,0:T(8,128)S(1)} %get-tuple-element.46), channel_id=1, source_target_pairs={{0,1},{1,0},{2,3},{3,2},{4,5},{5,4},{6,7},{7,6},{8,9},{9,8},{10,11... | collective-permute-start | bytes 61448 | tf_op jit(solution)/shard_map/ppermute | solution.py:47
  37.0 0.1 collective-permute-start.10
  37.1 1.3 %collective-permute-start.11 = (f32[8,640]{1,0:T(8,128)S(1)}, f32[8,640]{1,0:T(8,128)S(1)}, u32[]{:S(2)}, u32[]{:S(2)}) collective-permute-start(f32[8,640]{1,0:T(8,128)S(1)} %get-tuple-element.48), channel_id=1, source_target_pairs={{0,3},{1,2},{2,1},{3,0},{4,7},{5,6},{6,5},{7,4},{8,11},{9,10},{10,... | collective-permute-start | bytes 61448 | tf_op jit(solution)/shard_map/ppermute | solution.py:47
  38.5 3.7 %grid_rows.1 = (bf16[2048,512]{1,0:T(8,128)(2,1)}, f32[128,512]{1,0:T(8,128)S(1)}) custom-call(s32[3072]{0:T(1024)S(1)} %copy-done.1, s32[1,3072]{1,0:T(1,128)S(1)} %bitcast.7, bf16[3072,512]{1,0:T(8,128)(2,1)S(1)} %get-tuple-element.36.d_ref, bf16[512,512]{1,0:T(8,128)(2,1)S(1)} %get-tuple-element.37.weight_ref), custom_call_target="tpu_custom_call" | custom-call | flops 3221225472 | bytes 6291456 | tf_op jit(solution)/shard_map/grid_rows/pallas_call | solution.py:249
  42.2 1.0 %mesh_rows.1 = bf16[16,512]{1,0:T(8,128)(2,1)} custom-call(f32[8,640]{1,0:T(8,128)S(1)} %get-tuple-element.45.refs_0_, f32[8,640]{1,0:T(8,128)S(1)} %collective-permute-done.9.refs_1_, f32[8,640]{1,0:T(8,128)S(1)} %collective-permute-done.10.refs_2_, f32[8,640]{1,0:T(8,128)S(1)} %collective-permute-done.11.refs_3_, ...), custom_call_target="tpu_custom_call" | custom-call | flops 8388608 | bytes 524288 | tf_op jit(solution)/shard_map/mesh_rows/pallas_call | solution.py:326
  43.2 1.0 %head_rows.1 = bf16[2048,512]{1,0:T(8,128)(2,1)} custom-call(bf16[2048,512]{1,0:T(8,128)(2,1)} %get-tuple-element.38.grid_in, f32[128,512]{1,0:T(8,128)S(1)} %get-tuple-element.39.head_ref, f32[128,512]{1,0:T(8,128)S(1)} %collective-permute-done.5.rim_ref, bf16[512,512]{1,0:T(8,128)(2,1)S(1)} %get-tuple-element.37.weight_ref), custom_call_target="tpu_custom_call", output_to_operand_aliasing={{}: (0, {})} | custom-call | flops 67108864 | bytes 262144 | tf_op jit(solution)/shard_map/head_rows/pallas_call | solution.py:274
  (17 shorter events, 0.1 us)
Async XLA Ops:
  0.6 8.1 %collective-permute-start.1 = (bf16[16,512]{1,0:T(8,128)(2,1)}, bf16[16,512]{1,0:T(8,128)(2,1)S(1)}, u32[]{:S(2)}, u32[]{:S(2)}) collective-permute-start(bf16[16,512]{1,0:T(8,128)(2,1)} %param.14), channel_id=1, source_target_pairs={{0,8},{1,9},{2,10},{3,11},{4,12},{5,13},{6,14},{7,15},{8,0},{9,1},... | collective-permute-start | bytes 49160 | tf_op jit(solution)/shard_map/ppermute | solution.py:47
  4.7 3.9 %collective-permute-start = (bf16[16,512]{1,0:T(8,128)(2,1)}, bf16[16,512]{1,0:T(8,128)(2,1)S(1)}, u32[]{:S(2)}, u32[]{:S(2)}) collective-permute-start(bf16[16,512]{1,0:T(8,128)(2,1)} %param.14), channel_id=1, source_target_pairs={{0,4},{1,5},{2,6},{3,7},{4,0},{5,1},{6,2},{7,3},{8,12},{9,13},{10,... | collective-permute-start | bytes 49160 | tf_op jit(solution)/shard_map/ppermute | solution.py:47
  6.3 5.7 %collective-permute-start.2 = (bf16[16,512]{1,0:T(8,128)(2,1)}, bf16[16,512]{1,0:T(8,128)(2,1)S(1)}, u32[]{:S(2)}, u32[]{:S(2)}) collective-permute-start(bf16[16,512]{1,0:T(8,128)(2,1)} %param.14), channel_id=1, source_target_pairs={{0,12},{1,13},{2,14},{3,15},{4,8},{5,9},{6,10},{7,11},{8,4},{9,5},... | collective-permute-start | bytes 49160 | tf_op jit(solution)/shard_map/ppermute | solution.py:47
  12.1 7.9 %collective-permute-start.3 = (bf16[64,512]{1,0:T(8,128)(2,1)S(1)}, bf16[64,512]{1,0:T(8,128)(2,1)S(1)}, u32[]{:S(2)}, u32[]{:S(2)}) collective-permute-start(bf16[64,512]{1,0:T(8,128)(2,1)S(1)} %get-tuple-element.51.refs_2_), channel_id=1, source_target_pairs={{0,2},{1,3},{2,0},{3,1},{4,6},{5,7},{6,4},{7,5},{8,10},{9,11},{10,... | collective-permute-start | bytes 196616 | tf_op jit(solution)/shard_map/ppermute | solution.py:47
  20.0 5.7 %collective-permute-start.4 = (bf16[128,512]{1,0:T(8,128)(2,1)S(1)}, bf16[128,512]{1,0:T(8,128)(2,1)S(1)}, u32[]{:S(2)}, u32[]{:S(2)}) collective-permute-start(bf16[128,512]{1,0:T(8,128)(2,1)S(1)} %constant_dynamic-update-slice_fusion.4.refs_6_), channel_id=1, source_target_pairs={{0,1},{1,0},{2,3},{3,2},{4,5},{5,4},{6,7},{7,6},{8,9},{9,8},{10,11... | collective-permute-start | bytes 393224 | tf_op jit(solution)/shard_map/ppermute | solution.py:47
  20.1 5.6 %copy-start = (s32[3072]{0:T(1024)S(1)}, s32[3072]{0:T(1024)}, u32[]{:S(2)}) copy-start(s32[3072]{0:T(1024)} %param.12) | copy-start | bytes 36868
  20.1 5.6 %copy-start.1 = (s32[3072]{0:T(1024)S(1)}, s32[3072]{0:T(1024)}, u32[]{:S(2)}) copy-start(s32[3072]{0:T(1024)} %starts_ref.1) | copy-start | bytes 36868
  29.7 6.2 %collective-permute-start.6 = (f32[8,640]{1,0:T(8,128)S(1)}, f32[8,640]{1,0:T(8,128)S(1)}, u32[]{:S(2)}, u32[]{:S(2)}) collective-permute-start(f32[8,640]{1,0:T(8,128)S(1)} %get-tuple-element.42), channel_id=1, source_target_pairs={{0,4},{1,5},{2,6},{3,7},{4,0},{5,1},{6,2},{7,3},{8,12},{9,13},{10,... | collective-permute-start | bytes 61448 | tf_op jit(solution)/shard_map/ppermute | solution.py:47
  29.8 6.1 %collective-permute-start.7 = (f32[8,640]{1,0:T(8,128)S(1)}, f32[8,640]{1,0:T(8,128)S(1)}, u32[]{:S(2)}, u32[]{:S(2)}) collective-permute-start(f32[8,640]{1,0:T(8,128)S(1)} %get-tuple-element.43), channel_id=1, source_target_pairs={{0,8},{1,9},{2,10},{3,11},{4,12},{5,13},{6,14},{7,15},{8,0},{9,1},... | collective-permute-start | bytes 61448 | tf_op jit(solution)/shard_map/ppermute | solution.py:47
  30.6 5.6 %collective-permute-start.8 = (f32[8,640]{1,0:T(8,128)S(1)}, f32[8,640]{1,0:T(8,128)S(1)}, u32[]{:S(2)}, u32[]{:S(2)}) collective-permute-start(f32[8,640]{1,0:T(8,128)S(1)} %get-tuple-element.44), channel_id=1, source_target_pairs={{0,12},{1,13},{2,14},{3,15},{4,8},{5,9},{6,10},{7,11},{8,4},{9,5},... | collective-permute-start | bytes 61448 | tf_op jit(solution)/shard_map/ppermute | solution.py:47
  34.2 9.1 %collective-permute-start.5 = (f32[128,512]{1,0:T(8,128)S(1)}, f32[128,512]{1,0:T(8,128)S(1)}, u32[]{:S(2)}, u32[]{:S(2)}) collective-permute-start(f32[128,512]{1,0:T(8,128)S(1)} %get-tuple-element.40), channel_id=1, source_target_pairs={{0,1},{1,2},{2,3},{3,4},{4,5},{5,6},{6,7},{7,8},{8,9},{9,10},{10,1... | collective-permute-start | bytes 786440 | tf_op jit(solution)/shard_map/ppermute | solution.py:386
  36.2 6.0 %collective-permute-start.9 = (f32[8,640]{1,0:T(8,128)S(1)}, f32[8,640]{1,0:T(8,128)S(1)}, u32[]{:S(2)}, u32[]{:S(2)}) collective-permute-start(f32[8,640]{1,0:T(8,128)S(1)} %get-tuple-element.46), channel_id=1, source_target_pairs={{0,1},{1,0},{2,3},{3,2},{4,5},{5,4},{6,7},{7,6},{8,9},{9,8},{10,11... | collective-permute-start | bytes 61448 | tf_op jit(solution)/shard_map/ppermute | solution.py:47
  37.0 5.2 %collective-permute-start.10 = (f32[8,640]{1,0:T(8,128)S(1)}, f32[8,640]{1,0:T(8,128)S(1)}, u32[]{:S(2)}, u32[]{:S(2)}) collective-permute-start(f32[8,640]{1,0:T(8,128)S(1)} %get-tuple-element.47), channel_id=1, source_target_pairs={{0,2},{1,3},{2,0},{3,1},{4,6},{5,7},{6,4},{7,5},{8,10},{9,11},{10,... | collective-permute-start | bytes 61448 | tf_op jit(solution)/shard_map/ppermute | solution.py:47
  37.1 5.1 %collective-permute-start.11 = (f32[8,640]{1,0:T(8,128)S(1)}, f32[8,640]{1,0:T(8,128)S(1)}, u32[]{:S(2)}, u32[]{:S(2)}) collective-permute-start(f32[8,640]{1,0:T(8,128)S(1)} %get-tuple-element.48), channel_id=1, source_target_pairs={{0,3},{1,2},{2,1},{3,0},{4,7},{5,6},{6,5},{7,4},{8,11},{9,10},{10,... | collective-permute-start | bytes 61448 | tf_op jit(solution)/shard_map/ppermute | solution.py:47

commit v3 on v2

--- a/solution.py
+++ b/solution.py
@@ -22,19 +22,9 @@
 DMA = pltpu.SemaphoreType.DMA
 
 
-def gather_stages(count):
+def stages_of(count):
     top = count.bit_length() - 1
-    assert count == 1 << top and top > 1
-    stages = []
-    while top > 1:
-        low = max(1, top - 2)
-        stages.append((low, 1 << (top - low)))
-        top = low
-    return stages + [(0, 2)]
-
-
-def return_stages(count):
-    top = count.bit_length() - 1
+    assert count == 1 << top
     stages = []
     while top > 0:
         low = max(0, top - 2)
@@ -80,72 +70,133 @@
     return pltpu.CompilerParams(vmem_limit_bytes=limit * MIB)
 
 
-def edge_block(pre, weight, bias):
+def products(pre, weight, bias):
     p = pre.astype(F32)
     s = 0.5 * jnp.tanh(0.5 * p) + 0.5
     h = p * s
-    out = dot(h.astype(BF16), weight) + bias
-    centre = out - jnp.mean(out, axis=-1, keepdims=True)
-    inv = lax.rsqrt(jnp.mean(centre * centre, axis=-1, keepdims=True) + EPS)
-    normed = (centre * inv).astype(BF16)
-    q = dot_t(normed, weight).astype(BF16)
-    return normed, q, (s + h * (1.0 - s)) * inv
-
-
-def before_kernel(first, block, copies, pre_hbm, *refs):
-    sources, rest = refs[:copies], refs[copies:]
-    if copies:
-        me_ref, requests_ref, *rest = rest
-        targets, (ids_ref, *rest) = rest[:copies], rest[copies:]
-        weight_ref, bias_ref = targets[:2]
-    else:
-        weight_ref, bias_ref, _, *rest = rest
-    normed_ref, q_ref, gate_ref, pre_ref, sem, other_sem = rest
+    return dot(h.astype(BF16), weight) + bias, s + h * (1.0 - s)
+
+
+def edge_blocks(pre_ref, weight, bias, normed_ref, q_ref, gate_ref, block, arrive):
+    rows, last = pre_ref.shape[0], None
+    for at in range(0, rows + block, block):
+        this = None
+        if at < rows:
+            arrive(at)
+            this = products(pre_ref[at : at + block], weight, bias)
+        if last is not None:
+            out, gate = last
+            centre = out - jnp.mean(out, axis=-1, keepdims=True)
+            inv = lax.rsqrt(jnp.mean(centre * centre, axis=-1, keepdims=True) + EPS)
+            normed = (centre * inv).astype(BF16)
+            piece = slice(at - block, at)
+            normed_ref[piece] = normed
+            q_ref[piece] = dot_t(normed, weight).astype(BF16)
+            gate_ref[piece] = gate * inv
+        last = this
+
+
+def first_kernel(block, copies, pre_hbm, *refs):
+    sources, (me_ref, requests_hbm), refs = refs[:copies], refs[copies : copies + 2], refs[copies + 2 :]
+    targets, refs = refs[:copies], refs[copies:]
+    ids_ref, other_ref, normed_ref, q_ref, gate_ref, pre_ref, requests_ref, sem = refs
     rows = normed_ref.shape[0]
+
+    def load(k, source, target):
+        return pltpu.make_async_copy(source, target, sem.at[k])
+
+    others = [load(k, a, b) for k, (a, b) in enumerate(zip(sources, targets))]
+    starts = list(range(0, rows, block))
     loads = [
-        pltpu.make_async_copy(
-            pre_hbm.at[pl.ds(first + at, block)], pre_ref.at[pl.ds(at, block)], sem.at[at // block]
-        )
-        for at in range(0, rows, block)
+        load(copies + k, pre_hbm.at[pl.ds(at, block)], pre_ref.at[pl.ds(at, block)])
+        for k, at in enumerate(starts)
     ]
-    others = [pltpu.make_async_copy(a, b, other_sem.at[k]) for k, (a, b) in enumerate(zip(sources, targets))] if copies else []
-    for copy in others[:2] + loads + others[2:]:
+    more = load(copies + len(loads), pre_hbm.at[pl.ds(rows, rows)], other_ref)
+    asked = load(copies + len(loads) + 1, requests_hbm, requests_ref)
+    for copy in others[:2] + loads + others[2:] + [more, asked]:
         copy.start()
     for copy in others[:2]:
         copy.wait()
-    weight, bias = weight_ref[...], bias_ref[...]
-    for k, at in enumerate(range(0, rows, block)):
-        loads[k].wait()
-        piece = slice(at, at + block)
-        normed_ref[piece], q_ref[piece], gate_ref[piece] = edge_block(pre_ref[piece], weight, bias)
-    for copy in others[2:]:
+    edge_blocks(
+        pre_ref,
+        targets[0][...],
+        targets[1][...],
+        normed_ref,
+        q_ref,
+        gate_ref,
+        block,
+        lambda at: loads[at // block].wait(),
+    )
+    for copy in others[2:] + [more, asked]:
         copy.wait()
-    if copies:
-        slots, caps = ids_ref.shape[0], requests_ref.shape[2]
-        row = lax.broadcasted_iota(jnp.int32, ids_ref.shape, 0)
-        ids = jnp.zeros(ids_ref.shape, jnp.int32)
-        for r in range(slots):
-            ids = jnp.where(row == r, requests_ref[0, (r // caps) ^ me_ref[0], r % caps], ids)
-        ids_ref[...] = ids.astype(F32)
-
-
-def before(preact, first, rows, held, sources=(), given=(), me=None, requests=None, block=256):
-    width = preact.shape[1]
+    slots, caps = ids_ref.shape[0], requests_ref.shape[1]
+    row = lax.broadcasted_iota(jnp.int32, ids_ref.shape, 0)
+    ids = jnp.zeros(ids_ref.shape, jnp.int32)
+    for r in range(slots):
+        ids = jnp.where(row == r, requests_ref[0, r % caps, (r // caps) ^ me_ref[0]], ids)
+    ids_ref[...] = ids.astype(F32)
+
+
+def first_half(preact, sources, me, requests, block=512):
+    edges, width = preact.shape
+    rows = edges // 2
     copies = len(sources)
     outs = [in_vmem(a.shape, a.dtype) for a in sources]
-    if copies:
-        outs.append(in_vmem((requests.shape[1] * requests.shape[2], LANES), F32))
-    outs += [in_vmem((rows, width), BF16)] * 2 + [in_vmem((rows, width), F32)]
-    return pl.pallas_call(
-        functools.partial(before_kernel, first, block, copies),
-        in_specs=[HBM] * (1 + copies) + ([SMEM, SMEM] if copies else [VMEM, VMEM, ANY]),
+    outs += [in_vmem((requests.shape[1] * requests.shape[2], LANES), F32)]
+    outs += [in_vmem((rows, width), BF16)] * 3 + [in_vmem((rows, width), F32)]
+    return pl.pallas_call(
+        functools.partial(first_kernel, block, copies),
+        in_specs=[HBM] * (1 + copies) + [SMEM, HBM],
         out_specs=[VMEM] * len(outs),
         out_shape=outs,
-        scratch_shapes=[pltpu.VMEM((rows, width), BF16), DMA((rows // block,)), DMA((max(copies, 1),))],
+        scratch_shapes=[
+            pltpu.VMEM((rows, width), BF16),
+            pltpu.SMEM(requests.shape, jnp.int32),
+            DMA((copies + rows // block + 2,)),
+        ],
         cost_estimate=cost(6 * rows * width * width, 10 * rows * width),
         compiler_params=params(16),
-        name="before",
-    )(in_hbm(preact), *[in_hbm(a) for a in sources], *((me, requests) if copies else (*given, held)))
+        name="first_half",
+    )(in_hbm(preact), *[in_hbm(a) for a in sources], me, in_hbm(requests))
+
+
+def second_kernel(block, pre_ref, weight_ref, bias_ref, after_ref, normed_ref, q_ref, gate_ref):
+    edge_blocks(
+        pre_ref, weight_ref[...], bias_ref[...], normed_ref, q_ref, gate_ref, block, lambda at: None
+    )
+
+
+def second_half(pre, weight, bias, after, block=512):
+    rows, width = pre.shape
+    outs = [in_vmem((rows, width), BF16)] * 2 + [in_vmem((rows, width), F32)]
+    return pl.pallas_call(
+        functools.partial(second_kernel, block),
+        in_specs=[VMEM, VMEM, VMEM, ANY],
+        out_specs=[VMEM] * len(outs),
+        out_shape=outs,
+        cost_estimate=cost(6 * rows * width * width, 10 * rows * width),
+        compiler_params=params(16),
+        name="second_half",
+    )(pre, weight, bias, after)
+
+
+def join_kernel(parts, *refs):
+    out_ref, rows = refs[-1], refs[0].shape[0]
+    for k in range(parts):
+        out_ref[k * rows : (k + 1) * rows, :] = refs[k][...]
+
+
+def join(pieces, after):
+    rows, width = pieces[0].shape
+    return pl.pallas_call(
+        functools.partial(join_kernel, len(pieces)),
+        in_specs=[VMEM] * len(pieces) + [ANY],
+        out_specs=VMEM,
+        out_shape=in_vmem((len(pieces) * rows, width), pieces[0].dtype),
+        cost_estimate=cost(0, 4 * len(pieces) * rows * width),
+        compiler_params=params(8),
+        name="join",
+    )(*pieces, after)
 
 
 def after_kernel(
@@ -163,7 +214,7 @@
     piece_rows = pieces[0].shape[0]
     row = lax.broadcasted_iota(jnp.int32, (slots, 1), 0)
     far, place, step = row // 2, jnp.zeros_like(row), 1
-    for shift, radix in gather_stages(slots // 2):
+    for shift, radix in stages_of(slots // 2):
         place = place + ((far >> shift) & (radix - 1)) * step
         step *= radix
     place = place * owned + ids_ref[...][:, :1].astype(jnp.int32)
@@ -285,7 +336,7 @@
 
 
 def regroup_kernel(groups, parts, *refs):
-    outs = refs[parts:]
+    outs = refs[parts + 1 :]
     low = groups // len(outs)
     each = refs[0].shape[0] // groups
     for j, out_ref in enumerate(outs):
@@ -295,22 +346,22 @@
                 out_ref[to : to + each, :] = refs[k][at : at + each, :]
 
 
-def regroup(arrived, radix, low):
+def regroup(arrived, radix, low, after):
     rows, width = arrived[0].shape
     parts = len(arrived)
     return pl.pallas_call(
         functools.partial(regroup_kernel, radix * low, parts),
-        in_specs=[VMEM] * parts,
+        in_specs=[VMEM] * parts + [ANY],
         out_specs=[VMEM] * radix,
         out_shape=[in_vmem((rows * parts // radix, width), arrived[0].dtype)] * radix,
         cost_estimate=cost(0, 8 * rows * parts * width),
         compiler_params=params(8),
         name="regroup",
-    )(*arrived)
+    )(*arrived, after)
 
 
 def mesh_kernel(parts, *refs):
-    pieces, weight_ref, out_ref = refs[:parts], refs[parts], refs[parts + 1]
+    pieces, weight_ref, out_ref = refs[:parts], refs[parts], refs[-1]
     owned, width = out_ref.shape
     rows = jnp.concatenate([piece[...] for piece in pieces], axis=0)
     ids = rows[:, width:].T[:owned].astype(jnp.int32)
@@ -321,17 +372,17 @@
     out_ref[...] = (both[:owned] + both[owned:]).astype(BF16)
 
 
-def mesh_rows(pieces, weight, owned):
+def mesh_rows(pieces, weight, owned, after):
     width = weight.shape[0]
     return pl.pallas_call(
         functools.partial(mesh_kernel, len(pieces)),
-        in_specs=[VMEM] * (len(pieces) + 1),
+        in_specs=[VMEM] * (len(pieces) + 1) + [ANY],
         out_specs=VMEM,
         out_shape=like((owned, width), BF16),
         cost_estimate=cost(2 * owned * width * width, 2 * width * width),
         compiler_params=params(8),
         name="mesh_rows",
-    )(*pieces, weight)
+    )(*pieces, weight, in_hbm(after))
 
 
 def on_device(
@@ -350,21 +401,30 @@
     me = lax.axis_index("band")
     owned, width = mesh_cotangent.shape
     edges = saved_preact.shape[0]
-    half = edges // 2
-
-    held, seen = [mesh_cotangent], []
-    for shift, radix in gather_stages(count):
-        block = held[0] if len(held) == 1 else jnp.concatenate(held, axis=0)
-        seen.append(block)
-        held = [block] + [swap(block, count, j << shift) for j in range(1, radix)]
-
-    sources = (out_weight, out_bias.reshape(1, width), grid_weight, mesh_weight, ln_gain.reshape(1, width))
-    weight, bias, weight_g, weight_m, gain, ids, *first = before(
-        saved_preact, 0, half, None, sources, me=me.reshape(1), requests=mesh_requests
-    )
-    second = before(saved_preact, half, half, seen[1], given=(weight, bias))
-
-    stages = return_stages(count)
+    stages = stages_of(count)
+
+    sources = (
+        out_weight,
+        out_bias.reshape(1, width),
+        grid_weight,
+        mesh_weight,
+        ln_gain.reshape(1, width),
+        mesh_cotangent,
+    )
+    weight, bias, weight_g, weight_m, gain, own_rows, ids, more, *first = first_half(
+        saved_preact, sources, me.reshape(1), mesh_requests.swapaxes(1, 2)
+    )
+
+    held = [mesh_cotangent]
+    for number, (shift, radix) in enumerate(stages):
+        if number == 1:
+            held = [join([own_rows, *held[1:]], first[0])]
+        elif number > 1:
+            held = [join(held, ids)]
+        held += [swap(held[0], count, j << shift) for j in range(1, radix)]
+        if number == 1:
+            second = second_half(more, weight, bias, held[0])
+
     d_preact, rim, *chunks = after(
         me.reshape(1),
         ids,
@@ -378,15 +438,15 @@
         stages[0][1],
     )
 
+    grid_adjoint, head = grid_rows(edge_senders, d_preact, weight_g)
+    carried = lax.ppermute(rim, "band", [(i, i + 1) for i in range(count - 1)])
     arrived = None
     for shift, radix in stages:
         if arrived is not None:
-            chunks = regroup(arrived, radix, 1 << shift)
+            chunks = regroup(arrived, radix, 1 << shift, head)
         arrived = [chunks[0]] + [swap(chunks[j], count, j << shift) for j in range(1, radix)]
-    carried = lax.ppermute(rim, "band", [(i, i + 1) for i in range(count - 1)])
-    grid_adjoint, head = grid_rows(edge_senders, d_preact, weight_g)
     grid_adjoint = head_rows(grid_adjoint, head, carried, weight_g)
-    mesh_adjoint = mesh_rows(arrived, weight_m, owned)
+    mesh_adjoint = mesh_rows(arrived, weight_m, owned, grid_adjoint)
     return (grid_adjoint, mesh_adjoint)
 
 

time: 44.9 us -> 38 us (0.85)
  Pallas kernels: 21.7 us -> 16.7 us
  local copies, waits for them, and re-layouts: 1.57 us -> 0.01 us
  starting transfers between devices: 15.7 us -> 16.4 us
    pallas_call x2 -> x3, Pallas kernels: 12 us -> 6.9 us  [the longest x1 4.26 us: first_half(): pl.pallas_call(functools.partial(first_kernel, block, copies), in_specs=[...]
    unnamed x9 -> x4, local copies, waits for them, and re-layouts: 1.56 us -> 0.01 us
    ppermute x11 -> x12, starting transfers between devices: 14 us -> 14.9 us  [swap(): return lax.ppermute(block, 'band', [(i, i ^ mask) for i in range(count)])]
    ppermute x11 -> x12, waiting for transfers between devices: 4.42 us -> 4.03 us  [swap(): return lax.ppermute(block, 'band', [(i, i ^ mask) for i in range(count)])]
  transfers between devices with their start and end apart: 12 -> 13, of which waited for: 3 -> 4; matrix products, arithmetic and copies ran while one was open for 3% -> 0% of each run, Pallas kernels for 38% -> 31%
where the time goes in v3:
time: 38 us; the launch traced here: 37.9 us
  Pallas kernels  16.7 us (44%)
  starting transfers between devices  16.4 us (43%)
  waiting for transfers between devices  4.03 us (11%)
  between operations  0.76 us (2%)
    ppermute x12, starting transfers between devices, swap(): return lax.ppermute(block, 'band', [(i, i ^ mask) for i in range(count)])  14.9 us
    pallas_call x1, Pallas kernels, first_half(): pl.pallas_call(functools.partial(first_kernel, block, copies), in_specs=[...  4.26 us
    pallas_call x1, Pallas kernels, after(): pl.pallas_call(functools.partial(after_kernel, len(parts), len(pieces), c...  4.06 us
    ppermute x12, waiting for transfers between devices, swap(): return lax.ppermute(block, 'band', [(i, i ^ mask) for i in range(count)])  4.03 us
    pallas_call x1, Pallas kernels, grid_rows(): pl.pallas_call(functools.partial(grid_kernel, block), in_specs=[SMEM] + [...  3.72 us
    pallas_call x1, Pallas kernels, second_half(): pl.pallas_call(functools.partial(second_kernel, block), in_specs=[VMEM, V...  2.64 us
    ppermute x1, starting transfers between devices, on_device(): carried = lax.ppermute(rim, 'band', [(i, i + 1) for i in range(count - 1)])  1.47 us
    pallas_call x1, Pallas kernels, mesh_rows(): pl.pallas_call(functools.partial(mesh_kernel, len(pieces)), in_specs=[VME...  1 us
  transfers between devices with their start and end apart: 13, of which 4 were waited for; matrix products, arithmetic and copies ran while one was open for 0% of the time, Pallas kernels for 31%

profile of v3, /device:TPU:0, one launch (start us, length us, event | category | flops | bytes accessed | tf_op | source)
XLA Modules:
  0.0 37.9 jit_solution(14918286536198911518)
XLA Ops:
  0.6 3.1 %collective-permute-start = (bf16[16,512]{1,0:T(8,128)(2,1)}, bf16[16,512]{1,0:T(8,128)(2,1)S(1)}, u32[]{:S(2)}, u32[]{:S(2)}) collective-permute-start(bf16[16,512]{1,0:T(8,128)(2,1)} %refs_5_.1), channel_id=1, source_target_pairs={{0,4},{1,5},{2,6},{3,7},{4,0},{5,1},{6,2},{7,3},{8,12},{9,13},{10,... | collective-permute-start | bytes 49160 | tf_op jit(solution)/shard_map/ppermute | solution.py:37
  3.7 2.5 %collective-permute-start.2 = (bf16[16,512]{1,0:T(8,128)(2,1)}, bf16[16,512]{1,0:T(8,128)(2,1)S(1)}, u32[]{:S(2)}, u32[]{:S(2)}) collective-permute-start(bf16[16,512]{1,0:T(8,128)(2,1)} %refs_5_.1), channel_id=1, source_target_pairs={{0,12},{1,13},{2,14},{3,15},{4,8},{5,9},{6,10},{7,11},{8,4},{9,5},... | collective-permute-start | bytes 49160 | tf_op jit(solution)/shard_map/ppermute | solution.py:37
  6.2 0.1 collective-permute-start.1
  6.3 4.3 %first_half.1 = (bf16[512,512]{1,0:T(8,128)(2,1)S(1)}, f32[1,512]{1,0:T(1,128)S(1)}, bf16[512,512]{1,0:T(8,128)(2,1)S(1)}, bf16[512,512]{1,0:T(8,128)(2,1)S(1)},...) custom-call(bf16[3072,512]{1,0:T(8,128)(2,1)} %pre_hbm.1, ...), custom_call_target="tpu_custom_call" | custom-call | flops 2415919104 | bytes 7864320 | tf_op jit(solution)/shard_map/first_half/pallas_call | solution.py:147
  10.6 0.0 collective-permute-done.refs_1_
  10.6 0.0 collective-permute-done.2.refs_3_
  10.6 0.5 %collective-permute-done.1.refs_2_ = bf16[16,512]{1,0:T(8,128)(2,1)S(1)} collective-permute-done((bf16[16,512]{1,0:T(8,128)(2,1)}, bf16[16,512]{1,0:T(8,128)(2,1)S(1)}, u32[]{:S(2)}, u32[]{:S(2)}) %collective-permute-start.1) | collective-permute-done | bytes 16416 | tf_op jit(solution)/shard_map/ppermute | solution.py:37
  11.1 1.6 %collective-permute-start.4 = (bf16[64,512]{1,0:T(8,128)(2,1)S(1)}, bf16[64,512]{1,0:T(8,128)(2,1)S(1)}, u32[]{:S(2)}, u32[]{:S(2)}) collective-permute-start(bf16[64,512]{1,0:T(8,128)(2,1)S(1)} %join.1.after_ref.refs_6_), channel_id=1, source_target_pairs={{0,2},{1,3},{2,0},{3,1},{4,6},{5,7},{6,4},{7,5},{8,10},{9,11},{10,... | collective-permute-start | bytes 196616 | tf_op jit(solution)/shard_map/ppermute | solution.py:37
  12.6 0.3 collective-permute-start.3
  12.9 2.6 %second_half.1 = (bf16[1536,512]{1,0:T(8,128)(2,1)S(1)}, bf16[1536,512]{1,0:T(8,128)(2,1)S(1)}, f32[1536,512]{1,0:T(8,128)S(1)}) custom-call(bf16[1536,512]{1,0:T(8,128)(2,1)S(1)} %get-tuple-element.34.pre_ref, bf16[512,512]{1,0:T(8,128)(2,1)S(1)} %get-tuple-element.29.weight_ref, f32[1,512]{1,0:T(1,128)S(1)} %get-tuple-element.35.bias_ref, ...), custom_call_target="tpu_custom_call" | custom-call | flops 2415919104 | bytes 7864320 | tf_op jit(solution)/shard_map/second_half/pallas_call | solution.py:172
  15.6 1.3 %collective-permute-done.4.refs_8_ = bf16[64,512]{1,0:T(8,128)(2,1)S(1)} collective-permute-done((bf16[64,512]{1,0:T(8,128)(2,1)S(1)}, bf16[64,512]{1,0:T(8,128)(2,1)S(1)}, u32[]{:S(2)}, u32[]{:S(2)}) %collective-permute-start.4) | collective-permute-done | bytes 65568 | tf_op jit(solution)/shard_map/ppermute | solution.py:37
  16.9 4.1 %after.1 = (bf16[3072,512]{1,0:T(8,128)(2,1)S(1)}, f32[128,512]{1,0:T(8,128)S(1)}, f32[8,640]{1,0:T(8,128)S(1)}, f32[8,640]{1,0:T(8,128)S(1)}, f32[8,640]{1,0:T(8,128)S(1)}, /*index=5*/f32[8,640]{1,0:T(8,128)S(1)}) custom-call(s32[1]{0:T(128)} %bitcast.1.refs_6_.me_ref, f32[32,128]{1,0:T(8,128)S(1)} %get-tuple-element.28.ids_ref, s32[1,3072]{1,0:T(1,128)S(1)} %bitcast.6, ...), custom_call_target="tpu_custom_call" | custom-call | flops 4831838208 | bytes 12582912 | tf_op jit(solution)/shard_map/after/pallas_call | solution.py:262
  20.9 1.5 %collective-permute-start.7 = (f32[8,640]{1,0:T(8,128)S(1)}, f32[8,640]{1,0:T(8,128)S(1)}, u32[]{:S(2)}, u32[]{:S(2)}) collective-permute-start(f32[8,640]{1,0:T(8,128)S(1)} %get-tuple-element.46), channel_id=1, source_target_pairs={{0,4},{1,5},{2,6},{3,7},{4,0},{5,1},{6,2},{7,3},{8,12},{9,13},{10,... | collective-permute-start | bytes 61448 | tf_op jit(solution)/shard_map/ppermute | solution.py:37
  22.4 1.7 %collective-permute-start.8 = (f32[8,640]{1,0:T(8,128)S(1)}, f32[8,640]{1,0:T(8,128)S(1)}, u32[]{:S(2)}, u32[]{:S(2)}) collective-permute-start(f32[8,640]{1,0:T(8,128)S(1)} %get-tuple-element.47), channel_id=1, source_target_pairs={{0,8},{1,9},{2,10},{3,11},{4,12},{5,13},{6,14},{7,15},{8,0},{9,1},... | collective-permute-start | bytes 61448 | tf_op jit(solution)/shard_map/ppermute | solution.py:37
  24.1 1.3 %collective-permute-start.9 = (f32[8,640]{1,0:T(8,128)S(1)}, f32[8,640]{1,0:T(8,128)S(1)}, u32[]{:S(2)}, u32[]{:S(2)}) collective-permute-start(f32[8,640]{1,0:T(8,128)S(1)} %get-tuple-element.48), channel_id=1, source_target_pairs={{0,12},{1,13},{2,14},{3,15},{4,8},{5,9},{6,10},{7,11},{8,4},{9,5},... | collective-permute-start | bytes 61448 | tf_op jit(solution)/shard_map/ppermute | solution.py:37
  25.4 1.5 %collective-permute-start.6 = (f32[128,512]{1,0:T(8,128)S(1)}, f32[128,512]{1,0:T(8,128)S(1)}, u32[]{:S(2)}, u32[]{:S(2)}) collective-permute-start(f32[128,512]{1,0:T(8,128)S(1)} %get-tuple-element.44), channel_id=1, source_target_pairs={{0,1},{1,2},{2,3},{3,4},{4,5},{5,6},{6,7},{7,8},{8,9},{9,10},{10,1... | collective-permute-start | bytes 786440 | tf_op jit(solution)/shard_map/ppermute | solution.py:442
  26.9 3.7 %grid_rows.1 = (bf16[2048,512]{1,0:T(8,128)(2,1)}, f32[128,512]{1,0:T(8,128)S(1)}) custom-call(s32[3072]{0:T(1024)S(1)} %copy-done.1, s32[1,3072]{1,0:T(1,128)S(1)} %bitcast.8, bf16[3072,512]{1,0:T(8,128)(2,1)S(1)} %get-tuple-element.40.d_ref, bf16[512,512]{1,0:T(8,128)(2,1)S(1)} %get-tuple-element.41.weight_ref), custom_call_target="tpu_custom_call" | custom-call | flops 3221225472 | bytes 6291456 | tf_op jit(solution)/shard_map/grid_rows/pallas_call | solution.py:300
  30.7 1.5 %collective-permute-start.10 = (f32[8,640]{1,0:T(8,128)S(1)}, f32[8,640]{1,0:T(8,128)S(1)}, u32[]{:S(2)}, u32[]{:S(2)}) collective-permute-start(f32[8,640]{1,0:T(8,128)S(1)} %get-tuple-element.50), channel_id=1, source_target_pairs={{0,1},{1,0},{2,3},{3,2},{4,5},{5,4},{6,7},{7,6},{8,9},{9,8},{10,11... | collective-permute-start | bytes 61448 | tf_op jit(solution)/shard_map/ppermute | solution.py:37
  32.1 1.3 %collective-permute-start.11 = (f32[8,640]{1,0:T(8,128)S(1)}, f32[8,640]{1,0:T(8,128)S(1)}, u32[]{:S(2)}, u32[]{:S(2)}) collective-permute-start(f32[8,640]{1,0:T(8,128)S(1)} %get-tuple-element.51), channel_id=1, source_target_pairs={{0,2},{1,3},{2,0},{3,1},{4,6},{5,7},{6,4},{7,5},{8,10},{9,11},{10,... | collective-permute-start | bytes 61448 | tf_op jit(solution)/shard_map/ppermute | solution.py:37
  33.4 0.1 collective-permute-start.12
  33.6 1.0 %head_rows.1.refs_5_ = bf16[2048,512]{1,0:T(8,128)(2,1)} custom-call(bf16[2048,512]{1,0:T(8,128)(2,1)} %get-tuple-element.42.grid_in, f32[128,512]{1,0:T(8,128)S(1)} %get-tuple-element.43.head_ref.refs_4_, f32[128,512]{1,0:T(8,128)S(1)} %collective-permute-done.6.rim_ref, ...), custom_call_target="tpu_custom_call", output_to_operand_aliasing={{}: (0, {})} | custom-call | flops 67108864 | bytes 262144 | tf_op jit(solution)/shard_map/head_rows/pallas_call | solution.py:325
  34.6 1.4 %collective-permute-done.11.refs_2_ = f32[8,640]{1,0:T(8,128)S(1)} collective-permute-done((f32[8,640]{1,0:T(8,128)S(1)}, f32[8,640]{1,0:T(8,128)S(1)}, u32[]{:S(2)}, u32[]{:S(2)}) %collective-permute-start.11) | collective-permute-done | bytes 20512 | tf_op jit(solution)/shard_map/ppermute | solution.py:37
  35.9 0.9 %collective-permute-done.12.refs_3_ = f32[8,640]{1,0:T(8,128)S(1)} collective-permute-done((f32[8,640]{1,0:T(8,128)S(1)}, f32[8,640]{1,0:T(8,128)S(1)}, u32[]{:S(2)}, u32[]{:S(2)}) %collective-permute-start.12) | collective-permute-done | bytes 20512 | tf_op jit(solution)/shard_map/ppermute | solution.py:37
  36.9 1.0 %mesh_rows.1 = bf16[16,512]{1,0:T(8,128)(2,1)} custom-call(f32[8,640]{1,0:T(8,128)S(1)} %get-tuple-element.49.refs_0_, f32[8,640]{1,0:T(8,128)S(1)} %collective-permute-done.10.refs_1_, f32[8,640]{1,0:T(8,128)S(1)} %collective-permute-done.11.refs_2_, f32[8,640]{1,0:T(8,128)S(1)} %collective-permute-done.12.refs_3_, ...), custom_call_target="tpu_custom_call" | custom-call | flops 8388608 | bytes 524288 | tf_op jit(solution)/shard_map/mesh_rows/pallas_call | solution.py:377
  (14 shorter events, 0.1 us)
Async XLA Ops:
  0.6 9.9 %collective-permute-start = (bf16[16,512]{1,0:T(8,128)(2,1)}, bf16[16,512]{1,0:T(8,128)(2,1)S(1)}, u32[]{:S(2)}, u32[]{:S(2)}) collective-permute-start(bf16[16,512]{1,0:T(8,128)(2,1)} %refs_5_.1), channel_id=1, source_target_pairs={{0,4},{1,5},{2,6},{3,7},{4,0},{5,1},{6,2},{7,3},{8,12},{9,13},{10,... | collective-permute-start | bytes 49160 | tf_op jit(solution)/shard_map/ppermute | solution.py:37
  3.7 6.9 %collective-permute-start.2 = (bf16[16,512]{1,0:T(8,128)(2,1)}, bf16[16,512]{1,0:T(8,128)(2,1)S(1)}, u32[]{:S(2)}, u32[]{:S(2)}) collective-permute-start(bf16[16,512]{1,0:T(8,128)(2,1)} %refs_5_.1), channel_id=1, source_target_pairs={{0,12},{1,13},{2,14},{3,15},{4,8},{5,9},{6,10},{7,11},{8,4},{9,5},... | collective-permute-start | bytes 49160 | tf_op jit(solution)/shard_map/ppermute | solution.py:37
  6.2 4.9 %collective-permute-start.1 = (bf16[16,512]{1,0:T(8,128)(2,1)}, bf16[16,512]{1,0:T(8,128)(2,1)S(1)}, u32[]{:S(2)}, u32[]{:S(2)}) collective-permute-start(bf16[16,512]{1,0:T(8,128)(2,1)} %refs_5_.1), channel_id=1, source_target_pairs={{0,8},{1,9},{2,10},{3,11},{4,12},{5,13},{6,14},{7,15},{8,0},{9,1},... | collective-permute-start | bytes 49160 | tf_op jit(solution)/shard_map/ppermute | solution.py:37
  11.1 4.5 %collective-permute-start.5 = (bf16[64,512]{1,0:T(8,128)(2,1)S(1)}, bf16[64,512]{1,0:T(8,128)(2,1)S(1)}, u32[]{:S(2)}, u32[]{:S(2)}) collective-permute-start(bf16[64,512]{1,0:T(8,128)(2,1)S(1)} %join.1.after_ref.refs_6_), channel_id=1, source_target_pairs={{0,3},{1,2},{2,1},{3,0},{4,7},{5,6},{6,5},{7,4},{8,11},{9,10},{10,... | collective-permute-start | bytes 196616 | tf_op jit(solution)/shard_map/ppermute | solution.py:37
  11.1 5.8 %collective-permute-start.4 = (bf16[64,512]{1,0:T(8,128)(2,1)S(1)}, bf16[64,512]{1,0:T(8,128)(2,1)S(1)}, u32[]{:S(2)}, u32[]{:S(2)}) collective-permute-start(bf16[64,512]{1,0:T(8,128)(2,1)S(1)} %join.1.after_ref.refs_6_), channel_id=1, source_target_pairs={{0,2},{1,3},{2,0},{3,1},{4,6},{5,7},{6,4},{7,5},{8,10},{9,11},{10,... | collective-permute-start | bytes 196616 | tf_op jit(solution)/shard_map/ppermute | solution.py:37
  12.6 4.2 %collective-permute-start.3 = (bf16[64,512]{1,0:T(8,128)(2,1)S(1)}, bf16[64,512]{1,0:T(8,128)(2,1)S(1)}, u32[]{:S(2)}, u32[]{:S(2)}) collective-permute-start(bf16[64,512]{1,0:T(8,128)(2,1)S(1)} %join.1.after_ref.refs_6_), channel_id=1, source_target_pairs={{0,1},{1,0},{2,3},{3,2},{4,5},{5,4},{6,7},{7,6},{8,9},{9,8},{10,11... | collective-permute-start | bytes 196616 | tf_op jit(solution)/shard_map/ppermute | solution.py:37
  12.9 3.9 %copy-start = (s32[3072]{0:T(1024)S(1)}, s32[3072]{0:T(1024)}, u32[]{:S(2)}) copy-start(s32[3072]{0:T(1024)} %param.12) | copy-start | bytes 36868
  12.9 3.9 %copy-start.1 = (s32[3072]{0:T(1024)S(1)}, s32[3072]{0:T(1024)}, u32[]{:S(2)}) copy-start(s32[3072]{0:T(1024)} %starts_ref.1) | copy-start | bytes 36868
  20.9 9.7 %collective-permute-start.7 = (f32[8,640]{1,0:T(8,128)S(1)}, f32[8,640]{1,0:T(8,128)S(1)}, u32[]{:S(2)}, u32[]{:S(2)}) collective-permute-start(f32[8,640]{1,0:T(8,128)S(1)} %get-tuple-element.46), channel_id=1, source_target_pairs={{0,4},{1,5},{2,6},{3,7},{4,0},{5,1},{6,2},{7,3},{8,12},{9,13},{10,... | collective-permute-start | bytes 61448 | tf_op jit(solution)/shard_map/ppermute | solution.py:37
  22.4 8.2 %collective-permute-start.8 = (f32[8,640]{1,0:T(8,128)S(1)}, f32[8,640]{1,0:T(8,128)S(1)}, u32[]{:S(2)}, u32[]{:S(2)}) collective-permute-start(f32[8,640]{1,0:T(8,128)S(1)} %get-tuple-element.47), channel_id=1, source_target_pairs={{0,8},{1,9},{2,10},{3,11},{4,12},{5,13},{6,14},{7,15},{8,0},{9,1},... | collective-permute-start | bytes 61448 | tf_op jit(solution)/shard_map/ppermute | solution.py:37
  24.1 6.5 %collective-permute-start.9 = (f32[8,640]{1,0:T(8,128)S(1)}, f32[8,640]{1,0:T(8,128)S(1)}, u32[]{:S(2)}, u32[]{:S(2)}) collective-permute-start(f32[8,640]{1,0:T(8,128)S(1)} %get-tuple-element.48), channel_id=1, source_target_pairs={{0,12},{1,13},{2,14},{3,15},{4,8},{5,9},{6,10},{7,11},{8,4},{9,5},... | collective-permute-start | bytes 61448 | tf_op jit(solution)/shard_map/ppermute | solution.py:37
  25.4 8.2 %collective-permute-start.6 = (f32[128,512]{1,0:T(8,128)S(1)}, f32[128,512]{1,0:T(8,128)S(1)}, u32[]{:S(2)}, u32[]{:S(2)}) collective-permute-start(f32[128,512]{1,0:T(8,128)S(1)} %get-tuple-element.44), channel_id=1, source_target_pairs={{0,1},{1,2},{2,3},{3,4},{4,5},{5,6},{6,7},{7,8},{8,9},{9,10},{10,1... | collective-permute-start | bytes 786440 | tf_op jit(solution)/shard_map/ppermute | solution.py:442
  30.7 3.9 %collective-permute-start.10 = (f32[8,640]{1,0:T(8,128)S(1)}, f32[8,640]{1,0:T(8,128)S(1)}, u32[]{:S(2)}, u32[]{:S(2)}) collective-permute-start(f32[8,640]{1,0:T(8,128)S(1)} %get-tuple-element.50), channel_id=1, source_target_pairs={{0,1},{1,0},{2,3},{3,2},{4,5},{5,4},{6,7},{7,6},{8,9},{9,8},{10,11... | collective-permute-start | bytes 61448 | tf_op jit(solution)/shard_map/ppermute | solution.py:37
  32.1 3.8 %collective-permute-start.11 = (f32[8,640]{1,0:T(8,128)S(1)}, f32[8,640]{1,0:T(8,128)S(1)}, u32[]{:S(2)}, u32[]{:S(2)}) collective-permute-start(f32[8,640]{1,0:T(8,128)S(1)} %get-tuple-element.51), channel_id=1, source_target_pairs={{0,2},{1,3},{2,0},{3,1},{4,6},{5,7},{6,4},{7,5},{8,10},{9,11},{10,... | collective-permute-start | bytes 61448 | tf_op jit(solution)/shard_map/ppermute | solution.py:37
  33.4 3.4 %collective-permute-start.12 = (f32[8,640]{1,0:T(8,128)S(1)}, f32[8,640]{1,0:T(8,128)S(1)}, u32[]{:S(2)}, u32[]{:S(2)}) collective-permute-start(f32[8,640]{1,0:T(8,128)S(1)} %get-tuple-element.52), channel_id=1, source_target_pairs={{0,3},{1,2},{2,1},{3,0},{4,7},{5,6},{6,5},{7,4},{8,11},{9,10},{10,... | collective-permute-start | bytes 61448 | tf_op jit(solution)/shard_map/ppermute | solution.py:37

commit v4 on v3

v4 whole, which is shorter than its diff:
```python
import functools

import jax
import jax.numpy as jnp
from jax import lax
from jax.experimental import pallas as pl
from jax.experimental.pallas import tpu as pltpu
from jax.sharding import PartitionSpec as P

G_DEV = 2048
RIM = 128
LANES = 128
EPS = 1e-05
MIB = 1 << 20

BF16 = jnp.bfloat16
F32 = jnp.float32
VMEM = pl.BlockSpec(memory_space=pltpu.VMEM)
SMEM = pl.BlockSpec(memory_space=pltpu.SMEM)
HBM = pl.BlockSpec(memory_space=pltpu.HBM)
ANY = pl.BlockSpec(memory_space=pl.ANY)
DMA = pltpu.SemaphoreType.DMA


def stages_of(count):
    top = count.bit_length() - 1
    assert count == 1 << top
    stages = []
    while top > 0:
        low = max(0, top - 2)
        stages.append((low, 1 << (top - low)))
        top = low
    return stages


def distance_of(row, caps, count):
    group, distance, left = row // caps, 0, count
    for shift, radix in reversed(stages_of(count)):
        left //= radix
        distance = distance + ((group // left) % radix << shift)
    return distance


def swap(block, count, mask):
    return lax.ppermute(block, "band", [(i, i ^ mask) for i in range(count)])


def pass_on(block, count, distance):
    return lax.ppermute(block, "band", [(i, (i + distance) % count) for i in range(count)])


def like(shape, dtype):
    return jax.ShapeDtypeStruct(shape, dtype)


def in_hbm(x):
    return pltpu.with_memory_space_constraint(x, pltpu.HBM)


def in_vmem(shape, dtype):
    return pltpu.VMEM(shape, dtype)


def dot(a, b):
    return jnp.dot(a, b, preferred_element_type=F32)


def dot_t(a, b):
    return lax.dot_general(a, b, (((1,), (1,)), ((), ())), preferred_element_type=F32)


def split(x):
    high = x.astype(BF16)
    return high, (x - high.astype(F32)).astype(BF16)


def cost(flops, size):
    return pl.CostEstimate(flops=int(flops), bytes_accessed=int(size), transcendentals=0)


def params(limit):
    return pltpu.CompilerParams(vmem_limit_bytes=limit * MIB)


def products(pre, weight, bias):
    p = pre.astype(F32)
    s = 0.5 * jnp.tanh(0.5 * p) + 0.5
    h = p * s
    return dot(h.astype(BF16), weight) + bias, s + h * (1.0 - s)


def edge_blocks(pre_ref, weight, bias, normed_ref, q_ref, gate_ref, block, arrive):
    rows, last = pre_ref.shape[0], None
    for at in range(0, rows + block, block):
        this = None
        if at < rows:
            arrive(at)
            this = products(pre_ref[at : at + block], weight, bias)
        if last is not None:
            out, gate = last
            centre = out - jnp.mean(out, axis=-1, keepdims=True)
            inv = lax.rsqrt(jnp.mean(centre * centre, axis=-1, keepdims=True) + EPS)
            normed = (centre * inv).astype(BF16)
            piece = slice(at - block, at)
            normed_ref[piece] = normed
            q_ref[piece] = dot_t(normed, weight).astype(BF16)
            gate_ref[piece] = gate * inv
        last = this


def first_kernel(block, copies, pre_hbm, *refs):
    sources, (me_ref, requests_hbm), refs = refs[:copies], refs[copies : copies + 2], refs[copies + 2 :]
    targets, refs = refs[:copies], refs[copies:]
    ids_ref, other_ref, normed_ref, q_ref, gate_ref, pre_ref, requests_ref, sem = refs
    rows = normed_ref.shape[0]

    def load(k, source, target):
        return pltpu.make_async_copy(source, target, sem.at[k])

    others = [load(k, a, b) for k, (a, b) in enumerate(zip(sources, targets))]
    starts = list(range(0, rows, block))
    more_rows = other_ref.shape[0]
    loads = [
        load(copies + k, pre_hbm.at[pl.ds(at, block)], pre_ref.at[pl.ds(at, block)])
        for k, at in enumerate(starts)
    ]
    more = load(copies + len(loads), pre_hbm.at[pl.ds(rows, more_rows)], other_ref)
    asked = load(copies + len(loads) + 1, requests_hbm, requests_ref)
    for copy in others[:2] + loads + others[2:] + [more, asked]:
        copy.start()
    for copy in others[:2]:
        copy.wait()
    edge_blocks(
        pre_ref,
        targets[0][...],
        targets[1][...],
        normed_ref,
        q_ref,
        gate_ref,
        block,
        lambda at: loads[at // block].wait(),
    )
    for copy in others[2:] + [more, asked]:
        copy.wait()
    slots, caps = ids_ref.shape[0], requests_ref.shape[1]
    count = slots // caps
    row = lax.broadcasted_iota(jnp.int32, ids_ref.shape, 0)
    ids = jnp.zeros(ids_ref.shape, jnp.int32)
    for r in range(slots):
        owner = (me_ref[0] + distance_of(r, caps, count)) % count
        ids = jnp.where(row == r, requests_ref[0, r % caps, owner], ids)
    ids_ref[...] = ids.astype(F32)


def first_part(preact, rows, sources, me, requests, block=512):
    edges, width = preact.shape
    copies = len(sources)
    outs = [in_vmem(a.shape, a.dtype) for a in sources]
    outs += [in_vmem((requests.shape[1] * requests.shape[2], LANES), F32)]
    outs += [in_vmem((edges - rows, width), BF16)]
    outs += [in_vmem((rows, width), BF16)] * 2 + [in_vmem((rows, width), F32)]
    return pl.pallas_call(
        functools.partial(first_kernel, block, copies),
        in_specs=[HBM] * (1 + copies) + [SMEM, HBM],
        out_specs=[VMEM] * len(outs),
        out_shape=outs,
        scratch_shapes=[
            pltpu.VMEM((rows, width), BF16),
            pltpu.SMEM(requests.shape, jnp.int32),
            DMA((copies + rows // block + 2,)),
        ],
        cost_estimate=cost(6 * rows * width * width, 10 * rows * width),
        compiler_params=params(16),
        name="first_part",
    )(in_hbm(preact), *[in_hbm(a) for a in sources], me, in_hbm(requests))


def second_kernel(block, pre_ref, weight_ref, bias_ref, after_ref, normed_ref, q_ref, gate_ref):
    edge_blocks(
        pre_ref, weight_ref[...], bias_ref[...], normed_ref, q_ref, gate_ref, block, lambda at: None
    )


def second_part(pre, weight, bias, after, block=512):
    rows, width = pre.shape
    outs = [in_vmem((rows, width), BF16)] * 2 + [in_vmem((rows, width), F32)]
    return pl.pallas_call(
        functools.partial(second_kernel, block),
        in_specs=[VMEM, VMEM, VMEM, ANY],
        out_specs=[VMEM] * len(outs),
        out_shape=outs,
        cost_estimate=cost(6 * rows * width * width, 10 * rows * width),
        compiler_params=params(16),
        name="second_part",
    )(pre, weight, bias, after)


def join_kernel(parts, *refs):
    out_ref, rows = refs[-1], refs[0].shape[0]
    for k in range(parts):
        out_ref[k * rows : (k + 1) * rows, :] = refs[k][...]


def join(pieces, after):
    rows, width = pieces[0].shape
    return pl.pallas_call(
        functools.partial(join_kernel, len(pieces)),
        in_specs=[VMEM] * len(pieces) + [ANY],
        out_specs=VMEM,
        out_shape=in_vmem((len(pieces) * rows, width), pieces[0].dtype),
        cost_estimate=cost(0, 4 * len(pieces) * rows * width),
        compiler_params=params(8),
        name="join",
    )(*pieces, after)


def after_kernel(
    parts, chunks, owned, caps, block, me_ref, ids_ref, slots_ref, senders_ref, weight_ref, gain_ref, *refs
):
    edge_refs = [refs[3 * k : 3 * k + 3] for k in range(parts)]
    refs = refs[3 * parts :]
    d_ref, sums_refs = refs[-1 - chunks], refs[-chunks:]
    pieces = refs[: -1 - chunks]
    slots = ids_ref.shape[0]
    count = slots // caps
    edges, width = d_ref.shape
    me = me_ref[0]
    weight = weight_ref[...]

    row = lax.broadcasted_iota(jnp.int32, (slots, 1), 0)
    owner = (distance_of(row, caps, count) + me) % count
    far, place, step = owner ^ me, jnp.zeros_like(row), 1
    for shift, radix in stages_of(count):
        place = place + ((far >> shift) & (radix - 1)) * step
        step *= radix
    place = place * owned + ids_ref[...][:, :1].astype(jnp.int32)
    piece_rows = pieces[0].shape[0]
    column = lax.broadcasted_iota(jnp.int32, (slots, piece_rows), 1)
    rows = jnp.zeros((slots, width), F32)
    for k, piece in enumerate(pieces):
        pick = (place == column + k * piece_rows).astype(F32).astype(BF16)
        rows += dot(pick, piece[...])
    rows = rows * gain_ref[...]
    rows = rows - jnp.mean(rows, axis=-1, keepdims=True)
    mean_rows = (rows * (1.0 / width)).astype(BF16)
    both = dot_t(jnp.concatenate(split(rows), axis=0), weight)
    s_both = jnp.concatenate(split(both[:slots] + both[slots:]), axis=0)

    key = owner * caps + row % caps
    rim_row = lax.broadcasted_iota(jnp.int32, (RIM, block), 0) + G_DEV
    sums = jnp.zeros((slots, width), F32)
    rim = jnp.zeros((RIM, width), F32)
    edge_at = [(part, at) for part in edge_refs for at in range(0, part[0].shape[0], block)]
    last = None
    for number in range(len(edge_at) + 1):
        this = None
        if number < len(edge_at):
            (normed_ref, q_ref, gate_ref), at = edge_at[number]
            piece = slice(at, at + block)
            onehot_t = (key == slots_ref[:, number * block : (number + 1) * block]).astype(F32)
            onehot = onehot_t.T
            c = jnp.sum(onehot * dot_t(normed_ref[piece], mean_rows), axis=-1, keepdims=True)
            onehot = onehot.astype(BF16)
            s_rows = dot(jnp.concatenate([onehot, onehot], axis=1), s_both)
            this = (onehot_t.astype(BF16), c, s_rows, q_ref, gate_ref, piece)
        if last is not None:
            onehot_t, c, s_rows, q_ref, gate_ref, piece = last
            at = (number - 1) * block
            d = (gate_ref[piece] * (s_rows - c * q_ref[piece].astype(F32))).astype(BF16)
            d_ref[at : at + block, :] = d
            sums += dot(onehot_t, d)
            if at + block > G_DEV:
                pick = (rim_row == senders_ref[:, at : at + block]).astype(F32).astype(BF16)
                rim += dot(pick, d)
        last = this

    each = slots // chunks
    for k, sums_ref in enumerate(sums_refs):
        sums_ref[:each, :] = sums[k * each : (k + 1) * each]
        for at in range(0, width, LANES):
            sums_ref[each : 2 * each, at : at + LANES] = ids_ref[k * each : (k + 1) * each, :]
    sums_refs[1][2 * each :, :] = rim


def after(me, ids, slots, senders, weight, gain, parts, pieces, owned, caps, chunks, block=512):
    edges, width = slots.shape[1], weight.shape[0]
    each = ids.shape[0] // chunks
    sizes = [2 * each + (RIM if k == 1 else 0) for k in range(chunks)]
    return pl.pallas_call(
        functools.partial(after_kernel, len(parts), chunks, owned, caps, block),
        in_specs=[SMEM] + [VMEM] * (5 + 3 * len(parts) + len(pieces)),
        out_specs=[VMEM] * (1 + chunks),
        out_shape=[in_vmem((edges, width), BF16)] + [in_vmem((size, width), F32) for size in sizes],
        cost_estimate=cost(6 * edges * width * width, 8 * edges * width),
        compiler_params=params(20),
        name="after",
    )(me, ids, slots, senders, weight, gain, *[a for part in parts for a in part], *pieces)


def segments_kernel(block, starts_ref, senders_ref, d_ref, total_ref):
    edges, width = d_ref.shape
    total_ref[:8, :] = jnp.zeros((8, width), F32)
    row = lax.broadcasted_iota(jnp.int32, (block + 16, block), 0)
    for at in range(0, edges, block):
        base = pl.multiple_of(starts_ref[at] // 8 * 8, 8)
        onehot = (row == senders_ref[:, at : at + block] - base).astype(F32).astype(BF16)
        sums = dot(onehot, d_ref[at : at + block, :])
        total_ref[pl.ds(base, 8), :] += sums[:8]
        total_ref[pl.ds(pl.multiple_of(base + 8, 8), block + 8), :] = sums[8:]


def segments(senders, d_preact, block=256):
    edges, width = d_preact.shape
    return pl.pallas_call(
        functools.partial(segments_kernel, block),
        in_specs=[SMEM] + [VMEM] * 2,
        out_specs=VMEM,
        out_shape=in_vmem((G_DEV + RIM + block + 16, width), F32),
        cost_estimate=cost(4 * edges * width * width, 4 * edges * width),
        compiler_params=params(16),
        name="segments",
    )(senders, senders.reshape(1, edges), d_preact)


def grid_kernel(block, total_ref, carried_ref, weight_ref, out_hbm, out_ref, sem):
    weight = weight_ref[...]
    copies = []
    for k, at in enumerate(range(0, G_DEV, block)):
        rows = total_ref[at : at + block, :]
        if at == 0:
            rim = carried_ref[carried_ref.shape[0] - RIM :, :]
            rows = jnp.concatenate([rows[:RIM] + rim, rows[RIM:]], axis=0)
        out_ref[at : at + block, :] = dot_t(rows.astype(BF16), weight).astype(BF16)
        copies.append(
            pltpu.make_async_copy(out_ref.at[pl.ds(at, block)], out_hbm.at[pl.ds(at, block)], sem.at[k])
        )
        copies[-1].start()
    for copy in copies:
        copy.wait()


def grid_rows(total, carried, weight, block=512):
    width = weight.shape[0]
    return pl.pallas_call(
        functools.partial(grid_kernel, block),
        in_specs=[VMEM] * 3,
        out_specs=HBM,
        out_shape=like((G_DEV, width), BF16),
        scratch_shapes=[pltpu.VMEM((G_DEV, width), BF16), DMA((G_DEV // block,))],
        cost_estimate=cost(2 * G_DEV * width * width, 6 * G_DEV * width),
        compiler_params=params(16),
        name="grid_rows",
    )(total, carried, weight)


def regroup_kernel(groups, parts, rows, *refs):
    outs = refs[parts + 1 :]
    low = groups // len(outs)
    each = rows // groups
    for j, out_ref in enumerate(outs):
        half = out_ref.shape[0] // 2
        for g in range(low):
            for k in range(parts):
                to, at = (g * parts + k) * each, (j * low + g) * each
                out_ref[to : to + each, :] = refs[k][at : at + each, :]
                out_ref[half + to : half + to + each, :] = refs[k][rows + at : rows + at + each, :]


def regroup(arrived, radix, low, after):
    height, width = arrived[0].shape
    parts = len(arrived)
    return pl.pallas_call(
        functools.partial(regroup_kernel, radix * low, parts, height // 2),
        in_specs=[VMEM] * parts + [ANY],
        out_specs=[VMEM] * radix,
        out_shape=[in_vmem((height * parts // radix, width), arrived[0].dtype)] * radix,
        cost_estimate=cost(0, 8 * height * parts * width),
        compiler_params=params(8),
        name="regroup",
    )(*arrived, after)


def mesh_kernel(parts, *refs):
    pieces, weight_ref, out_ref = refs[:parts], refs[parts], refs[-1]
    owned, width = out_ref.shape
    half = pieces[0].shape[0] // 2
    rows = jnp.concatenate([piece[:half, :] for piece in pieces], axis=0)
    ids = jnp.concatenate([piece[half:, :LANES] for piece in pieces], axis=0)
    ids = ids.T[:owned].astype(jnp.int32)
    pick = (lax.broadcasted_iota(jnp.int32, ids.shape, 0) == ids).astype(F32).astype(BF16)
    high, low = split(rows)
    high, low = split(dot(pick, high) + dot(pick, low))
    both = dot_t(jnp.concatenate([high, low], axis=0), weight_ref[...])
    out_ref[...] = (both[:owned] + both[owned:]).astype(BF16)


def mesh_rows(pieces, weight, owned, after):
    width = weight.shape[0]
    return pl.pallas_call(
        functools.partial(mesh_kernel, len(pieces)),
        in_specs=[VMEM] * (len(pieces) + 1) + [ANY],
        out_specs=VMEM,
        out_shape=like((owned, width), BF16),
        cost_estimate=cost(2 * owned * width * width, 2 * width * width),
        compiler_params=params(8),
        name="mesh_rows",
    )(*pieces, weight, in_hbm(after))


def on_device(
    saved_preact,
    edge_senders,
    edge_slots,
    mesh_requests,
    mesh_cotangent,
    out_weight,
    out_bias,
    ln_gain,
    grid_weight,
    mesh_weight,
):
    count = lax.axis_size("band")
    me = lax.axis_index("band")
    owned, width = mesh_cotangent.shape
    edges = saved_preact.shape[0]
    stages = stages_of(count)

    sources = (
        out_weight,
        out_bias.reshape(1, width),
        grid_weight,
        mesh_weight,
        ln_gain.reshape(1, width),
        mesh_cotangent,
    )
    weight, bias, weight_g, weight_m, gain, own_rows, ids, more, *first = first_part(
        saved_preact, edges // 3, sources, me.reshape(1), mesh_requests.swapaxes(1, 2)
    )

    held = [mesh_cotangent]
    for number, (shift, radix) in enumerate(stages):
        if number == 1:
            held = [join([own_rows, *held[1:]], first[0])]
        elif number > 1:
            held = [join(held, ids)]
        held += [swap(held[0], count, j << shift) for j in range(1, radix)]
        if number == 1:
            second = second_part(more, weight, bias, held[0])

    back = stages[::-1]
    d_preact, *chunks = after(
        me.reshape(1),
        ids,
        edge_slots.reshape(1, edges),
        edge_senders.reshape(1, edges),
        weight,
        gain,
        [first, second],
        held,
        owned,
        mesh_requests.shape[2],
        back[0][1],
    )

    total = segments(edge_senders, d_preact)
    arrived, left = None, count
    for shift, radix in back:
        if arrived is not None:
            chunks = regroup(arrived, radix, left // radix, total)
        left //= radix
        arrived = [chunks[0]] + [pass_on(chunks[j], count, j << shift) for j in range(1, radix)]
        if shift == 0:
            grid_adjoint = grid_rows(total, arrived[1], weight_g)
    mesh_adjoint = mesh_rows(arrived, weight_m, owned, grid_adjoint)
    return (grid_adjoint, mesh_adjoint)


def solution(mesh):
    in_specs = (
        P(("groups", "band"), None),
        P("band"),
        P("band"),
        P("band", None, None),
        P(("groups", "band"), None),
        P(),
        P(),
        P(),
        P(),
        P(),
    )
    out_specs = (P(("groups", "band"), None), P(("groups", "band"), None))
    return jax.shard_map(
        on_device, mesh=mesh, in_specs=in_specs, out_specs=out_specs, check_vma=False
    )
```

time: 38 us -> 39.1 us (1.029)
  waiting for transfers between devices: 4.03 us -> 9.19 us
  starting transfers between devices: 16.4 us -> 13.3 us
  Pallas kernels: 16.7 us -> 15.8 us
    ppermute x12 -> x6, starting transfers between devices: 14.9 us -> 7.54 us  [swap(): return lax.ppermute(block, 'band', [(i, i ^ mask) for i in range(count)])]
    ppermute x1 -> x6, waiting for transfers between devices: 0.01 us -> 7.18 us  [pass_on(): lax.ppermute(block, 'band', [(i, (i + distance) % count) for i in range(c...]
    ppermute x1 -> x6, starting transfers between devices: 1.47 us -> 5.75 us  [pass_on(): lax.ppermute(block, 'band', [(i, (i + distance) % count) for i in range(c...]
    ppermute x12 -> x6, waiting for transfers between devices: 4.03 us -> 2.02 us  [swap(): return lax.ppermute(block, 'band', [(i, i ^ mask) for i in range(count)])]
    pallas_call x6, Pallas kernels: 15.7 us -> 14.8 us  [the longest x1 4.17 us: after(): pl.pallas_call(functools.partial(after_kernel, len(parts), chunks, owned,...]
  transfers between devices with their start and end apart: 13 -> 12, of which waited for: 4 -> 6; matrix products, arithmetic and copies ran while one was open for 0% -> 0% of each run, Pallas kernels for 31% -> 27%
where the time goes in v4:
time: 39.1 us; the launch traced here: 39 us
  Pallas kernels  15.8 us (40%)
  starting transfers between devices  13.3 us (34%)
  waiting for transfers between devices  9.19 us (24%)
  between operations  0.73 us (2%)
    ppermute x6, starting transfers between devices, swap(): return lax.ppermute(block, 'band', [(i, i ^ mask) for i in range(count)])  7.54 us
    ppermute x6, waiting for transfers between devices, pass_on(): lax.ppermute(block, 'band', [(i, (i + distance) % count) for i in range(c...  7.18 us
    ppermute x6, starting transfers between devices, pass_on(): lax.ppermute(block, 'band', [(i, (i + distance) % count) for i in range(c...  5.75 us
    pallas_call x1, Pallas kernels, after(): pl.pallas_call(functools.partial(after_kernel, len(parts), chunks, owned,...  4.17 us
    pallas_call x1, Pallas kernels, second_part(): pl.pallas_call(functools.partial(second_kernel, block), in_specs=[VMEM, V...  3.36 us
    pallas_call x1, Pallas kernels, first_part(): pl.pallas_call(functools.partial(first_kernel, block, copies), in_specs=[...  3.26 us
    pallas_call x1, Pallas kernels, grid_rows(): pl.pallas_call(functools.partial(grid_kernel, block), in_specs=[VMEM] * 3...  2.13 us
    ppermute x6, waiting for transfers between devices, swap(): return lax.ppermute(block, 'band', [(i, i ^ mask) for i in range(count)])  2.02 us
  transfers between devices with their start and end apart: 12, of which 6 were waited for; matrix products, arithmetic and copies ran while one was open for 0% of the time, Pallas kernels for 27%

profile of v4, /device:TPU:0, one launch (start us, length us, event | category | flops | bytes accessed | tf_op | source)
XLA Modules:
  0.0 39.0 jit_solution(12749215195081515370)
XLA Ops:
  0.6 3.1 %collective-permute-start = (bf16[16,512]{1,0:T(8,128)(2,1)}, bf16[16,512]{1,0:T(8,128)(2,1)S(1)}, u32[]{:S(2)}, u32[]{:S(2)}) collective-permute-start(bf16[16,512]{1,0:T(8,128)(2,1)} %refs_5_.1), channel_id=1, source_target_pairs={{0,4},{1,5},{2,6},{3,7},{4,0},{5,1},{6,2},{7,3},{8,12},{9,13},{10,... | collective-permute-start | bytes 49160 | tf_op jit(solution)/shard_map/ppermute | solution.py:45
  3.7 2.5 %collective-permute-start.2 = (bf16[16,512]{1,0:T(8,128)(2,1)}, bf16[16,512]{1,0:T(8,128)(2,1)S(1)}, u32[]{:S(2)}, u32[]{:S(2)}) collective-permute-start(bf16[16,512]{1,0:T(8,128)(2,1)} %refs_5_.1), channel_id=1, source_target_pairs={{0,12},{1,13},{2,14},{3,15},{4,8},{5,9},{6,10},{7,11},{8,4},{9,5},... | collective-permute-start | bytes 49160 | tf_op jit(solution)/shard_map/ppermute | solution.py:45
  6.2 0.1 collective-permute-start.1
  6.3 3.3 %first_part.1 = (bf16[512,512]{1,0:T(8,128)(2,1)S(1)}, f32[1,512]{1,0:T(1,128)S(1)}, bf16[512,512]{1,0:T(8,128)(2,1)S(1)}, bf16[512,512]{1,0:T(8,128)(2,1)S(1)},...) custom-call(bf16[3072,512]{1,0:T(8,128)(2,1)} %pre_hbm.1, ...), custom_call_target="tpu_custom_call" | custom-call | flops 1610612736 | bytes 5242880 | tf_op jit(solution)/shard_map/first_part/pallas_call | solution.py:162
  9.6 0.1 collective-permute-done.2.refs_3_
  9.7 1.4 %collective-permute-done.1.refs_2_ = bf16[16,512]{1,0:T(8,128)(2,1)S(1)} collective-permute-done((bf16[16,512]{1,0:T(8,128)(2,1)}, bf16[16,512]{1,0:T(8,128)(2,1)S(1)}, u32[]{:S(2)}, u32[]{:S(2)}) %collective-permute-start.1) | collective-permute-done | bytes 16416 | tf_op jit(solution)/shard_map/ppermute | solution.py:45
  11.1 1.6 %collective-permute-start.4 = (bf16[64,512]{1,0:T(8,128)(2,1)S(1)}, bf16[64,512]{1,0:T(8,128)(2,1)S(1)}, u32[]{:S(2)}, u32[]{:S(2)}) collective-permute-start(bf16[64,512]{1,0:T(8,128)(2,1)S(1)} %join.1.after_ref.refs_6_), channel_id=1, source_target_pairs={{0,2},{1,3},{2,0},{3,1},{4,6},{5,7},{6,4},{7,5},{8,10},{9,11},{10,... | collective-permute-start | bytes 196616 | tf_op jit(solution)/shard_map/ppermute | solution.py:45
  12.6 0.3 collective-permute-start.3
  12.9 3.4 %second_part.1 = (bf16[2048,512]{1,0:T(8,128)(2,1)S(1)}, bf16[2048,512]{1,0:T(8,128)(2,1)S(1)}, f32[2048,512]{1,0:T(8,128)S(1)}) custom-call(bf16[2048,512]{1,0:T(8,128)(2,1)S(1)} %get-tuple-element.31.pre_ref, bf16[512,512]{1,0:T(8,128)(2,1)S(1)} %get-tuple-element.26.weight_ref, f32[1,512]{1,0:T(1,128)S(1)} %get-tuple-element.32.bias_ref, ...), custom_call_target="tpu_custom_call" | custom-call | flops 3221225472 | bytes 10485760 | tf_op jit(solution)/shard_map/second_part/pallas_call | solution.py:187
  16.3 0.5 %collective-permute-done.4.refs_8_ = bf16[64,512]{1,0:T(8,128)(2,1)S(1)} collective-permute-done((bf16[64,512]{1,0:T(8,128)(2,1)S(1)}, bf16[64,512]{1,0:T(8,128)(2,1)S(1)}, u32[]{:S(2)}, u32[]{:S(2)}) %collective-permute-start.4) | collective-permute-done | bytes 65568 | tf_op jit(solution)/shard_map/ppermute | solution.py:45
  16.9 4.2 %after.1 = (bf16[3072,512]{1,0:T(8,128)(2,1)S(1)}, f32[16,512]{1,0:T(8,128)S(1)}, f32[144,512]{1,0:T(8,128)S(1)}, f32[16,512]{1,0:T(8,128)S(1)}, f32[16,512]{1,0:T(8,128)S(1)}) custom-call(s32[1]{0:T(128)} %bitcast.1.refs_6_.me_ref, f32[32,128]{1,0:T(8,128)S(1)} %get-tuple-element.25.ids_ref, s32[1,3072]{1,0:T(1,128)S(1)} %bitcast.6, s32[1,3072]{1,0:T(1,128)S(1)} %bitcast.7, ...), custom_call_target="tpu_custom_call" | custom-call | flops 4831838208 | bytes 12582912 | tf_op jit(solution)/shard_map/after/pallas_call | solution.py:289
  21.1 1.0 %collective-permute-start.7 = (f32[16,512]{1,0:T(8,128)S(1)}, f32[16,512]{1,0:T(8,128)S(1)}, u32[]{:S(2)}, u32[]{:S(2)}) collective-permute-start(f32[16,512]{1,0:T(8,128)S(1)} %get-tuple-element.41), channel_id=1, source_target_pairs={{0,2},{1,3},{2,4},{3,5},{4,6},{5,7},{6,8},{7,9},{8,10},{9,11},{10,... | collective-permute-start | bytes 98312 | tf_op jit(solution)/shard_map/ppermute | solution.py:49
  22.1 0.6 %collective-permute-start.8 = (f32[16,512]{1,0:T(8,128)S(1)}, f32[16,512]{1,0:T(8,128)S(1)}, u32[]{:S(2)}, u32[]{:S(2)}) collective-permute-start(f32[16,512]{1,0:T(8,128)S(1)} %get-tuple-element.42), channel_id=1, source_target_pairs={{0,3},{1,4},{2,5},{3,6},{4,7},{5,8},{6,9},{7,10},{8,11},{9,12},{10... | collective-permute-start | bytes 98312 | tf_op jit(solution)/shard_map/ppermute | solution.py:49
  22.7 0.2 collective-permute-start.6
  22.9 1.8 %segments.1.total_ref.refs_4_ = f32[2448,512]{1,0:T(8,128)S(1)} custom-call(s32[3072]{0:T(1024)S(1)} %copy-done.1, s32[1,3072]{1,0:T(1,128)S(1)} %bitcast.8, bf16[3072,512]{1,0:T(8,128)(2,1)S(1)} %get-tuple-element.37.d_ref), custom_call_target="tpu_custom_call" | custom-call | flops 3221225472 | bytes 6291456 | tf_op jit(solution)/shard_map/segments/pallas_call | solution.py:314
  24.7 3.2 %collective-permute-done.7.refs_2_ = f32[16,512]{1,0:T(8,128)S(1)} collective-permute-done((f32[16,512]{1,0:T(8,128)S(1)}, f32[16,512]{1,0:T(8,128)S(1)}, u32[]{:S(2)}, u32[]{:S(2)}) %collective-permute-start.7) | collective-permute-done | bytes 32800 | tf_op jit(solution)/shard_map/ppermute | solution.py:49
  27.9 3.7 %collective-permute-done.6.carried_ref.refs_1_ = f32[144,512]{1,0:T(8,128)S(1)} collective-permute-done((f32[144,512]{1,0:T(8,128)S(1)}, f32[144,512]{1,0:T(8,128)S(1)}, u32[]{:S(2)}, u32[]{:S(2)}) %collective-permute-start.6) | collective-permute-done | bytes 294944 | tf_op jit(solution)/shard_map/ppermute | solution.py:49
  31.6 0.1 regroup.1
  31.6 0.1 collective-permute-start.9
  31.7 1.8 %collective-permute-start.10 = (f32[16,512]{1,0:T(8,128)S(1)}, f32[16,512]{1,0:T(8,128)S(1)}, u32[]{:S(2)}, u32[]{:S(2)}) collective-permute-start(f32[16,512]{1,0:T(8,128)S(1)} %get-tuple-element.45), channel_id=1, source_target_pairs={{0,8},{1,9},{2,10},{3,11},{4,12},{5,13},{6,14},{7,15},{8,0},{9,1},... | collective-permute-start | bytes 98312 | tf_op jit(solution)/shard_map/ppermute | solution.py:49
  33.5 2.0 %collective-permute-start.11 = (f32[16,512]{1,0:T(8,128)S(1)}, f32[16,512]{1,0:T(8,128)S(1)}, u32[]{:S(2)}, u32[]{:S(2)}) collective-permute-start(f32[16,512]{1,0:T(8,128)S(1)} %get-tuple-element.46), channel_id=1, source_target_pairs={{0,12},{1,13},{2,14},{3,15},{4,0},{5,1},{6,2},{7,3},{8,4},{9,5},{1... | collective-permute-start | bytes 98312 | tf_op jit(solution)/shard_map/ppermute | solution.py:49
  35.5 2.1 %grid_rows.1.refs_5_ = bf16[2048,512]{1,0:T(8,128)(2,1)} custom-call(f32[2448,512]{1,0:T(8,128)S(1)} %segments.1.total_ref.refs_4_, f32[144,512]{1,0:T(8,128)S(1)} %collective-permute-done.6.carried_ref.refs_1_, bf16[512,512]{1,0:T(8,128)(2,1)S(1)} %get-tuple-element.39.weight_ref), custom_call_target="tpu_custom_call" | custom-call | flops 1073741824 | bytes 6291456 | tf_op jit(solution)/shard_map/grid_rows/pallas_call | solution.py:344
  37.7 0.3 collective-permute-done.11.refs_3_
  38.0 1.0 %mesh_rows.1 = bf16[16,512]{1,0:T(8,128)(2,1)} custom-call(f32[16,512]{1,0:T(8,128)S(1)} %get-tuple-element.43.refs_0_, f32[16,512]{1,0:T(8,128)S(1)} %collective-permute-done.9.refs_1_, f32[16,512]{1,0:T(8,128)S(1)} %collective-permute-done.10.refs_2_, f32[16,512]{1,0:T(8,128)S(1)} %collective-permute-done.11.refs_3_, ...), custom_call_target="tpu_custom_call" | custom-call | flops 8388608 | bytes 524288 | tf_op jit(solution)/shard_map/mesh_rows/pallas_call | solution.py:399
  (12 shorter events, 0.0 us)
Async XLA Ops:
  0.6 9.0 %collective-permute-start = (bf16[16,512]{1,0:T(8,128)(2,1)}, bf16[16,512]{1,0:T(8,128)(2,1)S(1)}, u32[]{:S(2)}, u32[]{:S(2)}) collective-permute-start(bf16[16,512]{1,0:T(8,128)(2,1)} %refs_5_.1), channel_id=1, source_target_pairs={{0,4},{1,5},{2,6},{3,7},{4,0},{5,1},{6,2},{7,3},{8,12},{9,13},{10,... | collective-permute-start | bytes 49160 | tf_op jit(solution)/shard_map/ppermute | solution.py:45
  3.7 6.0 %collective-permute-start.2 = (bf16[16,512]{1,0:T(8,128)(2,1)}, bf16[16,512]{1,0:T(8,128)(2,1)S(1)}, u32[]{:S(2)}, u32[]{:S(2)}) collective-permute-start(bf16[16,512]{1,0:T(8,128)(2,1)} %refs_5_.1), channel_id=1, source_target_pairs={{0,12},{1,13},{2,14},{3,15},{4,8},{5,9},{6,10},{7,11},{8,4},{9,5},... | collective-permute-start | bytes 49160 | tf_op jit(solution)/shard_map/ppermute | solution.py:45
  6.2 4.9 %collective-permute-start.1 = (bf16[16,512]{1,0:T(8,128)(2,1)}, bf16[16,512]{1,0:T(8,128)(2,1)S(1)}, u32[]{:S(2)}, u32[]{:S(2)}) collective-permute-start(bf16[16,512]{1,0:T(8,128)(2,1)} %refs_5_.1), channel_id=1, source_target_pairs={{0,8},{1,9},{2,10},{3,11},{4,12},{5,13},{6,14},{7,15},{8,0},{9,1},... | collective-permute-start | bytes 49160 | tf_op jit(solution)/shard_map/ppermute | solution.py:45
  11.1 5.2 %collective-permute-start.5 = (bf16[64,512]{1,0:T(8,128)(2,1)S(1)}, bf16[64,512]{1,0:T(8,128)(2,1)S(1)}, u32[]{:S(2)}, u32[]{:S(2)}) collective-permute-start(bf16[64,512]{1,0:T(8,128)(2,1)S(1)} %join.1.after_ref.refs_6_), channel_id=1, source_target_pairs={{0,3},{1,2},{2,1},{3,0},{4,7},{5,6},{6,5},{7,4},{8,11},{9,10},{10,... | collective-permute-start | bytes 196616 | tf_op jit(solution)/shard_map/ppermute | solution.py:45
  11.1 5.8 %collective-permute-start.4 = (bf16[64,512]{1,0:T(8,128)(2,1)S(1)}, bf16[64,512]{1,0:T(8,128)(2,1)S(1)}, u32[]{:S(2)}, u32[]{:S(2)}) collective-permute-start(bf16[64,512]{1,0:T(8,128)(2,1)S(1)} %join.1.after_ref.refs_6_), channel_id=1, source_target_pairs={{0,2},{1,3},{2,0},{3,1},{4,6},{5,7},{6,4},{7,5},{8,10},{9,11},{10,... | collective-permute-start | bytes 196616 | tf_op jit(solution)/shard_map/ppermute | solution.py:45
  12.6 4.2 %collective-permute-start.3 = (bf16[64,512]{1,0:T(8,128)(2,1)S(1)}, bf16[64,512]{1,0:T(8,128)(2,1)S(1)}, u32[]{:S(2)}, u32[]{:S(2)}) collective-permute-start(bf16[64,512]{1,0:T(8,128)(2,1)S(1)} %join.1.after_ref.refs_6_), channel_id=1, source_target_pairs={{0,1},{1,0},{2,3},{3,2},{4,5},{5,4},{6,7},{7,6},{8,9},{9,8},{10,11... | collective-permute-start | bytes 196616 | tf_op jit(solution)/shard_map/ppermute | solution.py:45
  12.9 3.9 %copy-start = (s32[3072]{0:T(1024)S(1)}, s32[3072]{0:T(1024)}, u32[]{:S(2)}) copy-start(s32[3072]{0:T(1024)} %param.12) | copy-start | bytes 36868
  12.9 3.9 %copy-start.1 = (s32[3072]{0:T(1024)S(1)}, s32[3072]{0:T(1024)}, u32[]{:S(2)}) copy-start(s32[3072]{0:T(1024)} %starts_ref.1) | copy-start | bytes 36868
  21.1 6.9 %collective-permute-start.7 = (f32[16,512]{1,0:T(8,128)S(1)}, f32[16,512]{1,0:T(8,128)S(1)}, u32[]{:S(2)}, u32[]{:S(2)}) collective-permute-start(f32[16,512]{1,0:T(8,128)S(1)} %get-tuple-element.41), channel_id=1, source_target_pairs={{0,2},{1,3},{2,4},{3,5},{4,6},{5,7},{6,8},{7,9},{8,10},{9,11},{10,... | collective-permute-start | bytes 98312 | tf_op jit(solution)/shard_map/ppermute | solution.py:49
  22.1 5.8 %collective-permute-start.8 = (f32[16,512]{1,0:T(8,128)S(1)}, f32[16,512]{1,0:T(8,128)S(1)}, u32[]{:S(2)}, u32[]{:S(2)}) collective-permute-start(f32[16,512]{1,0:T(8,128)S(1)} %get-tuple-element.42), channel_id=1, source_target_pairs={{0,3},{1,4},{2,5},{3,6},{4,7},{5,8},{6,9},{7,10},{8,11},{9,12},{10... | collective-permute-start | bytes 98312 | tf_op jit(solution)/shard_map/ppermute | solution.py:49
  22.7 8.9 %collective-permute-start.6 = (f32[144,512]{1,0:T(8,128)S(1)}, f32[144,512]{1,0:T(8,128)S(1)}, u32[]{:S(2)}, u32[]{:S(2)}) collective-permute-start(f32[144,512]{1,0:T(8,128)S(1)} %get-tuple-element.38), channel_id=1, source_target_pairs={{0,1},{1,2},{2,3},{3,4},{4,5},{5,6},{6,7},{7,8},{8,9},{9,10},{10,1... | collective-permute-start | bytes 884744 | tf_op jit(solution)/shard_map/ppermute | solution.py:49
  31.6 6.0 %collective-permute-start.9 = (f32[16,512]{1,0:T(8,128)S(1)}, f32[16,512]{1,0:T(8,128)S(1)}, u32[]{:S(2)}, u32[]{:S(2)}) collective-permute-start(f32[16,512]{1,0:T(8,128)S(1)} %get-tuple-element.44), channel_id=1, source_target_pairs={{0,4},{1,5},{2,6},{3,7},{4,8},{5,9},{6,10},{7,11},{8,12},{9,13},{1... | collective-permute-start | bytes 98312 | tf_op jit(solution)/shard_map/ppermute | solution.py:49
  31.7 6.0 %collective-permute-start.10 = (f32[16,512]{1,0:T(8,128)S(1)}, f32[16,512]{1,0:T(8,128)S(1)}, u32[]{:S(2)}, u32[]{:S(2)}) collective-permute-start(f32[16,512]{1,0:T(8,128)S(1)} %get-tuple-element.45), channel_id=1, source_target_pairs={{0,8},{1,9},{2,10},{3,11},{4,12},{5,13},{6,14},{7,15},{8,0},{9,1},... | collective-permute-start | bytes 98312 | tf_op jit(solution)/shard_map/ppermute | solution.py:49
  33.5 4.5 %collective-permute-start.11 = (f32[16,512]{1,0:T(8,128)S(1)}, f32[16,512]{1,0:T(8,128)S(1)}, u32[]{:S(2)}, u32[]{:S(2)}) collective-permute-start(f32[16,512]{1,0:T(8,128)S(1)} %get-tuple-element.46), channel_id=1, source_target_pairs={{0,12},{1,13},{2,14},{3,15},{4,0},{5,1},{6,2},{7,3},{8,4},{9,5},{1... | collective-permute-start | bytes 98312 | tf_op jit(solution)/shard_map/ppermute | solution.py:49

commit v5 on v4

--- a/solution.py
+++ b/solution.py
@@ -212,6 +212,26 @@
         compiler_params=params(8),
         name="join",
     )(*pieces, after)
+
+
+def height_of(rows):
+    return 2 * rows + max(rows, 16)
+
+
+def store_rows(ref, sums, ids):
+    rows, width = sums.shape
+    high, low = split(sums)
+    ref[: 2 * rows, :] = jnp.concatenate([high.astype(F32), low.astype(F32)], axis=0).astype(BF16)
+    if rows < 16:
+        ids = jnp.concatenate([ids, jnp.zeros((16 - rows, ids.shape[1]), F32)], axis=0)
+    for at in range(0, width, LANES):
+        ref[2 * rows : height_of(rows), at : at + LANES] = ids.astype(BF16)
+
+
+def load_rows(ref, rows):
+    both = ref[: 2 * rows, :].astype(F32)
+    ids = ref[2 * rows : height_of(rows), :LANES].astype(F32)
+    return both[:rows] + both[rows:], ids[:rows]
 
 
 def after_kernel(
@@ -276,21 +296,20 @@
 
     each = slots // chunks
     for k, sums_ref in enumerate(sums_refs):
-        sums_ref[:each, :] = sums[k * each : (k + 1) * each]
-        for at in range(0, width, LANES):
-            sums_ref[each : 2 * each, at : at + LANES] = ids_ref[k * each : (k + 1) * each, :]
-    sums_refs[1][2 * each :, :] = rim
+        piece = slice(k * each, (k + 1) * each)
+        store_rows(sums_ref, sums[piece], ids_ref[piece, :])
+    sums_refs[1][sums_refs[1].shape[0] - RIM :, :] = rim.astype(BF16)
 
 
 def after(me, ids, slots, senders, weight, gain, parts, pieces, owned, caps, chunks, block=512):
     edges, width = slots.shape[1], weight.shape[0]
     each = ids.shape[0] // chunks
-    sizes = [2 * each + (RIM if k == 1 else 0) for k in range(chunks)]
+    sizes = [height_of(each) + (RIM if k == 1 else 0) for k in range(chunks)]
     return pl.pallas_call(
         functools.partial(after_kernel, len(parts), chunks, owned, caps, block),
         in_specs=[SMEM] + [VMEM] * (5 + 3 * len(parts) + len(pieces)),
         out_specs=[VMEM] * (1 + chunks),
-        out_shape=[in_vmem((edges, width), BF16)] + [in_vmem((size, width), F32) for size in sizes],
+        out_shape=[in_vmem((edges, width), BF16)] + [in_vmem((size, width), BF16) for size in sizes],
         cost_estimate=cost(6 * edges * width * width, 8 * edges * width),
         compiler_params=params(20),
         name="after",
@@ -328,7 +347,7 @@
     for k, at in enumerate(range(0, G_DEV, block)):
         rows = total_ref[at : at + block, :]
         if at == 0:
-            rim = carried_ref[carried_ref.shape[0] - RIM :, :]
+            rim = carried_ref[carried_ref.shape[0] - RIM :, :].astype(F32)
             rows = jnp.concatenate([rows[:RIM] + rim, rows[RIM:]], axis=0)
         out_ref[at : at + block, :] = dot_t(rows.astype(BF16), weight).astype(BF16)
         copies.append(
@@ -357,36 +376,34 @@
     outs = refs[parts + 1 :]
     low = groups // len(outs)
     each = rows // groups
+    loaded = [load_rows(ref, rows) for ref in refs[:parts]]
     for j, out_ref in enumerate(outs):
-        half = out_ref.shape[0] // 2
-        for g in range(low):
-            for k in range(parts):
-                to, at = (g * parts + k) * each, (j * low + g) * each
-                out_ref[to : to + each, :] = refs[k][at : at + each, :]
-                out_ref[half + to : half + to + each, :] = refs[k][rows + at : rows + at + each, :]
-
-
-def regroup(arrived, radix, low, after):
-    height, width = arrived[0].shape
+        spans = [(k, (j * low + g) * each) for g in range(low) for k in range(parts)]
+        sums = jnp.concatenate([loaded[k][0][at : at + each] for k, at in spans], axis=0)
+        ids = jnp.concatenate([loaded[k][1][at : at + each] for k, at in spans], axis=0)
+        store_rows(out_ref, sums, ids)
+
+
+def regroup(arrived, radix, low, rows, after):
+    width = arrived[0].shape[1]
     parts = len(arrived)
     return pl.pallas_call(
-        functools.partial(regroup_kernel, radix * low, parts, height // 2),
+        functools.partial(regroup_kernel, radix * low, parts, rows),
         in_specs=[VMEM] * parts + [ANY],
         out_specs=[VMEM] * radix,
-        out_shape=[in_vmem((height * parts // radix, width), arrived[0].dtype)] * radix,
-        cost_estimate=cost(0, 8 * height * parts * width),
+        out_shape=[in_vmem((height_of(rows * parts // radix), width), BF16)] * radix,
+        cost_estimate=cost(0, 8 * rows * parts * width),
         compiler_params=params(8),
         name="regroup",
     )(*arrived, after)
 
 
-def mesh_kernel(parts, *refs):
+def mesh_kernel(parts, size, *refs):
     pieces, weight_ref, out_ref = refs[:parts], refs[parts], refs[-1]
     owned, width = out_ref.shape
-    half = pieces[0].shape[0] // 2
-    rows = jnp.concatenate([piece[:half, :] for piece in pieces], axis=0)
-    ids = jnp.concatenate([piece[half:, :LANES] for piece in pieces], axis=0)
-    ids = ids.T[:owned].astype(jnp.int32)
+    loaded = [load_rows(piece, size) for piece in pieces]
+    rows = jnp.concatenate([sums for sums, _ in loaded], axis=0)
+    ids = jnp.concatenate([ids for _, ids in loaded], axis=0).T[:owned].astype(jnp.int32)
     pick = (lax.broadcasted_iota(jnp.int32, ids.shape, 0) == ids).astype(F32).astype(BF16)
     high, low = split(rows)
     high, low = split(dot(pick, high) + dot(pick, low))
@@ -394,10 +411,10 @@
     out_ref[...] = (both[:owned] + both[owned:]).astype(BF16)
 
 
-def mesh_rows(pieces, weight, owned, after):
+def mesh_rows(pieces, size, weight, owned, after):
     width = weight.shape[0]
     return pl.pallas_call(
-        functools.partial(mesh_kernel, len(pieces)),
+        functools.partial(mesh_kernel, len(pieces), size),
         in_specs=[VMEM] * (len(pieces) + 1) + [ANY],
         out_specs=VMEM,
         out_shape=like((owned, width), BF16),
@@ -463,15 +480,16 @@
     )
 
     total = segments(edge_senders, d_preact)
-    arrived, left = None, count
+    arrived, left, size = None, count, ids.shape[0] // back[0][1]
     for shift, radix in back:
         if arrived is not None:
-            chunks = regroup(arrived, radix, left // radix, total)
+            chunks = regroup(arrived, radix, left // radix, size, total)
+            size = size * len(arrived) // radix
         left //= radix
         arrived = [chunks[0]] + [pass_on(chunks[j], count, j << shift) for j in range(1, radix)]
         if shift == 0:
             grid_adjoint = grid_rows(total, arrived[1], weight_g)
-    mesh_adjoint = mesh_rows(arrived, weight_m, owned, grid_adjoint)
+    mesh_adjoint = mesh_rows(arrived, size, weight_m, owned, grid_adjoint)
     return (grid_adjoint, mesh_adjoint)
 
 

time: 39.1 us -> 37.7 us (0.964)
  waiting for transfers between devices: 9.19 us -> 7.8 us
    ppermute x6, waiting for transfers between devices: 7.18 us -> 5.78 us  [pass_on(): lax.ppermute(block, 'band', [(i, (i + distance) % count) for i in range(c...]
  transfers between devices with their start and end apart: 12 -> 12, of which waited for: 6 -> 6; matrix products, arithmetic and copies ran while one was open for 0% -> 0% of each run, Pallas kernels for 27% -> 28%
where the time goes in v5:
time: 37.7 us; the launch traced here: 37.6 us
  Pallas kernels  15.7 us (42%)
  starting transfers between devices  13.3 us (35%)
  waiting for transfers between devices  7.8 us (21%)
  between operations  0.73 us (2%)
    ppermute x6, starting transfers between devices, swap(): return lax.ppermute(block, 'band', [(i, i ^ mask) for i in range(count)])  7.54 us
    ppermute x6, waiting for transfers between devices, pass_on(): lax.ppermute(block, 'band', [(i, (i + distance) % count) for i in range(c...  5.78 us
    ppermute x6, starting transfers between devices, pass_on(): lax.ppermute(block, 'band', [(i, (i + distance) % count) for i in range(c...  5.75 us
    pallas_call x1, Pallas kernels, after(): pl.pallas_call(functools.partial(after_kernel, len(parts), chunks, owned,...  4.18 us
    pallas_call x1, Pallas kernels, second_part(): pl.pallas_call(functools.partial(second_kernel, block), in_specs=[VMEM, V...  3.36 us
    pallas_call x1, Pallas kernels, first_part(): pl.pallas_call(functools.partial(first_kernel, block, copies), in_specs=[...  3.26 us
    pallas_call x1, Pallas kernels, grid_rows(): pl.pallas_call(functools.partial(grid_kernel, block), in_specs=[VMEM] * 3...  2.12 us
    ppermute x6, waiting for transfers between devices, swap(): return lax.ppermute(block, 'band', [(i, i ^ mask) for i in range(count)])  2.02 us
  transfers between devices with their start and end apart: 12, of which 6 were waited for; matrix products, arithmetic and copies ran while one was open for 0% of the time, Pallas kernels for 28%

profile of v5, /device:TPU:0, one launch (start us, length us, event | category | flops | bytes accessed | tf_op | source)
XLA Modules:
  0.0 37.6 jit_solution(3420599661720705438)
XLA Ops:
  0.6 3.1 %collective-permute-start = (bf16[16,512]{1,0:T(8,128)(2,1)}, bf16[16,512]{1,0:T(8,128)(2,1)S(1)}, u32[]{:S(2)}, u32[]{:S(2)}) collective-permute-start(bf16[16,512]{1,0:T(8,128)(2,1)} %refs_5_.1), channel_id=1, source_target_pairs={{0,4},{1,5},{2,6},{3,7},{4,0},{5,1},{6,2},{7,3},{8,12},{9,13},{10,... | collective-permute-start | bytes 49160 | tf_op jit(solution)/shard_map/ppermute | solution.py:45
  3.7 2.5 %collective-permute-start.2 = (bf16[16,512]{1,0:T(8,128)(2,1)}, bf16[16,512]{1,0:T(8,128)(2,1)S(1)}, u32[]{:S(2)}, u32[]{:S(2)}) collective-permute-start(bf16[16,512]{1,0:T(8,128)(2,1)} %refs_5_.1), channel_id=1, source_target_pairs={{0,12},{1,13},{2,14},{3,15},{4,8},{5,9},{6,10},{7,11},{8,4},{9,5},... | collective-permute-start | bytes 49160 | tf_op jit(solution)/shard_map/ppermute | solution.py:45
  6.2 0.1 collective-permute-start.1
  6.3 3.3 %first_part.1 = (bf16[512,512]{1,0:T(8,128)(2,1)S(1)}, f32[1,512]{1,0:T(1,128)S(1)}, bf16[512,512]{1,0:T(8,128)(2,1)S(1)}, bf16[512,512]{1,0:T(8,128)(2,1)S(1)},...) custom-call(bf16[3072,512]{1,0:T(8,128)(2,1)} %pre_hbm.1, ...), custom_call_target="tpu_custom_call" | custom-call | flops 1610612736 | bytes 5242880 | tf_op jit(solution)/shard_map/first_part/pallas_call | solution.py:162
  9.6 0.0 collective-permute-done.refs_1_
  9.6 0.1 collective-permute-done.2.refs_3_
  9.7 1.4 %collective-permute-done.1.refs_2_ = bf16[16,512]{1,0:T(8,128)(2,1)S(1)} collective-permute-done((bf16[16,512]{1,0:T(8,128)(2,1)}, bf16[16,512]{1,0:T(8,128)(2,1)S(1)}, u32[]{:S(2)}, u32[]{:S(2)}) %collective-permute-start.1) | collective-permute-done | bytes 16416 | tf_op jit(solution)/shard_map/ppermute | solution.py:45
  11.1 1.6 %collective-permute-start.4 = (bf16[64,512]{1,0:T(8,128)(2,1)S(1)}, bf16[64,512]{1,0:T(8,128)(2,1)S(1)}, u32[]{:S(2)}, u32[]{:S(2)}) collective-permute-start(bf16[64,512]{1,0:T(8,128)(2,1)S(1)} %join.1.after_ref.refs_6_), channel_id=1, source_target_pairs={{0,2},{1,3},{2,0},{3,1},{4,6},{5,7},{6,4},{7,5},{8,10},{9,11},{10,... | collective-permute-start | bytes 196616 | tf_op jit(solution)/shard_map/ppermute | solution.py:45
  12.6 0.3 collective-permute-start.3
  12.9 3.4 %second_part.1 = (bf16[2048,512]{1,0:T(8,128)(2,1)S(1)}, bf16[2048,512]{1,0:T(8,128)(2,1)S(1)}, f32[2048,512]{1,0:T(8,128)S(1)}) custom-call(bf16[2048,512]{1,0:T(8,128)(2,1)S(1)} %get-tuple-element.31.pre_ref, bf16[512,512]{1,0:T(8,128)(2,1)S(1)} %get-tuple-element.26.weight_ref, f32[1,512]{1,0:T(1,128)S(1)} %get-tuple-element.32.bias_ref, ...), custom_call_target="tpu_custom_call" | custom-call | flops 3221225472 | bytes 10485760 | tf_op jit(solution)/shard_map/second_part/pallas_call | solution.py:187
  16.3 0.5 %collective-permute-done.4.refs_8_ = bf16[64,512]{1,0:T(8,128)(2,1)S(1)} collective-permute-done((bf16[64,512]{1,0:T(8,128)(2,1)S(1)}, bf16[64,512]{1,0:T(8,128)(2,1)S(1)}, u32[]{:S(2)}, u32[]{:S(2)}) %collective-permute-start.4) | collective-permute-done | bytes 65568 | tf_op jit(solution)/shard_map/ppermute | solution.py:45
  16.9 4.2 %after.1 = (bf16[3072,512]{1,0:T(8,128)(2,1)S(1)}, bf16[32,512]{1,0:T(8,128)(2,1)S(1)}, bf16[160,512]{1,0:T(8,128)(2,1)S(1)}, bf16[32,512]{1,0:T(8,128)(2,1)S(1)}, bf16[32,512]{1,0:T(8,128)(2,1)S(1)}) custom-call(s32[1]{0:T(128)} %bitcast.1.refs_6_.me_ref, f32[32,128]{1,0:T(8,128)S(1)} %get-tuple-element.25.ids_ref, s32[1,3072]{1,0:T(1,128)S(1)} %bitcast.6, ...), custom_call_target="tpu_custom_call" | custom-call | flops 4831838208 | bytes 12582912 | tf_op jit(solution)/shard_map/after/pallas_call | solution.py:308
  21.1 1.0 %collective-permute-start.7 = (bf16[32,512]{1,0:T(8,128)(2,1)S(1)}, bf16[32,512]{1,0:T(8,128)(2,1)S(1)}, u32[]{:S(2)}, u32[]{:S(2)}) collective-permute-start(bf16[32,512]{1,0:T(8,128)(2,1)S(1)} %get-tuple-element.41), channel_id=1, source_target_pairs={{0,2},{1,3},{2,4},{3,5},{4,6},{5,7},{6,8},{7,9},{8,10},{9,11},{10,... | collective-permute-start | bytes 98312 | tf_op jit(solution)/shard_map/ppermute | solution.py:49
  22.1 0.6 %collective-permute-start.8 = (bf16[32,512]{1,0:T(8,128)(2,1)S(1)}, bf16[32,512]{1,0:T(8,128)(2,1)S(1)}, u32[]{:S(2)}, u32[]{:S(2)}) collective-permute-start(bf16[32,512]{1,0:T(8,128)(2,1)S(1)} %get-tuple-element.42), channel_id=1, source_target_pairs={{0,3},{1,4},{2,5},{3,6},{4,7},{5,8},{6,9},{7,10},{8,11},{9,12},{10... | collective-permute-start | bytes 98312 | tf_op jit(solution)/shard_map/ppermute | solution.py:49
  22.7 0.2 collective-permute-start.6
  22.9 1.8 %segments.1.total_ref.refs_4_ = f32[2448,512]{1,0:T(8,128)S(1)} custom-call(s32[3072]{0:T(1024)S(1)} %copy-done.1, s32[1,3072]{1,0:T(1,128)S(1)} %bitcast.8, bf16[3072,512]{1,0:T(8,128)(2,1)S(1)} %get-tuple-element.37.d_ref), custom_call_target="tpu_custom_call" | custom-call | flops 3221225472 | bytes 6291456 | tf_op jit(solution)/shard_map/segments/pallas_call | solution.py:333
  24.7 3.2 %collective-permute-done.7.refs_2_ = bf16[32,512]{1,0:T(8,128)(2,1)S(1)} collective-permute-done((bf16[32,512]{1,0:T(8,128)(2,1)S(1)}, bf16[32,512]{1,0:T(8,128)(2,1)S(1)}, u32[]{:S(2)}, u32[]{:S(2)}) %collective-permute-start.7) | collective-permute-done | bytes 32800 | tf_op jit(solution)/shard_map/ppermute | solution.py:49
  27.9 2.3 %collective-permute-done.6.carried_ref.refs_1_ = bf16[160,512]{1,0:T(8,128)(2,1)S(1)} collective-permute-done((bf16[160,512]{1,0:T(8,128)(2,1)S(1)}, bf16[160,512]{1,0:T(8,128)(2,1)S(1)}, u32[]{:S(2)}, u32[]{:S(2)}) %collective-permute-start.6) | collective-permute-done | bytes 163872 | tf_op jit(solution)/shard_map/ppermute | solution.py:49
  30.2 0.1 collective-permute-start.9
  30.3 1.8 %collective-permute-start.10 = (bf16[32,512]{1,0:T(8,128)(2,1)S(1)}, bf16[32,512]{1,0:T(8,128)(2,1)S(1)}, u32[]{:S(2)}, u32[]{:S(2)}) collective-permute-start(bf16[32,512]{1,0:T(8,128)(2,1)S(1)} %get-tuple-element.45), channel_id=1, source_target_pairs={{0,8},{1,9},{2,10},{3,11},{4,12},{5,13},{6,14},{7,15},{8,0},{9,1},... | collective-permute-start | bytes 98312 | tf_op jit(solution)/shard_map/ppermute | solution.py:49
  32.1 2.0 %collective-permute-start.11 = (bf16[32,512]{1,0:T(8,128)(2,1)S(1)}, bf16[32,512]{1,0:T(8,128)(2,1)S(1)}, u32[]{:S(2)}, u32[]{:S(2)}) collective-permute-start(bf16[32,512]{1,0:T(8,128)(2,1)S(1)} %get-tuple-element.46), channel_id=1, source_target_pairs={{0,12},{1,13},{2,14},{3,15},{4,0},{5,1},{6,2},{7,3},{8,4},{9,5},{1... | collective-permute-start | bytes 98312 | tf_op jit(solution)/shard_map/ppermute | solution.py:49
  34.1 2.1 %grid_rows.1.refs_5_ = bf16[2048,512]{1,0:T(8,128)(2,1)} custom-call(f32[2448,512]{1,0:T(8,128)S(1)} %segments.1.total_ref.refs_4_, bf16[160,512]{1,0:T(8,128)(2,1)S(1)} %collective-permute-done.6.carried_ref.refs_1_, bf16[512,512]{1,0:T(8,128)(2,1)S(1)} %get-tuple-element.39.weight_ref), custom_call_target="tpu_custom_call" | custom-call | flops 1073741824 | bytes 6291456 | tf_op jit(solution)/shard_map/grid_rows/pallas_call | solution.py:363
  36.2 0.3 collective-permute-done.11.refs_3_
  36.5 1.0 %mesh_rows.1 = bf16[16,512]{1,0:T(8,128)(2,1)} custom-call(bf16[32,512]{1,0:T(8,128)(2,1)S(1)} %get-tuple-element.43.refs_0_, bf16[32,512]{1,0:T(8,128)(2,1)S(1)} %collective-permute-done.9.refs_1_, bf16[32,512]{1,0:T(8,128)(2,1)S(1)} %collective-permute-done.10.refs_2_, bf16[32,512]{1,0:T(8,128)(2,1)S(1)} %collective-permute-done.11.refs_3_, ...), custom_call_target="tpu_custom_call" | custom-call | flops 8388608 | bytes 524288 | tf_op jit(solution)/shard_map/mesh_rows/pallas_call | solution.py:416
  (12 shorter events, 0.1 us)
Async XLA Ops:
  0.6 9.0 %collective-permute-start = (bf16[16,512]{1,0:T(8,128)(2,1)}, bf16[16,512]{1,0:T(8,128)(2,1)S(1)}, u32[]{:S(2)}, u32[]{:S(2)}) collective-permute-start(bf16[16,512]{1,0:T(8,128)(2,1)} %refs_5_.1), channel_id=1, source_target_pairs={{0,4},{1,5},{2,6},{3,7},{4,0},{5,1},{6,2},{7,3},{8,12},{9,13},{10,... | collective-permute-start | bytes 49160 | tf_op jit(solution)/shard_map/ppermute | solution.py:45
  3.7 6.0 %collective-permute-start.2 = (bf16[16,512]{1,0:T(8,128)(2,1)}, bf16[16,512]{1,0:T(8,128)(2,1)S(1)}, u32[]{:S(2)}, u32[]{:S(2)}) collective-permute-start(bf16[16,512]{1,0:T(8,128)(2,1)} %refs_5_.1), channel_id=1, source_target_pairs={{0,12},{1,13},{2,14},{3,15},{4,8},{5,9},{6,10},{7,11},{8,4},{9,5},... | collective-permute-start | bytes 49160 | tf_op jit(solution)/shard_map/ppermute | solution.py:45
  6.2 4.9 %collective-permute-start.1 = (bf16[16,512]{1,0:T(8,128)(2,1)}, bf16[16,512]{1,0:T(8,128)(2,1)S(1)}, u32[]{:S(2)}, u32[]{:S(2)}) collective-permute-start(bf16[16,512]{1,0:T(8,128)(2,1)} %refs_5_.1), channel_id=1, source_target_pairs={{0,8},{1,9},{2,10},{3,11},{4,12},{5,13},{6,14},{7,15},{8,0},{9,1},... | collective-permute-start | bytes 49160 | tf_op jit(solution)/shard_map/ppermute | solution.py:45
  11.1 5.2 %collective-permute-start.5 = (bf16[64,512]{1,0:T(8,128)(2,1)S(1)}, bf16[64,512]{1,0:T(8,128)(2,1)S(1)}, u32[]{:S(2)}, u32[]{:S(2)}) collective-permute-start(bf16[64,512]{1,0:T(8,128)(2,1)S(1)} %join.1.after_ref.refs_6_), channel_id=1, source_target_pairs={{0,3},{1,2},{2,1},{3,0},{4,7},{5,6},{6,5},{7,4},{8,11},{9,10},{10,... | collective-permute-start | bytes 196616 | tf_op jit(solution)/shard_map/ppermute | solution.py:45
  11.1 5.8 %collective-permute-start.4 = (bf16[64,512]{1,0:T(8,128)(2,1)S(1)}, bf16[64,512]{1,0:T(8,128)(2,1)S(1)}, u32[]{:S(2)}, u32[]{:S(2)}) collective-permute-start(bf16[64,512]{1,0:T(8,128)(2,1)S(1)} %join.1.after_ref.refs_6_), channel_id=1, source_target_pairs={{0,2},{1,3},{2,0},{3,1},{4,6},{5,7},{6,4},{7,5},{8,10},{9,11},{10,... | collective-permute-start | bytes 196616 | tf_op jit(solution)/shard_map/ppermute | solution.py:45
  12.6 4.2 %collective-permute-start.3 = (bf16[64,512]{1,0:T(8,128)(2,1)S(1)}, bf16[64,512]{1,0:T(8,128)(2,1)S(1)}, u32[]{:S(2)}, u32[]{:S(2)}) collective-permute-start(bf16[64,512]{1,0:T(8,128)(2,1)S(1)} %join.1.after_ref.refs_6_), channel_id=1, source_target_pairs={{0,1},{1,0},{2,3},{3,2},{4,5},{5,4},{6,7},{7,6},{8,9},{9,8},{10,11... | collective-permute-start | bytes 196616 | tf_op jit(solution)/shard_map/ppermute | solution.py:45
  12.9 3.9 %copy-start = (s32[3072]{0:T(1024)S(1)}, s32[3072]{0:T(1024)}, u32[]{:S(2)}) copy-start(s32[3072]{0:T(1024)} %param.12) | copy-start | bytes 36868
  12.9 3.9 %copy-start.1 = (s32[3072]{0:T(1024)S(1)}, s32[3072]{0:T(1024)}, u32[]{:S(2)}) copy-start(s32[3072]{0:T(1024)} %starts_ref.1) | copy-start | bytes 36868
  21.1 6.9 %collective-permute-start.7 = (bf16[32,512]{1,0:T(8,128)(2,1)S(1)}, bf16[32,512]{1,0:T(8,128)(2,1)S(1)}, u32[]{:S(2)}, u32[]{:S(2)}) collective-permute-start(bf16[32,512]{1,0:T(8,128)(2,1)S(1)} %get-tuple-element.41), channel_id=1, source_target_pairs={{0,2},{1,3},{2,4},{3,5},{4,6},{5,7},{6,8},{7,9},{8,10},{9,11},{10,... | collective-permute-start | bytes 98312 | tf_op jit(solution)/shard_map/ppermute | solution.py:49
  22.1 5.8 %collective-permute-start.8 = (bf16[32,512]{1,0:T(8,128)(2,1)S(1)}, bf16[32,512]{1,0:T(8,128)(2,1)S(1)}, u32[]{:S(2)}, u32[]{:S(2)}) collective-permute-start(bf16[32,512]{1,0:T(8,128)(2,1)S(1)} %get-tuple-element.42), channel_id=1, source_target_pairs={{0,3},{1,4},{2,5},{3,6},{4,7},{5,8},{6,9},{7,10},{8,11},{9,12},{10... | collective-permute-start | bytes 98312 | tf_op jit(solution)/shard_map/ppermute | solution.py:49
  22.7 7.5 %collective-permute-start.6 = (bf16[160,512]{1,0:T(8,128)(2,1)S(1)}, bf16[160,512]{1,0:T(8,128)(2,1)S(1)}, u32[]{:S(2)}, u32[]{:S(2)}) collective-permute-start(bf16[160,512]{1,0:T(8,128)(2,1)S(1)} %get-tuple-element.38), channel_id=1, source_target_pairs={{0,1},{1,2},{2,3},{3,4},{4,5},{5,6},{6,7},{7,8},{8,9},{9,10},{10,1... | collective-permute-start | bytes 491528 | tf_op jit(solution)/shard_map/ppermute | solution.py:49
  30.2 6.0 %collective-permute-start.9 = (bf16[32,512]{1,0:T(8,128)(2,1)S(1)}, bf16[32,512]{1,0:T(8,128)(2,1)S(1)}, u32[]{:S(2)}, u32[]{:S(2)}) collective-permute-start(bf16[32,512]{1,0:T(8,128)(2,1)S(1)} %get-tuple-element.44), channel_id=1, source_target_pairs={{0,4},{1,5},{2,6},{3,7},{4,8},{5,9},{6,10},{7,11},{8,12},{9,13},{1... | collective-permute-start | bytes 98312 | tf_op jit(solution)/shard_map/ppermute | solution.py:49
  30.3 6.0 %collective-permute-start.10 = (bf16[32,512]{1,0:T(8,128)(2,1)S(1)}, bf16[32,512]{1,0:T(8,128)(2,1)S(1)}, u32[]{:S(2)}, u32[]{:S(2)}) collective-permute-start(bf16[32,512]{1,0:T(8,128)(2,1)S(1)} %get-tuple-element.45), channel_id=1, source_target_pairs={{0,8},{1,9},{2,10},{3,11},{4,12},{5,13},{6,14},{7,15},{8,0},{9,1},... | collective-permute-start | bytes 98312 | tf_op jit(solution)/shard_map/ppermute | solution.py:49
  32.1 4.5 %collective-permute-start.11 = (bf16[32,512]{1,0:T(8,128)(2,1)S(1)}, bf16[32,512]{1,0:T(8,128)(2,1)S(1)}, u32[]{:S(2)}, u32[]{:S(2)}) collective-permute-start(bf16[32,512]{1,0:T(8,128)(2,1)S(1)} %get-tuple-element.46), channel_id=1, source_target_pairs={{0,12},{1,13},{2,14},{3,15},{4,0},{5,1},{6,2},{7,3},{8,4},{9,5},{1... | collective-permute-start | bytes 98312 | tf_op jit(solution)/shard_map/ppermute | solution.py:49

commit v6 on v5

--- a/solution.py
+++ b/solution.py
@@ -43,10 +43,6 @@
 
 def swap(block, count, mask):
     return lax.ppermute(block, "band", [(i, i ^ mask) for i in range(count)])
-
-
-def pass_on(block, count, distance):
-    return lax.ppermute(block, "band", [(i, (i + distance) % count) for i in range(count)])
 
 
 def like(shape, dtype):
@@ -147,7 +143,7 @@
     row = lax.broadcasted_iota(jnp.int32, ids_ref.shape, 0)
     ids = jnp.zeros(ids_ref.shape, jnp.int32)
     for r in range(slots):
-        owner = (me_ref[0] + distance_of(r, caps, count)) % count
+        owner = me_ref[0] ^ distance_of(r, caps, count)
         ids = jnp.where(row == r, requests_ref[0, r % caps, owner], ids)
     ids_ref[...] = ids.astype(F32)
 
@@ -239,8 +235,7 @@
 ):
     edge_refs = [refs[3 * k : 3 * k + 3] for k in range(parts)]
     refs = refs[3 * parts :]
-    d_ref, sums_refs = refs[-1 - chunks], refs[-chunks:]
-    pieces = refs[: -1 - chunks]
+    pieces, (d_ref, rim_ref), sums_refs = refs[: -2 - chunks], refs[-2 - chunks : -chunks], refs[-chunks:]
     slots = ids_ref.shape[0]
     count = slots // caps
     edges, width = d_ref.shape
@@ -248,10 +243,9 @@
     weight = weight_ref[...]
 
     row = lax.broadcasted_iota(jnp.int32, (slots, 1), 0)
-    owner = (distance_of(row, caps, count) + me) % count
-    far, place, step = owner ^ me, jnp.zeros_like(row), 1
+    distance, place, step = distance_of(row, caps, count), jnp.zeros_like(row), 1
     for shift, radix in stages_of(count):
-        place = place + ((far >> shift) & (radix - 1)) * step
+        place = place + ((distance >> shift) & (radix - 1)) * step
         step *= radix
     place = place * owned + ids_ref[...][:, :1].astype(jnp.int32)
     piece_rows = pieces[0].shape[0]
@@ -266,7 +260,7 @@
     both = dot_t(jnp.concatenate(split(rows), axis=0), weight)
     s_both = jnp.concatenate(split(both[:slots] + both[slots:]), axis=0)
 
-    key = owner * caps + row % caps
+    key = (distance ^ me) * caps + row % caps
     rim_row = lax.broadcasted_iota(jnp.int32, (RIM, block), 0) + G_DEV
     sums = jnp.zeros((slots, width), F32)
     rim = jnp.zeros((RIM, width), F32)
@@ -298,18 +292,18 @@
     for k, sums_ref in enumerate(sums_refs):
         piece = slice(k * each, (k + 1) * each)
         store_rows(sums_ref, sums[piece], ids_ref[piece, :])
-    sums_refs[1][sums_refs[1].shape[0] - RIM :, :] = rim.astype(BF16)
+    rim_ref[...] = rim.astype(BF16)
 
 
 def after(me, ids, slots, senders, weight, gain, parts, pieces, owned, caps, chunks, block=512):
     edges, width = slots.shape[1], weight.shape[0]
     each = ids.shape[0] // chunks
-    sizes = [height_of(each) + (RIM if k == 1 else 0) for k in range(chunks)]
     return pl.pallas_call(
         functools.partial(after_kernel, len(parts), chunks, owned, caps, block),
         in_specs=[SMEM] + [VMEM] * (5 + 3 * len(parts) + len(pieces)),
-        out_specs=[VMEM] * (1 + chunks),
-        out_shape=[in_vmem((edges, width), BF16)] + [in_vmem((size, width), BF16) for size in sizes],
+        out_specs=[VMEM] * (2 + chunks),
+        out_shape=[in_vmem((edges, width), BF16), in_vmem((RIM, width), BF16)]
+        + [in_vmem((height_of(each), width), BF16)] * chunks,
         cost_estimate=cost(6 * edges * width * width, 8 * edges * width),
         compiler_params=params(20),
         name="after",
@@ -347,8 +341,7 @@
     for k, at in enumerate(range(0, G_DEV, block)):
         rows = total_ref[at : at + block, :]
         if at == 0:
-            rim = carried_ref[carried_ref.shape[0] - RIM :, :].astype(F32)
-            rows = jnp.concatenate([rows[:RIM] + rim, rows[RIM:]], axis=0)
+            rows = jnp.concatenate([rows[:RIM] + carried_ref[...].astype(F32), rows[RIM:]], axis=0)
         out_ref[at : at + block, :] = dot_t(rows.astype(BF16), weight).astype(BF16)
         copies.append(
             pltpu.make_async_copy(out_ref.at[pl.ds(at, block)], out_hbm.at[pl.ds(at, block)], sem.at[k])
@@ -465,7 +458,7 @@
             second = second_part(more, weight, bias, held[0])
 
     back = stages[::-1]
-    d_preact, *chunks = after(
+    d_preact, rim, *chunks = after(
         me.reshape(1),
         ids,
         edge_slots.reshape(1, edges),
@@ -480,15 +473,15 @@
     )
 
     total = segments(edge_senders, d_preact)
+    carried = lax.ppermute(rim, "band", [(i, i + 1) for i in range(count - 1)])
     arrived, left, size = None, count, ids.shape[0] // back[0][1]
     for shift, radix in back:
         if arrived is not None:
             chunks = regroup(arrived, radix, left // radix, size, total)
             size = size * len(arrived) // radix
         left //= radix
-        arrived = [chunks[0]] + [pass_on(chunks[j], count, j << shift) for j in range(1, radix)]
-        if shift == 0:
-            grid_adjoint = grid_rows(total, arrived[1], weight_g)
+        arrived = [chunks[0]] + [swap(chunks[j], count, j << shift) for j in range(1, radix)]
+    grid_adjoint = grid_rows(total, carried, weight_g)
     mesh_adjoint = mesh_rows(arrived, size, weight_m, owned, grid_adjoint)
     return (grid_adjoint, mesh_adjoint)
 

time: 37.7 us -> 36.1 us (0.958)
  waiting for transfers between devices: 7.8 us -> 3.34 us
  starting transfers between devices: 13.3 us -> 16.2 us
    ppermute x6 -> x12, starting transfers between devices: 7.54 us -> 13.9 us  [swap(): return lax.ppermute(block, 'band', [(i, i ^ mask) for i in range(count)])]
    ppermute x6 -> x1, waiting for transfers between devices: 5.78 us -> 0.01 us  [on_device(): carried = lax.ppermute(rim, 'band', [(i, i + 1) for i in range(count - 1)])]
    ppermute x6 -> x1, starting transfers between devices: 5.75 us -> 2.24 us  [on_device(): carried = lax.ppermute(rim, 'band', [(i, i + 1) for i in range(count - 1)])]
    ppermute x6 -> x12, waiting for transfers between devices: 2.02 us -> 3.33 us  [swap(): return lax.ppermute(block, 'band', [(i, i ^ mask) for i in range(count)])]
  transfers between devices with their start and end apart: 12 -> 13, of which waited for: 6 -> 4; matrix products, arithmetic and copies ran while one was open for 0% -> 0% of each run, Pallas kernels for 28% -> 29%
where the time goes in v6:
time: 36.1 us; the launch traced here: 35.9 us
  starting transfers between devices  16.2 us (45%)
  Pallas kernels  15.7 us (43%)
  waiting for transfers between devices  3.34 us (9%)
  between operations  0.76 us (2%)
    ppermute x12, starting transfers between devices, swap(): return lax.ppermute(block, 'band', [(i, i ^ mask) for i in range(count)])  13.9 us
    pallas_call x1, Pallas kernels, after(): pl.pallas_call(functools.partial(after_kernel, len(parts), chunks, owned,...  4.16 us
    pallas_call x1, Pallas kernels, second_part(): pl.pallas_call(functools.partial(second_kernel, block), in_specs=[VMEM, V...  3.35 us
    ppermute x12, waiting for transfers between devices, swap(): return lax.ppermute(block, 'band', [(i, i ^ mask) for i in range(count)])  3.33 us
    pallas_call x1, Pallas kernels, first_part(): pl.pallas_call(functools.partial(first_kernel, block, copies), in_specs=[...  3.23 us
    ppermute x1, starting transfers between devices, on_device(): carried = lax.ppermute(rim, 'band', [(i, i + 1) for i in range(count - 1)])  2.24 us
    pallas_call x1, Pallas kernels, grid_rows(): pl.pallas_call(functools.partial(grid_kernel, block), in_specs=[VMEM] * 3...  2.12 us
    pallas_call x1, Pallas kernels, segments(): pl.pallas_call(functools.partial(segments_kernel, block), in_specs=[SMEM]...  1.77 us
  transfers between devices with their start and end apart: 13, of which 4 were waited for; matrix products, arithmetic and copies ran while one was open for 0% of the time, Pallas kernels for 29%

profile of v6, /device:TPU:0, one launch (start us, length us, event | category | flops | bytes accessed | tf_op | source)
XLA Modules:
  0.0 35.9 jit_solution(8357044751446011729)
XLA Ops:
  0.6 3.1 %collective-permute-start = (bf16[16,512]{1,0:T(8,128)(2,1)}, bf16[16,512]{1,0:T(8,128)(2,1)S(1)}, u32[]{:S(2)}, u32[]{:S(2)}) collective-permute-start(bf16[16,512]{1,0:T(8,128)(2,1)} %refs_5_.1), channel_id=1, source_target_pairs={{0,4},{1,5},{2,6},{3,7},{4,0},{5,1},{6,2},{7,3},{8,12},{9,13},{10,... | collective-permute-start | bytes 49160 | tf_op jit(solution)/shard_map/ppermute | solution.py:45
  3.7 2.5 %collective-permute-start.2 = (bf16[16,512]{1,0:T(8,128)(2,1)}, bf16[16,512]{1,0:T(8,128)(2,1)S(1)}, u32[]{:S(2)}, u32[]{:S(2)}) collective-permute-start(bf16[16,512]{1,0:T(8,128)(2,1)} %refs_5_.1), channel_id=1, source_target_pairs={{0,12},{1,13},{2,14},{3,15},{4,8},{5,9},{6,10},{7,11},{8,4},{9,5},... | collective-permute-start | bytes 49160 | tf_op jit(solution)/shard_map/ppermute | solution.py:45
  6.2 0.1 collective-permute-start.1
  6.3 3.2 %first_part.1 = (bf16[512,512]{1,0:T(8,128)(2,1)S(1)}, f32[1,512]{1,0:T(1,128)S(1)}, bf16[512,512]{1,0:T(8,128)(2,1)S(1)}, bf16[512,512]{1,0:T(8,128)(2,1)S(1)},...) custom-call(bf16[3072,512]{1,0:T(8,128)(2,1)} %pre_hbm.1, ...), custom_call_target="tpu_custom_call" | custom-call | flops 1610612736 | bytes 5242880 | tf_op jit(solution)/shard_map/first_part/pallas_call | solution.py:158
  9.6 0.1 collective-permute-done.2.refs_3_
  9.7 1.4 %collective-permute-done.1.refs_2_ = bf16[16,512]{1,0:T(8,128)(2,1)S(1)} collective-permute-done((bf16[16,512]{1,0:T(8,128)(2,1)}, bf16[16,512]{1,0:T(8,128)(2,1)S(1)}, u32[]{:S(2)}, u32[]{:S(2)}) %collective-permute-start.1) | collective-permute-done | bytes 16416 | tf_op jit(solution)/shard_map/ppermute | solution.py:45
  11.1 1.6 %collective-permute-start.4 = (bf16[64,512]{1,0:T(8,128)(2,1)S(1)}, bf16[64,512]{1,0:T(8,128)(2,1)S(1)}, u32[]{:S(2)}, u32[]{:S(2)}) collective-permute-start(bf16[64,512]{1,0:T(8,128)(2,1)S(1)} %join.1.after_ref.refs_6_), channel_id=1, source_target_pairs={{0,2},{1,3},{2,0},{3,1},{4,6},{5,7},{6,4},{7,5},{8,10},{9,11},{10,... | collective-permute-start | bytes 196616 | tf_op jit(solution)/shard_map/ppermute | solution.py:45
  12.6 0.3 collective-permute-start.3
  12.9 3.4 %second_part.1 = (bf16[2048,512]{1,0:T(8,128)(2,1)S(1)}, bf16[2048,512]{1,0:T(8,128)(2,1)S(1)}, f32[2048,512]{1,0:T(8,128)S(1)}) custom-call(bf16[2048,512]{1,0:T(8,128)(2,1)S(1)} %get-tuple-element.32.pre_ref, bf16[512,512]{1,0:T(8,128)(2,1)S(1)} %get-tuple-element.27.weight_ref, f32[1,512]{1,0:T(1,128)S(1)} %get-tuple-element.33.bias_ref, ...), custom_call_target="tpu_custom_call" | custom-call | flops 3221225472 | bytes 10485760 | tf_op jit(solution)/shard_map/second_part/pallas_call | solution.py:183
  16.3 0.0 collective-permute-done.5.refs_9_
  16.3 0.6 %collective-permute-done.4.refs_8_ = bf16[64,512]{1,0:T(8,128)(2,1)S(1)} collective-permute-done((bf16[64,512]{1,0:T(8,128)(2,1)S(1)}, bf16[64,512]{1,0:T(8,128)(2,1)S(1)}, u32[]{:S(2)}, u32[]{:S(2)}) %collective-permute-start.4) | collective-permute-done | bytes 65568 | tf_op jit(solution)/shard_map/ppermute | solution.py:45
  16.9 0.0 collective-permute-done.3.refs_7_
  16.9 4.2 %after.1 = (bf16[3072,512]{1,0:T(8,128)(2,1)S(1)}, bf16[128,512]{1,0:T(8,128)(2,1)S(1)}, bf16[32,512]{1,0:T(8,128)(2,1)S(1)}, bf16[32,512]{1,0:T(8,128)(2,1)S(1)...) custom-call(s32[1]{0:T(128)} %bitcast.1.refs_6_.me_ref, f32[32,128]{1,0:T(8,128)S(1)} %get-tuple-element.26.ids_ref, ...), custom_call_target="tpu_custom_call" | custom-call | flops 4831838208 | bytes 12582912 | tf_op jit(solution)/shard_map/after/pallas_call | solution.py:301
  21.0 0.1 collective-permute-start.7
  21.2 1.0 %collective-permute-start.8 = (bf16[32,512]{1,0:T(8,128)(2,1)S(1)}, bf16[32,512]{1,0:T(8,128)(2,1)S(1)}, u32[]{:S(2)}, u32[]{:S(2)}) collective-permute-start(bf16[32,512]{1,0:T(8,128)(2,1)S(1)} %get-tuple-element.43), channel_id=1, source_target_pairs={{0,2},{1,3},{2,0},{3,1},{4,6},{5,7},{6,4},{7,5},{8,10},{9,11},{10,... | collective-permute-start | bytes 98312 | tf_op jit(solution)/shard_map/ppermute | solution.py:45
  22.1 0.8 %collective-permute-start.9 = (bf16[32,512]{1,0:T(8,128)(2,1)S(1)}, bf16[32,512]{1,0:T(8,128)(2,1)S(1)}, u32[]{:S(2)}, u32[]{:S(2)}) collective-permute-start(bf16[32,512]{1,0:T(8,128)(2,1)S(1)} %get-tuple-element.44), channel_id=1, source_target_pairs={{0,3},{1,2},{2,1},{3,0},{4,7},{5,6},{6,5},{7,4},{8,11},{9,10},{10,... | collective-permute-start | bytes 98312 | tf_op jit(solution)/shard_map/ppermute | solution.py:45
  23.0 2.2 %collective-permute-start.6 = (bf16[128,512]{1,0:T(8,128)(2,1)S(1)}, bf16[128,512]{1,0:T(8,128)(2,1)S(1)}, u32[]{:S(2)}, u32[]{:S(2)}) collective-permute-start(bf16[128,512]{1,0:T(8,128)(2,1)S(1)} %get-tuple-element.39), channel_id=1, source_target_pairs={{0,1},{1,2},{2,3},{3,4},{4,5},{5,6},{6,7},{7,8},{8,9},{9,10},{10,1... | collective-permute-start | bytes 393224 | tf_op jit(solution)/shard_map/ppermute | solution.py:476
  25.2 1.8 %segments.1.total_ref.refs_4_ = f32[2448,512]{1,0:T(8,128)S(1)} custom-call(s32[3072]{0:T(1024)S(1)} %copy-done.1, s32[1,3072]{1,0:T(1,128)S(1)} %bitcast.8, bf16[3072,512]{1,0:T(8,128)(2,1)S(1)} %get-tuple-element.38.d_ref), custom_call_target="tpu_custom_call" | custom-call | flops 3221225472 | bytes 6291456 | tf_op jit(solution)/shard_map/segments/pallas_call | solution.py:327
  27.1 0.8 %collective-permute-start.10 = (bf16[32,512]{1,0:T(8,128)(2,1)S(1)}, bf16[32,512]{1,0:T(8,128)(2,1)S(1)}, u32[]{:S(2)}, u32[]{:S(2)}) collective-permute-start(bf16[32,512]{1,0:T(8,128)(2,1)S(1)} %get-tuple-element.46), channel_id=1, source_target_pairs={{0,4},{1,5},{2,6},{3,7},{4,0},{5,1},{6,2},{7,3},{8,12},{9,13},{10,... | collective-permute-start | bytes 98312 | tf_op jit(solution)/shard_map/ppermute | solution.py:45
  27.9 1.4 %collective-permute-start.11 = (bf16[32,512]{1,0:T(8,128)(2,1)S(1)}, bf16[32,512]{1,0:T(8,128)(2,1)S(1)}, u32[]{:S(2)}, u32[]{:S(2)}) collective-permute-start(bf16[32,512]{1,0:T(8,128)(2,1)S(1)} %get-tuple-element.47), channel_id=1, source_target_pairs={{0,8},{1,9},{2,10},{3,11},{4,12},{5,13},{6,14},{7,15},{8,0},{9,1},... | collective-permute-start | bytes 98312 | tf_op jit(solution)/shard_map/ppermute | solution.py:45
  29.2 2.3 %collective-permute-start.12 = (bf16[32,512]{1,0:T(8,128)(2,1)S(1)}, bf16[32,512]{1,0:T(8,128)(2,1)S(1)}, u32[]{:S(2)}, u32[]{:S(2)}) collective-permute-start(bf16[32,512]{1,0:T(8,128)(2,1)S(1)} %get-tuple-element.48), channel_id=1, source_target_pairs={{0,12},{1,13},{2,14},{3,15},{4,8},{5,9},{6,10},{7,11},{8,4},{9,5},... | collective-permute-start | bytes 98312 | tf_op jit(solution)/shard_map/ppermute | solution.py:45
  31.5 2.1 %grid_rows.1.refs_5_ = bf16[2048,512]{1,0:T(8,128)(2,1)} custom-call(f32[2448,512]{1,0:T(8,128)S(1)} %segments.1.total_ref.refs_4_, bf16[128,512]{1,0:T(8,128)(2,1)S(1)} %collective-permute-done.6.carried_ref, bf16[512,512]{1,0:T(8,128)(2,1)S(1)} %get-tuple-element.40.weight_ref), custom_call_target="tpu_custom_call" | custom-call | flops 1073741824 | bytes 6291456 | tf_op jit(solution)/shard_map/grid_rows/pallas_call | solution.py:356
  33.7 1.3 %collective-permute-done.12.refs_3_ = bf16[32,512]{1,0:T(8,128)(2,1)S(1)} collective-permute-done((bf16[32,512]{1,0:T(8,128)(2,1)S(1)}, bf16[32,512]{1,0:T(8,128)(2,1)S(1)}, u32[]{:S(2)}, u32[]{:S(2)}) %collective-permute-start.12) | collective-permute-done | bytes 32800 | tf_op jit(solution)/shard_map/ppermute | solution.py:45
  34.9 1.0 %mesh_rows.1 = bf16[16,512]{1,0:T(8,128)(2,1)} custom-call(bf16[32,512]{1,0:T(8,128)(2,1)S(1)} %get-tuple-element.45.refs_0_, bf16[32,512]{1,0:T(8,128)(2,1)S(1)} %collective-permute-done.10.refs_1_, bf16[32,512]{1,0:T(8,128)(2,1)S(1)} %collective-permute-done.11.refs_2_, bf16[32,512]{1,0:T(8,128)(2,1)S(1)} %collective-permute-done.12.refs_3_, ...), custom_call_target="tpu_custom_call" | custom-call | flops 8388608 | bytes 524288 | tf_op jit(solution)/shard_map/mesh_rows/pallas_call | solution.py:409
  (14 shorter events, 0.1 us)
Async XLA Ops:
  0.6 8.9 %collective-permute-start = (bf16[16,512]{1,0:T(8,128)(2,1)}, bf16[16,512]{1,0:T(8,128)(2,1)S(1)}, u32[]{:S(2)}, u32[]{:S(2)}) collective-permute-start(bf16[16,512]{1,0:T(8,128)(2,1)} %refs_5_.1), channel_id=1, source_target_pairs={{0,4},{1,5},{2,6},{3,7},{4,0},{5,1},{6,2},{7,3},{8,12},{9,13},{10,... | collective-permute-start | bytes 49160 | tf_op jit(solution)/shard_map/ppermute | solution.py:45
  3.7 6.0 %collective-permute-start.2 = (bf16[16,512]{1,0:T(8,128)(2,1)}, bf16[16,512]{1,0:T(8,128)(2,1)S(1)}, u32[]{:S(2)}, u32[]{:S(2)}) collective-permute-start(bf16[16,512]{1,0:T(8,128)(2,1)} %refs_5_.1), channel_id=1, source_target_pairs={{0,12},{1,13},{2,14},{3,15},{4,8},{5,9},{6,10},{7,11},{8,4},{9,5},... | collective-permute-start | bytes 49160 | tf_op jit(solution)/shard_map/ppermute | solution.py:45
  6.2 4.9 %collective-permute-start.1 = (bf16[16,512]{1,0:T(8,128)(2,1)}, bf16[16,512]{1,0:T(8,128)(2,1)S(1)}, u32[]{:S(2)}, u32[]{:S(2)}) collective-permute-start(bf16[16,512]{1,0:T(8,128)(2,1)} %refs_5_.1), channel_id=1, source_target_pairs={{0,8},{1,9},{2,10},{3,11},{4,12},{5,13},{6,14},{7,15},{8,0},{9,1},... | collective-permute-start | bytes 49160 | tf_op jit(solution)/shard_map/ppermute | solution.py:45
  11.1 5.2 %collective-permute-start.5 = (bf16[64,512]{1,0:T(8,128)(2,1)S(1)}, bf16[64,512]{1,0:T(8,128)(2,1)S(1)}, u32[]{:S(2)}, u32[]{:S(2)}) collective-permute-start(bf16[64,512]{1,0:T(8,128)(2,1)S(1)} %join.1.after_ref.refs_6_), channel_id=1, source_target_pairs={{0,3},{1,2},{2,1},{3,0},{4,7},{5,6},{6,5},{7,4},{8,11},{9,10},{10,... | collective-permute-start | bytes 196616 | tf_op jit(solution)/shard_map/ppermute | solution.py:45
  11.1 5.8 %collective-permute-start.4 = (bf16[64,512]{1,0:T(8,128)(2,1)S(1)}, bf16[64,512]{1,0:T(8,128)(2,1)S(1)}, u32[]{:S(2)}, u32[]{:S(2)}) collective-permute-start(bf16[64,512]{1,0:T(8,128)(2,1)S(1)} %join.1.after_ref.refs_6_), channel_id=1, source_target_pairs={{0,2},{1,3},{2,0},{3,1},{4,6},{5,7},{6,4},{7,5},{8,10},{9,11},{10,... | collective-permute-start | bytes 196616 | tf_op jit(solution)/shard_map/ppermute | solution.py:45
  12.6 4.2 %collective-permute-start.3 = (bf16[64,512]{1,0:T(8,128)(2,1)S(1)}, bf16[64,512]{1,0:T(8,128)(2,1)S(1)}, u32[]{:S(2)}, u32[]{:S(2)}) collective-permute-start(bf16[64,512]{1,0:T(8,128)(2,1)S(1)} %join.1.after_ref.refs_6_), channel_id=1, source_target_pairs={{0,1},{1,0},{2,3},{3,2},{4,5},{5,4},{6,7},{7,6},{8,9},{9,8},{10,11... | collective-permute-start | bytes 196616 | tf_op jit(solution)/shard_map/ppermute | solution.py:45
  12.9 3.9 %copy-start = (s32[3072]{0:T(1024)S(1)}, s32[3072]{0:T(1024)}, u32[]{:S(2)}) copy-start(s32[3072]{0:T(1024)} %param.12) | copy-start | bytes 36868
  12.9 3.9 %copy-start.1 = (s32[3072]{0:T(1024)S(1)}, s32[3072]{0:T(1024)}, u32[]{:S(2)}) copy-start(s32[3072]{0:T(1024)} %starts_ref.1) | copy-start | bytes 36868
  21.0 6.0 %collective-permute-start.7 = (bf16[32,512]{1,0:T(8,128)(2,1)S(1)}, bf16[32,512]{1,0:T(8,128)(2,1)S(1)}, u32[]{:S(2)}, u32[]{:S(2)}) collective-permute-start(bf16[32,512]{1,0:T(8,128)(2,1)S(1)} %get-tuple-element.42), channel_id=1, source_target_pairs={{0,1},{1,0},{2,3},{3,2},{4,5},{5,4},{6,7},{7,6},{8,9},{9,8},{10,11... | collective-permute-start | bytes 98312 | tf_op jit(solution)/shard_map/ppermute | solution.py:45
  21.2 5.8 %collective-permute-start.8 = (bf16[32,512]{1,0:T(8,128)(2,1)S(1)}, bf16[32,512]{1,0:T(8,128)(2,1)S(1)}, u32[]{:S(2)}, u32[]{:S(2)}) collective-permute-start(bf16[32,512]{1,0:T(8,128)(2,1)S(1)} %get-tuple-element.43), channel_id=1, source_target_pairs={{0,2},{1,3},{2,0},{3,1},{4,6},{5,7},{6,4},{7,5},{8,10},{9,11},{10,... | collective-permute-start | bytes 98312 | tf_op jit(solution)/shard_map/ppermute | solution.py:45
  22.1 4.9 %collective-permute-start.9 = (bf16[32,512]{1,0:T(8,128)(2,1)S(1)}, bf16[32,512]{1,0:T(8,128)(2,1)S(1)}, u32[]{:S(2)}, u32[]{:S(2)}) collective-permute-start(bf16[32,512]{1,0:T(8,128)(2,1)S(1)} %get-tuple-element.44), channel_id=1, source_target_pairs={{0,3},{1,2},{2,1},{3,0},{4,7},{5,6},{6,5},{7,4},{8,11},{9,10},{10,... | collective-permute-start | bytes 98312 | tf_op jit(solution)/shard_map/ppermute | solution.py:45
  23.0 8.6 %collective-permute-start.6 = (bf16[128,512]{1,0:T(8,128)(2,1)S(1)}, bf16[128,512]{1,0:T(8,128)(2,1)S(1)}, u32[]{:S(2)}, u32[]{:S(2)}) collective-permute-start(bf16[128,512]{1,0:T(8,128)(2,1)S(1)} %get-tuple-element.39), channel_id=1, source_target_pairs={{0,1},{1,2},{2,3},{3,4},{4,5},{5,6},{6,7},{7,8},{8,9},{9,10},{10,1... | collective-permute-start | bytes 393224 | tf_op jit(solution)/shard_map/ppermute | solution.py:476
  27.1 6.6 %collective-permute-start.10 = (bf16[32,512]{1,0:T(8,128)(2,1)S(1)}, bf16[32,512]{1,0:T(8,128)(2,1)S(1)}, u32[]{:S(2)}, u32[]{:S(2)}) collective-permute-start(bf16[32,512]{1,0:T(8,128)(2,1)S(1)} %get-tuple-element.46), channel_id=1, source_target_pairs={{0,4},{1,5},{2,6},{3,7},{4,0},{5,1},{6,2},{7,3},{8,12},{9,13},{10,... | collective-permute-start | bytes 98312 | tf_op jit(solution)/shard_map/ppermute | solution.py:45
  27.9 5.8 %collective-permute-start.11 = (bf16[32,512]{1,0:T(8,128)(2,1)S(1)}, bf16[32,512]{1,0:T(8,128)(2,1)S(1)}, u32[]{:S(2)}, u32[]{:S(2)}) collective-permute-start(bf16[32,512]{1,0:T(8,128)(2,1)S(1)} %get-tuple-element.47), channel_id=1, source_target_pairs={{0,8},{1,9},{2,10},{3,11},{4,12},{5,13},{6,14},{7,15},{8,0},{9,1},... | collective-permute-start | bytes 98312 | tf_op jit(solution)/shard_map/ppermute | solution.py:45
  29.2 5.7 %collective-permute-start.12 = (bf16[32,512]{1,0:T(8,128)(2,1)S(1)}, bf16[32,512]{1,0:T(8,128)(2,1)S(1)}, u32[]{:S(2)}, u32[]{:S(2)}) collective-permute-start(bf16[32,512]{1,0:T(8,128)(2,1)S(1)} %get-tuple-element.48), channel_id=1, source_target_pairs={{0,12},{1,13},{2,14},{3,15},{4,8},{5,9},{6,10},{7,11},{8,4},{9,5},... | collective-permute-start | bytes 98312 | tf_op jit(solution)/shard_map/ppermute | solution.py:45

commit v7 on v6

--- a/solution.py
+++ b/solution.py
@@ -22,22 +22,17 @@
 DMA = pltpu.SemaphoreType.DMA
 
 
-def stages_of(count):
+def bits_of(count):
     top = count.bit_length() - 1
     assert count == 1 << top
-    stages = []
-    while top > 0:
-        low = max(0, top - 2)
-        stages.append((low, 1 << (top - low)))
-        top = low
-    return stages
+    return list(range(top))[::-1]
 
 
 def distance_of(row, caps, count):
     group, distance, left = row // caps, 0, count
-    for shift, radix in reversed(stages_of(count)):
-        left //= radix
-        distance = distance + ((group // left) % radix << shift)
+    for bit in reversed(bits_of(count)):
+        left //= 2
+        distance = distance + ((group // left) % 2 << bit)
     return distance
 
 
@@ -106,23 +101,22 @@
 
 def first_kernel(block, copies, pre_hbm, *refs):
     sources, (me_ref, requests_hbm), refs = refs[:copies], refs[copies : copies + 2], refs[copies + 2 :]
-    targets, refs = refs[:copies], refs[copies:]
-    ids_ref, other_ref, normed_ref, q_ref, gate_ref, pre_ref, requests_ref, sem = refs
+    targets, (ids_ref, *refs) = refs[:copies], refs[copies:]
+    *later, normed_ref, q_ref, gate_ref, pre_ref, requests_ref, sem = refs
     rows = normed_ref.shape[0]
 
     def load(k, source, target):
         return pltpu.make_async_copy(source, target, sem.at[k])
 
     others = [load(k, a, b) for k, (a, b) in enumerate(zip(sources, targets))]
-    starts = list(range(0, rows, block))
-    more_rows = other_ref.shape[0]
-    loads = [
-        load(copies + k, pre_hbm.at[pl.ds(at, block)], pre_ref.at[pl.ds(at, block)])
-        for k, at in enumerate(starts)
-    ]
-    more = load(copies + len(loads), pre_hbm.at[pl.ds(rows, more_rows)], other_ref)
-    asked = load(copies + len(loads) + 1, requests_hbm, requests_ref)
-    for copy in others[:2] + loads + others[2:] + [more, asked]:
+    parts, at = [], 0
+    for target in [pre_ref.at[pl.ds(k, block)] for k in range(0, rows, block)] + later:
+        size = target.shape[0]
+        parts.append(load(copies + len(parts), pre_hbm.at[pl.ds(at, size)], target))
+        at += size
+    loads, more = parts[: rows // block], parts[rows // block :]
+    asked = load(copies + len(parts), requests_hbm, requests_ref)
+    for copy in others[:2] + loads + others[2:] + more + [asked]:
         copy.start()
     for copy in others[:2]:
         copy.wait()
@@ -136,7 +130,7 @@
         block,
         lambda at: loads[at // block].wait(),
     )
-    for copy in others[2:] + [more, asked]:
+    for copy in others[2:] + more + [asked]:
         copy.wait()
     slots, caps = ids_ref.shape[0], requests_ref.shape[1]
     count = slots // caps
@@ -148,12 +142,12 @@
     ids_ref[...] = ids.astype(F32)
 
 
-def first_part(preact, rows, sources, me, requests, block=512):
-    edges, width = preact.shape
+def first_part(preact, sizes, sources, me, requests, block=512):
+    width, rows = preact.shape[1], sizes[0]
     copies = len(sources)
     outs = [in_vmem(a.shape, a.dtype) for a in sources]
     outs += [in_vmem((requests.shape[1] * requests.shape[2], LANES), F32)]
-    outs += [in_vmem((edges - rows, width), BF16)]
+    outs += [in_vmem((size, width), BF16) for size in sizes[1:]]
     outs += [in_vmem((rows, width), BF16)] * 2 + [in_vmem((rows, width), F32)]
     return pl.pallas_call(
         functools.partial(first_kernel, block, copies),
@@ -163,7 +157,7 @@
         scratch_shapes=[
             pltpu.VMEM((rows, width), BF16),
             pltpu.SMEM(requests.shape, jnp.int32),
-            DMA((copies + rows // block + 2,)),
+            DMA((copies + rows // block + len(sizes),)),
         ],
         cost_estimate=cost(6 * rows * width * width, 10 * rows * width),
         compiler_params=params(16),
@@ -171,23 +165,23 @@
     )(in_hbm(preact), *[in_hbm(a) for a in sources], me, in_hbm(requests))
 
 
-def second_kernel(block, pre_ref, weight_ref, bias_ref, after_ref, normed_ref, q_ref, gate_ref):
+def later_kernel(block, pre_ref, weight_ref, bias_ref, after_ref, normed_ref, q_ref, gate_ref):
     edge_blocks(
         pre_ref, weight_ref[...], bias_ref[...], normed_ref, q_ref, gate_ref, block, lambda at: None
     )
 
 
-def second_part(pre, weight, bias, after, block=512):
+def later_part(pre, weight, bias, after, block=512):
     rows, width = pre.shape
     outs = [in_vmem((rows, width), BF16)] * 2 + [in_vmem((rows, width), F32)]
     return pl.pallas_call(
-        functools.partial(second_kernel, block),
+        functools.partial(later_kernel, block),
         in_specs=[VMEM, VMEM, VMEM, ANY],
         out_specs=[VMEM] * len(outs),
         out_shape=outs,
         cost_estimate=cost(6 * rows * width * width, 10 * rows * width),
         compiler_params=params(16),
-        name="second_part",
+        name="later_part",
     )(pre, weight, bias, after)
 
 
@@ -244,9 +238,9 @@
 
     row = lax.broadcasted_iota(jnp.int32, (slots, 1), 0)
     distance, place, step = distance_of(row, caps, count), jnp.zeros_like(row), 1
-    for shift, radix in stages_of(count):
-        place = place + ((distance >> shift) & (radix - 1)) * step
-        step *= radix
+    for bit in bits_of(count):
+        place = place + ((distance >> bit) & 1) * step
+        step *= 2
     place = place * owned + ids_ref[...][:, :1].astype(jnp.int32)
     piece_rows = pieces[0].shape[0]
     column = lax.broadcasted_iota(jnp.int32, (slots, piece_rows), 1)
@@ -335,34 +329,38 @@
     )(senders, senders.reshape(1, edges), d_preact)
 
 
-def grid_kernel(block, total_ref, carried_ref, weight_ref, out_hbm, out_ref, sem):
+def grid_kernel(first, block, total_ref, carried_ref, weight_ref, after_ref, out_hbm, out_ref, sem):
     weight = weight_ref[...]
     copies = []
-    for k, at in enumerate(range(0, G_DEV, block)):
-        rows = total_ref[at : at + block, :]
-        if at == 0:
+    for k, at in enumerate(range(0, out_ref.shape[0], block)):
+        rows = total_ref[first + at : first + at + block, :]
+        if first + at == 0:
             rows = jnp.concatenate([rows[:RIM] + carried_ref[...].astype(F32), rows[RIM:]], axis=0)
         out_ref[at : at + block, :] = dot_t(rows.astype(BF16), weight).astype(BF16)
         copies.append(
-            pltpu.make_async_copy(out_ref.at[pl.ds(at, block)], out_hbm.at[pl.ds(at, block)], sem.at[k])
+            pltpu.make_async_copy(
+                out_ref.at[pl.ds(at, block)], out_hbm.at[pl.ds(first + at, block)], sem.at[k]
+            )
         )
         copies[-1].start()
     for copy in copies:
         copy.wait()
 
 
-def grid_rows(total, carried, weight, block=512):
+def grid_rows(first, rows, total, carried, weight, after, block=512):
     width = weight.shape[0]
-    return pl.pallas_call(
-        functools.partial(grid_kernel, block),
-        in_specs=[VMEM] * 3,
+    whole = after.shape == (G_DEV, width)
+    return pl.pallas_call(
+        functools.partial(grid_kernel, first, block),
+        in_specs=[VMEM] * 3 + [HBM if whole else ANY],
         out_specs=HBM,
         out_shape=like((G_DEV, width), BF16),
-        scratch_shapes=[pltpu.VMEM((G_DEV, width), BF16), DMA((G_DEV // block,))],
-        cost_estimate=cost(2 * G_DEV * width * width, 6 * G_DEV * width),
+        scratch_shapes=[pltpu.VMEM((rows, width), BF16), DMA((rows // block,))],
+        input_output_aliases={3: 0} if whole else {},
+        cost_estimate=cost(2 * rows * width * width, 6 * rows * width),
         compiler_params=params(16),
         name="grid_rows",
-    )(total, carried, weight)
+    )(total, carried, weight, after)
 
 
 def regroup_kernel(groups, parts, rows, *refs):
@@ -404,17 +402,17 @@
     out_ref[...] = (both[:owned] + both[owned:]).astype(BF16)
 
 
-def mesh_rows(pieces, size, weight, owned, after):
+def mesh_rows(pieces, size, weight, owned):
     width = weight.shape[0]
     return pl.pallas_call(
         functools.partial(mesh_kernel, len(pieces), size),
-        in_specs=[VMEM] * (len(pieces) + 1) + [ANY],
+        in_specs=[VMEM] * (len(pieces) + 1),
         out_specs=VMEM,
         out_shape=like((owned, width), BF16),
         cost_estimate=cost(2 * owned * width * width, 2 * width * width),
         compiler_params=params(8),
         name="mesh_rows",
-    )(*pieces, weight, in_hbm(after))
+    )(*pieces, weight)
 
 
 def on_device(
@@ -433,7 +431,8 @@
     me = lax.axis_index("band")
     owned, width = mesh_cotangent.shape
     edges = saved_preact.shape[0]
-    stages = stages_of(count)
+    bits = bits_of(count)
+    sizes = [edges // 6, edges // 3, edges // 3, edges // 6]
 
     sources = (
         out_weight,
@@ -443,21 +442,18 @@
         ln_gain.reshape(1, width),
         mesh_cotangent,
     )
-    weight, bias, weight_g, weight_m, gain, own_rows, ids, more, *first = first_part(
-        saved_preact, edges // 3, sources, me.reshape(1), mesh_requests.swapaxes(1, 2)
-    )
-
-    held = [mesh_cotangent]
-    for number, (shift, radix) in enumerate(stages):
-        if number == 1:
-            held = [join([own_rows, *held[1:]], first[0])]
-        elif number > 1:
-            held = [join(held, ids)]
-        held += [swap(held[0], count, j << shift) for j in range(1, radix)]
-        if number == 1:
-            second = second_part(more, weight, bias, held[0])
-
-    back = stages[::-1]
+    weight, bias, weight_g, weight_m, gain, own_rows, ids, *later = first_part(
+        saved_preact, sizes, sources, me.reshape(1), mesh_requests.swapaxes(1, 2)
+    )
+    later, parts = later[:-3], [later[-3:]]
+
+    held = [mesh_cotangent, swap(mesh_cotangent, count, 1 << bits[0])]
+    for bit in bits[1:]:
+        whole = join([own_rows, held[1]] if len(parts) == 1 and bit == bits[1] else held, parts[-1][0])
+        held = [whole, swap(whole, count, 1 << bit)]
+        if later:
+            parts.append(later_part(later.pop(0), weight, bias, whole))
+
     d_preact, rim, *chunks = after(
         me.reshape(1),
         ids,
@@ -465,24 +461,28 @@
         edge_senders.reshape(1, edges),
         weight,
         gain,
-        [first, second],
+        parts,
         held,
         owned,
         mesh_requests.shape[2],
-        back[0][1],
-    )
-
-    total = segments(edge_senders, d_preact)
+        2,
+    )
+
     carried = lax.ppermute(rim, "band", [(i, i + 1) for i in range(count - 1)])
-    arrived, left, size = None, count, ids.shape[0] // back[0][1]
-    for shift, radix in back:
-        if arrived is not None:
-            chunks = regroup(arrived, radix, left // radix, size, total)
-            size = size * len(arrived) // radix
-        left //= radix
-        arrived = [chunks[0]] + [swap(chunks[j], count, j << shift) for j in range(1, radix)]
-    grid_adjoint = grid_rows(total, carried, weight_g)
-    mesh_adjoint = mesh_rows(arrived, size, weight_m, owned, grid_adjoint)
+    left, size = count, ids.shape[0] // 2
+    for number, bit in enumerate(reversed(bits)):
+        if number:
+            chunks = regroup(arrived, 2, left // 2, size, last)
+        left //= 2
+        arrived = [chunks[0], swap(chunks[1], count, 1 << bit)]
+        if number == 0:
+            last = total = segments(edge_senders, d_preact)
+        elif number == 1:
+            last = in_hbm(grid_rows(G_DEV // 2, G_DEV // 2, total, rim, weight_g, chunks[0]))
+        elif number == 2:
+            last = in_hbm(grid_rows(0, G_DEV // 2, total, carried, weight_g, last))
+    grid_adjoint = last
+    mesh_adjoint = mesh_rows(arrived, size, weight_m, owned)
     return (grid_adjoint, mesh_adjoint)
 
 

time: 36.1 us -> 40.4 us (1.12)
  waiting for transfers between devices: 3.34 us -> 6.38 us
  Pallas kernels: 15.7 us -> 17.7 us
  starting transfers between devices: 16.2 us -> 15.4 us
    ppermute x12 -> x8, waiting for transfers between devices: 3.33 us -> 6.38 us  [swap(): return lax.ppermute(block, 'band', [(i, i ^ mask) for i in range(count)])]
    pallas_call x2 -> x5, Pallas kernels: 5.48 us -> 8.09 us  [the longest x3 4.98 us: later_part(): pl.pallas_call(functools.partial(later_kernel, block), in_specs=[VMEM, VM...]
    ppermute x12 -> x8, starting transfers between devices: 13.9 us -> 13.2 us  [swap(): return lax.ppermute(block, 'band', [(i, i ^ mask) for i in range(count)])]
    pallas_call x1, Pallas kernels: 3.23 us -> 2.52 us  [first_part(): pl.pallas_call(functools.partial(first_kernel, block, copies), in_specs=[...]
  transfers between devices with their start and end apart: 13 -> 9, of which waited for: 4 -> 6; matrix products, arithmetic and copies ran while one was open for 0% -> 0% of each run, Pallas kernels for 29% -> 31%
where the time goes in v7:
time: 40.4 us; the launch traced here: 40.2 us
  Pallas kernels  17.7 us (44%)
  starting transfers between devices  15.4 us (38%)
  waiting for transfers between devices  6.38 us (16%)
  between operations  0.76 us (2%)
    ppermute x8, starting transfers between devices, swap(): return lax.ppermute(block, 'band', [(i, i ^ mask) for i in range(count)])  13.2 us
    ppermute x8, waiting for transfers between devices, swap(): return lax.ppermute(block, 'band', [(i, i ^ mask) for i in range(count)])  6.38 us
    pallas_call x3, Pallas kernels, later_part(): pl.pallas_call(functools.partial(later_kernel, block), in_specs=[VMEM, VM...  4.98 us
    pallas_call x1, Pallas kernels, after(): pl.pallas_call(functools.partial(after_kernel, len(parts), chunks, owned,...  4.18 us
    pallas_call x2, Pallas kernels, grid_rows(): pl.pallas_call(functools.partial(grid_kernel, first, block), in_specs=[VM...  3.12 us
    pallas_call x1, Pallas kernels, first_part(): pl.pallas_call(functools.partial(first_kernel, block, copies), in_specs=[...  2.52 us
    ppermute x1, starting transfers between devices, on_device(): carried = lax.ppermute(rim, 'band', [(i, i + 1) for i in range(count - 1)])  2.25 us
    pallas_call x1, Pallas kernels, segments(): pl.pallas_call(functools.partial(segments_kernel, block), in_specs=[SMEM]...  1.77 us
  transfers between devices with their start and end apart: 9, of which 6 were waited for; matrix products, arithmetic and copies ran while one was open for 0% of the time, Pallas kernels for 31%

profile of v7, /device:TPU:0, one launch (start us, length us, event | category | flops | bytes accessed | tf_op | source)
XLA Modules:
  0.0 40.2 jit_solution(13497558032957355915)
XLA Ops:
  0.6 4.1 %collective-permute-start = (bf16[16,512]{1,0:T(8,128)(2,1)}, bf16[16,512]{1,0:T(8,128)(2,1)S(1)}, u32[]{:S(2)}, u32[]{:S(2)}) collective-permute-start(bf16[16,512]{1,0:T(8,128)(2,1)} %refs_5_.1), channel_id=1, source_target_pairs={{0,8},{1,9},{2,10},{3,11},{4,12},{5,13},{6,14},{7,15},{8,0},{9,1},... | collective-permute-start | bytes 49160 | tf_op jit(solution)/shard_map/ppermute | solution.py:40
  4.7 2.5 %first_part.1 = (bf16[512,512]{1,0:T(8,128)(2,1)S(1)}, f32[1,512]{1,0:T(1,128)S(1)}, bf16[512,512]{1,0:T(8,128)(2,1)S(1)}, bf16[512,512]{1,0:T(8,128)(2,1)S(1)},...) custom-call(bf16[3072,512]{1,0:T(8,128)(2,1)} %pre_hbm.1, ...), custom_call_target="tpu_custom_call" | custom-call | flops 805306368 | bytes 2621440 | tf_op jit(solution)/shard_map/first_part/pallas_call | solution.py:152
  7.3 1.6 %collective-permute-start.1 = (bf16[32,512]{1,0:T(8,128)(2,1)S(1)}, bf16[32,512]{1,0:T(8,128)(2,1)S(1)}, u32[]{:S(2)}, u32[]{:S(2)}) collective-permute-start(bf16[32,512]{1,0:T(8,128)(2,1)S(1)} %join.3.after_ref.refs_0_), channel_id=1, source_target_pairs={{0,4},{1,5},{2,6},{3,7},{4,0},{5,1},{6,2},{7,3},{8,12},{9,13},{10,... | collective-permute-start | bytes 98312 | tf_op jit(solution)/shard_map/ppermute | solution.py:40
  8.9 1.9 %later_part.3 = (bf16[1024,512]{1,0:T(8,128)(2,1)S(1)}, bf16[1024,512]{1,0:T(8,128)(2,1)S(1)}, f32[1024,512]{1,0:T(8,128)S(1)}) custom-call(bf16[1024,512]{1,0:T(8,128)(2,1)S(1)} %get-tuple-element.40.pre_ref, bf16[512,512]{1,0:T(8,128)(2,1)S(1)} %get-tuple-element.35.weight_ref, f32[1,512]{1,0:T(1,128)S(1)} %get-tuple-element.41.bias_ref, ...), custom_call_target="tpu_custom_call" | custom-call | flops 1610612736 | bytes 5242880 | tf_op jit(solution)/shard_map/later_part/pallas_call | solution.py:177
  10.9 0.4 %collective-permute-done.1.refs_1_ = bf16[32,512]{1,0:T(8,128)(2,1)S(1)} collective-permute-done((bf16[32,512]{1,0:T(8,128)(2,1)S(1)}, bf16[32,512]{1,0:T(8,128)(2,1)S(1)}, u32[]{:S(2)}, u32[]{:S(2)}) %collective-permute-start.1) | collective-permute-done | bytes 32800 | tf_op jit(solution)/shard_map/ppermute | solution.py:40
  11.3 1.5 %collective-permute-start.2 = (bf16[64,512]{1,0:T(8,128)(2,1)S(1)}, bf16[64,512]{1,0:T(8,128)(2,1)S(1)}, u32[]{:S(2)}, u32[]{:S(2)}) collective-permute-start(bf16[64,512]{1,0:T(8,128)(2,1)S(1)} %join.4.after_ref.refs_0_), channel_id=1, source_target_pairs={{0,2},{1,3},{2,0},{3,1},{4,6},{5,7},{6,4},{7,5},{8,10},{9,11},{10,... | collective-permute-start | bytes 196616 | tf_op jit(solution)/shard_map/ppermute | solution.py:40
  12.8 1.9 %later_part.4 = (bf16[1024,512]{1,0:T(8,128)(2,1)S(1)}, bf16[1024,512]{1,0:T(8,128)(2,1)S(1)}, f32[1024,512]{1,0:T(8,128)S(1)}) custom-call(bf16[1024,512]{1,0:T(8,128)(2,1)S(1)} %get-tuple-element.46.pre_ref, bf16[512,512]{1,0:T(8,128)(2,1)S(1)} %get-tuple-element.35.weight_ref, f32[1,512]{1,0:T(1,128)S(1)} %get-tuple-element.41.bias_ref, ...), custom_call_target="tpu_custom_call" | custom-call | flops 1610612736 | bytes 5242880 | tf_op jit(solution)/shard_map/later_part/pallas_call | solution.py:177
  14.7 0.9 %collective-permute-done.2.refs_1_ = bf16[64,512]{1,0:T(8,128)(2,1)S(1)} collective-permute-done((bf16[64,512]{1,0:T(8,128)(2,1)S(1)}, bf16[64,512]{1,0:T(8,128)(2,1)S(1)}, u32[]{:S(2)}, u32[]{:S(2)}) %collective-permute-start.2) | collective-permute-done | bytes 65568 | tf_op jit(solution)/shard_map/ppermute | solution.py:40
  15.6 0.1 collective-permute-start.3
  15.6 1.2 %later_part.5 = (bf16[512,512]{1,0:T(8,128)(2,1)S(1)}, bf16[512,512]{1,0:T(8,128)(2,1)S(1)}, f32[512,512]{1,0:T(8,128)S(1)}) custom-call(bf16[512,512]{1,0:T(8,128)(2,1)S(1)} %get-tuple-element.50.pre_ref, bf16[512,512]{1,0:T(8,128)(2,1)S(1)} %get-tuple-element.35.weight_ref, f32[1,512]{1,0:T(1,128)S(1)} %get-tuple-element.41.bias_ref, ...), custom_call_target="tpu_custom_call" | custom-call | flops 805306368 | bytes 2621440 | tf_op jit(solution)/shard_map/later_part/pallas_call | solution.py:177
  16.8 0.2 collective-permute-done.3.refs_13_
  17.0 4.2 %after.1 = (bf16[3072,512]{1,0:T(8,128)(2,1)S(1)}, bf16[128,512]{1,0:T(8,128)(2,1)S(1)}, bf16[48,512]{1,0:T(8,128)(2,1)S(1)}, bf16[48,512]{1,0:T(8,128)(2,1)S(1)}) custom-call(s32[1]{0:T(128)} %bitcast.1.refs_6_.me_ref, f32[32,128]{1,0:T(8,128)S(1)} %get-tuple-element.34.ids_ref, s32[1,3072]{1,0:T(1,128)S(1)} %bitcast.6, s32[1,3072]{1,0:T(1,128)S(1)} %bitcast.7, ...), custom_call_target="tpu_custom_call" | custom-call | flops 4831838208 | bytes 12582912 | tf_op jit(solution)/shard_map/after/pallas_call | solution.py:295
  21.2 0.4 %collective-permute-start.5 = (bf16[48,512]{1,0:T(8,128)(2,1)S(1)}, bf16[48,512]{1,0:T(8,128)(2,1)S(1)}, u32[]{:S(2)}, u32[]{:S(2)}) collective-permute-start(bf16[48,512]{1,0:T(8,128)(2,1)S(1)} %get-tuple-element.58), channel_id=1, source_target_pairs={{0,1},{1,0},{2,3},{3,2},{4,5},{5,4},{6,7},{7,6},{8,9},{9,8},{10,11... | collective-permute-start | bytes 147464 | tf_op jit(solution)/shard_map/ppermute | solution.py:40
  21.6 2.2 %collective-permute-start.4 = (bf16[128,512]{1,0:T(8,128)(2,1)S(1)}, bf16[128,512]{1,0:T(8,128)(2,1)S(1)}, u32[]{:S(2)}, u32[]{:S(2)}) collective-permute-start(bf16[128,512]{1,0:T(8,128)(2,1)S(1)} %get-tuple-element.55.carried_ref), channel_id=1, source_target_pairs={{0,1},{1,2},{2,3},{3,4},{4,5},{5,6},{6,7},{7,8},{8,9},{9,10},{10,1... | collective-permute-start | bytes 393224 | tf_op jit(solution)/shard_map/ppermute | solution.py:471
  23.8 1.8 %segments.1.refs_2_.total_ref = f32[2448,512]{1,0:T(8,128)S(1)} custom-call(s32[3072]{0:T(1024)S(1)} %copy-done.1, s32[1,3072]{1,0:T(1,128)S(1)} %bitcast.8, bf16[3072,512]{1,0:T(8,128)(2,1)S(1)} %get-tuple-element.54.d_ref), custom_call_target="tpu_custom_call" | custom-call | flops 3221225472 | bytes 6291456 | tf_op jit(solution)/shard_map/segments/pallas_call | solution.py:321
  25.7 1.6 %collective-permute-start.6 = (bf16[48,512]{1,0:T(8,128)(2,1)S(1)}, bf16[48,512]{1,0:T(8,128)(2,1)S(1)}, u32[]{:S(2)}, u32[]{:S(2)}) collective-permute-start(bf16[48,512]{1,0:T(8,128)(2,1)S(1)} %get-tuple-element.60), channel_id=1, source_target_pairs={{0,2},{1,3},{2,0},{3,1},{4,6},{5,7},{6,4},{7,5},{8,10},{9,11},{10,... | collective-permute-start | bytes 147464 | tf_op jit(solution)/shard_map/ppermute | solution.py:40
  27.2 1.6 %grid_rows.2.after_ref.refs_2_ = bf16[2048,512]{1,0:T(8,128)(2,1)} custom-call(f32[2448,512]{1,0:T(8,128)S(1)} %segments.1.refs_2_.total_ref, bf16[128,512]{1,0:T(8,128)(2,1)S(1)} %get-tuple-element.55.carried_ref, bf16[512,512]{1,0:T(8,128)(2,1)S(1)} %get-tuple-element.56.weight_ref, bf16[48,512]{1,0:T(8,128)(2,1)S(1)} %get-tuple-element.59.after_ref.refs_0_), custom_call_target="tpu_custom_call" | custom-call | flops 536870912 | bytes 3145728 | tf_op jit(solution)/shard_map/grid_rows/pallas_call | solution.py:353
  28.8 1.2 %collective-permute-done.6.refs_1_ = bf16[48,512]{1,0:T(8,128)(2,1)S(1)} collective-permute-done((bf16[48,512]{1,0:T(8,128)(2,1)S(1)}, bf16[48,512]{1,0:T(8,128)(2,1)S(1)}, u32[]{:S(2)}, u32[]{:S(2)}) %collective-permute-start.6) | collective-permute-done | bytes 49184 | tf_op jit(solution)/shard_map/ppermute | solution.py:40
  30.0 1.6 %collective-permute-start.7 = (bf16[48,512]{1,0:T(8,128)(2,1)S(1)}, bf16[48,512]{1,0:T(8,128)(2,1)S(1)}, u32[]{:S(2)}, u32[]{:S(2)}) collective-permute-start(bf16[48,512]{1,0:T(8,128)(2,1)S(1)} %get-tuple-element.62), channel_id=1, source_target_pairs={{0,4},{1,5},{2,6},{3,7},{4,0},{5,1},{6,2},{7,3},{8,12},{9,13},{10,... | collective-permute-start | bytes 147464 | tf_op jit(solution)/shard_map/ppermute | solution.py:40
  31.6 1.6 %grid_rows.3.refs_2_ = bf16[2048,512]{1,0:T(8,128)(2,1)} custom-call(f32[2448,512]{1,0:T(8,128)S(1)} %segments.1.refs_2_.total_ref, bf16[128,512]{1,0:T(8,128)(2,1)S(1)} %collective-permute-done.4.carried_ref, bf16[512,512]{1,0:T(8,128)(2,1)S(1)} %get-tuple-element.56.weight_ref, ...), custom_call_target="tpu_custom_call", output_to_operand_aliasing={{}: (3, {})} | custom-call | flops 536870912 | bytes 3145728 | tf_op jit(solution)/shard_map/grid_rows/pallas_call | solution.py:353
  33.2 1.0 %collective-permute-done.7.refs_1_ = bf16[48,512]{1,0:T(8,128)(2,1)S(1)} collective-permute-done((bf16[48,512]{1,0:T(8,128)(2,1)S(1)}, bf16[48,512]{1,0:T(8,128)(2,1)S(1)}, u32[]{:S(2)}, u32[]{:S(2)}) %collective-permute-start.7) | collective-permute-done | bytes 49184 | tf_op jit(solution)/shard_map/ppermute | solution.py:40
  34.1 2.3 %collective-permute-start.8 = (bf16[48,512]{1,0:T(8,128)(2,1)S(1)}, bf16[48,512]{1,0:T(8,128)(2,1)S(1)}, u32[]{:S(2)}, u32[]{:S(2)}) collective-permute-start(bf16[48,512]{1,0:T(8,128)(2,1)S(1)} %get-tuple-element.64), channel_id=1, source_target_pairs={{0,8},{1,9},{2,10},{3,11},{4,12},{5,13},{6,14},{7,15},{8,0},{9,1},... | collective-permute-start | bytes 147464 | tf_op jit(solution)/shard_map/ppermute | solution.py:40
  36.4 2.8 %collective-permute-done.8.refs_1_ = bf16[48,512]{1,0:T(8,128)(2,1)S(1)} collective-permute-done((bf16[48,512]{1,0:T(8,128)(2,1)S(1)}, bf16[48,512]{1,0:T(8,128)(2,1)S(1)}, u32[]{:S(2)}, u32[]{:S(2)}) %collective-permute-start.8) | collective-permute-done | bytes 49184 | tf_op jit(solution)/shard_map/ppermute | solution.py:40
  39.2 1.0 %mesh_rows.1 = bf16[16,512]{1,0:T(8,128)(2,1)} custom-call(bf16[48,512]{1,0:T(8,128)(2,1)S(1)} %get-tuple-element.63.refs_0_, bf16[48,512]{1,0:T(8,128)(2,1)S(1)} %collective-permute-done.8.refs_1_, bf16[512,512]{1,0:T(8,128)(2,1)S(1)} %get-tuple-element.65.refs_2_), custom_call_target="tpu_custom_call" | custom-call | flops 8388608 | bytes 524288 | tf_op jit(solution)/shard_map/mesh_rows/pallas_call | solution.py:407
  (13 shorter events, 0.1 us)
Async XLA Ops:
  0.6 6.6 %collective-permute-start = (bf16[16,512]{1,0:T(8,128)(2,1)}, bf16[16,512]{1,0:T(8,128)(2,1)S(1)}, u32[]{:S(2)}, u32[]{:S(2)}) collective-permute-start(bf16[16,512]{1,0:T(8,128)(2,1)} %refs_5_.1), channel_id=1, source_target_pairs={{0,8},{1,9},{2,10},{3,11},{4,12},{5,13},{6,14},{7,15},{8,0},{9,1},... | collective-permute-start | bytes 49160 | tf_op jit(solution)/shard_map/ppermute | solution.py:40
  7.3 4.0 %collective-permute-start.1 = (bf16[32,512]{1,0:T(8,128)(2,1)S(1)}, bf16[32,512]{1,0:T(8,128)(2,1)S(1)}, u32[]{:S(2)}, u32[]{:S(2)}) collective-permute-start(bf16[32,512]{1,0:T(8,128)(2,1)S(1)} %join.3.after_ref.refs_0_), channel_id=1, source_target_pairs={{0,4},{1,5},{2,6},{3,7},{4,0},{5,1},{6,2},{7,3},{8,12},{9,13},{10,... | collective-permute-start | bytes 98312 | tf_op jit(solution)/shard_map/ppermute | solution.py:40
  11.3 4.3 %collective-permute-start.2 = (bf16[64,512]{1,0:T(8,128)(2,1)S(1)}, bf16[64,512]{1,0:T(8,128)(2,1)S(1)}, u32[]{:S(2)}, u32[]{:S(2)}) collective-permute-start(bf16[64,512]{1,0:T(8,128)(2,1)S(1)} %join.4.after_ref.refs_0_), channel_id=1, source_target_pairs={{0,2},{1,3},{2,0},{3,1},{4,6},{5,7},{6,4},{7,5},{8,10},{9,11},{10,... | collective-permute-start | bytes 196616 | tf_op jit(solution)/shard_map/ppermute | solution.py:40
  15.5 1.4 %copy-start = (s32[3072]{0:T(1024)S(1)}, s32[3072]{0:T(1024)}, u32[]{:S(2)}) copy-start(s32[3072]{0:T(1024)} %param.12) | copy-start | bytes 36868
  15.5 1.4 %copy-start.1 = (s32[3072]{0:T(1024)S(1)}, s32[3072]{0:T(1024)}, u32[]{:S(2)}) copy-start(s32[3072]{0:T(1024)} %starts_ref.1) | copy-start | bytes 36868
  15.6 1.4 %collective-permute-start.3 = (bf16[128,512]{1,0:T(8,128)(2,1)S(1)}, bf16[128,512]{1,0:T(8,128)(2,1)S(1)}, u32[]{:S(2)}, u32[]{:S(2)}) collective-permute-start(bf16[128,512]{1,0:T(8,128)(2,1)S(1)} %join.5.after_ref.refs_12_), channel_id=1, source_target_pairs={{0,1},{1,0},{2,3},{3,2},{4,5},{5,4},{6,7},{7,6},{8,9},{9,8},{10,11... | collective-permute-start | bytes 393224 | tf_op jit(solution)/shard_map/ppermute | solution.py:40
  21.2 4.4 %collective-permute-start.5 = (bf16[48,512]{1,0:T(8,128)(2,1)S(1)}, bf16[48,512]{1,0:T(8,128)(2,1)S(1)}, u32[]{:S(2)}, u32[]{:S(2)}) collective-permute-start(bf16[48,512]{1,0:T(8,128)(2,1)S(1)} %get-tuple-element.58), channel_id=1, source_target_pairs={{0,1},{1,0},{2,3},{3,2},{4,5},{5,4},{6,7},{7,6},{8,9},{9,8},{10,11... | collective-permute-start | bytes 147464 | tf_op jit(solution)/shard_map/ppermute | solution.py:40
  21.6 10.0 %collective-permute-start.4 = (bf16[128,512]{1,0:T(8,128)(2,1)S(1)}, bf16[128,512]{1,0:T(8,128)(2,1)S(1)}, u32[]{:S(2)}, u32[]{:S(2)}) collective-permute-start(bf16[128,512]{1,0:T(8,128)(2,1)S(1)} %get-tuple-element.55.carried_ref), channel_id=1, source_target_pairs={{0,1},{1,2},{2,3},{3,4},{4,5},{5,6},{6,7},{7,8},{8,9},{9,10},{10,1... | collective-permute-start | bytes 393224 | tf_op jit(solution)/shard_map/ppermute | solution.py:471
  25.7 4.3 %collective-permute-start.6 = (bf16[48,512]{1,0:T(8,128)(2,1)S(1)}, bf16[48,512]{1,0:T(8,128)(2,1)S(1)}, u32[]{:S(2)}, u32[]{:S(2)}) collective-permute-start(bf16[48,512]{1,0:T(8,128)(2,1)S(1)} %get-tuple-element.60), channel_id=1, source_target_pairs={{0,2},{1,3},{2,0},{3,1},{4,6},{5,7},{6,4},{7,5},{8,10},{9,11},{10,... | collective-permute-start | bytes 147464 | tf_op jit(solution)/shard_map/ppermute | solution.py:40
  30.0 4.2 %collective-permute-start.7 = (bf16[48,512]{1,0:T(8,128)(2,1)S(1)}, bf16[48,512]{1,0:T(8,128)(2,1)S(1)}, u32[]{:S(2)}, u32[]{:S(2)}) collective-permute-start(bf16[48,512]{1,0:T(8,128)(2,1)S(1)} %get-tuple-element.62), channel_id=1, source_target_pairs={{0,4},{1,5},{2,6},{3,7},{4,0},{5,1},{6,2},{7,3},{8,12},{9,13},{10,... | collective-permute-start | bytes 147464 | tf_op jit(solution)/shard_map/ppermute | solution.py:40
  34.1 5.1 %collective-permute-start.8 = (bf16[48,512]{1,0:T(8,128)(2,1)S(1)}, bf16[48,512]{1,0:T(8,128)(2,1)S(1)}, u32[]{:S(2)}, u32[]{:S(2)}) collective-permute-start(bf16[48,512]{1,0:T(8,128)(2,1)S(1)} %get-tuple-element.64), channel_id=1, source_target_pairs={{0,8},{1,9},{2,10},{3,11},{4,12},{5,13},{6,14},{7,15},{8,0},{9,1},... | collective-permute-start | bytes 147464 | tf_op jit(solution)/shard_map/ppermute | solution.py:40

commit v8 on v4

--- a/solution.py
+++ b/solution.py
@@ -45,10 +45,6 @@
     return lax.ppermute(block, "band", [(i, i ^ mask) for i in range(count)])
 
 
-def pass_on(block, count, distance):
-    return lax.ppermute(block, "band", [(i, (i + distance) % count) for i in range(count)])
-
-
 def like(shape, dtype):
     return jax.ShapeDtypeStruct(shape, dtype)
 
@@ -82,20 +78,20 @@
     return pltpu.CompilerParams(vmem_limit_bytes=limit * MIB)
 
 
-def products(pre, weight, bias):
-    p = pre.astype(F32)
-    s = 0.5 * jnp.tanh(0.5 * p) + 0.5
-    h = p * s
-    return dot(h.astype(BF16), weight) + bias, s + h * (1.0 - s)
-
-
-def edge_blocks(pre_ref, weight, bias, normed_ref, q_ref, gate_ref, block, arrive):
+def edge_blocks(pre_ref, weight_ref, bias_ref, normed_ref, q_ref, gate_ref, block, arrive, weigh):
     rows, last = pre_ref.shape[0], None
     for at in range(0, rows + block, block):
         this = None
         if at < rows:
             arrive(at)
-            this = products(pre_ref[at : at + block], weight, bias)
+            p = pre_ref[at : at + block].astype(F32)
+            s = 0.5 * jnp.tanh(0.5 * p) + 0.5
+            h = p * s
+            hidden, gate = h.astype(BF16), s + h * (1.0 - s)
+            if at == 0:
+                weigh()
+                weight, bias = weight_ref[...], bias_ref[...]
+            this = dot(hidden, weight) + bias, gate
         if last is not None:
             out, gate = last
             centre = out - jnp.mean(out, axis=-1, keepdims=True)
@@ -126,19 +122,23 @@
     ]
     more = load(copies + len(loads), pre_hbm.at[pl.ds(rows, more_rows)], other_ref)
     asked = load(copies + len(loads) + 1, requests_hbm, requests_ref)
-    for copy in others[:2] + loads + others[2:] + [more, asked]:
+    for copy in loads[:1] + others[:2] + loads[1:] + others[2:] + [more, asked]:
         copy.start()
-    for copy in others[:2]:
-        copy.wait()
+
+    def weigh():
+        for copy in others[:2]:
+            copy.wait()
+
     edge_blocks(
         pre_ref,
-        targets[0][...],
-        targets[1][...],
+        targets[0],
+        targets[1],
         normed_ref,
         q_ref,
         gate_ref,
         block,
         lambda at: loads[at // block].wait(),
+        weigh,
     )
     for copy in others[2:] + [more, asked]:
         copy.wait()
@@ -147,7 +147,7 @@
     row = lax.broadcasted_iota(jnp.int32, ids_ref.shape, 0)
     ids = jnp.zeros(ids_ref.shape, jnp.int32)
     for r in range(slots):
-        owner = (me_ref[0] + distance_of(r, caps, count)) % count
+        owner = me_ref[0] ^ distance_of(r, caps, count)
         ids = jnp.where(row == r, requests_ref[0, r % caps, owner], ids)
     ids_ref[...] = ids.astype(F32)
 
@@ -177,7 +177,7 @@
 
 def second_kernel(block, pre_ref, weight_ref, bias_ref, after_ref, normed_ref, q_ref, gate_ref):
     edge_blocks(
-        pre_ref, weight_ref[...], bias_ref[...], normed_ref, q_ref, gate_ref, block, lambda at: None
+        pre_ref, weight_ref, bias_ref, normed_ref, q_ref, gate_ref, block, lambda at: None, lambda: None
     )
 
 
@@ -219,8 +219,7 @@
 ):
     edge_refs = [refs[3 * k : 3 * k + 3] for k in range(parts)]
     refs = refs[3 * parts :]
-    d_ref, sums_refs = refs[-1 - chunks], refs[-chunks:]
-    pieces = refs[: -1 - chunks]
+    pieces, (d_ref, rim_ref), sums_refs = refs[: -2 - chunks], refs[-2 - chunks : -chunks], refs[-chunks:]
     slots = ids_ref.shape[0]
     count = slots // caps
     edges, width = d_ref.shape
@@ -228,10 +227,9 @@
     weight = weight_ref[...]
 
     row = lax.broadcasted_iota(jnp.int32, (slots, 1), 0)
-    owner = (distance_of(row, caps, count) + me) % count
-    far, place, step = owner ^ me, jnp.zeros_like(row), 1
+    distance, place, step = distance_of(row, caps, count), jnp.zeros_like(row), 1
     for shift, radix in stages_of(count):
-        place = place + ((far >> shift) & (radix - 1)) * step
+        place = place + ((distance >> shift) & (radix - 1)) * step
         step *= radix
     place = place * owned + ids_ref[...][:, :1].astype(jnp.int32)
     piece_rows = pieces[0].shape[0]
@@ -246,7 +244,9 @@
     both = dot_t(jnp.concatenate(split(rows), axis=0), weight)
     s_both = jnp.concatenate(split(both[:slots] + both[slots:]), axis=0)
 
-    key = owner * caps + row % caps
+    key = (distance ^ me) * caps + row % caps
+    key = jnp.concatenate([key, key], axis=0)
+    mean_rows = jnp.concatenate([mean_rows, jnp.zeros_like(mean_rows)], axis=0)
     rim_row = lax.broadcasted_iota(jnp.int32, (RIM, block), 0) + G_DEV
     sums = jnp.zeros((slots, width), F32)
     rim = jnp.zeros((RIM, width), F32)
@@ -260,9 +260,8 @@
             onehot_t = (key == slots_ref[:, number * block : (number + 1) * block]).astype(F32)
             onehot = onehot_t.T
             c = jnp.sum(onehot * dot_t(normed_ref[piece], mean_rows), axis=-1, keepdims=True)
-            onehot = onehot.astype(BF16)
-            s_rows = dot(jnp.concatenate([onehot, onehot], axis=1), s_both)
-            this = (onehot_t.astype(BF16), c, s_rows, q_ref, gate_ref, piece)
+            s_rows = dot(onehot.astype(BF16), s_both)
+            this = (onehot_t[:slots].astype(BF16), c, s_rows, q_ref, gate_ref, piece)
         if last is not None:
             onehot_t, c, s_rows, q_ref, gate_ref, piece = last
             at = (number - 1) * block
@@ -276,21 +275,20 @@
 
     each = slots // chunks
     for k, sums_ref in enumerate(sums_refs):
-        sums_ref[:each, :] = sums[k * each : (k + 1) * each]
-        for at in range(0, width, LANES):
-            sums_ref[each : 2 * each, at : at + LANES] = ids_ref[k * each : (k + 1) * each, :]
-    sums_refs[1][2 * each :, :] = rim
+        sums_ref[:, :width] = sums[k * each : (k + 1) * each]
+        sums_ref[:, width:] = ids_ref[k * each : (k + 1) * each, :]
+    rim_ref[...] = rim.astype(BF16)
 
 
 def after(me, ids, slots, senders, weight, gain, parts, pieces, owned, caps, chunks, block=512):
     edges, width = slots.shape[1], weight.shape[0]
     each = ids.shape[0] // chunks
-    sizes = [2 * each + (RIM if k == 1 else 0) for k in range(chunks)]
     return pl.pallas_call(
         functools.partial(after_kernel, len(parts), chunks, owned, caps, block),
         in_specs=[SMEM] + [VMEM] * (5 + 3 * len(parts) + len(pieces)),
-        out_specs=[VMEM] * (1 + chunks),
-        out_shape=[in_vmem((edges, width), BF16)] + [in_vmem((size, width), F32) for size in sizes],
+        out_specs=[VMEM] * (2 + chunks),
+        out_shape=[in_vmem((edges, width), BF16), in_vmem((RIM, width), BF16)]
+        + [in_vmem((each, width + LANES), F32)] * chunks,
         cost_estimate=cost(6 * edges * width * width, 8 * edges * width),
         compiler_params=params(20),
         name="after",
@@ -328,8 +326,7 @@
     for k, at in enumerate(range(0, G_DEV, block)):
         rows = total_ref[at : at + block, :]
         if at == 0:
-            rim = carried_ref[carried_ref.shape[0] - RIM :, :]
-            rows = jnp.concatenate([rows[:RIM] + rim, rows[RIM:]], axis=0)
+            rows = jnp.concatenate([rows[:RIM] + carried_ref[...].astype(F32), rows[RIM:]], axis=0)
         out_ref[at : at + block, :] = dot_t(rows.astype(BF16), weight).astype(BF16)
         copies.append(
             pltpu.make_async_copy(out_ref.at[pl.ds(at, block)], out_hbm.at[pl.ds(at, block)], sem.at[k])
@@ -353,28 +350,26 @@
     )(total, carried, weight)
 
 
-def regroup_kernel(groups, parts, rows, *refs):
+def regroup_kernel(groups, parts, *refs):
     outs = refs[parts + 1 :]
     low = groups // len(outs)
-    each = rows // groups
+    each = refs[0].shape[0] // groups
     for j, out_ref in enumerate(outs):
-        half = out_ref.shape[0] // 2
         for g in range(low):
             for k in range(parts):
                 to, at = (g * parts + k) * each, (j * low + g) * each
                 out_ref[to : to + each, :] = refs[k][at : at + each, :]
-                out_ref[half + to : half + to + each, :] = refs[k][rows + at : rows + at + each, :]
 
 
 def regroup(arrived, radix, low, after):
-    height, width = arrived[0].shape
+    rows, width = arrived[0].shape
     parts = len(arrived)
     return pl.pallas_call(
-        functools.partial(regroup_kernel, radix * low, parts, height // 2),
+        functools.partial(regroup_kernel, radix * low, parts),
         in_specs=[VMEM] * parts + [ANY],
         out_specs=[VMEM] * radix,
-        out_shape=[in_vmem((height * parts // radix, width), arrived[0].dtype)] * radix,
-        cost_estimate=cost(0, 8 * height * parts * width),
+        out_shape=[in_vmem((rows * parts // radix, width), F32)] * radix,
+        cost_estimate=cost(0, 8 * rows * parts * width),
         compiler_params=params(8),
         name="regroup",
     )(*arrived, after)
@@ -383,14 +378,12 @@
 def mesh_kernel(parts, *refs):
     pieces, weight_ref, out_ref = refs[:parts], refs[parts], refs[-1]
     owned, width = out_ref.shape
-    half = pieces[0].shape[0] // 2
-    rows = jnp.concatenate([piece[:half, :] for piece in pieces], axis=0)
-    ids = jnp.concatenate([piece[half:, :LANES] for piece in pieces], axis=0)
-    ids = ids.T[:owned].astype(jnp.int32)
-    pick = (lax.broadcasted_iota(jnp.int32, ids.shape, 0) == ids).astype(F32).astype(BF16)
-    high, low = split(rows)
-    high, low = split(dot(pick, high) + dot(pick, low))
-    both = dot_t(jnp.concatenate([high, low], axis=0), weight_ref[...])
+    rows = jnp.concatenate([piece[:, :width] for piece in pieces], axis=0)
+    ids = jnp.concatenate([piece[:, width:] for piece in pieces], axis=0)
+    ids = jnp.concatenate([ids, ids], axis=0).T[:owned].astype(jnp.int32)
+    pick = (lax.broadcasted_iota(jnp.int32, ids.shape, 0) == ids).astype(F32)
+    total = dot(pick.astype(BF16), jnp.concatenate(split(rows), axis=0))
+    both = dot_t(jnp.concatenate(split(total), axis=0), weight_ref[...])
     out_ref[...] = (both[:owned] + both[owned:]).astype(BF16)
 
 
@@ -448,7 +441,7 @@
             second = second_part(more, weight, bias, held[0])
 
     back = stages[::-1]
-    d_preact, *chunks = after(
+    d_preact, rim, *chunks = after(
         me.reshape(1),
         ids,
         edge_slots.reshape(1, edges),
@@ -463,14 +456,14 @@
     )
 
     total = segments(edge_senders, d_preact)
+    carried = lax.ppermute(rim, "band", [(i, (i + 1) % count) for i in range(count)])
     arrived, left = None, count
     for shift, radix in back:
         if arrived is not None:
             chunks = regroup(arrived, radix, left // radix, total)
         left //= radix
-        arrived = [chunks[0]] + [pass_on(chunks[j], count, j << shift) for j in range(1, radix)]
-        if shift == 0:
-            grid_adjoint = grid_rows(total, arrived[1], weight_g)
+        arrived = [chunks[0]] + [swap(chunks[j], count, j << shift) for j in range(1, radix)]
+    grid_adjoint = grid_rows(total, carried, weight_g)
     mesh_adjoint = mesh_rows(arrived, weight_m, owned, grid_adjoint)
     return (grid_adjoint, mesh_adjoint)
 

time: 39.1 us -> 34 us (0.87)
  waiting for transfers between devices: 9.19 us -> 3.42 us
  starting transfers between devices: 13.3 us -> 14.3 us
  Pallas kernels: 15.8 us -> 15.4 us
    ppermute x6 -> x1, waiting for transfers between devices: 7.18 us -> 0.31 us  [on_device(): lax.ppermute(rim, 'band', [(i, (i + 1) % count) for i in range(count)])]
    ppermute x6 -> x12, starting transfers between devices: 7.54 us -> 13.9 us  [swap(): return lax.ppermute(block, 'band', [(i, i ^ mask) for i in range(count)])]
    ppermute x6 -> x1, starting transfers between devices: 5.75 us -> 0.34 us  [on_device(): lax.ppermute(rim, 'band', [(i, (i + 1) % count) for i in range(count)])]
    ppermute x6 -> x12, waiting for transfers between devices: 2.02 us -> 3.11 us  [swap(): return lax.ppermute(block, 'band', [(i, i ^ mask) for i in range(count)])]
    pallas_call x1, Pallas kernels: 4.17 us -> 3.53 us  [after(): pl.pallas_call(functools.partial(after_kernel, len(parts), chunks, owned,...]
  transfers between devices with their start and end apart: 12 -> 13, of which waited for: 6 -> 5; matrix products, arithmetic and copies ran while one was open for 0% -> 0% of each run, Pallas kernels for 27% -> 32%
where the time goes in v8:
time: 34 us; the launch traced here: 33.9 us
  Pallas kernels  15.4 us (45%)
  starting transfers between devices  14.3 us (42%)
  waiting for transfers between devices  3.42 us (10%)
  between operations  0.74 us (2%)
    ppermute x12, starting transfers between devices, swap(): return lax.ppermute(block, 'band', [(i, i ^ mask) for i in range(count)])  13.9 us
    pallas_call x1, Pallas kernels, first_part(): pl.pallas_call(functools.partial(first_kernel, block, copies), in_specs=[...  3.61 us
    pallas_call x1, Pallas kernels, after(): pl.pallas_call(functools.partial(after_kernel, len(parts), chunks, owned,...  3.53 us
    pallas_call x1, Pallas kernels, second_part(): pl.pallas_call(functools.partial(second_kernel, block), in_specs=[VMEM, V...  3.36 us
    ppermute x12, waiting for transfers between devices, swap(): return lax.ppermute(block, 'band', [(i, i ^ mask) for i in range(count)])  3.11 us
    pallas_call x1, Pallas kernels, grid_rows(): pl.pallas_call(functools.partial(grid_kernel, block), in_specs=[VMEM] * 3...  2.12 us
    pallas_call x1, Pallas kernels, segments(): pl.pallas_call(functools.partial(segments_kernel, block), in_specs=[SMEM]...  1.77 us
    pallas_call x1, Pallas kernels, mesh_rows(): pl.pallas_call(functools.partial(mesh_kernel, len(pieces)), in_specs=[VME...  0.99 us
  transfers between devices with their start and end apart: 13, of which 5 were waited for; matrix products, arithmetic and copies ran while one was open for 0% of the time, Pallas kernels for 32%

profile of v8, /device:TPU:0, one launch (start us, length us, event | category | flops | bytes accessed | tf_op | source)
XLA Modules:
  0.0 33.9 jit_solution(7680111898354635249)
XLA Ops:
  0.6 3.1 %collective-permute-start = (bf16[16,512]{1,0:T(8,128)(2,1)}, bf16[16,512]{1,0:T(8,128)(2,1)S(1)}, u32[]{:S(2)}, u32[]{:S(2)}) collective-permute-start(bf16[16,512]{1,0:T(8,128)(2,1)} %refs_5_.1), channel_id=1, source_target_pairs={{0,4},{1,5},{2,6},{3,7},{4,0},{5,1},{6,2},{7,3},{8,12},{9,13},{10,... | collective-permute-start | bytes 49160 | tf_op jit(solution)/shard_map/ppermute | solution.py:45
  3.7 2.5 %collective-permute-start.2 = (bf16[16,512]{1,0:T(8,128)(2,1)}, bf16[16,512]{1,0:T(8,128)(2,1)S(1)}, u32[]{:S(2)}, u32[]{:S(2)}) collective-permute-start(bf16[16,512]{1,0:T(8,128)(2,1)} %refs_5_.1), channel_id=1, source_target_pairs={{0,12},{1,13},{2,14},{3,15},{4,8},{5,9},{6,10},{7,11},{8,4},{9,5},... | collective-permute-start | bytes 49160 | tf_op jit(solution)/shard_map/ppermute | solution.py:45
  6.2 0.1 collective-permute-start.1
  6.3 3.6 %first_part.1 = (bf16[512,512]{1,0:T(8,128)(2,1)S(1)}, f32[1,512]{1,0:T(1,128)S(1)}, bf16[512,512]{1,0:T(8,128)(2,1)S(1)}, bf16[512,512]{1,0:T(8,128)(2,1)S(1)},...) custom-call(bf16[3072,512]{1,0:T(8,128)(2,1)} %pre_hbm.1, ...), custom_call_target="tpu_custom_call" | custom-call | flops 1610612736 | bytes 5242880 | tf_op jit(solution)/shard_map/first_part/pallas_call | solution.py:162
  9.9 0.0 collective-permute-done.2.refs_3_
  10.0 1.1 %collective-permute-done.1.refs_2_ = bf16[16,512]{1,0:T(8,128)(2,1)S(1)} collective-permute-done((bf16[16,512]{1,0:T(8,128)(2,1)}, bf16[16,512]{1,0:T(8,128)(2,1)S(1)}, u32[]{:S(2)}, u32[]{:S(2)}) %collective-permute-start.1) | collective-permute-done | bytes 16416 | tf_op jit(solution)/shard_map/ppermute | solution.py:45
  11.1 1.6 %collective-permute-start.4 = (bf16[64,512]{1,0:T(8,128)(2,1)S(1)}, bf16[64,512]{1,0:T(8,128)(2,1)S(1)}, u32[]{:S(2)}, u32[]{:S(2)}) collective-permute-start(bf16[64,512]{1,0:T(8,128)(2,1)S(1)} %join.1.after_ref.refs_6_), channel_id=1, source_target_pairs={{0,2},{1,3},{2,0},{3,1},{4,6},{5,7},{6,4},{7,5},{8,10},{9,11},{10,... | collective-permute-start | bytes 196616 | tf_op jit(solution)/shard_map/ppermute | solution.py:45
  12.6 0.3 collective-permute-start.3
  12.9 3.4 %second_part.1 = (bf16[2048,512]{1,0:T(8,128)(2,1)S(1)}, bf16[2048,512]{1,0:T(8,128)(2,1)S(1)}, f32[2048,512]{1,0:T(8,128)S(1)}) custom-call(bf16[2048,512]{1,0:T(8,128)(2,1)S(1)} %get-tuple-element.32.pre_ref, bf16[512,512]{1,0:T(8,128)(2,1)S(1)} %get-tuple-element.27.weight_ref, f32[1,512]{1,0:T(1,128)S(1)} %get-tuple-element.33.bias_ref, ...), custom_call_target="tpu_custom_call" | custom-call | flops 3221225472 | bytes 10485760 | tf_op jit(solution)/shard_map/second_part/pallas_call | solution.py:187
  16.3 0.6 %collective-permute-done.4.refs_8_ = bf16[64,512]{1,0:T(8,128)(2,1)S(1)} collective-permute-done((bf16[64,512]{1,0:T(8,128)(2,1)S(1)}, bf16[64,512]{1,0:T(8,128)(2,1)S(1)}, u32[]{:S(2)}, u32[]{:S(2)}) %collective-permute-start.4) | collective-permute-done | bytes 65568 | tf_op jit(solution)/shard_map/ppermute | solution.py:45
  16.9 3.5 %after.1 = (bf16[3072,512]{1,0:T(8,128)(2,1)S(1)}, bf16[128,512]{1,0:T(8,128)(2,1)S(1)}, f32[8,640]{1,0:T(8,128)S(1)}, f32[8,640]{1,0:T(8,128)S(1)}, f32[8,640]{1,0:T(8,128)S(1)}, /*index=5*/f32[8,640]{1,0:T(8,128)S(1)}) custom-call(s32[1]{0:T(128)} %bitcast.1.refs_6_.me_ref, f32[32,128]{1,0:T(8,128)S(1)} %get-tuple-element.26.ids_ref, ...), custom_call_target="tpu_custom_call" | custom-call | flops 4831838208 | bytes 12582912 | tf_op jit(solution)/shard_map/after/pallas_call | solution.py:286
  20.4 0.1 collective-permute-start.7
  20.5 1.0 %collective-permute-start.8 = (f32[8,640]{1,0:T(8,128)S(1)}, f32[8,640]{1,0:T(8,128)S(1)}, u32[]{:S(2)}, u32[]{:S(2)}) collective-permute-start(f32[8,640]{1,0:T(8,128)S(1)} %get-tuple-element.43), channel_id=1, source_target_pairs={{0,2},{1,3},{2,0},{3,1},{4,6},{5,7},{6,4},{7,5},{8,10},{9,11},{10,... | collective-permute-start | bytes 61448 | tf_op jit(solution)/shard_map/ppermute | solution.py:45
  21.5 0.8 %collective-permute-start.9 = (f32[8,640]{1,0:T(8,128)S(1)}, f32[8,640]{1,0:T(8,128)S(1)}, u32[]{:S(2)}, u32[]{:S(2)}) collective-permute-start(f32[8,640]{1,0:T(8,128)S(1)} %get-tuple-element.44), channel_id=1, source_target_pairs={{0,3},{1,2},{2,1},{3,0},{4,7},{5,6},{6,5},{7,4},{8,11},{9,10},{10,... | collective-permute-start | bytes 61448 | tf_op jit(solution)/shard_map/ppermute | solution.py:45
  22.4 0.3 %collective-permute-start.6 = (bf16[128,512]{1,0:T(8,128)(2,1)S(1)}, bf16[128,512]{1,0:T(8,128)(2,1)S(1)}, u32[]{:S(2)}, u32[]{:S(2)}) collective-permute-start(bf16[128,512]{1,0:T(8,128)(2,1)S(1)} %get-tuple-element.39), channel_id=1, source_target_pairs={{0,1},{1,2},{2,3},{3,4},{4,5},{5,6},{6,7},{7,8},{8,9},{9,10},{10,1... | collective-permute-start | bytes 393224 | tf_op jit(solution)/shard_map/ppermute | solution.py:459
  22.7 1.8 %segments.1.total_ref.refs_4_ = f32[2448,512]{1,0:T(8,128)S(1)} custom-call(s32[3072]{0:T(1024)S(1)} %copy-done.1, s32[1,3072]{1,0:T(1,128)S(1)} %bitcast.8, bf16[3072,512]{1,0:T(8,128)(2,1)S(1)} %get-tuple-element.38.d_ref), custom_call_target="tpu_custom_call" | custom-call | flops 3221225472 | bytes 6291456 | tf_op jit(solution)/shard_map/segments/pallas_call | solution.py:312
  24.5 0.2 collective-permute-done.9.refs_3_
  24.8 0.8 %collective-permute-start.10 = (f32[8,640]{1,0:T(8,128)S(1)}, f32[8,640]{1,0:T(8,128)S(1)}, u32[]{:S(2)}, u32[]{:S(2)}) collective-permute-start(f32[8,640]{1,0:T(8,128)S(1)} %get-tuple-element.46), channel_id=1, source_target_pairs={{0,4},{1,5},{2,6},{3,7},{4,0},{5,1},{6,2},{7,3},{8,12},{9,13},{10,... | collective-permute-start | bytes 61448 | tf_op jit(solution)/shard_map/ppermute | solution.py:45
  25.6 1.7 %collective-permute-start.11 = (f32[8,640]{1,0:T(8,128)S(1)}, f32[8,640]{1,0:T(8,128)S(1)}, u32[]{:S(2)}, u32[]{:S(2)}) collective-permute-start(f32[8,640]{1,0:T(8,128)S(1)} %get-tuple-element.47), channel_id=1, source_target_pairs={{0,8},{1,9},{2,10},{3,11},{4,12},{5,13},{6,14},{7,15},{8,0},{9,1},... | collective-permute-start | bytes 61448 | tf_op jit(solution)/shard_map/ppermute | solution.py:45
  27.3 1.9 %collective-permute-start.12 = (f32[8,640]{1,0:T(8,128)S(1)}, f32[8,640]{1,0:T(8,128)S(1)}, u32[]{:S(2)}, u32[]{:S(2)}) collective-permute-start(f32[8,640]{1,0:T(8,128)S(1)} %get-tuple-element.48), channel_id=1, source_target_pairs={{0,12},{1,13},{2,14},{3,15},{4,8},{5,9},{6,10},{7,11},{8,4},{9,5},... | collective-permute-start | bytes 61448 | tf_op jit(solution)/shard_map/ppermute | solution.py:45
  29.2 0.3 collective-permute-done.6.carried_ref
  29.5 2.1 %grid_rows.1.refs_5_ = bf16[2048,512]{1,0:T(8,128)(2,1)} custom-call(f32[2448,512]{1,0:T(8,128)S(1)} %segments.1.total_ref.refs_4_, bf16[128,512]{1,0:T(8,128)(2,1)S(1)} %collective-permute-done.6.carried_ref, bf16[512,512]{1,0:T(8,128)(2,1)S(1)} %get-tuple-element.40.weight_ref), custom_call_target="tpu_custom_call" | custom-call | flops 1073741824 | bytes 6291456 | tf_op jit(solution)/shard_map/grid_rows/pallas_call | solution.py:341
  31.7 1.2 %collective-permute-done.12.refs_3_ = f32[8,640]{1,0:T(8,128)S(1)} collective-permute-done((f32[8,640]{1,0:T(8,128)S(1)}, f32[8,640]{1,0:T(8,128)S(1)}, u32[]{:S(2)}, u32[]{:S(2)}) %collective-permute-start.12) | collective-permute-done | bytes 20512 | tf_op jit(solution)/shard_map/ppermute | solution.py:45
  32.9 1.0 %mesh_rows.1 = bf16[16,512]{1,0:T(8,128)(2,1)} custom-call(f32[8,640]{1,0:T(8,128)S(1)} %get-tuple-element.45.refs_0_, f32[8,640]{1,0:T(8,128)S(1)} %collective-permute-done.10.refs_1_, f32[8,640]{1,0:T(8,128)S(1)} %collective-permute-done.11.refs_2_, f32[8,640]{1,0:T(8,128)S(1)} %collective-permute-done.12.refs_3_, ...), custom_call_target="tpu_custom_call" | custom-call | flops 8388608 | bytes 524288 | tf_op jit(solution)/shard_map/mesh_rows/pallas_call | solution.py:392
  (14 shorter events, 0.1 us)
Async XLA Ops:
  0.6 9.3 %collective-permute-start = (bf16[16,512]{1,0:T(8,128)(2,1)}, bf16[16,512]{1,0:T(8,128)(2,1)S(1)}, u32[]{:S(2)}, u32[]{:S(2)}) collective-permute-start(bf16[16,512]{1,0:T(8,128)(2,1)} %refs_5_.1), channel_id=1, source_target_pairs={{0,4},{1,5},{2,6},{3,7},{4,0},{5,1},{6,2},{7,3},{8,12},{9,13},{10,... | collective-permute-start | bytes 49160 | tf_op jit(solution)/shard_map/ppermute | solution.py:45
  3.7 6.2 %collective-permute-start.2 = (bf16[16,512]{1,0:T(8,128)(2,1)}, bf16[16,512]{1,0:T(8,128)(2,1)S(1)}, u32[]{:S(2)}, u32[]{:S(2)}) collective-permute-start(bf16[16,512]{1,0:T(8,128)(2,1)} %refs_5_.1), channel_id=1, source_target_pairs={{0,12},{1,13},{2,14},{3,15},{4,8},{5,9},{6,10},{7,11},{8,4},{9,5},... | collective-permute-start | bytes 49160 | tf_op jit(solution)/shard_map/ppermute | solution.py:45
  6.2 4.9 %collective-permute-start.1 = (bf16[16,512]{1,0:T(8,128)(2,1)}, bf16[16,512]{1,0:T(8,128)(2,1)S(1)}, u32[]{:S(2)}, u32[]{:S(2)}) collective-permute-start(bf16[16,512]{1,0:T(8,128)(2,1)} %refs_5_.1), channel_id=1, source_target_pairs={{0,8},{1,9},{2,10},{3,11},{4,12},{5,13},{6,14},{7,15},{8,0},{9,1},... | collective-permute-start | bytes 49160 | tf_op jit(solution)/shard_map/ppermute | solution.py:45
  11.1 5.2 %collective-permute-start.5 = (bf16[64,512]{1,0:T(8,128)(2,1)S(1)}, bf16[64,512]{1,0:T(8,128)(2,1)S(1)}, u32[]{:S(2)}, u32[]{:S(2)}) collective-permute-start(bf16[64,512]{1,0:T(8,128)(2,1)S(1)} %join.1.after_ref.refs_6_), channel_id=1, source_target_pairs={{0,3},{1,2},{2,1},{3,0},{4,7},{5,6},{6,5},{7,4},{8,11},{9,10},{10,... | collective-permute-start | bytes 196616 | tf_op jit(solution)/shard_map/ppermute | solution.py:45
  11.1 5.8 %collective-permute-start.4 = (bf16[64,512]{1,0:T(8,128)(2,1)S(1)}, bf16[64,512]{1,0:T(8,128)(2,1)S(1)}, u32[]{:S(2)}, u32[]{:S(2)}) collective-permute-start(bf16[64,512]{1,0:T(8,128)(2,1)S(1)} %join.1.after_ref.refs_6_), channel_id=1, source_target_pairs={{0,2},{1,3},{2,0},{3,1},{4,6},{5,7},{6,4},{7,5},{8,10},{9,11},{10,... | collective-permute-start | bytes 196616 | tf_op jit(solution)/shard_map/ppermute | solution.py:45
  12.6 4.2 %collective-permute-start.3 = (bf16[64,512]{1,0:T(8,128)(2,1)S(1)}, bf16[64,512]{1,0:T(8,128)(2,1)S(1)}, u32[]{:S(2)}, u32[]{:S(2)}) collective-permute-start(bf16[64,512]{1,0:T(8,128)(2,1)S(1)} %join.1.after_ref.refs_6_), channel_id=1, source_target_pairs={{0,1},{1,0},{2,3},{3,2},{4,5},{5,4},{6,7},{7,6},{8,9},{9,8},{10,11... | collective-permute-start | bytes 196616 | tf_op jit(solution)/shard_map/ppermute | solution.py:45
  12.9 3.9 %copy-start = (s32[3072]{0:T(1024)S(1)}, s32[3072]{0:T(1024)}, u32[]{:S(2)}) copy-start(s32[3072]{0:T(1024)} %param.12) | copy-start | bytes 36868
  12.9 3.9 %copy-start.1 = (s32[3072]{0:T(1024)S(1)}, s32[3072]{0:T(1024)}, u32[]{:S(2)}) copy-start(s32[3072]{0:T(1024)} %starts_ref.1) | copy-start | bytes 36868
  20.4 4.1 %collective-permute-start.7 = (f32[8,640]{1,0:T(8,128)S(1)}, f32[8,640]{1,0:T(8,128)S(1)}, u32[]{:S(2)}, u32[]{:S(2)}) collective-permute-start(f32[8,640]{1,0:T(8,128)S(1)} %get-tuple-element.42), channel_id=1, source_target_pairs={{0,1},{1,0},{2,3},{3,2},{4,5},{5,4},{6,7},{7,6},{8,9},{9,8},{10,11... | collective-permute-start | bytes 61448 | tf_op jit(solution)/shard_map/ppermute | solution.py:45
  20.5 3.9 %collective-permute-start.8 = (f32[8,640]{1,0:T(8,128)S(1)}, f32[8,640]{1,0:T(8,128)S(1)}, u32[]{:S(2)}, u32[]{:S(2)}) collective-permute-start(f32[8,640]{1,0:T(8,128)S(1)} %get-tuple-element.43), channel_id=1, source_target_pairs={{0,2},{1,3},{2,0},{3,1},{4,6},{5,7},{6,4},{7,5},{8,10},{9,11},{10,... | collective-permute-start | bytes 61448 | tf_op jit(solution)/shard_map/ppermute | solution.py:45
  21.5 3.2 %collective-permute-start.9 = (f32[8,640]{1,0:T(8,128)S(1)}, f32[8,640]{1,0:T(8,128)S(1)}, u32[]{:S(2)}, u32[]{:S(2)}) collective-permute-start(f32[8,640]{1,0:T(8,128)S(1)} %get-tuple-element.44), channel_id=1, source_target_pairs={{0,3},{1,2},{2,1},{3,0},{4,7},{5,6},{6,5},{7,4},{8,11},{9,10},{10,... | collective-permute-start | bytes 61448 | tf_op jit(solution)/shard_map/ppermute | solution.py:45
  22.4 7.2 %collective-permute-start.6 = (bf16[128,512]{1,0:T(8,128)(2,1)S(1)}, bf16[128,512]{1,0:T(8,128)(2,1)S(1)}, u32[]{:S(2)}, u32[]{:S(2)}) collective-permute-start(bf16[128,512]{1,0:T(8,128)(2,1)S(1)} %get-tuple-element.39), channel_id=1, source_target_pairs={{0,1},{1,2},{2,3},{3,4},{4,5},{5,6},{6,7},{7,8},{8,9},{9,10},{10,1... | collective-permute-start | bytes 393224 | tf_op jit(solution)/shard_map/ppermute | solution.py:459
  24.8 6.9 %collective-permute-start.10 = (f32[8,640]{1,0:T(8,128)S(1)}, f32[8,640]{1,0:T(8,128)S(1)}, u32[]{:S(2)}, u32[]{:S(2)}) collective-permute-start(f32[8,640]{1,0:T(8,128)S(1)} %get-tuple-element.46), channel_id=1, source_target_pairs={{0,4},{1,5},{2,6},{3,7},{4,0},{5,1},{6,2},{7,3},{8,12},{9,13},{10,... | collective-permute-start | bytes 61448 | tf_op jit(solution)/shard_map/ppermute | solution.py:45
  25.6 6.1 %collective-permute-start.11 = (f32[8,640]{1,0:T(8,128)S(1)}, f32[8,640]{1,0:T(8,128)S(1)}, u32[]{:S(2)}, u32[]{:S(2)}) collective-permute-start(f32[8,640]{1,0:T(8,128)S(1)} %get-tuple-element.47), channel_id=1, source_target_pairs={{0,8},{1,9},{2,10},{3,11},{4,12},{5,13},{6,14},{7,15},{8,0},{9,1},... | collective-permute-start | bytes 61448 | tf_op jit(solution)/shard_map/ppermute | solution.py:45
  27.3 5.6 %collective-permute-start.12 = (f32[8,640]{1,0:T(8,128)S(1)}, f32[8,640]{1,0:T(8,128)S(1)}, u32[]{:S(2)}, u32[]{:S(2)}) collective-permute-start(f32[8,640]{1,0:T(8,128)S(1)} %get-tuple-element.48), channel_id=1, source_target_pairs={{0,12},{1,13},{2,14},{3,15},{4,8},{5,9},{6,10},{7,11},{8,4},{9,5},... | collective-permute-start | bytes 61448 | tf_op jit(solution)/shard_map/ppermute | solution.py:45

commit v9 on v8

--- a/solution.py
+++ b/solution.py
@@ -11,6 +11,7 @@
 RIM = 128
 LANES = 128
 EPS = 1e-05
+CHUNK = 32
 MIB = 1 << 20
 
 BF16 = jnp.bfloat16
@@ -78,36 +79,38 @@
     return pltpu.CompilerParams(vmem_limit_bytes=limit * MIB)
 
 
-def edge_blocks(pre_ref, weight_ref, bias_ref, normed_ref, q_ref, gate_ref, block, arrive, weigh):
+def edge_blocks(pre_ref, weight_ref, bias_ref, normed_ref, q_ref, gate_ref, hidden_ref, block, arrive):
+    weight, bias = weight_ref[...], bias_ref[...]
     rows, last = pre_ref.shape[0], None
     for at in range(0, rows + block, block):
         this = None
         if at < rows:
             arrive(at)
-            p = pre_ref[at : at + block].astype(F32)
-            s = 0.5 * jnp.tanh(0.5 * p) + 0.5
-            h = p * s
-            hidden, gate = h.astype(BF16), s + h * (1.0 - s)
-            if at == 0:
-                weigh()
-                weight, bias = weight_ref[...], bias_ref[...]
-            this = dot(hidden, weight) + bias, gate
+            for row in range(at, at + block, CHUNK):
+                piece = slice(row, row + CHUNK)
+                half = 0.5 * pre_ref[piece].astype(F32)
+                t = jnp.tanh(half)
+                double = 1.0 + t
+                h = half * double
+                hidden_ref[piece] = h.astype(BF16)
+                gate_ref[piece] = double + h * (1.0 - t)
+            this = dot(hidden_ref[at : at + block], weight)
         if last is not None:
-            out, gate = last
-            centre = out - jnp.mean(out, axis=-1, keepdims=True)
-            inv = lax.rsqrt(jnp.mean(centre * centre, axis=-1, keepdims=True) + EPS)
-            normed = (centre * inv).astype(BF16)
-            piece = slice(at - block, at)
-            normed_ref[piece] = normed
-            q_ref[piece] = dot_t(normed, weight).astype(BF16)
-            gate_ref[piece] = gate * inv
+            for row in range(0, block, CHUNK):
+                piece = slice(at - block + row, at - block + row + CHUNK)
+                out = last[row : row + CHUNK] + bias
+                centre = out - jnp.mean(out, axis=-1, keepdims=True)
+                inv = lax.rsqrt(jnp.mean(centre * centre, axis=-1, keepdims=True) + EPS)
+                normed_ref[piece] = (centre * inv).astype(BF16)
+                gate_ref[piece] = gate_ref[piece] * (0.5 * inv)
+            q_ref[at - block : at] = dot_t(normed_ref[at - block : at], weight).astype(BF16)
         last = this
 
 
 def first_kernel(block, copies, pre_hbm, *refs):
     sources, (me_ref, requests_hbm), refs = refs[:copies], refs[copies : copies + 2], refs[copies + 2 :]
     targets, refs = refs[:copies], refs[copies:]
-    ids_ref, other_ref, normed_ref, q_ref, gate_ref, pre_ref, requests_ref, sem = refs
+    ids_ref, other_ref, normed_ref, q_ref, gate_ref, pre_ref, hidden_ref, requests_ref, sem = refs
     rows = normed_ref.shape[0]
 
     def load(k, source, target):
@@ -122,13 +125,10 @@
     ]
     more = load(copies + len(loads), pre_hbm.at[pl.ds(rows, more_rows)], other_ref)
     asked = load(copies + len(loads) + 1, requests_hbm, requests_ref)
-    for copy in loads[:1] + others[:2] + loads[1:] + others[2:] + [more, asked]:
+    for copy in others[:2] + loads + others[2:] + [more, asked]:
         copy.start()
-
-    def weigh():
-        for copy in others[:2]:
-            copy.wait()
-
+    for copy in others[:2]:
+        copy.wait()
     edge_blocks(
         pre_ref,
         targets[0],
@@ -136,9 +136,9 @@
         normed_ref,
         q_ref,
         gate_ref,
+        hidden_ref,
         block,
         lambda at: loads[at // block].wait(),
-        weigh,
     )
     for copy in others[2:] + [more, asked]:
         copy.wait()
@@ -166,6 +166,7 @@
         out_shape=outs,
         scratch_shapes=[
             pltpu.VMEM((rows, width), BF16),
+            pltpu.VMEM((rows, width), BF16),
             pltpu.SMEM(requests.shape, jnp.int32),
             DMA((copies + rows // block + 2,)),
         ],
@@ -175,9 +176,9 @@
     )(in_hbm(preact), *[in_hbm(a) for a in sources], me, in_hbm(requests))
 
 
-def second_kernel(block, pre_ref, weight_ref, bias_ref, after_ref, normed_ref, q_ref, gate_ref):
+def second_kernel(block, pre_ref, weight_ref, bias_ref, after_ref, normed_ref, q_ref, gate_ref, hidden_ref):
     edge_blocks(
-        pre_ref, weight_ref, bias_ref, normed_ref, q_ref, gate_ref, block, lambda at: None, lambda: None
+        pre_ref, weight_ref, bias_ref, normed_ref, q_ref, gate_ref, hidden_ref, block, lambda at: None
     )
 
 
@@ -189,6 +190,7 @@
         in_specs=[VMEM, VMEM, VMEM, ANY],
         out_specs=[VMEM] * len(outs),
         out_shape=outs,
+        scratch_shapes=[pltpu.VMEM((rows, width), BF16)],
         cost_estimate=cost(6 * rows * width * width, 10 * rows * width),
         compiler_params=params(16),
         name="second_part",
@@ -259,14 +261,18 @@
             piece = slice(at, at + block)
             onehot_t = (key == slots_ref[:, number * block : (number + 1) * block]).astype(F32)
             onehot = onehot_t.T
-            c = jnp.sum(onehot * dot_t(normed_ref[piece], mean_rows), axis=-1, keepdims=True)
+            g = dot_t(normed_ref[piece], mean_rows)
             s_rows = dot(onehot.astype(BF16), s_both)
-            this = (onehot_t[:slots].astype(BF16), c, s_rows, q_ref, gate_ref, piece)
+            this = (onehot_t[:slots].astype(BF16), onehot, g, s_rows, q_ref, gate_ref, at)
         if last is not None:
-            onehot_t, c, s_rows, q_ref, gate_ref, piece = last
+            onehot_t, onehot, g, s_rows, q_ref, gate_ref, first = last
             at = (number - 1) * block
-            d = (gate_ref[piece] * (s_rows - c * q_ref[piece].astype(F32))).astype(BF16)
-            d_ref[at : at + block, :] = d
+            for row in range(0, block, CHUNK):
+                piece, inner = slice(first + row, first + row + CHUNK), slice(row, row + CHUNK)
+                c = jnp.sum(onehot[inner] * g[inner], axis=-1, keepdims=True)
+                d = gate_ref[piece] * (s_rows[inner] - c * q_ref[piece].astype(F32))
+                d_ref[at + row : at + row + CHUNK, :] = d.astype(BF16)
+            d = d_ref[at : at + block, :]
             sums += dot(onehot_t, d)
             if at + block > G_DEV:
                 pick = (rim_row == senders_ref[:, at : at + block]).astype(F32).astype(BF16)

time: 34 us -> 33.3 us (0.979)
  Pallas kernels: 15.4 us -> 14.6 us
    pallas_call x1, Pallas kernels: 3.61 us -> 3.2 us  [first_part(): pl.pallas_call(functools.partial(first_kernel, block, copies), in_specs=[...]
  transfers between devices with their start and end apart: 13 -> 13, of which waited for: 5 -> 6; matrix products, arithmetic and copies ran while one was open for 0% -> 0% of each run, Pallas kernels for 32% -> 31%
where the time goes in v9:
time: 33.3 us; the launch traced here: 33.1 us
  Pallas kernels  14.6 us (44%)
  starting transfers between devices  14.3 us (43%)
  waiting for transfers between devices  3.53 us (11%)
  between operations  0.74 us (2%)
    ppermute x12, starting transfers between devices, swap(): return lax.ppermute(block, 'band', [(i, i ^ mask) for i in range(count)])  13.9 us
    pallas_call x1, Pallas kernels, after(): pl.pallas_call(functools.partial(after_kernel, len(parts), chunks, owned,...  3.37 us
    pallas_call x1, Pallas kernels, first_part(): pl.pallas_call(functools.partial(first_kernel, block, copies), in_specs=[...  3.2 us
    pallas_call x1, Pallas kernels, second_part(): pl.pallas_call(functools.partial(second_kernel, block), in_specs=[VMEM, V...  3.1 us
    ppermute x12, waiting for transfers between devices, swap(): return lax.ppermute(block, 'band', [(i, i ^ mask) for i in range(count)])  3.05 us
    pallas_call x1, Pallas kernels, grid_rows(): pl.pallas_call(functools.partial(grid_kernel, block), in_specs=[VMEM] * 3...  2.12 us
    pallas_call x1, Pallas kernels, segments(): pl.pallas_call(functools.partial(segments_kernel, block), in_specs=[SMEM]...  1.77 us
    pallas_call x1, Pallas kernels, mesh_rows(): pl.pallas_call(functools.partial(mesh_kernel, len(pieces)), in_specs=[VME...  0.99 us
  transfers between devices with their start and end apart: 13, of which 6 were waited for; matrix products, arithmetic and copies ran while one was open for 0% of the time, Pallas kernels for 31%

profile of v9, /device:TPU:0, one launch (start us, length us, event | category | flops | bytes accessed | tf_op | source)
XLA Modules:
  0.0 33.1 jit_solution(9125029571690388094)
XLA Ops:
  0.6 3.1 %collective-permute-start = (bf16[16,512]{1,0:T(8,128)(2,1)}, bf16[16,512]{1,0:T(8,128)(2,1)S(1)}, u32[]{:S(2)}, u32[]{:S(2)}) collective-permute-start(bf16[16,512]{1,0:T(8,128)(2,1)} %refs_5_.1), channel_id=1, source_target_pairs={{0,4},{1,5},{2,6},{3,7},{4,0},{5,1},{6,2},{7,3},{8,12},{9,13},{10,... | collective-permute-start | bytes 49160 | tf_op jit(solution)/shard_map/ppermute | solution.py:46
  3.7 2.5 %collective-permute-start.2 = (bf16[16,512]{1,0:T(8,128)(2,1)}, bf16[16,512]{1,0:T(8,128)(2,1)S(1)}, u32[]{:S(2)}, u32[]{:S(2)}) collective-permute-start(bf16[16,512]{1,0:T(8,128)(2,1)} %refs_5_.1), channel_id=1, source_target_pairs={{0,12},{1,13},{2,14},{3,15},{4,8},{5,9},{6,10},{7,11},{8,4},{9,5},... | collective-permute-start | bytes 49160 | tf_op jit(solution)/shard_map/ppermute | solution.py:46
  6.2 0.1 collective-permute-start.1
  6.3 3.2 %first_part.1 = (bf16[512,512]{1,0:T(8,128)(2,1)S(1)}, f32[1,512]{1,0:T(1,128)S(1)}, bf16[512,512]{1,0:T(8,128)(2,1)S(1)}, bf16[512,512]{1,0:T(8,128)(2,1)S(1)},...) custom-call(bf16[3072,512]{1,0:T(8,128)(2,1)} %pre_hbm.1, ...), custom_call_target="tpu_custom_call" | custom-call | flops 1610612736 | bytes 5242880 | tf_op jit(solution)/shard_map/first_part/pallas_call | solution.py:162
  9.5 0.2 collective-permute-done.2.refs_3_
  9.7 1.4 %collective-permute-done.1.refs_2_ = bf16[16,512]{1,0:T(8,128)(2,1)S(1)} collective-permute-done((bf16[16,512]{1,0:T(8,128)(2,1)}, bf16[16,512]{1,0:T(8,128)(2,1)S(1)}, u32[]{:S(2)}, u32[]{:S(2)}) %collective-permute-start.1) | collective-permute-done | bytes 16416 | tf_op jit(solution)/shard_map/ppermute | solution.py:46
  11.1 1.6 %collective-permute-start.4 = (bf16[64,512]{1,0:T(8,128)(2,1)S(1)}, bf16[64,512]{1,0:T(8,128)(2,1)S(1)}, u32[]{:S(2)}, u32[]{:S(2)}) collective-permute-start(bf16[64,512]{1,0:T(8,128)(2,1)S(1)} %join.1.after_ref.refs_6_), channel_id=1, source_target_pairs={{0,2},{1,3},{2,0},{3,1},{4,6},{5,7},{6,4},{7,5},{8,10},{9,11},{10,... | collective-permute-start | bytes 196616 | tf_op jit(solution)/shard_map/ppermute | solution.py:46
  12.6 0.3 collective-permute-start.3
  12.9 3.1 %second_part.1 = (bf16[2048,512]{1,0:T(8,128)(2,1)S(1)}, bf16[2048,512]{1,0:T(8,128)(2,1)S(1)}, f32[2048,512]{1,0:T(8,128)S(1)}) custom-call(bf16[2048,512]{1,0:T(8,128)(2,1)S(1)} %get-tuple-element.32.pre_ref, bf16[512,512]{1,0:T(8,128)(2,1)S(1)} %get-tuple-element.27.weight_ref, f32[1,512]{1,0:T(1,128)S(1)} %get-tuple-element.33.bias_ref, ...), custom_call_target="tpu_custom_call" | custom-call | flops 3221225472 | bytes 10485760 | tf_op jit(solution)/shard_map/second_part/pallas_call | solution.py:188
  16.0 0.8 %collective-permute-done.4.refs_8_ = bf16[64,512]{1,0:T(8,128)(2,1)S(1)} collective-permute-done((bf16[64,512]{1,0:T(8,128)(2,1)S(1)}, bf16[64,512]{1,0:T(8,128)(2,1)S(1)}, u32[]{:S(2)}, u32[]{:S(2)}) %collective-permute-start.4) | collective-permute-done | bytes 65568 | tf_op jit(solution)/shard_map/ppermute | solution.py:46
  16.9 3.4 %after.1 = (bf16[3072,512]{1,0:T(8,128)(2,1)S(1)}, bf16[128,512]{1,0:T(8,128)(2,1)S(1)}, f32[8,640]{1,0:T(8,128)S(1)}, f32[8,640]{1,0:T(8,128)S(1)}, f32[8,640]{1,0:T(8,128)S(1)}, /*index=5*/f32[8,640]{1,0:T(8,128)S(1)}) custom-call(s32[1]{0:T(128)} %bitcast.1.refs_6_.me_ref, f32[32,128]{1,0:T(8,128)S(1)} %get-tuple-element.26.ids_ref, ...), custom_call_target="tpu_custom_call" | custom-call | flops 4831838208 | bytes 12582912 | tf_op jit(solution)/shard_map/after/pallas_call | solution.py:292
  20.2 0.1 collective-permute-start.7
  20.4 0.7 %collective-permute-start.8 = (f32[8,640]{1,0:T(8,128)S(1)}, f32[8,640]{1,0:T(8,128)S(1)}, u32[]{:S(2)}, u32[]{:S(2)}) collective-permute-start(f32[8,640]{1,0:T(8,128)S(1)} %get-tuple-element.43), channel_id=1, source_target_pairs={{0,2},{1,3},{2,0},{3,1},{4,6},{5,7},{6,4},{7,5},{8,10},{9,11},{10,... | collective-permute-start | bytes 61448 | tf_op jit(solution)/shard_map/ppermute | solution.py:46
  21.1 1.1 %collective-permute-start.9 = (f32[8,640]{1,0:T(8,128)S(1)}, f32[8,640]{1,0:T(8,128)S(1)}, u32[]{:S(2)}, u32[]{:S(2)}) collective-permute-start(f32[8,640]{1,0:T(8,128)S(1)} %get-tuple-element.44), channel_id=1, source_target_pairs={{0,3},{1,2},{2,1},{3,0},{4,7},{5,6},{6,5},{7,4},{8,11},{9,10},{10,... | collective-permute-start | bytes 61448 | tf_op jit(solution)/shard_map/ppermute | solution.py:46
  22.2 0.3 %collective-permute-start.6 = (bf16[128,512]{1,0:T(8,128)(2,1)S(1)}, bf16[128,512]{1,0:T(8,128)(2,1)S(1)}, u32[]{:S(2)}, u32[]{:S(2)}) collective-permute-start(bf16[128,512]{1,0:T(8,128)(2,1)S(1)} %get-tuple-element.39), channel_id=1, source_target_pairs={{0,1},{1,2},{2,3},{3,4},{4,5},{5,6},{6,7},{7,8},{8,9},{9,10},{10,1... | collective-permute-start | bytes 393224 | tf_op jit(solution)/shard_map/ppermute | solution.py:465
  22.5 1.8 %segments.1.total_ref.refs_4_ = f32[2448,512]{1,0:T(8,128)S(1)} custom-call(s32[3072]{0:T(1024)S(1)} %copy-done.1, s32[1,3072]{1,0:T(1,128)S(1)} %bitcast.8, bf16[3072,512]{1,0:T(8,128)(2,1)S(1)} %get-tuple-element.38.d_ref), custom_call_target="tpu_custom_call" | custom-call | flops 3221225472 | bytes 6291456 | tf_op jit(solution)/shard_map/segments/pallas_call | solution.py:318
  24.3 0.1 collective-permute-done.9.refs_3_
  24.4 0.8 %collective-permute-start.10 = (f32[8,640]{1,0:T(8,128)S(1)}, f32[8,640]{1,0:T(8,128)S(1)}, u32[]{:S(2)}, u32[]{:S(2)}) collective-permute-start(f32[8,640]{1,0:T(8,128)S(1)} %get-tuple-element.46), channel_id=1, source_target_pairs={{0,4},{1,5},{2,6},{3,7},{4,0},{5,1},{6,2},{7,3},{8,12},{9,13},{10,... | collective-permute-start | bytes 61448 | tf_op jit(solution)/shard_map/ppermute | solution.py:46
  25.2 1.3 %collective-permute-start.11 = (f32[8,640]{1,0:T(8,128)S(1)}, f32[8,640]{1,0:T(8,128)S(1)}, u32[]{:S(2)}, u32[]{:S(2)}) collective-permute-start(f32[8,640]{1,0:T(8,128)S(1)} %get-tuple-element.47), channel_id=1, source_target_pairs={{0,8},{1,9},{2,10},{3,11},{4,12},{5,13},{6,14},{7,15},{8,0},{9,1},... | collective-permute-start | bytes 61448 | tf_op jit(solution)/shard_map/ppermute | solution.py:46
  26.6 2.3 %collective-permute-start.12 = (f32[8,640]{1,0:T(8,128)S(1)}, f32[8,640]{1,0:T(8,128)S(1)}, u32[]{:S(2)}, u32[]{:S(2)}) collective-permute-start(f32[8,640]{1,0:T(8,128)S(1)} %get-tuple-element.48), channel_id=1, source_target_pairs={{0,12},{1,13},{2,14},{3,15},{4,8},{5,9},{6,10},{7,11},{8,4},{9,5},... | collective-permute-start | bytes 61448 | tf_op jit(solution)/shard_map/ppermute | solution.py:46
  28.9 0.5 %collective-permute-done.6.carried_ref = bf16[128,512]{1,0:T(8,128)(2,1)S(1)} collective-permute-done((bf16[128,512]{1,0:T(8,128)(2,1)S(1)}, bf16[128,512]{1,0:T(8,128)(2,1)S(1)}, u32[]{:S(2)}, u32[]{:S(2)}) %collective-permute-start.6) | collective-permute-done | bytes 131104 | tf_op jit(solution)/shard_map/ppermute | solution.py:465
  29.4 2.1 %grid_rows.1.refs_5_ = bf16[2048,512]{1,0:T(8,128)(2,1)} custom-call(f32[2448,512]{1,0:T(8,128)S(1)} %segments.1.total_ref.refs_4_, bf16[128,512]{1,0:T(8,128)(2,1)S(1)} %collective-permute-done.6.carried_ref, bf16[512,512]{1,0:T(8,128)(2,1)S(1)} %get-tuple-element.40.weight_ref), custom_call_target="tpu_custom_call" | custom-call | flops 1073741824 | bytes 6291456 | tf_op jit(solution)/shard_map/grid_rows/pallas_call | solution.py:347
  31.5 0.6 %collective-permute-done.12.refs_3_ = f32[8,640]{1,0:T(8,128)S(1)} collective-permute-done((f32[8,640]{1,0:T(8,128)S(1)}, f32[8,640]{1,0:T(8,128)S(1)}, u32[]{:S(2)}, u32[]{:S(2)}) %collective-permute-start.12) | collective-permute-done | bytes 20512 | tf_op jit(solution)/shard_map/ppermute | solution.py:46
  32.1 1.0 %mesh_rows.1 = bf16[16,512]{1,0:T(8,128)(2,1)} custom-call(f32[8,640]{1,0:T(8,128)S(1)} %get-tuple-element.45.refs_0_, f32[8,640]{1,0:T(8,128)S(1)} %collective-permute-done.10.refs_1_, f32[8,640]{1,0:T(8,128)S(1)} %collective-permute-done.11.refs_2_, f32[8,640]{1,0:T(8,128)S(1)} %collective-permute-done.12.refs_3_, ...), custom_call_target="tpu_custom_call" | custom-call | flops 8388608 | bytes 524288 | tf_op jit(solution)/shard_map/mesh_rows/pallas_call | solution.py:398
  (14 shorter events, 0.1 us)
Async XLA Ops:
  0.6 8.9 %collective-permute-start = (bf16[16,512]{1,0:T(8,128)(2,1)}, bf16[16,512]{1,0:T(8,128)(2,1)S(1)}, u32[]{:S(2)}, u32[]{:S(2)}) collective-permute-start(bf16[16,512]{1,0:T(8,128)(2,1)} %refs_5_.1), channel_id=1, source_target_pairs={{0,4},{1,5},{2,6},{3,7},{4,0},{5,1},{6,2},{7,3},{8,12},{9,13},{10,... | collective-permute-start | bytes 49160 | tf_op jit(solution)/shard_map/ppermute | solution.py:46
  3.7 6.0 %collective-permute-start.2 = (bf16[16,512]{1,0:T(8,128)(2,1)}, bf16[16,512]{1,0:T(8,128)(2,1)S(1)}, u32[]{:S(2)}, u32[]{:S(2)}) collective-permute-start(bf16[16,512]{1,0:T(8,128)(2,1)} %refs_5_.1), channel_id=1, source_target_pairs={{0,12},{1,13},{2,14},{3,15},{4,8},{5,9},{6,10},{7,11},{8,4},{9,5},... | collective-permute-start | bytes 49160 | tf_op jit(solution)/shard_map/ppermute | solution.py:46
  6.2 4.9 %collective-permute-start.1 = (bf16[16,512]{1,0:T(8,128)(2,1)}, bf16[16,512]{1,0:T(8,128)(2,1)S(1)}, u32[]{:S(2)}, u32[]{:S(2)}) collective-permute-start(bf16[16,512]{1,0:T(8,128)(2,1)} %refs_5_.1), channel_id=1, source_target_pairs={{0,8},{1,9},{2,10},{3,11},{4,12},{5,13},{6,14},{7,15},{8,0},{9,1},... | collective-permute-start | bytes 49160 | tf_op jit(solution)/shard_map/ppermute | solution.py:46
  11.1 5.0 %collective-permute-start.5 = (bf16[64,512]{1,0:T(8,128)(2,1)S(1)}, bf16[64,512]{1,0:T(8,128)(2,1)S(1)}, u32[]{:S(2)}, u32[]{:S(2)}) collective-permute-start(bf16[64,512]{1,0:T(8,128)(2,1)S(1)} %join.1.after_ref.refs_6_), channel_id=1, source_target_pairs={{0,3},{1,2},{2,1},{3,0},{4,7},{5,6},{6,5},{7,4},{8,11},{9,10},{10,... | collective-permute-start | bytes 196616 | tf_op jit(solution)/shard_map/ppermute | solution.py:46
  11.1 5.8 %collective-permute-start.4 = (bf16[64,512]{1,0:T(8,128)(2,1)S(1)}, bf16[64,512]{1,0:T(8,128)(2,1)S(1)}, u32[]{:S(2)}, u32[]{:S(2)}) collective-permute-start(bf16[64,512]{1,0:T(8,128)(2,1)S(1)} %join.1.after_ref.refs_6_), channel_id=1, source_target_pairs={{0,2},{1,3},{2,0},{3,1},{4,6},{5,7},{6,4},{7,5},{8,10},{9,11},{10,... | collective-permute-start | bytes 196616 | tf_op jit(solution)/shard_map/ppermute | solution.py:46
  12.6 4.2 %collective-permute-start.3 = (bf16[64,512]{1,0:T(8,128)(2,1)S(1)}, bf16[64,512]{1,0:T(8,128)(2,1)S(1)}, u32[]{:S(2)}, u32[]{:S(2)}) collective-permute-start(bf16[64,512]{1,0:T(8,128)(2,1)S(1)} %join.1.after_ref.refs_6_), channel_id=1, source_target_pairs={{0,1},{1,0},{2,3},{3,2},{4,5},{5,4},{6,7},{7,6},{8,9},{9,8},{10,11... | collective-permute-start | bytes 196616 | tf_op jit(solution)/shard_map/ppermute | solution.py:46
  12.9 3.9 %copy-start = (s32[3072]{0:T(1024)S(1)}, s32[3072]{0:T(1024)}, u32[]{:S(2)}) copy-start(s32[3072]{0:T(1024)} %param.12) | copy-start | bytes 36868
  12.9 3.9 %copy-start.1 = (s32[3072]{0:T(1024)S(1)}, s32[3072]{0:T(1024)}, u32[]{:S(2)}) copy-start(s32[3072]{0:T(1024)} %starts_ref.1) | copy-start | bytes 36868
  20.2 4.1 %collective-permute-start.7 = (f32[8,640]{1,0:T(8,128)S(1)}, f32[8,640]{1,0:T(8,128)S(1)}, u32[]{:S(2)}, u32[]{:S(2)}) collective-permute-start(f32[8,640]{1,0:T(8,128)S(1)} %get-tuple-element.42), channel_id=1, source_target_pairs={{0,1},{1,0},{2,3},{3,2},{4,5},{5,4},{6,7},{7,6},{8,9},{9,8},{10,11... | collective-permute-start | bytes 61448 | tf_op jit(solution)/shard_map/ppermute | solution.py:46
  20.4 3.9 %collective-permute-start.8 = (f32[8,640]{1,0:T(8,128)S(1)}, f32[8,640]{1,0:T(8,128)S(1)}, u32[]{:S(2)}, u32[]{:S(2)}) collective-permute-start(f32[8,640]{1,0:T(8,128)S(1)} %get-tuple-element.43), channel_id=1, source_target_pairs={{0,2},{1,3},{2,0},{3,1},{4,6},{5,7},{6,4},{7,5},{8,10},{9,11},{10,... | collective-permute-start | bytes 61448 | tf_op jit(solution)/shard_map/ppermute | solution.py:46
  21.1 3.3 %collective-permute-start.9 = (f32[8,640]{1,0:T(8,128)S(1)}, f32[8,640]{1,0:T(8,128)S(1)}, u32[]{:S(2)}, u32[]{:S(2)}) collective-permute-start(f32[8,640]{1,0:T(8,128)S(1)} %get-tuple-element.44), channel_id=1, source_target_pairs={{0,3},{1,2},{2,1},{3,0},{4,7},{5,6},{6,5},{7,4},{8,11},{9,10},{10,... | collective-permute-start | bytes 61448 | tf_op jit(solution)/shard_map/ppermute | solution.py:46
  22.2 7.2 %collective-permute-start.6 = (bf16[128,512]{1,0:T(8,128)(2,1)S(1)}, bf16[128,512]{1,0:T(8,128)(2,1)S(1)}, u32[]{:S(2)}, u32[]{:S(2)}) collective-permute-start(bf16[128,512]{1,0:T(8,128)(2,1)S(1)} %get-tuple-element.39), channel_id=1, source_target_pairs={{0,1},{1,2},{2,3},{3,4},{4,5},{5,6},{6,7},{7,8},{8,9},{9,10},{10,1... | collective-permute-start | bytes 393224 | tf_op jit(solution)/shard_map/ppermute | solution.py:465
  24.4 7.1 %collective-permute-start.10 = (f32[8,640]{1,0:T(8,128)S(1)}, f32[8,640]{1,0:T(8,128)S(1)}, u32[]{:S(2)}, u32[]{:S(2)}) collective-permute-start(f32[8,640]{1,0:T(8,128)S(1)} %get-tuple-element.46), channel_id=1, source_target_pairs={{0,4},{1,5},{2,6},{3,7},{4,0},{5,1},{6,2},{7,3},{8,12},{9,13},{10,... | collective-permute-start | bytes 61448 | tf_op jit(solution)/shard_map/ppermute | solution.py:46
  25.2 6.3 %collective-permute-start.11 = (f32[8,640]{1,0:T(8,128)S(1)}, f32[8,640]{1,0:T(8,128)S(1)}, u32[]{:S(2)}, u32[]{:S(2)}) collective-permute-start(f32[8,640]{1,0:T(8,128)S(1)} %get-tuple-element.47), channel_id=1, source_target_pairs={{0,8},{1,9},{2,10},{3,11},{4,12},{5,13},{6,14},{7,15},{8,0},{9,1},... | collective-permute-start | bytes 61448 | tf_op jit(solution)/shard_map/ppermute | solution.py:46
  26.6 5.6 %collective-permute-start.12 = (f32[8,640]{1,0:T(8,128)S(1)}, f32[8,640]{1,0:T(8,128)S(1)}, u32[]{:S(2)}, u32[]{:S(2)}) collective-permute-start(f32[8,640]{1,0:T(8,128)S(1)} %get-tuple-element.48), channel_id=1, source_target_pairs={{0,12},{1,13},{2,14},{3,15},{4,8},{5,9},{6,10},{7,11},{8,4},{9,5},... | collective-permute-start | bytes 61448 | tf_op jit(solution)/shard_map/ppermute | solution.py:46

commit v10 on v9

--- a/solution.py
+++ b/solution.py
@@ -79,7 +79,7 @@
     return pltpu.CompilerParams(vmem_limit_bytes=limit * MIB)
 
 
-def edge_blocks(pre_ref, weight_ref, bias_ref, normed_ref, q_ref, gate_ref, hidden_ref, block, arrive):
+def edge_blocks(pre_ref, weight_ref, bias_ref, normed_ref, q_ref, gate_ref, inv_ref, hidden_ref, block, arrive):
     weight, bias = weight_ref[...], bias_ref[...]
     rows, last = pre_ref.shape[0], None
     for at in range(0, rows + block, block):
@@ -102,15 +102,19 @@
                 centre = out - jnp.mean(out, axis=-1, keepdims=True)
                 inv = lax.rsqrt(jnp.mean(centre * centre, axis=-1, keepdims=True) + EPS)
                 normed_ref[piece] = (centre * inv).astype(BF16)
-                gate_ref[piece] = gate_ref[piece] * (0.5 * inv)
+                inv_ref[piece] = jnp.broadcast_to(0.5 * inv, (CHUNK, LANES))
             q_ref[at - block : at] = dot_t(normed_ref[at - block : at], weight).astype(BF16)
         last = this
+
+
+def edge_outs(rows, width):
+    return [in_vmem((rows, width), BF16)] * 2 + [in_vmem((rows, width), F32), in_vmem((rows, LANES), F32)]
 
 
 def first_kernel(block, copies, pre_hbm, *refs):
     sources, (me_ref, requests_hbm), refs = refs[:copies], refs[copies : copies + 2], refs[copies + 2 :]
     targets, refs = refs[:copies], refs[copies:]
-    ids_ref, other_ref, normed_ref, q_ref, gate_ref, pre_ref, hidden_ref, requests_ref, sem = refs
+    ids_ref, other_ref, normed_ref, q_ref, gate_ref, inv_ref, pre_ref, hidden_ref, requests_ref, sem = refs
     rows = normed_ref.shape[0]
 
     def load(k, source, target):
@@ -136,6 +140,7 @@
         normed_ref,
         q_ref,
         gate_ref,
+        inv_ref,
         hidden_ref,
         block,
         lambda at: loads[at // block].wait(),
@@ -158,7 +163,7 @@
     outs = [in_vmem(a.shape, a.dtype) for a in sources]
     outs += [in_vmem((requests.shape[1] * requests.shape[2], LANES), F32)]
     outs += [in_vmem((edges - rows, width), BF16)]
-    outs += [in_vmem((rows, width), BF16)] * 2 + [in_vmem((rows, width), F32)]
+    outs += edge_outs(rows, width)
     return pl.pallas_call(
         functools.partial(first_kernel, block, copies),
         in_specs=[HBM] * (1 + copies) + [SMEM, HBM],
@@ -176,15 +181,17 @@
     )(in_hbm(preact), *[in_hbm(a) for a in sources], me, in_hbm(requests))
 
 
-def second_kernel(block, pre_ref, weight_ref, bias_ref, after_ref, normed_ref, q_ref, gate_ref, hidden_ref):
+def second_kernel(
+    block, pre_ref, weight_ref, bias_ref, after_ref, normed_ref, q_ref, gate_ref, inv_ref, hidden_ref
+):
     edge_blocks(
-        pre_ref, weight_ref, bias_ref, normed_ref, q_ref, gate_ref, hidden_ref, block, lambda at: None
+        pre_ref, weight_ref, bias_ref, normed_ref, q_ref, gate_ref, inv_ref, hidden_ref, block, lambda at: None
     )
 
 
 def second_part(pre, weight, bias, after, block=512):
     rows, width = pre.shape
-    outs = [in_vmem((rows, width), BF16)] * 2 + [in_vmem((rows, width), F32)]
+    outs = edge_outs(rows, width)
     return pl.pallas_call(
         functools.partial(second_kernel, block),
         in_specs=[VMEM, VMEM, VMEM, ANY],
@@ -217,11 +224,11 @@
 
 
 def after_kernel(
-    parts, chunks, owned, caps, block, me_ref, ids_ref, slots_ref, senders_ref, weight_ref, gain_ref, *refs
+    parts, chunks, owned, caps, block, me_ref, ids_ref, slots_ref, weight_ref, gain_ref, *refs
 ):
-    edge_refs = [refs[3 * k : 3 * k + 3] for k in range(parts)]
-    refs = refs[3 * parts :]
-    pieces, (d_ref, rim_ref), sums_refs = refs[: -2 - chunks], refs[-2 - chunks : -chunks], refs[-chunks:]
+    edge_refs = [refs[4 * k : 4 * k + 4] for k in range(parts)]
+    refs = refs[4 * parts :]
+    pieces, d_ref, sums_refs = refs[: -1 - chunks], refs[-1 - chunks], refs[-chunks:]
     slots = ids_ref.shape[0]
     count = slots // caps
     edges, width = d_ref.shape
@@ -249,61 +256,57 @@
     key = (distance ^ me) * caps + row % caps
     key = jnp.concatenate([key, key], axis=0)
     mean_rows = jnp.concatenate([mean_rows, jnp.zeros_like(mean_rows)], axis=0)
-    rim_row = lax.broadcasted_iota(jnp.int32, (RIM, block), 0) + G_DEV
     sums = jnp.zeros((slots, width), F32)
-    rim = jnp.zeros((RIM, width), F32)
     edge_at = [(part, at) for part in edge_refs for at in range(0, part[0].shape[0], block)]
     last = None
     for number in range(len(edge_at) + 1):
         this = None
         if number < len(edge_at):
-            (normed_ref, q_ref, gate_ref), at = edge_at[number]
+            (normed_ref, q_ref, gate_ref, inv_ref), at = edge_at[number]
             piece = slice(at, at + block)
             onehot_t = (key == slots_ref[:, number * block : (number + 1) * block]).astype(F32)
             onehot = onehot_t.T
             g = dot_t(normed_ref[piece], mean_rows)
             s_rows = dot(onehot.astype(BF16), s_both)
-            this = (onehot_t[:slots].astype(BF16), onehot, g, s_rows, q_ref, gate_ref, at)
+            this = (onehot_t[:slots].astype(BF16), onehot, g, s_rows, q_ref, gate_ref, inv_ref, at)
         if last is not None:
-            onehot_t, onehot, g, s_rows, q_ref, gate_ref, first = last
+            onehot_t, onehot, g, s_rows, q_ref, gate_ref, inv_ref, first = last
             at = (number - 1) * block
             for row in range(0, block, CHUNK):
                 piece, inner = slice(first + row, first + row + CHUNK), slice(row, row + CHUNK)
                 c = jnp.sum(onehot[inner] * g[inner], axis=-1, keepdims=True)
-                d = gate_ref[piece] * (s_rows[inner] - c * q_ref[piece].astype(F32))
+                inv = jnp.concatenate([inv_ref[piece]] * (width // LANES), axis=1)
+                d = gate_ref[piece] * inv * (s_rows[inner] - c * q_ref[piece].astype(F32))
                 d_ref[at + row : at + row + CHUNK, :] = d.astype(BF16)
             d = d_ref[at : at + block, :]
             sums += dot(onehot_t, d)
-            if at + block > G_DEV:
-                pick = (rim_row == senders_ref[:, at : at + block]).astype(F32).astype(BF16)
-                rim += dot(pick, d)
         last = this
 
     each = slots // chunks
     for k, sums_ref in enumerate(sums_refs):
         sums_ref[:, :width] = sums[k * each : (k + 1) * each]
         sums_ref[:, width:] = ids_ref[k * each : (k + 1) * each, :]
-    rim_ref[...] = rim.astype(BF16)
-
-
-def after(me, ids, slots, senders, weight, gain, parts, pieces, owned, caps, chunks, block=512):
+
+
+def after(me, ids, slots, weight, gain, parts, pieces, owned, caps, chunks, block=512):
     edges, width = slots.shape[1], weight.shape[0]
     each = ids.shape[0] // chunks
     return pl.pallas_call(
         functools.partial(after_kernel, len(parts), chunks, owned, caps, block),
-        in_specs=[SMEM] + [VMEM] * (5 + 3 * len(parts) + len(pieces)),
-        out_specs=[VMEM] * (2 + chunks),
-        out_shape=[in_vmem((edges, width), BF16), in_vmem((RIM, width), BF16)]
+        in_specs=[SMEM] + [VMEM] * (4 + 4 * len(parts) + len(pieces)),
+        out_specs=[VMEM] * (1 + chunks),
+        out_shape=[in_vmem((edges, width), BF16)]
         + [in_vmem((each, width + LANES), F32)] * chunks,
         cost_estimate=cost(6 * edges * width * width, 8 * edges * width),
         compiler_params=params(20),
         name="after",
-    )(me, ids, slots, senders, weight, gain, *[a for part in parts for a in part], *pieces)
+    )(me, ids, slots, weight, gain, *[a for part in parts for a in part], *pieces)
 
 
 def segments_kernel(block, starts_ref, senders_ref, d_ref, total_ref):
     edges, width = d_ref.shape
     total_ref[:8, :] = jnp.zeros((8, width), F32)
+    total_ref[G_DEV : G_DEV + RIM, :] = jnp.zeros((RIM, width), F32)
     row = lax.broadcasted_iota(jnp.int32, (block + 16, block), 0)
     for at in range(0, edges, block):
         base = pl.multiple_of(starts_ref[at] // 8 * 8, 8)
@@ -357,7 +360,8 @@
 
 
 def regroup_kernel(groups, parts, *refs):
-    outs = refs[parts + 1 :]
+    total_ref, rim_ref, *outs = refs[parts:]
+    rim_ref[...] = total_ref[G_DEV : G_DEV + RIM, :].astype(BF16)
     low = groups // len(outs)
     each = refs[0].shape[0] // groups
     for j, out_ref in enumerate(outs):
@@ -367,18 +371,19 @@
                 out_ref[to : to + each, :] = refs[k][at : at + each, :]
 
 
-def regroup(arrived, radix, low, after):
+def regroup(arrived, radix, low, total):
     rows, width = arrived[0].shape
     parts = len(arrived)
     return pl.pallas_call(
         functools.partial(regroup_kernel, radix * low, parts),
-        in_specs=[VMEM] * parts + [ANY],
-        out_specs=[VMEM] * radix,
-        out_shape=[in_vmem((rows * parts // radix, width), F32)] * radix,
+        in_specs=[VMEM] * (parts + 1),
+        out_specs=[VMEM] * (1 + radix),
+        out_shape=[in_vmem((RIM, total.shape[1]), BF16)]
+        + [in_vmem((rows * parts // radix, width), F32)] * radix,
         cost_estimate=cost(0, 8 * rows * parts * width),
         compiler_params=params(8),
         name="regroup",
-    )(*arrived, after)
+    )(*arrived, total)
 
 
 def mesh_kernel(parts, *refs):
@@ -433,7 +438,7 @@
         mesh_cotangent,
     )
     weight, bias, weight_g, weight_m, gain, own_rows, ids, more, *first = first_part(
-        saved_preact, edges // 3, sources, me.reshape(1), mesh_requests.swapaxes(1, 2)
+        saved_preact, edges // 6, sources, me.reshape(1), mesh_requests.swapaxes(1, 2)
     )
 
     held = [mesh_cotangent]
@@ -447,11 +452,10 @@
             second = second_part(more, weight, bias, held[0])
 
     back = stages[::-1]
-    d_preact, rim, *chunks = after(
+    d_preact, *chunks = after(
         me.reshape(1),
         ids,
         edge_slots.reshape(1, edges),
-        edge_senders.reshape(1, edges),
         weight,
         gain,
         [first, second],
@@ -462,11 +466,12 @@
     )
 
     total = segments(edge_senders, d_preact)
-    carried = lax.ppermute(rim, "band", [(i, (i + 1) % count) for i in range(count)])
-    arrived, left = None, count
+    arrived, carried, left = None, None, count
     for shift, radix in back:
         if arrived is not None:
-            chunks = regroup(arrived, radix, left // radix, total)
+            rim, *chunks = regroup(arrived, radix, left // radix, total)
+            if carried is None:
+                carried = lax.ppermute(rim, "band", [(i, (i + 1) % count) for i in range(count)])
         left //= radix
         arrived = [chunks[0]] + [swap(chunks[j], count, j << shift) for j in range(1, radix)]
     grid_adjoint = grid_rows(total, carried, weight_g)

time: 33.3 us -> 35.9 us (1.078)
  waiting for transfers between devices: 3.53 us -> 6.18 us
    ppermute x1, waiting for transfers between devices: 0.48 us -> 2.85 us  [on_device(): lax.ppermute(rim, 'band', [(i, (i + 1) % count) for i in range(count)])]
    pallas_call x1, Pallas kernels: 3.2 us -> 2.56 us  [first_part(): pl.pallas_call(functools.partial(first_kernel, block, copies), in_specs=[...]
    pallas_call x1, Pallas kernels: 3.1 us -> 3.68 us  [second_part(): pl.pallas_call(functools.partial(second_kernel, block), in_specs=[VMEM, V...]
  transfers between devices with their start and end apart: 13 -> 13, of which waited for: 6 -> 6; matrix products, arithmetic and copies ran while one was open for 0% -> 0% of each run, Pallas kernels for 31% -> 28%
where the time goes in v10:
time: 35.9 us; the launch traced here: 35.8 us
  Pallas kernels  14.8 us (41%)
  starting transfers between devices  14.1 us (39%)
  waiting for transfers between devices  6.18 us (17%)
  between operations  0.73 us (2%)
    ppermute x12, starting transfers between devices, swap(): return lax.ppermute(block, 'band', [(i, i ^ mask) for i in range(count)])  13.8 us
    pallas_call x1, Pallas kernels, second_part(): pl.pallas_call(functools.partial(second_kernel, block), in_specs=[VMEM, V...  3.68 us
    pallas_call x1, Pallas kernels, after(): pl.pallas_call(functools.partial(after_kernel, len(parts), chunks, owned,...  3.58 us
    ppermute x12, waiting for transfers between devices, swap(): return lax.ppermute(block, 'band', [(i, i ^ mask) for i in range(count)])  3.33 us
    ppermute x1, waiting for transfers between devices, on_device(): lax.ppermute(rim, 'band', [(i, (i + 1) % count) for i in range(count)])  2.85 us
    pallas_call x1, Pallas kernels, first_part(): pl.pallas_call(functools.partial(first_kernel, block, copies), in_specs=[...  2.56 us
    pallas_call x1, Pallas kernels, grid_rows(): pl.pallas_call(functools.partial(grid_kernel, block), in_specs=[VMEM] * 3...  2.14 us
    pallas_call x1, Pallas kernels, segments(): pl.pallas_call(functools.partial(segments_kernel, block), in_specs=[SMEM]...  1.77 us
  transfers between devices with their start and end apart: 13, of which 6 were waited for; matrix products, arithmetic and copies ran while one was open for 0% of the time, Pallas kernels for 28%

profile of v10, /device:TPU:0, one launch (start us, length us, event | category | flops | bytes accessed | tf_op | source)
XLA Modules:
  0.0 35.8 jit_solution(16999950184427080111)
XLA Ops:
  0.6 3.1 %collective-permute-start = (bf16[16,512]{1,0:T(8,128)(2,1)}, bf16[16,512]{1,0:T(8,128)(2,1)S(1)}, u32[]{:S(2)}, u32[]{:S(2)}) collective-permute-start(bf16[16,512]{1,0:T(8,128)(2,1)} %refs_5_.1), channel_id=1, source_target_pairs={{0,4},{1,5},{2,6},{3,7},{4,0},{5,1},{6,2},{7,3},{8,12},{9,13},{10,... | collective-permute-start | bytes 49160 | tf_op jit(solution)/shard_map/ppermute | solution.py:46
  3.7 2.5 %collective-permute-start.2 = (bf16[16,512]{1,0:T(8,128)(2,1)}, bf16[16,512]{1,0:T(8,128)(2,1)S(1)}, u32[]{:S(2)}, u32[]{:S(2)}) collective-permute-start(bf16[16,512]{1,0:T(8,128)(2,1)} %refs_5_.1), channel_id=1, source_target_pairs={{0,12},{1,13},{2,14},{3,15},{4,8},{5,9},{6,10},{7,11},{8,4},{9,5},... | collective-permute-start | bytes 49160 | tf_op jit(solution)/shard_map/ppermute | solution.py:46
  6.2 0.1 collective-permute-start.1
  6.3 2.6 %first_part.1 = (bf16[512,512]{1,0:T(8,128)(2,1)S(1)}, f32[1,512]{1,0:T(1,128)S(1)}, bf16[512,512]{1,0:T(8,128)(2,1)S(1)}, bf16[512,512]{1,0:T(8,128)(2,1)S(1)},...) custom-call(bf16[3072,512]{1,0:T(8,128)(2,1)} %pre_hbm.1, ...), custom_call_target="tpu_custom_call" | custom-call | flops 805306368 | bytes 2621440 | tf_op jit(solution)/shard_map/first_part/pallas_call | solution.py:167
  8.9 0.8 %collective-permute-done.2.refs_3_ = bf16[16,512]{1,0:T(8,128)(2,1)S(1)} collective-permute-done((bf16[16,512]{1,0:T(8,128)(2,1)}, bf16[16,512]{1,0:T(8,128)(2,1)S(1)}, u32[]{:S(2)}, u32[]{:S(2)}) %collective-permute-start.2) | collective-permute-done | bytes 16416 | tf_op jit(solution)/shard_map/ppermute | solution.py:46
  9.7 1.4 %collective-permute-done.1.refs_2_ = bf16[16,512]{1,0:T(8,128)(2,1)S(1)} collective-permute-done((bf16[16,512]{1,0:T(8,128)(2,1)}, bf16[16,512]{1,0:T(8,128)(2,1)S(1)}, u32[]{:S(2)}, u32[]{:S(2)}) %collective-permute-start.1) | collective-permute-done | bytes 16416 | tf_op jit(solution)/shard_map/ppermute | solution.py:46
  11.1 1.6 %collective-permute-start.4 = (bf16[64,512]{1,0:T(8,128)(2,1)S(1)}, bf16[64,512]{1,0:T(8,128)(2,1)S(1)}, u32[]{:S(2)}, u32[]{:S(2)}) collective-permute-start(bf16[64,512]{1,0:T(8,128)(2,1)S(1)} %join.1.after_ref.refs_8_), channel_id=1, source_target_pairs={{0,2},{1,3},{2,0},{3,1},{4,6},{5,7},{6,4},{7,5},{8,10},{9,11},{10,... | collective-permute-start | bytes 196616 | tf_op jit(solution)/shard_map/ppermute | solution.py:46
  12.6 0.3 collective-permute-start.3
  12.9 3.7 %second_part.1 = (bf16[2560,512]{1,0:T(8,128)(2,1)S(1)}, bf16[2560,512]{1,0:T(8,128)(2,1)S(1)}, f32[2560,512]{1,0:T(8,128)S(1)}, f32[2560,128]{1,0:T(8,128)S(1)}) custom-call(bf16[2560,512]{1,0:T(8,128)(2,1)S(1)} %get-tuple-element.35.pre_ref, bf16[512,512]{1,0:T(8,128)(2,1)S(1)} %get-tuple-element.29.weight_ref, f32[1,512]{1,0:T(1,128)S(1)} %get-tuple-element.36.bias_ref, ...), custom_call_target="tpu_custom_call" | custom-call | flops 4026531840 | bytes 13107200 | tf_op jit(solution)/shard_map/second_part/pallas_call | solution.py:195
  16.6 0.2 collective-permute-done.4.refs_10_
  16.9 3.6 %after.1 = (bf16[3072,512]{1,0:T(8,128)(2,1)S(1)}, f32[8,640]{1,0:T(8,128)S(1)}, f32[8,640]{1,0:T(8,128)S(1)}, f32[8,640]{1,0:T(8,128)S(1)}, f32[8,640]{1,0:T(8,128)S(1)}) custom-call(s32[1]{0:T(128)} %bitcast.1.refs_6_.me_ref, f32[32,128]{1,0:T(8,128)S(1)} %get-tuple-element.28.ids_ref, s32[1,3072]{1,0:T(1,128)S(1)} %bitcast.6, ...), custom_call_target="tpu_custom_call" | custom-call | flops 4831838208 | bytes 12582912 | tf_op jit(solution)/shard_map/after/pallas_call | solution.py:294
  20.5 0.1 collective-permute-start.6
  20.6 1.3 %collective-permute-start.7 = (f32[8,640]{1,0:T(8,128)S(1)}, f32[8,640]{1,0:T(8,128)S(1)}, u32[]{:S(2)}, u32[]{:S(2)}) collective-permute-start(f32[8,640]{1,0:T(8,128)S(1)} %get-tuple-element.45), channel_id=1, source_target_pairs={{0,2},{1,3},{2,0},{3,1},{4,6},{5,7},{6,4},{7,5},{8,10},{9,11},{10,... | collective-permute-start | bytes 61448 | tf_op jit(solution)/shard_map/ppermute | solution.py:46
  21.9 0.5 %collective-permute-start.8 = (f32[8,640]{1,0:T(8,128)S(1)}, f32[8,640]{1,0:T(8,128)S(1)}, u32[]{:S(2)}, u32[]{:S(2)}) collective-permute-start(f32[8,640]{1,0:T(8,128)S(1)} %get-tuple-element.46), channel_id=1, source_target_pairs={{0,3},{1,2},{2,1},{3,0},{4,7},{5,6},{6,5},{7,4},{8,11},{9,10},{10,... | collective-permute-start | bytes 61448 | tf_op jit(solution)/shard_map/ppermute | solution.py:46
  22.4 1.8 %segments.1.refs_4_.total_ref = f32[2448,512]{1,0:T(8,128)S(1)} custom-call(s32[3072]{0:T(1024)S(1)} %copy-done.1, s32[1,3072]{1,0:T(1,128)S(1)} %bitcast.7, bf16[3072,512]{1,0:T(8,128)(2,1)S(1)} %get-tuple-element.42.d_ref), custom_call_target="tpu_custom_call" | custom-call | flops 3221225472 | bytes 6291456 | tf_op jit(solution)/shard_map/segments/pallas_call | solution.py:321
  24.2 0.2 collective-permute-done.7.refs_2_
  24.4 0.7 %collective-permute-done.8.refs_3_ = f32[8,640]{1,0:T(8,128)S(1)} collective-permute-done((f32[8,640]{1,0:T(8,128)S(1)}, f32[8,640]{1,0:T(8,128)S(1)}, u32[]{:S(2)}, u32[]{:S(2)}) %collective-permute-start.8) | collective-permute-done | bytes 20512 | tf_op jit(solution)/shard_map/ppermute | solution.py:46
  25.1 0.2 collective-permute-start.9
  25.4 0.7 %collective-permute-start.10 = (f32[8,640]{1,0:T(8,128)S(1)}, f32[8,640]{1,0:T(8,128)S(1)}, u32[]{:S(2)}, u32[]{:S(2)}) collective-permute-start(f32[8,640]{1,0:T(8,128)S(1)} %get-tuple-element.50), channel_id=1, source_target_pairs={{0,4},{1,5},{2,6},{3,7},{4,0},{5,1},{6,2},{7,3},{8,12},{9,13},{10,... | collective-permute-start | bytes 61448 | tf_op jit(solution)/shard_map/ppermute | solution.py:46
  26.1 1.2 %collective-permute-start.11 = (f32[8,640]{1,0:T(8,128)S(1)}, f32[8,640]{1,0:T(8,128)S(1)}, u32[]{:S(2)}, u32[]{:S(2)}) collective-permute-start(f32[8,640]{1,0:T(8,128)S(1)} %get-tuple-element.51), channel_id=1, source_target_pairs={{0,8},{1,9},{2,10},{3,11},{4,12},{5,13},{6,14},{7,15},{8,0},{9,1},... | collective-permute-start | bytes 61448 | tf_op jit(solution)/shard_map/ppermute | solution.py:46
  27.3 2.5 %collective-permute-start.12 = (f32[8,640]{1,0:T(8,128)S(1)}, f32[8,640]{1,0:T(8,128)S(1)}, u32[]{:S(2)}, u32[]{:S(2)}) collective-permute-start(f32[8,640]{1,0:T(8,128)S(1)} %get-tuple-element.52), channel_id=1, source_target_pairs={{0,12},{1,13},{2,14},{3,15},{4,8},{5,9},{6,10},{7,11},{8,4},{9,5},... | collective-permute-start | bytes 61448 | tf_op jit(solution)/shard_map/ppermute | solution.py:46
  29.7 2.9 %collective-permute-done.9.carried_ref = bf16[128,512]{1,0:T(8,128)(2,1)S(1)} collective-permute-done((bf16[128,512]{1,0:T(8,128)(2,1)S(1)}, bf16[128,512]{1,0:T(8,128)(2,1)S(1)}, u32[]{:S(2)}, u32[]{:S(2)}) %collective-permute-start.9) | collective-permute-done | bytes 131104 | tf_op jit(solution)/shard_map/ppermute | solution.py:474
  32.6 2.1 %grid_rows.1.refs_5_ = bf16[2048,512]{1,0:T(8,128)(2,1)} custom-call(f32[2448,512]{1,0:T(8,128)S(1)} %segments.1.refs_4_.total_ref, bf16[128,512]{1,0:T(8,128)(2,1)S(1)} %collective-permute-done.9.carried_ref, bf16[512,512]{1,0:T(8,128)(2,1)S(1)} %get-tuple-element.48.weight_ref), custom_call_target="tpu_custom_call" | custom-call | flops 1073741824 | bytes 6291456 | tf_op jit(solution)/shard_map/grid_rows/pallas_call | solution.py:350
  34.8 1.0 %mesh_rows.1 = bf16[16,512]{1,0:T(8,128)(2,1)} custom-call(f32[8,640]{1,0:T(8,128)S(1)} %get-tuple-element.49.refs_0_, f32[8,640]{1,0:T(8,128)S(1)} %collective-permute-done.10.refs_1_, f32[8,640]{1,0:T(8,128)S(1)} %collective-permute-done.11.refs_2_, f32[8,640]{1,0:T(8,128)S(1)} %collective-permute-done.12.refs_3_, ...), custom_call_target="tpu_custom_call" | custom-call | flops 8388608 | bytes 524288 | tf_op jit(solution)/shard_map/mesh_rows/pallas_call | solution.py:403
  (14 shorter events, 0.1 us)
Async XLA Ops:
  0.6 8.3 %collective-permute-start = (bf16[16,512]{1,0:T(8,128)(2,1)}, bf16[16,512]{1,0:T(8,128)(2,1)S(1)}, u32[]{:S(2)}, u32[]{:S(2)}) collective-permute-start(bf16[16,512]{1,0:T(8,128)(2,1)} %refs_5_.1), channel_id=1, source_target_pairs={{0,4},{1,5},{2,6},{3,7},{4,0},{5,1},{6,2},{7,3},{8,12},{9,13},{10,... | collective-permute-start | bytes 49160 | tf_op jit(solution)/shard_map/ppermute | solution.py:46
  3.7 6.0 %collective-permute-start.2 = (bf16[16,512]{1,0:T(8,128)(2,1)}, bf16[16,512]{1,0:T(8,128)(2,1)S(1)}, u32[]{:S(2)}, u32[]{:S(2)}) collective-permute-start(bf16[16,512]{1,0:T(8,128)(2,1)} %refs_5_.1), channel_id=1, source_target_pairs={{0,12},{1,13},{2,14},{3,15},{4,8},{5,9},{6,10},{7,11},{8,4},{9,5},... | collective-permute-start | bytes 49160 | tf_op jit(solution)/shard_map/ppermute | solution.py:46
  6.2 4.9 %collective-permute-start.1 = (bf16[16,512]{1,0:T(8,128)(2,1)}, bf16[16,512]{1,0:T(8,128)(2,1)S(1)}, u32[]{:S(2)}, u32[]{:S(2)}) collective-permute-start(bf16[16,512]{1,0:T(8,128)(2,1)} %refs_5_.1), channel_id=1, source_target_pairs={{0,8},{1,9},{2,10},{3,11},{4,12},{5,13},{6,14},{7,15},{8,0},{9,1},... | collective-permute-start | bytes 49160 | tf_op jit(solution)/shard_map/ppermute | solution.py:46
  11.1 5.6 %collective-permute-start.5 = (bf16[64,512]{1,0:T(8,128)(2,1)S(1)}, bf16[64,512]{1,0:T(8,128)(2,1)S(1)}, u32[]{:S(2)}, u32[]{:S(2)}) collective-permute-start(bf16[64,512]{1,0:T(8,128)(2,1)S(1)} %join.1.after_ref.refs_8_), channel_id=1, source_target_pairs={{0,3},{1,2},{2,1},{3,0},{4,7},{5,6},{6,5},{7,4},{8,11},{9,10},{10,... | collective-permute-start | bytes 196616 | tf_op jit(solution)/shard_map/ppermute | solution.py:46
  11.1 5.8 %collective-permute-start.4 = (bf16[64,512]{1,0:T(8,128)(2,1)S(1)}, bf16[64,512]{1,0:T(8,128)(2,1)S(1)}, u32[]{:S(2)}, u32[]{:S(2)}) collective-permute-start(bf16[64,512]{1,0:T(8,128)(2,1)S(1)} %join.1.after_ref.refs_8_), channel_id=1, source_target_pairs={{0,2},{1,3},{2,0},{3,1},{4,6},{5,7},{6,4},{7,5},{8,10},{9,11},{10,... | collective-permute-start | bytes 196616 | tf_op jit(solution)/shard_map/ppermute | solution.py:46
  12.6 4.2 %collective-permute-start.3 = (bf16[64,512]{1,0:T(8,128)(2,1)S(1)}, bf16[64,512]{1,0:T(8,128)(2,1)S(1)}, u32[]{:S(2)}, u32[]{:S(2)}) collective-permute-start(bf16[64,512]{1,0:T(8,128)(2,1)S(1)} %join.1.after_ref.refs_8_), channel_id=1, source_target_pairs={{0,1},{1,0},{2,3},{3,2},{4,5},{5,4},{6,7},{7,6},{8,9},{9,8},{10,11... | collective-permute-start | bytes 196616 | tf_op jit(solution)/shard_map/ppermute | solution.py:46
  12.9 3.9 %copy-start = (s32[3072]{0:T(1024)S(1)}, s32[3072]{0:T(1024)}, u32[]{:S(2)}) copy-start(s32[3072]{0:T(1024)} %param.12) | copy-start | bytes 36868
  16.9 5.5 %copy-start.1 = (s32[3072]{0:T(1024)S(1)}, s32[3072]{0:T(1024)}, u32[]{:S(2)}) copy-start(s32[3072]{0:T(1024)} %starts_ref.1) | copy-start | bytes 36868
  20.5 3.7 %collective-permute-start.6 = (f32[8,640]{1,0:T(8,128)S(1)}, f32[8,640]{1,0:T(8,128)S(1)}, u32[]{:S(2)}, u32[]{:S(2)}) collective-permute-start(f32[8,640]{1,0:T(8,128)S(1)} %get-tuple-element.44), channel_id=1, source_target_pairs={{0,1},{1,0},{2,3},{3,2},{4,5},{5,4},{6,7},{7,6},{8,9},{9,8},{10,11... | collective-permute-start | bytes 61448 | tf_op jit(solution)/shard_map/ppermute | solution.py:46
  20.6 3.8 %collective-permute-start.7 = (f32[8,640]{1,0:T(8,128)S(1)}, f32[8,640]{1,0:T(8,128)S(1)}, u32[]{:S(2)}, u32[]{:S(2)}) collective-permute-start(f32[8,640]{1,0:T(8,128)S(1)} %get-tuple-element.45), channel_id=1, source_target_pairs={{0,2},{1,3},{2,0},{3,1},{4,6},{5,7},{6,4},{7,5},{8,10},{9,11},{10,... | collective-permute-start | bytes 61448 | tf_op jit(solution)/shard_map/ppermute | solution.py:46
  21.9 3.2 %collective-permute-start.8 = (f32[8,640]{1,0:T(8,128)S(1)}, f32[8,640]{1,0:T(8,128)S(1)}, u32[]{:S(2)}, u32[]{:S(2)}) collective-permute-start(f32[8,640]{1,0:T(8,128)S(1)} %get-tuple-element.46), channel_id=1, source_target_pairs={{0,3},{1,2},{2,1},{3,0},{4,7},{5,6},{6,5},{7,4},{8,11},{9,10},{10,... | collective-permute-start | bytes 61448 | tf_op jit(solution)/shard_map/ppermute | solution.py:46
  25.1 7.5 %collective-permute-start.9 = (bf16[128,512]{1,0:T(8,128)(2,1)S(1)}, bf16[128,512]{1,0:T(8,128)(2,1)S(1)}, u32[]{:S(2)}, u32[]{:S(2)}) collective-permute-start(bf16[128,512]{1,0:T(8,128)(2,1)S(1)} %get-tuple-element.47), channel_id=1, source_target_pairs={{0,1},{1,2},{2,3},{3,4},{4,5},{5,6},{6,7},{7,8},{8,9},{9,10},{10,1... | collective-permute-start | bytes 393224 | tf_op jit(solution)/shard_map/ppermute | solution.py:474
  25.4 9.4 %collective-permute-start.10 = (f32[8,640]{1,0:T(8,128)S(1)}, f32[8,640]{1,0:T(8,128)S(1)}, u32[]{:S(2)}, u32[]{:S(2)}) collective-permute-start(f32[8,640]{1,0:T(8,128)S(1)} %get-tuple-element.50), channel_id=1, source_target_pairs={{0,4},{1,5},{2,6},{3,7},{4,0},{5,1},{6,2},{7,3},{8,12},{9,13},{10,... | collective-permute-start | bytes 61448 | tf_op jit(solution)/shard_map/ppermute | solution.py:46
  26.1 8.7 %collective-permute-start.11 = (f32[8,640]{1,0:T(8,128)S(1)}, f32[8,640]{1,0:T(8,128)S(1)}, u32[]{:S(2)}, u32[]{:S(2)}) collective-permute-start(f32[8,640]{1,0:T(8,128)S(1)} %get-tuple-element.51), channel_id=1, source_target_pairs={{0,8},{1,9},{2,10},{3,11},{4,12},{5,13},{6,14},{7,15},{8,0},{9,1},... | collective-permute-start | bytes 61448 | tf_op jit(solution)/shard_map/ppermute | solution.py:46
  27.3 7.5 %collective-permute-start.12 = (f32[8,640]{1,0:T(8,128)S(1)}, f32[8,640]{1,0:T(8,128)S(1)}, u32[]{:S(2)}, u32[]{:S(2)}) collective-permute-start(f32[8,640]{1,0:T(8,128)S(1)} %get-tuple-element.52), channel_id=1, source_target_pairs={{0,12},{1,13},{2,14},{3,15},{4,8},{5,9},{6,10},{7,11},{8,4},{9,5},... | collective-permute-start | bytes 61448 | tf_op jit(solution)/shard_map/ppermute | solution.py:46

commit v11 on v9

--- a/solution.py
+++ b/solution.py
@@ -79,16 +79,16 @@
     return pltpu.CompilerParams(vmem_limit_bytes=limit * MIB)
 
 
-def edge_blocks(pre_ref, weight_ref, bias_ref, normed_ref, q_ref, gate_ref, hidden_ref, block, arrive):
+def edge_blocks(pre_at, weight_ref, bias_ref, normed_ref, q_ref, gate_ref, hidden_ref, block):
     weight, bias = weight_ref[...], bias_ref[...]
-    rows, last = pre_ref.shape[0], None
+    rows, last = normed_ref.shape[0], None
     for at in range(0, rows + block, block):
         this = None
         if at < rows:
-            arrive(at)
+            pre_ref, first = pre_at(at)
             for row in range(at, at + block, CHUNK):
                 piece = slice(row, row + CHUNK)
-                half = 0.5 * pre_ref[piece].astype(F32)
+                half = 0.5 * pre_ref[row - first : row - first + CHUNK].astype(F32)
                 t = jnp.tanh(half)
                 double = 1.0 + t
                 h = half * double
@@ -107,38 +107,36 @@
         last = this
 
 
+def arriving(loads, pre_ref, block, first=0):
+    def pre_at(at):
+        loads[(at - first) // block].wait()
+        return pre_ref, first
+
+    return pre_at
+
+
 def first_kernel(block, copies, pre_hbm, *refs):
     sources, (me_ref, requests_hbm), refs = refs[:copies], refs[copies : copies + 2], refs[copies + 2 :]
     targets, refs = refs[:copies], refs[copies:]
-    ids_ref, other_ref, normed_ref, q_ref, gate_ref, pre_ref, hidden_ref, requests_ref, sem = refs
+    ids_ref, next_ref, normed_ref, q_ref, gate_ref, pre_ref, hidden_ref, requests_ref, sem = refs
     rows = normed_ref.shape[0]
 
     def load(k, source, target):
         return pltpu.make_async_copy(source, target, sem.at[k])
 
     others = [load(k, a, b) for k, (a, b) in enumerate(zip(sources, targets))]
-    starts = list(range(0, rows, block))
-    more_rows = other_ref.shape[0]
     loads = [
-        load(copies + k, pre_hbm.at[pl.ds(at, block)], pre_ref.at[pl.ds(at, block)])
-        for k, at in enumerate(starts)
+        load(copies + at // block, pre_hbm.at[pl.ds(at, block)], pre_ref.at[pl.ds(at, block)])
+        for at in range(0, rows, block)
     ]
-    more = load(copies + len(loads), pre_hbm.at[pl.ds(rows, more_rows)], other_ref)
+    more = load(copies + len(loads), pre_hbm.at[pl.ds(rows, next_ref.shape[0])], next_ref)
     asked = load(copies + len(loads) + 1, requests_hbm, requests_ref)
     for copy in others[:2] + loads + others[2:] + [more, asked]:
         copy.start()
     for copy in others[:2]:
         copy.wait()
     edge_blocks(
-        pre_ref,
-        targets[0],
-        targets[1],
-        normed_ref,
-        q_ref,
-        gate_ref,
-        hidden_ref,
-        block,
-        lambda at: loads[at // block].wait(),
+        arriving(loads, pre_ref, block), targets[0], targets[1], normed_ref, q_ref, gate_ref, hidden_ref, block
     )
     for copy in others[2:] + [more, asked]:
         copy.wait()
@@ -153,11 +151,11 @@
 
 
 def first_part(preact, rows, sources, me, requests, block=512):
-    edges, width = preact.shape
+    width = preact.shape[1]
     copies = len(sources)
     outs = [in_vmem(a.shape, a.dtype) for a in sources]
     outs += [in_vmem((requests.shape[1] * requests.shape[2], LANES), F32)]
-    outs += [in_vmem((edges - rows, width), BF16)]
+    outs += [in_vmem((block, width), BF16)]
     outs += [in_vmem((rows, width), BF16)] * 2 + [in_vmem((rows, width), F32)]
     return pl.pallas_call(
         functools.partial(first_kernel, block, copies),
@@ -176,25 +174,53 @@
     )(in_hbm(preact), *[in_hbm(a) for a in sources], me, in_hbm(requests))
 
 
-def second_kernel(block, pre_ref, weight_ref, bias_ref, after_ref, normed_ref, q_ref, gate_ref, hidden_ref):
+def second_kernel(block, copies, next_ref, weight_ref, bias_ref, after_ref, pre_hbm, *refs):
+    sources, targets, refs = refs[:copies], refs[copies : 2 * copies], refs[2 * copies :]
+    normed_ref, q_ref, gate_ref, pre_ref, hidden_ref, sem = refs
+    done = pre_hbm.shape[0] - normed_ref.shape[0] + block
+    loads = [
+        pltpu.make_async_copy(
+            pre_hbm.at[pl.ds(done + at, block)], pre_ref.at[pl.ds(at, block)], sem.at[copies + at // block]
+        )
+        for at in range(0, pre_ref.shape[0], block)
+    ]
+    others = [pltpu.make_async_copy(a, b, sem.at[k]) for k, (a, b) in enumerate(zip(sources, targets))]
+    for copy in loads + others:
+        copy.start()
+    later = arriving(loads, pre_ref, block, block)
     edge_blocks(
-        pre_ref, weight_ref, bias_ref, normed_ref, q_ref, gate_ref, hidden_ref, block, lambda at: None
-    )
-
-
-def second_part(pre, weight, bias, after, block=512):
-    rows, width = pre.shape
-    outs = [in_vmem((rows, width), BF16)] * 2 + [in_vmem((rows, width), F32)]
-    return pl.pallas_call(
-        functools.partial(second_kernel, block),
-        in_specs=[VMEM, VMEM, VMEM, ANY],
+        lambda at: later(at) if at else (next_ref, 0),
+        weight_ref,
+        bias_ref,
+        normed_ref,
+        q_ref,
+        gate_ref,
+        hidden_ref,
+        block,
+    )
+    for copy in others:
+        copy.wait()
+
+
+def second_part(preact, rows, following, weight, bias, sources, after):
+    block, width = following.shape
+    copies = len(sources)
+    outs = [in_vmem(a.shape, a.dtype) for a in sources]
+    outs += [in_vmem((rows, width), BF16)] * 2 + [in_vmem((rows, width), F32)]
+    return pl.pallas_call(
+        functools.partial(second_kernel, block, copies),
+        in_specs=[VMEM, VMEM, VMEM, ANY, HBM] + [HBM] * copies,
         out_specs=[VMEM] * len(outs),
         out_shape=outs,
-        scratch_shapes=[pltpu.VMEM((rows, width), BF16)],
+        scratch_shapes=[
+            pltpu.VMEM((rows - block, width), BF16),
+            pltpu.VMEM((rows, width), BF16),
+            DMA((copies + (rows - block) // block,)),
+        ],
         cost_estimate=cost(6 * rows * width * width, 10 * rows * width),
-        compiler_params=params(16),
+        compiler_params=params(20),
         name="second_part",
-    )(pre, weight, bias, after)
+    )(following, weight, bias, after, in_hbm(preact), *[in_hbm(a) for a in sources])
 
 
 def join_kernel(parts, *refs):
@@ -427,13 +453,11 @@
     sources = (
         out_weight,
         out_bias.reshape(1, width),
-        grid_weight,
-        mesh_weight,
         ln_gain.reshape(1, width),
         mesh_cotangent,
     )
-    weight, bias, weight_g, weight_m, gain, own_rows, ids, more, *first = first_part(
-        saved_preact, edges // 3, sources, me.reshape(1), mesh_requests.swapaxes(1, 2)
+    weight, bias, gain, own_rows, ids, following, *first = first_part(
+        saved_preact, edges // 6, sources, me.reshape(1), mesh_requests.swapaxes(1, 2)
     )
 
     held = [mesh_cotangent]
@@ -444,7 +468,9 @@
             held = [join(held, ids)]
         held += [swap(held[0], count, j << shift) for j in range(1, radix)]
         if number == 1:
-            second = second_part(more, weight, bias, held[0])
+            weight_g, weight_m, *second = second_part(
+                saved_preact, edges - edges // 6, following, weight, bias, (grid_weight, mesh_weight), held[0]
+            )
 
     back = stages[::-1]
     d_preact, rim, *chunks = after(

time: 33.3 us -> 35.5 us (1.066)
  Pallas kernels: 14.6 us -> 16.2 us
  waiting for transfers between devices: 3.53 us -> 3.94 us
    pallas_call x1, Pallas kernels: 3.1 us -> 5.56 us  [second_part(): pl.pallas_call(functools.partial(second_kernel, block, copies), in_specs=...]
    ppermute x12, waiting for transfers between devices: 3.05 us -> 3.94 us  [swap(): return lax.ppermute(block, 'band', [(i, i ^ mask) for i in range(count)])]
    pallas_call x1, Pallas kernels: 3.2 us -> 2.37 us  [first_part(): pl.pallas_call(functools.partial(first_kernel, block, copies), in_specs=[...]
    ppermute x1, waiting for transfers between devices: 0.48 us -> 0.01 us  [on_device(): lax.ppermute(rim, 'band', [(i, (i + 1) % count) for i in range(count)])]
  transfers between devices with their start and end apart: 13 -> 13, of which waited for: 6 -> 4; matrix products, arithmetic and copies ran while one was open for 0% -> 0% of each run, Pallas kernels for 31% -> 34%
where the time goes in v11:
time: 35.5 us; the launch traced here: 35.3 us
  Pallas kernels  16.2 us (46%)
  starting transfers between devices  14.4 us (41%)
  waiting for transfers between devices  3.94 us (11%)
  between operations  0.76 us (2%)
    ppermute x12, starting transfers between devices, swap(): return lax.ppermute(block, 'band', [(i, i ^ mask) for i in range(count)])  13.9 us
    pallas_call x1, Pallas kernels, second_part(): pl.pallas_call(functools.partial(second_kernel, block, copies), in_specs=...  5.56 us
    ppermute x12, waiting for transfers between devices, swap(): return lax.ppermute(block, 'band', [(i, i ^ mask) for i in range(count)])  3.94 us
    pallas_call x1, Pallas kernels, after(): pl.pallas_call(functools.partial(after_kernel, len(parts), chunks, owned,...  3.35 us
    pallas_call x1, Pallas kernels, first_part(): pl.pallas_call(functools.partial(first_kernel, block, copies), in_specs=[...  2.37 us
    pallas_call x1, Pallas kernels, grid_rows(): pl.pallas_call(functools.partial(grid_kernel, block), in_specs=[VMEM] * 3...  2.12 us
    pallas_call x1, Pallas kernels, segments(): pl.pallas_call(functools.partial(segments_kernel, block), in_specs=[SMEM]...  1.77 us
    pallas_call x1, Pallas kernels, mesh_rows(): pl.pallas_call(functools.partial(mesh_kernel, len(pieces)), in_specs=[VME...  0.99 us
  transfers between devices with their start and end apart: 13, of which 4 were waited for; matrix products, arithmetic and copies ran while one was open for 0% of the time, Pallas kernels for 34%

profile of v11, /device:TPU:0, one launch (start us, length us, event | category | flops | bytes accessed | tf_op | source)
XLA Modules:
  0.0 35.3 jit_solution(7771267189319519949)
XLA Ops:
  0.6 3.1 %collective-permute-start = (bf16[16,512]{1,0:T(8,128)(2,1)}, bf16[16,512]{1,0:T(8,128)(2,1)S(1)}, u32[]{:S(2)}, u32[]{:S(2)}) collective-permute-start(bf16[16,512]{1,0:T(8,128)(2,1)} %refs_3_.1), channel_id=1, source_target_pairs={{0,4},{1,5},{2,6},{3,7},{4,0},{5,1},{6,2},{7,3},{8,12},{9,13},{10,... | collective-permute-start | bytes 49160 | tf_op jit(solution)/shard_map/ppermute | solution.py:46
  3.7 2.5 %collective-permute-start.2 = (bf16[16,512]{1,0:T(8,128)(2,1)}, bf16[16,512]{1,0:T(8,128)(2,1)S(1)}, u32[]{:S(2)}, u32[]{:S(2)}) collective-permute-start(bf16[16,512]{1,0:T(8,128)(2,1)} %refs_3_.1), channel_id=1, source_target_pairs={{0,12},{1,13},{2,14},{3,15},{4,8},{5,9},{6,10},{7,11},{8,4},{9,5},... | collective-permute-start | bytes 49160 | tf_op jit(solution)/shard_map/ppermute | solution.py:46
  6.2 0.1 collective-permute-start.1
  6.3 2.4 %first_part.1 = (bf16[512,512]{1,0:T(8,128)(2,1)S(1)}, f32[1,512]{1,0:T(1,128)S(1)}, f32[1,512]{1,0:T(1,128)S(1)}, bf16[16,512]{1,0:T(8,128)(2,1)S(1)}, f32[32,1...) custom-call(bf16[3072,512]{1,0:T(8,128)(2,1)} %pre_hbm.3, ...), custom_call_target="tpu_custom_call" | custom-call | flops 805306368 | bytes 2621440 | tf_op jit(solution)/shard_map/first_part/pallas_call | solution.py:160
  8.7 0.0 collective-permute-done.refs_1_
  8.7 1.0 %collective-permute-done.2.refs_3_ = bf16[16,512]{1,0:T(8,128)(2,1)S(1)} collective-permute-done((bf16[16,512]{1,0:T(8,128)(2,1)}, bf16[16,512]{1,0:T(8,128)(2,1)S(1)}, u32[]{:S(2)}, u32[]{:S(2)}) %collective-permute-start.2) | collective-permute-done | bytes 16416 | tf_op jit(solution)/shard_map/ppermute | solution.py:46
  9.7 1.4 %collective-permute-done.1.refs_2_ = bf16[16,512]{1,0:T(8,128)(2,1)S(1)} collective-permute-done((bf16[16,512]{1,0:T(8,128)(2,1)}, bf16[16,512]{1,0:T(8,128)(2,1)S(1)}, u32[]{:S(2)}, u32[]{:S(2)}) %collective-permute-start.1) | collective-permute-done | bytes 16416 | tf_op jit(solution)/shard_map/ppermute | solution.py:46
  11.1 1.6 %collective-permute-start.4 = (bf16[64,512]{1,0:T(8,128)(2,1)S(1)}, bf16[64,512]{1,0:T(8,128)(2,1)S(1)}, u32[]{:S(2)}, u32[]{:S(2)}) collective-permute-start(bf16[64,512]{1,0:T(8,128)(2,1)S(1)} %join.1.after_ref.refs_6_), channel_id=1, source_target_pairs={{0,2},{1,3},{2,0},{3,1},{4,6},{5,7},{6,4},{7,5},{8,10},{9,11},{10,... | collective-permute-start | bytes 196616 | tf_op jit(solution)/shard_map/ppermute | solution.py:46
  12.6 0.3 collective-permute-start.3
  12.9 5.6 %second_part.1 = (bf16[512,512]{1,0:T(8,128)(2,1)S(1)}, bf16[512,512]{1,0:T(8,128)(2,1)S(1)}, bf16[2560,512]{1,0:T(8,128)(2,1)S(1)}, bf16[2560,512]{1,0:T(8,128)(2,1)S(1)}, f32[2560,512]{1,0:T(8,128)S(1)}) custom-call(bf16[512,512]{1,0:T(8,128)(2,1)S(1)} %get-tuple-element.32.next_ref, bf16[512,512]{1,0:T(8,128)(2,1)S(1)} %get-tuple-element.27.weight_ref, ...), custom_call_target="tpu_custom_call" | custom-call | flops 4026531840 | bytes 13107200 | tf_op jit(solution)/shard_map/second_part/pallas_call | solution.py:210
  18.5 0.0 collective-permute-done.5.refs_9_
  18.5 3.4 %after.1 = (bf16[3072,512]{1,0:T(8,128)(2,1)S(1)}, bf16[128,512]{1,0:T(8,128)(2,1)S(1)}, f32[8,640]{1,0:T(8,128)S(1)}, f32[8,640]{1,0:T(8,128)S(1)}, f32[8,640]{1,0:T(8,128)S(1)}, /*index=5*/f32[8,640]{1,0:T(8,128)S(1)}) custom-call(s32[1]{0:T(128)} %bitcast.1.refs_4_.me_ref, f32[32,128]{1,0:T(8,128)S(1)} %get-tuple-element.26.ids_ref, ...), custom_call_target="tpu_custom_call" | custom-call | flops 4831838208 | bytes 12582912 | tf_op jit(solution)/shard_map/after/pallas_call | solution.py:318
  21.9 0.3 collective-permute-start.7
  22.2 1.3 %collective-permute-start.8 = (f32[8,640]{1,0:T(8,128)S(1)}, f32[8,640]{1,0:T(8,128)S(1)}, u32[]{:S(2)}, u32[]{:S(2)}) collective-permute-start(f32[8,640]{1,0:T(8,128)S(1)} %get-tuple-element.43), channel_id=1, source_target_pairs={{0,2},{1,3},{2,0},{3,1},{4,6},{5,7},{6,4},{7,5},{8,10},{9,11},{10,... | collective-permute-start | bytes 61448 | tf_op jit(solution)/shard_map/ppermute | solution.py:46
  23.5 0.3 collective-permute-start.9
  23.8 0.5 %collective-permute-start.6 = (bf16[128,512]{1,0:T(8,128)(2,1)S(1)}, bf16[128,512]{1,0:T(8,128)(2,1)S(1)}, u32[]{:S(2)}, u32[]{:S(2)}) collective-permute-start(bf16[128,512]{1,0:T(8,128)(2,1)S(1)} %get-tuple-element.39), channel_id=1, source_target_pairs={{0,1},{1,2},{2,3},{3,4},{4,5},{5,6},{6,7},{7,8},{8,9},{9,10},{10,1... | collective-permute-start | bytes 393224 | tf_op jit(solution)/shard_map/ppermute | solution.py:491
  24.3 1.8 %segments.1.total_ref.refs_4_ = f32[2448,512]{1,0:T(8,128)S(1)} custom-call(s32[3072]{0:T(1024)S(1)} %copy-done.1, s32[1,3072]{1,0:T(1,128)S(1)} %bitcast.8, bf16[3072,512]{1,0:T(8,128)(2,1)S(1)} %get-tuple-element.38.d_ref), custom_call_target="tpu_custom_call" | custom-call | flops 3221225472 | bytes 6291456 | tf_op jit(solution)/shard_map/segments/pallas_call | solution.py:344
  26.1 0.6 %collective-permute-done.9.refs_3_ = f32[8,640]{1,0:T(8,128)S(1)} collective-permute-done((f32[8,640]{1,0:T(8,128)S(1)}, f32[8,640]{1,0:T(8,128)S(1)}, u32[]{:S(2)}, u32[]{:S(2)}) %collective-permute-start.9) | collective-permute-done | bytes 20512 | tf_op jit(solution)/shard_map/ppermute | solution.py:46
  26.8 0.8 %collective-permute-start.10 = (f32[8,640]{1,0:T(8,128)S(1)}, f32[8,640]{1,0:T(8,128)S(1)}, u32[]{:S(2)}, u32[]{:S(2)}) collective-permute-start(f32[8,640]{1,0:T(8,128)S(1)} %get-tuple-element.46), channel_id=1, source_target_pairs={{0,4},{1,5},{2,6},{3,7},{4,0},{5,1},{6,2},{7,3},{8,12},{9,13},{10,... | collective-permute-start | bytes 61448 | tf_op jit(solution)/shard_map/ppermute | solution.py:46
  27.6 1.2 %collective-permute-start.11 = (f32[8,640]{1,0:T(8,128)S(1)}, f32[8,640]{1,0:T(8,128)S(1)}, u32[]{:S(2)}, u32[]{:S(2)}) collective-permute-start(f32[8,640]{1,0:T(8,128)S(1)} %get-tuple-element.47), channel_id=1, source_target_pairs={{0,8},{1,9},{2,10},{3,11},{4,12},{5,13},{6,14},{7,15},{8,0},{9,1},... | collective-permute-start | bytes 61448 | tf_op jit(solution)/shard_map/ppermute | solution.py:46
  28.7 2.5 %collective-permute-start.12 = (f32[8,640]{1,0:T(8,128)S(1)}, f32[8,640]{1,0:T(8,128)S(1)}, u32[]{:S(2)}, u32[]{:S(2)}) collective-permute-start(f32[8,640]{1,0:T(8,128)S(1)} %get-tuple-element.48), channel_id=1, source_target_pairs={{0,12},{1,13},{2,14},{3,15},{4,8},{5,9},{6,10},{7,11},{8,4},{9,5},... | collective-permute-start | bytes 61448 | tf_op jit(solution)/shard_map/ppermute | solution.py:46
  31.2 2.1 %grid_rows.1.refs_5_ = bf16[2048,512]{1,0:T(8,128)(2,1)} custom-call(f32[2448,512]{1,0:T(8,128)S(1)} %segments.1.total_ref.refs_4_, bf16[128,512]{1,0:T(8,128)(2,1)S(1)} %collective-permute-done.6.carried_ref, bf16[512,512]{1,0:T(8,128)(2,1)S(1)} %get-tuple-element.40.weight_ref), custom_call_target="tpu_custom_call" | custom-call | flops 1073741824 | bytes 6291456 | tf_op jit(solution)/shard_map/grid_rows/pallas_call | solution.py:373
  33.4 0.9 %collective-permute-done.12.refs_3_ = f32[8,640]{1,0:T(8,128)S(1)} collective-permute-done((f32[8,640]{1,0:T(8,128)S(1)}, f32[8,640]{1,0:T(8,128)S(1)}, u32[]{:S(2)}, u32[]{:S(2)}) %collective-permute-start.12) | collective-permute-done | bytes 20512 | tf_op jit(solution)/shard_map/ppermute | solution.py:46
  34.3 1.0 %mesh_rows.1 = bf16[16,512]{1,0:T(8,128)(2,1)} custom-call(f32[8,640]{1,0:T(8,128)S(1)} %get-tuple-element.45.refs_0_, f32[8,640]{1,0:T(8,128)S(1)} %collective-permute-done.10.refs_1_, f32[8,640]{1,0:T(8,128)S(1)} %collective-permute-done.11.refs_2_, f32[8,640]{1,0:T(8,128)S(1)} %collective-permute-done.12.refs_3_, ...), custom_call_target="tpu_custom_call" | custom-call | flops 8388608 | bytes 524288 | tf_op jit(solution)/shard_map/mesh_rows/pallas_call | solution.py:424
  (14 shorter events, 0.1 us)
Async XLA Ops:
  0.6 8.1 %collective-permute-start = (bf16[16,512]{1,0:T(8,128)(2,1)}, bf16[16,512]{1,0:T(8,128)(2,1)S(1)}, u32[]{:S(2)}, u32[]{:S(2)}) collective-permute-start(bf16[16,512]{1,0:T(8,128)(2,1)} %refs_3_.1), channel_id=1, source_target_pairs={{0,4},{1,5},{2,6},{3,7},{4,0},{5,1},{6,2},{7,3},{8,12},{9,13},{10,... | collective-permute-start | bytes 49160 | tf_op jit(solution)/shard_map/ppermute | solution.py:46
  3.7 6.0 %collective-permute-start.2 = (bf16[16,512]{1,0:T(8,128)(2,1)}, bf16[16,512]{1,0:T(8,128)(2,1)S(1)}, u32[]{:S(2)}, u32[]{:S(2)}) collective-permute-start(bf16[16,512]{1,0:T(8,128)(2,1)} %refs_3_.1), channel_id=1, source_target_pairs={{0,12},{1,13},{2,14},{3,15},{4,8},{5,9},{6,10},{7,11},{8,4},{9,5},... | collective-permute-start | bytes 49160 | tf_op jit(solution)/shard_map/ppermute | solution.py:46
  6.2 4.9 %collective-permute-start.1 = (bf16[16,512]{1,0:T(8,128)(2,1)}, bf16[16,512]{1,0:T(8,128)(2,1)S(1)}, u32[]{:S(2)}, u32[]{:S(2)}) collective-permute-start(bf16[16,512]{1,0:T(8,128)(2,1)} %refs_3_.1), channel_id=1, source_target_pairs={{0,8},{1,9},{2,10},{3,11},{4,12},{5,13},{6,14},{7,15},{8,0},{9,1},... | collective-permute-start | bytes 49160 | tf_op jit(solution)/shard_map/ppermute | solution.py:46
  11.1 7.4 %collective-permute-start.5 = (bf16[64,512]{1,0:T(8,128)(2,1)S(1)}, bf16[64,512]{1,0:T(8,128)(2,1)S(1)}, u32[]{:S(2)}, u32[]{:S(2)}) collective-permute-start(bf16[64,512]{1,0:T(8,128)(2,1)S(1)} %join.1.after_ref.refs_6_), channel_id=1, source_target_pairs={{0,3},{1,2},{2,1},{3,0},{4,7},{5,6},{6,5},{7,4},{8,11},{9,10},{10,... | collective-permute-start | bytes 196616 | tf_op jit(solution)/shard_map/ppermute | solution.py:46
  11.1 7.4 %collective-permute-start.4 = (bf16[64,512]{1,0:T(8,128)(2,1)S(1)}, bf16[64,512]{1,0:T(8,128)(2,1)S(1)}, u32[]{:S(2)}, u32[]{:S(2)}) collective-permute-start(bf16[64,512]{1,0:T(8,128)(2,1)S(1)} %join.1.after_ref.refs_6_), channel_id=1, source_target_pairs={{0,2},{1,3},{2,0},{3,1},{4,6},{5,7},{6,4},{7,5},{8,10},{9,11},{10,... | collective-permute-start | bytes 196616 | tf_op jit(solution)/shard_map/ppermute | solution.py:46
  12.6 5.9 %collective-permute-start.3 = (bf16[64,512]{1,0:T(8,128)(2,1)S(1)}, bf16[64,512]{1,0:T(8,128)(2,1)S(1)}, u32[]{:S(2)}, u32[]{:S(2)}) collective-permute-start(bf16[64,512]{1,0:T(8,128)(2,1)S(1)} %join.1.after_ref.refs_6_), channel_id=1, source_target_pairs={{0,1},{1,0},{2,3},{3,2},{4,5},{5,4},{6,7},{7,6},{8,9},{9,8},{10,11... | collective-permute-start | bytes 196616 | tf_op jit(solution)/shard_map/ppermute | solution.py:46
  12.9 5.6 %copy-start = (s32[3072]{0:T(1024)S(1)}, s32[3072]{0:T(1024)}, u32[]{:S(2)}) copy-start(s32[3072]{0:T(1024)} %param.12) | copy-start | bytes 36868
  12.9 5.6 %copy-start.1 = (s32[3072]{0:T(1024)S(1)}, s32[3072]{0:T(1024)}, u32[]{:S(2)}) copy-start(s32[3072]{0:T(1024)} %starts_ref.1) | copy-start | bytes 36868
  21.9 4.2 %collective-permute-start.7 = (f32[8,640]{1,0:T(8,128)S(1)}, f32[8,640]{1,0:T(8,128)S(1)}, u32[]{:S(2)}, u32[]{:S(2)}) collective-permute-start(f32[8,640]{1,0:T(8,128)S(1)} %get-tuple-element.42), channel_id=1, source_target_pairs={{0,1},{1,0},{2,3},{3,2},{4,5},{5,4},{6,7},{7,6},{8,9},{9,8},{10,11... | collective-permute-start | bytes 61448 | tf_op jit(solution)/shard_map/ppermute | solution.py:46
  22.2 3.9 %collective-permute-start.8 = (f32[8,640]{1,0:T(8,128)S(1)}, f32[8,640]{1,0:T(8,128)S(1)}, u32[]{:S(2)}, u32[]{:S(2)}) collective-permute-start(f32[8,640]{1,0:T(8,128)S(1)} %get-tuple-element.43), channel_id=1, source_target_pairs={{0,2},{1,3},{2,0},{3,1},{4,6},{5,7},{6,4},{7,5},{8,10},{9,11},{10,... | collective-permute-start | bytes 61448 | tf_op jit(solution)/shard_map/ppermute | solution.py:46
  23.5 3.2 %collective-permute-start.9 = (f32[8,640]{1,0:T(8,128)S(1)}, f32[8,640]{1,0:T(8,128)S(1)}, u32[]{:S(2)}, u32[]{:S(2)}) collective-permute-start(f32[8,640]{1,0:T(8,128)S(1)} %get-tuple-element.44), channel_id=1, source_target_pairs={{0,3},{1,2},{2,1},{3,0},{4,7},{5,6},{6,5},{7,4},{8,11},{9,10},{10,... | collective-permute-start | bytes 61448 | tf_op jit(solution)/shard_map/ppermute | solution.py:46
  23.8 7.4 %collective-permute-start.6 = (bf16[128,512]{1,0:T(8,128)(2,1)S(1)}, bf16[128,512]{1,0:T(8,128)(2,1)S(1)}, u32[]{:S(2)}, u32[]{:S(2)}) collective-permute-start(bf16[128,512]{1,0:T(8,128)(2,1)S(1)} %get-tuple-element.39), channel_id=1, source_target_pairs={{0,1},{1,2},{2,3},{3,4},{4,5},{5,6},{6,7},{7,8},{8,9},{9,10},{10,1... | collective-permute-start | bytes 393224 | tf_op jit(solution)/shard_map/ppermute | solution.py:491
  26.8 6.6 %collective-permute-start.10 = (f32[8,640]{1,0:T(8,128)S(1)}, f32[8,640]{1,0:T(8,128)S(1)}, u32[]{:S(2)}, u32[]{:S(2)}) collective-permute-start(f32[8,640]{1,0:T(8,128)S(1)} %get-tuple-element.46), channel_id=1, source_target_pairs={{0,4},{1,5},{2,6},{3,7},{4,0},{5,1},{6,2},{7,3},{8,12},{9,13},{10,... | collective-permute-start | bytes 61448 | tf_op jit(solution)/shard_map/ppermute | solution.py:46
  27.6 5.8 %collective-permute-start.11 = (f32[8,640]{1,0:T(8,128)S(1)}, f32[8,640]{1,0:T(8,128)S(1)}, u32[]{:S(2)}, u32[]{:S(2)}) collective-permute-start(f32[8,640]{1,0:T(8,128)S(1)} %get-tuple-element.47), channel_id=1, source_target_pairs={{0,8},{1,9},{2,10},{3,11},{4,12},{5,13},{6,14},{7,15},{8,0},{9,1},... | collective-permute-start | bytes 61448 | tf_op jit(solution)/shard_map/ppermute | solution.py:46
  28.7 5.6 %collective-permute-start.12 = (f32[8,640]{1,0:T(8,128)S(1)}, f32[8,640]{1,0:T(8,128)S(1)}, u32[]{:S(2)}, u32[]{:S(2)}) collective-permute-start(f32[8,640]{1,0:T(8,128)S(1)} %get-tuple-element.48), channel_id=1, source_target_pairs={{0,12},{1,13},{2,14},{3,15},{4,8},{5,9},{6,10},{7,11},{8,4},{9,5},... | collective-permute-start | bytes 61448 | tf_op jit(solution)/shard_map/ppermute | solution.py:46

commit v12 on v9

--- a/solution.py
+++ b/solution.py
@@ -214,6 +214,19 @@
         compiler_params=params(8),
         name="join",
     )(*pieces, after)
+
+
+def pack(ref, sums, ids):
+    half = sums.shape[1] // 2
+    left = jnp.concatenate([sums[:, :half], ids], axis=1)
+    right = jnp.concatenate([sums[:, half:], ids], axis=1)
+    ref[...] = jnp.concatenate([left, right], axis=0).astype(BF16)
+
+
+def unpack(ref):
+    rows, half = ref.shape[0] // 2, ref.shape[1] - LANES
+    both = ref[...].astype(F32)
+    return jnp.concatenate([both[:rows, :half], both[rows:, :half]], axis=1), both[:rows, half:]
 
 
 def after_kernel(
@@ -281,8 +294,7 @@
 
     each = slots // chunks
     for k, sums_ref in enumerate(sums_refs):
-        sums_ref[:, :width] = sums[k * each : (k + 1) * each]
-        sums_ref[:, width:] = ids_ref[k * each : (k + 1) * each, :]
+        pack(sums_ref, sums[k * each : (k + 1) * each], ids_ref[k * each : (k + 1) * each, :])
     rim_ref[...] = rim.astype(BF16)
 
 
@@ -294,7 +306,7 @@
         in_specs=[SMEM] + [VMEM] * (5 + 3 * len(parts) + len(pieces)),
         out_specs=[VMEM] * (2 + chunks),
         out_shape=[in_vmem((edges, width), BF16), in_vmem((RIM, width), BF16)]
-        + [in_vmem((each, width + LANES), F32)] * chunks,
+        + [in_vmem((2 * each, width // 2 + LANES), BF16)] * chunks,
         cost_estimate=cost(6 * edges * width * width, 8 * edges * width),
         compiler_params=params(20),
         name="after",
@@ -359,12 +371,11 @@
 def regroup_kernel(groups, parts, *refs):
     outs = refs[parts + 1 :]
     low = groups // len(outs)
-    each = refs[0].shape[0] // groups
+    loaded = [unpack(ref) for ref in refs[:parts]]
+    each = loaded[0][0].shape[0] // groups
     for j, out_ref in enumerate(outs):
-        for g in range(low):
-            for k in range(parts):
-                to, at = (g * parts + k) * each, (j * low + g) * each
-                out_ref[to : to + each, :] = refs[k][at : at + each, :]
+        spans = [(k, (j * low + g) * each) for g in range(low) for k in range(parts)]
+        pack(out_ref, *[jnp.concatenate([loaded[k][n][at : at + each] for k, at in spans], axis=0) for n in (0, 1)])
 
 
 def regroup(arrived, radix, low, after):
@@ -374,7 +385,7 @@
         functools.partial(regroup_kernel, radix * low, parts),
         in_specs=[VMEM] * parts + [ANY],
         out_specs=[VMEM] * radix,
-        out_shape=[in_vmem((rows * parts // radix, width), F32)] * radix,
+        out_shape=[in_vmem((rows * parts // radix, width), BF16)] * radix,
         cost_estimate=cost(0, 8 * rows * parts * width),
         compiler_params=params(8),
         name="regroup",
@@ -384,11 +395,11 @@
 def mesh_kernel(parts, *refs):
     pieces, weight_ref, out_ref = refs[:parts], refs[parts], refs[-1]
     owned, width = out_ref.shape
-    rows = jnp.concatenate([piece[:, :width] for piece in pieces], axis=0)
-    ids = jnp.concatenate([piece[:, width:] for piece in pieces], axis=0)
-    ids = jnp.concatenate([ids, ids], axis=0).T[:owned].astype(jnp.int32)
+    loaded = [unpack(piece) for piece in pieces]
+    rows = jnp.concatenate([sums for sums, _ in loaded], axis=0)
+    ids = jnp.concatenate([ids for _, ids in loaded], axis=0).T[:owned].astype(jnp.int32)
     pick = (lax.broadcasted_iota(jnp.int32, ids.shape, 0) == ids).astype(F32)
-    total = dot(pick.astype(BF16), jnp.concatenate(split(rows), axis=0))
+    total = dot(pick.astype(BF16), rows.astype(BF16))
     both = dot_t(jnp.concatenate(split(total), axis=0), weight_ref[...])
     out_ref[...] = (both[:owned] + both[owned:]).astype(BF16)
 

time: 33.3 us -> 33.1 us (level)
  transfers between devices with their start and end apart: 13 -> 13, of which waited for: 6 -> 5; matrix products, arithmetic and copies ran while one was open for 0% -> 0% of each run, Pallas kernels for 31% -> 31%
where the time goes in v12:
time: 33.1 us; the launch traced here: 33 us
  Pallas kernels  14.6 us (44%)
  starting transfers between devices  14.3 us (43%)
  waiting for transfers between devices  3.37 us (10%)
  between operations  0.75 us (2%)
    ppermute x12, starting transfers between devices, swap(): return lax.ppermute(block, 'band', [(i, i ^ mask) for i in range(count)])  13.9 us
    pallas_call x1, Pallas kernels, after(): pl.pallas_call(functools.partial(after_kernel, len(parts), chunks, owned,...  3.37 us
    pallas_call x1, Pallas kernels, first_part(): pl.pallas_call(functools.partial(first_kernel, block, copies), in_specs=[...  3.2 us
    pallas_call x1, Pallas kernels, second_part(): pl.pallas_call(functools.partial(second_kernel, block), in_specs=[VMEM, V...  3.1 us
    ppermute x12, waiting for transfers between devices, swap(): return lax.ppermute(block, 'band', [(i, i ^ mask) for i in range(count)])  2.82 us
    pallas_call x1, Pallas kernels, grid_rows(): pl.pallas_call(functools.partial(grid_kernel, block), in_specs=[VMEM] * 3...  2.12 us
    pallas_call x1, Pallas kernels, segments(): pl.pallas_call(functools.partial(segments_kernel, block), in_specs=[SMEM]...  1.77 us
    pallas_call x1, Pallas kernels, mesh_rows(): pl.pallas_call(functools.partial(mesh_kernel, len(pieces)), in_specs=[VME...  0.99 us
  transfers between devices with their start and end apart: 13, of which 5 were waited for; matrix products, arithmetic and copies ran while one was open for 0% of the time, Pallas kernels for 31%

profile of v12, /device:TPU:0, one launch (start us, length us, event | category | flops | bytes accessed | tf_op | source)
XLA Modules:
  0.0 33.0 jit_solution(17814091446994701187)
XLA Ops:
  0.6 3.1 %collective-permute-start = (bf16[16,512]{1,0:T(8,128)(2,1)}, bf16[16,512]{1,0:T(8,128)(2,1)S(1)}, u32[]{:S(2)}, u32[]{:S(2)}) collective-permute-start(bf16[16,512]{1,0:T(8,128)(2,1)} %refs_5_.1), channel_id=1, source_target_pairs={{0,4},{1,5},{2,6},{3,7},{4,0},{5,1},{6,2},{7,3},{8,12},{9,13},{10,... | collective-permute-start | bytes 49160 | tf_op jit(solution)/shard_map/ppermute | solution.py:46
  3.7 2.5 %collective-permute-start.2 = (bf16[16,512]{1,0:T(8,128)(2,1)}, bf16[16,512]{1,0:T(8,128)(2,1)S(1)}, u32[]{:S(2)}, u32[]{:S(2)}) collective-permute-start(bf16[16,512]{1,0:T(8,128)(2,1)} %refs_5_.1), channel_id=1, source_target_pairs={{0,12},{1,13},{2,14},{3,15},{4,8},{5,9},{6,10},{7,11},{8,4},{9,5},... | collective-permute-start | bytes 49160 | tf_op jit(solution)/shard_map/ppermute | solution.py:46
  6.2 0.1 collective-permute-start.1
  6.3 3.2 %first_part.1 = (bf16[512,512]{1,0:T(8,128)(2,1)S(1)}, f32[1,512]{1,0:T(1,128)S(1)}, bf16[512,512]{1,0:T(8,128)(2,1)S(1)}, bf16[512,512]{1,0:T(8,128)(2,1)S(1)},...) custom-call(bf16[3072,512]{1,0:T(8,128)(2,1)} %pre_hbm.1, ...), custom_call_target="tpu_custom_call" | custom-call | flops 1610612736 | bytes 5242880 | tf_op jit(solution)/shard_map/first_part/pallas_call | solution.py:162
  9.5 0.2 collective-permute-done.2.refs_3_
  9.7 1.4 %collective-permute-done.1.refs_2_ = bf16[16,512]{1,0:T(8,128)(2,1)S(1)} collective-permute-done((bf16[16,512]{1,0:T(8,128)(2,1)}, bf16[16,512]{1,0:T(8,128)(2,1)S(1)}, u32[]{:S(2)}, u32[]{:S(2)}) %collective-permute-start.1) | collective-permute-done | bytes 16416 | tf_op jit(solution)/shard_map/ppermute | solution.py:46
  11.1 1.6 %collective-permute-start.4 = (bf16[64,512]{1,0:T(8,128)(2,1)S(1)}, bf16[64,512]{1,0:T(8,128)(2,1)S(1)}, u32[]{:S(2)}, u32[]{:S(2)}) collective-permute-start(bf16[64,512]{1,0:T(8,128)(2,1)S(1)} %join.1.after_ref.refs_6_), channel_id=1, source_target_pairs={{0,2},{1,3},{2,0},{3,1},{4,6},{5,7},{6,4},{7,5},{8,10},{9,11},{10,... | collective-permute-start | bytes 196616 | tf_op jit(solution)/shard_map/ppermute | solution.py:46
  12.6 0.3 collective-permute-start.3
  12.9 3.1 %second_part.1 = (bf16[2048,512]{1,0:T(8,128)(2,1)S(1)}, bf16[2048,512]{1,0:T(8,128)(2,1)S(1)}, f32[2048,512]{1,0:T(8,128)S(1)}) custom-call(bf16[2048,512]{1,0:T(8,128)(2,1)S(1)} %get-tuple-element.32.pre_ref, bf16[512,512]{1,0:T(8,128)(2,1)S(1)} %get-tuple-element.27.weight_ref, f32[1,512]{1,0:T(1,128)S(1)} %get-tuple-element.33.bias_ref, ...), custom_call_target="tpu_custom_call" | custom-call | flops 3221225472 | bytes 10485760 | tf_op jit(solution)/shard_map/second_part/pallas_call | solution.py:188
  16.0 0.0 collective-permute-done.5.refs_9_
  16.0 0.8 %collective-permute-done.4.refs_8_ = bf16[64,512]{1,0:T(8,128)(2,1)S(1)} collective-permute-done((bf16[64,512]{1,0:T(8,128)(2,1)S(1)}, bf16[64,512]{1,0:T(8,128)(2,1)S(1)}, u32[]{:S(2)}, u32[]{:S(2)}) %collective-permute-start.4) | collective-permute-done | bytes 65568 | tf_op jit(solution)/shard_map/ppermute | solution.py:46
  16.9 3.4 %after.1 = (bf16[3072,512]{1,0:T(8,128)(2,1)S(1)}, bf16[128,512]{1,0:T(8,128)(2,1)S(1)}, bf16[16,384]{1,0:T(8,128)(2,1)S(1)}, bf16[16,384]{1,0:T(8,128)(2,1)S(1)...) custom-call(s32[1]{0:T(128)} %bitcast.1.refs_6_.me_ref, f32[32,128]{1,0:T(8,128)S(1)} %get-tuple-element.26.ids_ref, ...), custom_call_target="tpu_custom_call" | custom-call | flops 4831838208 | bytes 12582912 | tf_op jit(solution)/shard_map/after/pallas_call | solution.py:304
  20.2 0.1 collective-permute-start.7
  20.4 0.7 %collective-permute-start.8 = (bf16[16,384]{1,0:T(8,128)(2,1)S(1)}, bf16[16,384]{1,0:T(8,128)(2,1)S(1)}, u32[]{:S(2)}, u32[]{:S(2)}) collective-permute-start(bf16[16,384]{1,0:T(8,128)(2,1)S(1)} %get-tuple-element.43), channel_id=1, source_target_pairs={{0,2},{1,3},{2,0},{3,1},{4,6},{5,7},{6,4},{7,5},{8,10},{9,11},{10,... | collective-permute-start | bytes 36872 | tf_op jit(solution)/shard_map/ppermute | solution.py:46
  21.1 1.1 %collective-permute-start.9 = (bf16[16,384]{1,0:T(8,128)(2,1)S(1)}, bf16[16,384]{1,0:T(8,128)(2,1)S(1)}, u32[]{:S(2)}, u32[]{:S(2)}) collective-permute-start(bf16[16,384]{1,0:T(8,128)(2,1)S(1)} %get-tuple-element.44), channel_id=1, source_target_pairs={{0,3},{1,2},{2,1},{3,0},{4,7},{5,6},{6,5},{7,4},{8,11},{9,10},{10,... | collective-permute-start | bytes 36872 | tf_op jit(solution)/shard_map/ppermute | solution.py:46
  22.2 0.3 %collective-permute-start.6 = (bf16[128,512]{1,0:T(8,128)(2,1)S(1)}, bf16[128,512]{1,0:T(8,128)(2,1)S(1)}, u32[]{:S(2)}, u32[]{:S(2)}) collective-permute-start(bf16[128,512]{1,0:T(8,128)(2,1)S(1)} %get-tuple-element.39), channel_id=1, source_target_pairs={{0,1},{1,2},{2,3},{3,4},{4,5},{5,6},{6,7},{7,8},{8,9},{9,10},{10,1... | collective-permute-start | bytes 393224 | tf_op jit(solution)/shard_map/ppermute | solution.py:476
  22.5 1.8 %segments.1.total_ref.refs_4_ = f32[2448,512]{1,0:T(8,128)S(1)} custom-call(s32[3072]{0:T(1024)S(1)} %copy-done.1, s32[1,3072]{1,0:T(1,128)S(1)} %bitcast.8, bf16[3072,512]{1,0:T(8,128)(2,1)S(1)} %get-tuple-element.38.d_ref), custom_call_target="tpu_custom_call" | custom-call | flops 3221225472 | bytes 6291456 | tf_op jit(solution)/shard_map/segments/pallas_call | solution.py:330
  24.4 0.8 %collective-permute-start.10 = (bf16[16,384]{1,0:T(8,128)(2,1)S(1)}, bf16[16,384]{1,0:T(8,128)(2,1)S(1)}, u32[]{:S(2)}, u32[]{:S(2)}) collective-permute-start(bf16[16,384]{1,0:T(8,128)(2,1)S(1)} %get-tuple-element.46), channel_id=1, source_target_pairs={{0,4},{1,5},{2,6},{3,7},{4,0},{5,1},{6,2},{7,3},{8,12},{9,13},{10,... | collective-permute-start | bytes 36872 | tf_op jit(solution)/shard_map/ppermute | solution.py:46
  25.2 1.3 %collective-permute-start.11 = (bf16[16,384]{1,0:T(8,128)(2,1)S(1)}, bf16[16,384]{1,0:T(8,128)(2,1)S(1)}, u32[]{:S(2)}, u32[]{:S(2)}) collective-permute-start(bf16[16,384]{1,0:T(8,128)(2,1)S(1)} %get-tuple-element.47), channel_id=1, source_target_pairs={{0,8},{1,9},{2,10},{3,11},{4,12},{5,13},{6,14},{7,15},{8,0},{9,1},... | collective-permute-start | bytes 36872 | tf_op jit(solution)/shard_map/ppermute | solution.py:46
  26.5 2.3 %collective-permute-start.12 = (bf16[16,384]{1,0:T(8,128)(2,1)S(1)}, bf16[16,384]{1,0:T(8,128)(2,1)S(1)}, u32[]{:S(2)}, u32[]{:S(2)}) collective-permute-start(bf16[16,384]{1,0:T(8,128)(2,1)S(1)} %get-tuple-element.48), channel_id=1, source_target_pairs={{0,12},{1,13},{2,14},{3,15},{4,8},{5,9},{6,10},{7,11},{8,4},{9,5},... | collective-permute-start | bytes 36872 | tf_op jit(solution)/shard_map/ppermute | solution.py:46
  28.8 0.6 %collective-permute-done.6.carried_ref = bf16[128,512]{1,0:T(8,128)(2,1)S(1)} collective-permute-done((bf16[128,512]{1,0:T(8,128)(2,1)S(1)}, bf16[128,512]{1,0:T(8,128)(2,1)S(1)}, u32[]{:S(2)}, u32[]{:S(2)}) %collective-permute-start.6) | collective-permute-done | bytes 131104 | tf_op jit(solution)/shard_map/ppermute | solution.py:476
  29.4 2.1 %grid_rows.1.refs_5_ = bf16[2048,512]{1,0:T(8,128)(2,1)} custom-call(f32[2448,512]{1,0:T(8,128)S(1)} %segments.1.total_ref.refs_4_, bf16[128,512]{1,0:T(8,128)(2,1)S(1)} %collective-permute-done.6.carried_ref, bf16[512,512]{1,0:T(8,128)(2,1)S(1)} %get-tuple-element.40.weight_ref), custom_call_target="tpu_custom_call" | custom-call | flops 1073741824 | bytes 6291456 | tf_op jit(solution)/shard_map/grid_rows/pallas_call | solution.py:359
  31.5 0.5 %collective-permute-done.12.refs_3_ = bf16[16,384]{1,0:T(8,128)(2,1)S(1)} collective-permute-done((bf16[16,384]{1,0:T(8,128)(2,1)S(1)}, bf16[16,384]{1,0:T(8,128)(2,1)S(1)}, u32[]{:S(2)}, u32[]{:S(2)}) %collective-permute-start.12) | collective-permute-done | bytes 12320 | tf_op jit(solution)/shard_map/ppermute | solution.py:46
  32.0 1.0 %mesh_rows.1 = bf16[16,512]{1,0:T(8,128)(2,1)} custom-call(bf16[16,384]{1,0:T(8,128)(2,1)S(1)} %get-tuple-element.45.refs_0_, bf16[16,384]{1,0:T(8,128)(2,1)S(1)} %collective-permute-done.10.refs_1_, bf16[16,384]{1,0:T(8,128)(2,1)S(1)} %collective-permute-done.11.refs_2_, bf16[16,384]{1,0:T(8,128)(2,1)S(1)} %collective-permute-done.12.refs_3_, ...), custom_call_target="tpu_custom_call" | custom-call | flops 8388608 | bytes 524288 | tf_op jit(solution)/shard_map/mesh_rows/pallas_call | solution.py:409
  (14 shorter events, 0.1 us)
Async XLA Ops:
  0.6 8.9 %collective-permute-start = (bf16[16,512]{1,0:T(8,128)(2,1)}, bf16[16,512]{1,0:T(8,128)(2,1)S(1)}, u32[]{:S(2)}, u32[]{:S(2)}) collective-permute-start(bf16[16,512]{1,0:T(8,128)(2,1)} %refs_5_.1), channel_id=1, source_target_pairs={{0,4},{1,5},{2,6},{3,7},{4,0},{5,1},{6,2},{7,3},{8,12},{9,13},{10,... | collective-permute-start | bytes 49160 | tf_op jit(solution)/shard_map/ppermute | solution.py:46
  3.7 6.0 %collective-permute-start.2 = (bf16[16,512]{1,0:T(8,128)(2,1)}, bf16[16,512]{1,0:T(8,128)(2,1)S(1)}, u32[]{:S(2)}, u32[]{:S(2)}) collective-permute-start(bf16[16,512]{1,0:T(8,128)(2,1)} %refs_5_.1), channel_id=1, source_target_pairs={{0,12},{1,13},{2,14},{3,15},{4,8},{5,9},{6,10},{7,11},{8,4},{9,5},... | collective-permute-start | bytes 49160 | tf_op jit(solution)/shard_map/ppermute | solution.py:46
  6.2 4.9 %collective-permute-start.1 = (bf16[16,512]{1,0:T(8,128)(2,1)}, bf16[16,512]{1,0:T(8,128)(2,1)S(1)}, u32[]{:S(2)}, u32[]{:S(2)}) collective-permute-start(bf16[16,512]{1,0:T(8,128)(2,1)} %refs_5_.1), channel_id=1, source_target_pairs={{0,8},{1,9},{2,10},{3,11},{4,12},{5,13},{6,14},{7,15},{8,0},{9,1},... | collective-permute-start | bytes 49160 | tf_op jit(solution)/shard_map/ppermute | solution.py:46
  11.1 5.0 %collective-permute-start.5 = (bf16[64,512]{1,0:T(8,128)(2,1)S(1)}, bf16[64,512]{1,0:T(8,128)(2,1)S(1)}, u32[]{:S(2)}, u32[]{:S(2)}) collective-permute-start(bf16[64,512]{1,0:T(8,128)(2,1)S(1)} %join.1.after_ref.refs_6_), channel_id=1, source_target_pairs={{0,3},{1,2},{2,1},{3,0},{4,7},{5,6},{6,5},{7,4},{8,11},{9,10},{10,... | collective-permute-start | bytes 196616 | tf_op jit(solution)/shard_map/ppermute | solution.py:46
  11.1 5.8 %collective-permute-start.4 = (bf16[64,512]{1,0:T(8,128)(2,1)S(1)}, bf16[64,512]{1,0:T(8,128)(2,1)S(1)}, u32[]{:S(2)}, u32[]{:S(2)}) collective-permute-start(bf16[64,512]{1,0:T(8,128)(2,1)S(1)} %join.1.after_ref.refs_6_), channel_id=1, source_target_pairs={{0,2},{1,3},{2,0},{3,1},{4,6},{5,7},{6,4},{7,5},{8,10},{9,11},{10,... | collective-permute-start | bytes 196616 | tf_op jit(solution)/shard_map/ppermute | solution.py:46
  12.6 4.2 %collective-permute-start.3 = (bf16[64,512]{1,0:T(8,128)(2,1)S(1)}, bf16[64,512]{1,0:T(8,128)(2,1)S(1)}, u32[]{:S(2)}, u32[]{:S(2)}) collective-permute-start(bf16[64,512]{1,0:T(8,128)(2,1)S(1)} %join.1.after_ref.refs_6_), channel_id=1, source_target_pairs={{0,1},{1,0},{2,3},{3,2},{4,5},{5,4},{6,7},{7,6},{8,9},{9,8},{10,11... | collective-permute-start | bytes 196616 | tf_op jit(solution)/shard_map/ppermute | solution.py:46
  12.9 3.9 %copy-start = (s32[3072]{0:T(1024)S(1)}, s32[3072]{0:T(1024)}, u32[]{:S(2)}) copy-start(s32[3072]{0:T(1024)} %param.12) | copy-start | bytes 36868
  12.9 3.9 %copy-start.1 = (s32[3072]{0:T(1024)S(1)}, s32[3072]{0:T(1024)}, u32[]{:S(2)}) copy-start(s32[3072]{0:T(1024)} %starts_ref.1) | copy-start | bytes 36868
  20.2 4.1 %collective-permute-start.7 = (bf16[16,384]{1,0:T(8,128)(2,1)S(1)}, bf16[16,384]{1,0:T(8,128)(2,1)S(1)}, u32[]{:S(2)}, u32[]{:S(2)}) collective-permute-start(bf16[16,384]{1,0:T(8,128)(2,1)S(1)} %get-tuple-element.42), channel_id=1, source_target_pairs={{0,1},{1,0},{2,3},{3,2},{4,5},{5,4},{6,7},{7,6},{8,9},{9,8},{10,11... | collective-permute-start | bytes 36872 | tf_op jit(solution)/shard_map/ppermute | solution.py:46
  20.4 3.9 %collective-permute-start.8 = (bf16[16,384]{1,0:T(8,128)(2,1)S(1)}, bf16[16,384]{1,0:T(8,128)(2,1)S(1)}, u32[]{:S(2)}, u32[]{:S(2)}) collective-permute-start(bf16[16,384]{1,0:T(8,128)(2,1)S(1)} %get-tuple-element.43), channel_id=1, source_target_pairs={{0,2},{1,3},{2,0},{3,1},{4,6},{5,7},{6,4},{7,5},{8,10},{9,11},{10,... | collective-permute-start | bytes 36872 | tf_op jit(solution)/shard_map/ppermute | solution.py:46
  21.1 3.2 %collective-permute-start.9 = (bf16[16,384]{1,0:T(8,128)(2,1)S(1)}, bf16[16,384]{1,0:T(8,128)(2,1)S(1)}, u32[]{:S(2)}, u32[]{:S(2)}) collective-permute-start(bf16[16,384]{1,0:T(8,128)(2,1)S(1)} %get-tuple-element.44), channel_id=1, source_target_pairs={{0,3},{1,2},{2,1},{3,0},{4,7},{5,6},{6,5},{7,4},{8,11},{9,10},{10,... | collective-permute-start | bytes 36872 | tf_op jit(solution)/shard_map/ppermute | solution.py:46
  22.2 7.2 %collective-permute-start.6 = (bf16[128,512]{1,0:T(8,128)(2,1)S(1)}, bf16[128,512]{1,0:T(8,128)(2,1)S(1)}, u32[]{:S(2)}, u32[]{:S(2)}) collective-permute-start(bf16[128,512]{1,0:T(8,128)(2,1)S(1)} %get-tuple-element.39), channel_id=1, source_target_pairs={{0,1},{1,2},{2,3},{3,4},{4,5},{5,6},{6,7},{7,8},{8,9},{9,10},{10,1... | collective-permute-start | bytes 393224 | tf_op jit(solution)/shard_map/ppermute | solution.py:476
  24.4 7.1 %collective-permute-start.10 = (bf16[16,384]{1,0:T(8,128)(2,1)S(1)}, bf16[16,384]{1,0:T(8,128)(2,1)S(1)}, u32[]{:S(2)}, u32[]{:S(2)}) collective-permute-start(bf16[16,384]{1,0:T(8,128)(2,1)S(1)} %get-tuple-element.46), channel_id=1, source_target_pairs={{0,4},{1,5},{2,6},{3,7},{4,0},{5,1},{6,2},{7,3},{8,12},{9,13},{10,... | collective-permute-start | bytes 36872 | tf_op jit(solution)/shard_map/ppermute | solution.py:46
  25.2 6.4 %collective-permute-start.11 = (bf16[16,384]{1,0:T(8,128)(2,1)S(1)}, bf16[16,384]{1,0:T(8,128)(2,1)S(1)}, u32[]{:S(2)}, u32[]{:S(2)}) collective-permute-start(bf16[16,384]{1,0:T(8,128)(2,1)S(1)} %get-tuple-element.47), channel_id=1, source_target_pairs={{0,8},{1,9},{2,10},{3,11},{4,12},{5,13},{6,14},{7,15},{8,0},{9,1},... | collective-permute-start | bytes 36872 | tf_op jit(solution)/shard_map/ppermute | solution.py:46
  26.5 5.5 %collective-permute-start.12 = (bf16[16,384]{1,0:T(8,128)(2,1)S(1)}, bf16[16,384]{1,0:T(8,128)(2,1)S(1)}, u32[]{:S(2)}, u32[]{:S(2)}) collective-permute-start(bf16[16,384]{1,0:T(8,128)(2,1)S(1)} %get-tuple-element.48), channel_id=1, source_target_pairs={{0,12},{1,13},{2,14},{3,15},{4,8},{5,9},{6,10},{7,11},{8,4},{9,5},... | collective-permute-start | bytes 36872 | tf_op jit(solution)/shard_map/ppermute | solution.py:46

commit v13 on v12

--- a/solution.py
+++ b/solution.py
@@ -36,7 +36,7 @@
 
 def distance_of(row, caps, count):
     group, distance, left = row // caps, 0, count
-    for shift, radix in reversed(stages_of(count)):
+    for shift, radix in stages_of(count):
         left //= radix
         distance = distance + ((group // left) % radix << shift)
     return distance
@@ -125,10 +125,18 @@
     ]
     more = load(copies + len(loads), pre_hbm.at[pl.ds(rows, more_rows)], other_ref)
     asked = load(copies + len(loads) + 1, requests_hbm, requests_ref)
-    for copy in others[:2] + loads + others[2:] + [more, asked]:
+    for copy in [asked] + others[:2] + loads + others[2:] + [more]:
         copy.start()
-    for copy in others[:2]:
+    for copy in others[:2] + [asked]:
         copy.wait()
+    slots, caps = ids_ref.shape[0], requests_ref.shape[1]
+    count = slots // caps
+    row = lax.broadcasted_iota(jnp.int32, ids_ref.shape, 0)
+    ids = jnp.zeros(ids_ref.shape, jnp.int32)
+    for r in range(slots):
+        owner = me_ref[0] ^ distance_of(r, caps, count)
+        ids = jnp.where(row == r, requests_ref[0, r % caps, owner], ids)
+    ids_ref[...] = ids.astype(F32)
     edge_blocks(
         pre_ref,
         targets[0],
@@ -140,16 +148,8 @@
         block,
         lambda at: loads[at // block].wait(),
     )
-    for copy in others[2:] + [more, asked]:
+    for copy in others[2:] + [more]:
         copy.wait()
-    slots, caps = ids_ref.shape[0], requests_ref.shape[1]
-    count = slots // caps
-    row = lax.broadcasted_iota(jnp.int32, ids_ref.shape, 0)
-    ids = jnp.zeros(ids_ref.shape, jnp.int32)
-    for r in range(slots):
-        owner = me_ref[0] ^ distance_of(r, caps, count)
-        ids = jnp.where(row == r, requests_ref[0, r % caps, owner], ids)
-    ids_ref[...] = ids.astype(F32)
 
 
 def first_part(preact, rows, sources, me, requests, block=512):
@@ -457,7 +457,7 @@
         if number == 1:
             second = second_part(more, weight, bias, held[0])
 
-    back = stages[::-1]
+    back = stages
     d_preact, rim, *chunks = after(
         me.reshape(1),
         ids,

time: 33.1 us -> 35.2 us (1.063)
  waiting for transfers between devices: 3.37 us -> 5.82 us
  starting transfers between devices: 14.3 us -> 13.9 us
    ppermute x1, waiting for transfers between devices: 0.55 us -> 2.09 us  [on_device(): lax.ppermute(rim, 'band', [(i, (i + 1) % count) for i in range(count)])]
    ppermute x12, waiting for transfers between devices: 2.82 us -> 3.73 us  [swap(): return lax.ppermute(block, 'band', [(i, i ^ mask) for i in range(count)])]
  transfers between devices with their start and end apart: 13 -> 13, of which waited for: 5 -> 5; matrix products, arithmetic and copies ran while one was open for 0% -> 0% of each run, Pallas kernels for 31% -> 29%
where the time goes in v13:
time: 35.2 us; the launch traced here: 35 us
  Pallas kernels  14.5 us (41%)
  starting transfers between devices  13.9 us (39%)
  waiting for transfers between devices  5.82 us (17%)
  between operations  0.75 us (2%)
    ppermute x12, starting transfers between devices, swap(): return lax.ppermute(block, 'band', [(i, i ^ mask) for i in range(count)])  13.9 us
    ppermute x12, waiting for transfers between devices, swap(): return lax.ppermute(block, 'band', [(i, i ^ mask) for i in range(count)])  3.73 us
    pallas_call x1, Pallas kernels, after(): pl.pallas_call(functools.partial(after_kernel, len(parts), chunks, owned,...  3.37 us
    pallas_call x1, Pallas kernels, first_part(): pl.pallas_call(functools.partial(first_kernel, block, copies), in_specs=[...  3.15 us
    pallas_call x1, Pallas kernels, second_part(): pl.pallas_call(functools.partial(second_kernel, block), in_specs=[VMEM, V...  3.1 us
    pallas_call x1, Pallas kernels, grid_rows(): pl.pallas_call(functools.partial(grid_kernel, block), in_specs=[VMEM] * 3...  2.12 us
    ppermute x1, waiting for transfers between devices, on_device(): lax.ppermute(rim, 'band', [(i, (i + 1) % count) for i in range(count)])  2.09 us
    pallas_call x1, Pallas kernels, segments(): pl.pallas_call(functools.partial(segments_kernel, block), in_specs=[SMEM]...  1.77 us
  transfers between devices with their start and end apart: 13, of which 5 were waited for; matrix products, arithmetic and copies ran while one was open for 0% of the time, Pallas kernels for 29%

profile of v13, /device:TPU:0, one launch (start us, length us, event | category | flops | bytes accessed | tf_op | source)
XLA Modules:
  0.0 35.0 jit_solution(6794768510934880937)
XLA Ops:
  0.6 3.1 %collective-permute-start = (bf16[16,512]{1,0:T(8,128)(2,1)}, bf16[16,512]{1,0:T(8,128)(2,1)S(1)}, u32[]{:S(2)}, u32[]{:S(2)}) collective-permute-start(bf16[16,512]{1,0:T(8,128)(2,1)} %refs_5_.1), channel_id=1, source_target_pairs={{0,4},{1,5},{2,6},{3,7},{4,0},{5,1},{6,2},{7,3},{8,12},{9,13},{10,... | collective-permute-start | bytes 49160 | tf_op jit(solution)/shard_map/ppermute | solution.py:46
  3.7 2.5 %collective-permute-start.2 = (bf16[16,512]{1,0:T(8,128)(2,1)}, bf16[16,512]{1,0:T(8,128)(2,1)S(1)}, u32[]{:S(2)}, u32[]{:S(2)}) collective-permute-start(bf16[16,512]{1,0:T(8,128)(2,1)} %refs_5_.1), channel_id=1, source_target_pairs={{0,12},{1,13},{2,14},{3,15},{4,8},{5,9},{6,10},{7,11},{8,4},{9,5},... | collective-permute-start | bytes 49160 | tf_op jit(solution)/shard_map/ppermute | solution.py:46
  6.2 0.1 collective-permute-start.1
  6.3 3.1 %first_part.1 = (bf16[512,512]{1,0:T(8,128)(2,1)S(1)}, f32[1,512]{1,0:T(1,128)S(1)}, bf16[512,512]{1,0:T(8,128)(2,1)S(1)}, bf16[512,512]{1,0:T(8,128)(2,1)S(1)},...) custom-call(bf16[3072,512]{1,0:T(8,128)(2,1)} %pre_hbm.1, ...), custom_call_target="tpu_custom_call" | custom-call | flops 1610612736 | bytes 5242880 | tf_op jit(solution)/shard_map/first_part/pallas_call | solution.py:162
  9.5 0.0 collective-permute-done.refs_1_
  9.5 0.2 collective-permute-done.2.refs_3_
  9.7 1.4 %collective-permute-done.1.refs_2_ = bf16[16,512]{1,0:T(8,128)(2,1)S(1)} collective-permute-done((bf16[16,512]{1,0:T(8,128)(2,1)}, bf16[16,512]{1,0:T(8,128)(2,1)S(1)}, u32[]{:S(2)}, u32[]{:S(2)}) %collective-permute-start.1) | collective-permute-done | bytes 16416 | tf_op jit(solution)/shard_map/ppermute | solution.py:46
  11.1 0.0 collective-permute-start.5
  11.1 1.6 %collective-permute-start.4 = (bf16[64,512]{1,0:T(8,128)(2,1)S(1)}, bf16[64,512]{1,0:T(8,128)(2,1)S(1)}, u32[]{:S(2)}, u32[]{:S(2)}) collective-permute-start(bf16[64,512]{1,0:T(8,128)(2,1)S(1)} %join.1.after_ref.refs_6_), channel_id=1, source_target_pairs={{0,2},{1,3},{2,0},{3,1},{4,6},{5,7},{6,4},{7,5},{8,10},{9,11},{10,... | collective-permute-start | bytes 196616 | tf_op jit(solution)/shard_map/ppermute | solution.py:46
  12.6 0.3 collective-permute-start.3
  12.9 3.1 %second_part.1 = (bf16[2048,512]{1,0:T(8,128)(2,1)S(1)}, bf16[2048,512]{1,0:T(8,128)(2,1)S(1)}, f32[2048,512]{1,0:T(8,128)S(1)}) custom-call(bf16[2048,512]{1,0:T(8,128)(2,1)S(1)} %get-tuple-element.32.pre_ref, bf16[512,512]{1,0:T(8,128)(2,1)S(1)} %get-tuple-element.27.weight_ref, f32[1,512]{1,0:T(1,128)S(1)} %get-tuple-element.33.bias_ref, ...), custom_call_target="tpu_custom_call" | custom-call | flops 3221225472 | bytes 10485760 | tf_op jit(solution)/shard_map/second_part/pallas_call | solution.py:188
  16.0 0.8 %collective-permute-done.4.refs_8_ = bf16[64,512]{1,0:T(8,128)(2,1)S(1)} collective-permute-done((bf16[64,512]{1,0:T(8,128)(2,1)S(1)}, bf16[64,512]{1,0:T(8,128)(2,1)S(1)}, u32[]{:S(2)}, u32[]{:S(2)}) %collective-permute-start.4) | collective-permute-done | bytes 65568 | tf_op jit(solution)/shard_map/ppermute | solution.py:46
  16.9 3.4 %after.1 = (bf16[3072,512]{1,0:T(8,128)(2,1)S(1)}, bf16[128,512]{1,0:T(8,128)(2,1)S(1)}, bf16[16,384]{1,0:T(8,128)(2,1)S(1)}, bf16[16,384]{1,0:T(8,128)(2,1)S(1)...) custom-call(s32[1]{0:T(128)} %bitcast.1.refs_6_.me_ref, f32[32,128]{1,0:T(8,128)S(1)} %get-tuple-element.26.ids_ref, ...), custom_call_target="tpu_custom_call" | custom-call | flops 4831838208 | bytes 12582912 | tf_op jit(solution)/shard_map/after/pallas_call | solution.py:304
  20.3 0.8 %collective-permute-start.7 = (bf16[16,384]{1,0:T(8,128)(2,1)S(1)}, bf16[16,384]{1,0:T(8,128)(2,1)S(1)}, u32[]{:S(2)}, u32[]{:S(2)}) collective-permute-start(bf16[16,384]{1,0:T(8,128)(2,1)S(1)} %get-tuple-element.42), channel_id=1, source_target_pairs={{0,4},{1,5},{2,6},{3,7},{4,0},{5,1},{6,2},{7,3},{8,12},{9,13},{10,... | collective-permute-start | bytes 36872 | tf_op jit(solution)/shard_map/ppermute | solution.py:46
  21.0 1.3 %collective-permute-start.8 = (bf16[16,384]{1,0:T(8,128)(2,1)S(1)}, bf16[16,384]{1,0:T(8,128)(2,1)S(1)}, u32[]{:S(2)}, u32[]{:S(2)}) collective-permute-start(bf16[16,384]{1,0:T(8,128)(2,1)S(1)} %get-tuple-element.43), channel_id=1, source_target_pairs={{0,8},{1,9},{2,10},{3,11},{4,12},{5,13},{6,14},{7,15},{8,0},{9,1},... | collective-permute-start | bytes 36872 | tf_op jit(solution)/shard_map/ppermute | solution.py:46
  22.3 2.4 %collective-permute-start.9 = (bf16[16,384]{1,0:T(8,128)(2,1)S(1)}, bf16[16,384]{1,0:T(8,128)(2,1)S(1)}, u32[]{:S(2)}, u32[]{:S(2)}) collective-permute-start(bf16[16,384]{1,0:T(8,128)(2,1)S(1)} %get-tuple-element.44), channel_id=1, source_target_pairs={{0,12},{1,13},{2,14},{3,15},{4,8},{5,9},{6,10},{7,11},{8,4},{9,5},... | collective-permute-start | bytes 36872 | tf_op jit(solution)/shard_map/ppermute | solution.py:46
  24.7 1.8 %segments.1.total_ref.refs_4_ = f32[2448,512]{1,0:T(8,128)S(1)} custom-call(s32[3072]{0:T(1024)S(1)} %copy-done.1, s32[1,3072]{1,0:T(1,128)S(1)} %bitcast.8, bf16[3072,512]{1,0:T(8,128)(2,1)S(1)} %get-tuple-element.38.d_ref), custom_call_target="tpu_custom_call" | custom-call | flops 3221225472 | bytes 6291456 | tf_op jit(solution)/shard_map/segments/pallas_call | solution.py:330
  26.5 1.3 %collective-permute-done.9.refs_3_ = bf16[16,384]{1,0:T(8,128)(2,1)S(1)} collective-permute-done((bf16[16,384]{1,0:T(8,128)(2,1)S(1)}, bf16[16,384]{1,0:T(8,128)(2,1)S(1)}, u32[]{:S(2)}, u32[]{:S(2)}) %collective-permute-start.9) | collective-permute-done | bytes 12320 | tf_op jit(solution)/shard_map/ppermute | solution.py:46
  27.8 0.1 collective-permute-start.10
  27.9 0.8 %collective-permute-start.11 = (bf16[16,384]{1,0:T(8,128)(2,1)S(1)}, bf16[16,384]{1,0:T(8,128)(2,1)S(1)}, u32[]{:S(2)}, u32[]{:S(2)}) collective-permute-start(bf16[16,384]{1,0:T(8,128)(2,1)S(1)} %get-tuple-element.47), channel_id=1, source_target_pairs={{0,2},{1,3},{2,0},{3,1},{4,6},{5,7},{6,4},{7,5},{8,10},{9,11},{10,... | collective-permute-start | bytes 36872 | tf_op jit(solution)/shard_map/ppermute | solution.py:46
  28.7 1.1 %collective-permute-start.12 = (bf16[16,384]{1,0:T(8,128)(2,1)S(1)}, bf16[16,384]{1,0:T(8,128)(2,1)S(1)}, u32[]{:S(2)}, u32[]{:S(2)}) collective-permute-start(bf16[16,384]{1,0:T(8,128)(2,1)S(1)} %get-tuple-element.48), channel_id=1, source_target_pairs={{0,3},{1,2},{2,1},{3,0},{4,7},{5,6},{6,5},{7,4},{8,11},{9,10},{10,... | collective-permute-start | bytes 36872 | tf_op jit(solution)/shard_map/ppermute | solution.py:46
  29.8 2.1 %collective-permute-done.6.carried_ref = bf16[128,512]{1,0:T(8,128)(2,1)S(1)} collective-permute-done((bf16[128,512]{1,0:T(8,128)(2,1)S(1)}, bf16[128,512]{1,0:T(8,128)(2,1)S(1)}, u32[]{:S(2)}, u32[]{:S(2)}) %collective-permute-start.6) | collective-permute-done | bytes 131104 | tf_op jit(solution)/shard_map/ppermute | solution.py:476
  31.9 2.1 %grid_rows.1.refs_5_ = bf16[2048,512]{1,0:T(8,128)(2,1)} custom-call(f32[2448,512]{1,0:T(8,128)S(1)} %segments.1.total_ref.refs_4_, bf16[128,512]{1,0:T(8,128)(2,1)S(1)} %collective-permute-done.6.carried_ref, bf16[512,512]{1,0:T(8,128)(2,1)S(1)} %get-tuple-element.40.weight_ref), custom_call_target="tpu_custom_call" | custom-call | flops 1073741824 | bytes 6291456 | tf_op jit(solution)/shard_map/grid_rows/pallas_call | solution.py:359
  34.0 1.0 %mesh_rows.1 = bf16[16,512]{1,0:T(8,128)(2,1)} custom-call(bf16[16,384]{1,0:T(8,128)(2,1)S(1)} %get-tuple-element.45.refs_0_, bf16[16,384]{1,0:T(8,128)(2,1)S(1)} %collective-permute-done.10.refs_1_, bf16[16,384]{1,0:T(8,128)(2,1)S(1)} %collective-permute-done.11.refs_2_, bf16[16,384]{1,0:T(8,128)(2,1)S(1)} %collective-permute-done.12.refs_3_, ...), custom_call_target="tpu_custom_call" | custom-call | flops 8388608 | bytes 524288 | tf_op jit(solution)/shard_map/mesh_rows/pallas_call | solution.py:409
  (14 shorter events, 0.1 us)
Async XLA Ops:
  0.6 8.8 %collective-permute-start = (bf16[16,512]{1,0:T(8,128)(2,1)}, bf16[16,512]{1,0:T(8,128)(2,1)S(1)}, u32[]{:S(2)}, u32[]{:S(2)}) collective-permute-start(bf16[16,512]{1,0:T(8,128)(2,1)} %refs_5_.1), channel_id=1, source_target_pairs={{0,4},{1,5},{2,6},{3,7},{4,0},{5,1},{6,2},{7,3},{8,12},{9,13},{10,... | collective-permute-start | bytes 49160 | tf_op jit(solution)/shard_map/ppermute | solution.py:46
  3.7 6.0 %collective-permute-start.2 = (bf16[16,512]{1,0:T(8,128)(2,1)}, bf16[16,512]{1,0:T(8,128)(2,1)S(1)}, u32[]{:S(2)}, u32[]{:S(2)}) collective-permute-start(bf16[16,512]{1,0:T(8,128)(2,1)} %refs_5_.1), channel_id=1, source_target_pairs={{0,12},{1,13},{2,14},{3,15},{4,8},{5,9},{6,10},{7,11},{8,4},{9,5},... | collective-permute-start | bytes 49160 | tf_op jit(solution)/shard_map/ppermute | solution.py:46
  6.2 4.9 %collective-permute-start.1 = (bf16[16,512]{1,0:T(8,128)(2,1)}, bf16[16,512]{1,0:T(8,128)(2,1)S(1)}, u32[]{:S(2)}, u32[]{:S(2)}) collective-permute-start(bf16[16,512]{1,0:T(8,128)(2,1)} %refs_5_.1), channel_id=1, source_target_pairs={{0,8},{1,9},{2,10},{3,11},{4,12},{5,13},{6,14},{7,15},{8,0},{9,1},... | collective-permute-start | bytes 49160 | tf_op jit(solution)/shard_map/ppermute | solution.py:46
  11.1 5.0 %collective-permute-start.5 = (bf16[64,512]{1,0:T(8,128)(2,1)S(1)}, bf16[64,512]{1,0:T(8,128)(2,1)S(1)}, u32[]{:S(2)}, u32[]{:S(2)}) collective-permute-start(bf16[64,512]{1,0:T(8,128)(2,1)S(1)} %join.1.after_ref.refs_6_), channel_id=1, source_target_pairs={{0,3},{1,2},{2,1},{3,0},{4,7},{5,6},{6,5},{7,4},{8,11},{9,10},{10,... | collective-permute-start | bytes 196616 | tf_op jit(solution)/shard_map/ppermute | solution.py:46
  11.1 5.8 %collective-permute-start.4 = (bf16[64,512]{1,0:T(8,128)(2,1)S(1)}, bf16[64,512]{1,0:T(8,128)(2,1)S(1)}, u32[]{:S(2)}, u32[]{:S(2)}) collective-permute-start(bf16[64,512]{1,0:T(8,128)(2,1)S(1)} %join.1.after_ref.refs_6_), channel_id=1, source_target_pairs={{0,2},{1,3},{2,0},{3,1},{4,6},{5,7},{6,4},{7,5},{8,10},{9,11},{10,... | collective-permute-start | bytes 196616 | tf_op jit(solution)/shard_map/ppermute | solution.py:46
  12.6 4.2 %collective-permute-start.3 = (bf16[64,512]{1,0:T(8,128)(2,1)S(1)}, bf16[64,512]{1,0:T(8,128)(2,1)S(1)}, u32[]{:S(2)}, u32[]{:S(2)}) collective-permute-start(bf16[64,512]{1,0:T(8,128)(2,1)S(1)} %join.1.after_ref.refs_6_), channel_id=1, source_target_pairs={{0,1},{1,0},{2,3},{3,2},{4,5},{5,4},{6,7},{7,6},{8,9},{9,8},{10,11... | collective-permute-start | bytes 196616 | tf_op jit(solution)/shard_map/ppermute | solution.py:46
  12.9 3.9 %copy-start = (s32[3072]{0:T(1024)S(1)}, s32[3072]{0:T(1024)}, u32[]{:S(2)}) copy-start(s32[3072]{0:T(1024)} %param.12) | copy-start | bytes 36868
  12.9 3.9 %copy-start.1 = (s32[3072]{0:T(1024)S(1)}, s32[3072]{0:T(1024)}, u32[]{:S(2)}) copy-start(s32[3072]{0:T(1024)} %starts_ref.1) | copy-start | bytes 36868
  20.3 6.2 %collective-permute-start.7 = (bf16[16,384]{1,0:T(8,128)(2,1)S(1)}, bf16[16,384]{1,0:T(8,128)(2,1)S(1)}, u32[]{:S(2)}, u32[]{:S(2)}) collective-permute-start(bf16[16,384]{1,0:T(8,128)(2,1)S(1)} %get-tuple-element.42), channel_id=1, source_target_pairs={{0,4},{1,5},{2,6},{3,7},{4,0},{5,1},{6,2},{7,3},{8,12},{9,13},{10,... | collective-permute-start | bytes 36872 | tf_op jit(solution)/shard_map/ppermute | solution.py:46
  21.0 5.4 %collective-permute-start.8 = (bf16[16,384]{1,0:T(8,128)(2,1)S(1)}, bf16[16,384]{1,0:T(8,128)(2,1)S(1)}, u32[]{:S(2)}, u32[]{:S(2)}) collective-permute-start(bf16[16,384]{1,0:T(8,128)(2,1)S(1)} %get-tuple-element.43), channel_id=1, source_target_pairs={{0,8},{1,9},{2,10},{3,11},{4,12},{5,13},{6,14},{7,15},{8,0},{9,1},... | collective-permute-start | bytes 36872 | tf_op jit(solution)/shard_map/ppermute | solution.py:46
  22.3 5.5 %collective-permute-start.9 = (bf16[16,384]{1,0:T(8,128)(2,1)S(1)}, bf16[16,384]{1,0:T(8,128)(2,1)S(1)}, u32[]{:S(2)}, u32[]{:S(2)}) collective-permute-start(bf16[16,384]{1,0:T(8,128)(2,1)S(1)} %get-tuple-element.44), channel_id=1, source_target_pairs={{0,12},{1,13},{2,14},{3,15},{4,8},{5,9},{6,10},{7,11},{8,4},{9,5},... | collective-permute-start | bytes 36872 | tf_op jit(solution)/shard_map/ppermute | solution.py:46
  24.7 7.2 %collective-permute-start.6 = (bf16[128,512]{1,0:T(8,128)(2,1)S(1)}, bf16[128,512]{1,0:T(8,128)(2,1)S(1)}, u32[]{:S(2)}, u32[]{:S(2)}) collective-permute-start(bf16[128,512]{1,0:T(8,128)(2,1)S(1)} %get-tuple-element.39), channel_id=1, source_target_pairs={{0,1},{1,2},{2,3},{3,4},{4,5},{5,6},{6,7},{7,8},{8,9},{9,10},{10,1... | collective-permute-start | bytes 393224 | tf_op jit(solution)/shard_map/ppermute | solution.py:476
  27.8 6.2 %collective-permute-start.10 = (bf16[16,384]{1,0:T(8,128)(2,1)S(1)}, bf16[16,384]{1,0:T(8,128)(2,1)S(1)}, u32[]{:S(2)}, u32[]{:S(2)}) collective-permute-start(bf16[16,384]{1,0:T(8,128)(2,1)S(1)} %get-tuple-element.46), channel_id=1, source_target_pairs={{0,1},{1,0},{2,3},{3,2},{4,5},{5,4},{6,7},{7,6},{8,9},{9,8},{10,11... | collective-permute-start | bytes 36872 | tf_op jit(solution)/shard_map/ppermute | solution.py:46
  27.9 6.1 %collective-permute-start.11 = (bf16[16,384]{1,0:T(8,128)(2,1)S(1)}, bf16[16,384]{1,0:T(8,128)(2,1)S(1)}, u32[]{:S(2)}, u32[]{:S(2)}) collective-permute-start(bf16[16,384]{1,0:T(8,128)(2,1)S(1)} %get-tuple-element.47), channel_id=1, source_target_pairs={{0,2},{1,3},{2,0},{3,1},{4,6},{5,7},{6,4},{7,5},{8,10},{9,11},{10,... | collective-permute-start | bytes 36872 | tf_op jit(solution)/shard_map/ppermute | solution.py:46
  28.7 5.3 %collective-permute-start.12 = (bf16[16,384]{1,0:T(8,128)(2,1)S(1)}, bf16[16,384]{1,0:T(8,128)(2,1)S(1)}, u32[]{:S(2)}, u32[]{:S(2)}) collective-permute-start(bf16[16,384]{1,0:T(8,128)(2,1)S(1)} %get-tuple-element.48), channel_id=1, source_target_pairs={{0,3},{1,2},{2,1},{3,0},{4,7},{5,6},{6,5},{7,4},{8,11},{9,10},{10,... | collective-permute-start | bytes 36872 | tf_op jit(solution)/shard_map/ppermute | solution.py:46

commit v14 on v13

--- a/solution.py
+++ b/solution.py
@@ -36,7 +36,7 @@
 
 def distance_of(row, caps, count):
     group, distance, left = row // caps, 0, count
-    for shift, radix in stages_of(count):
+    for shift, radix in reversed(stages_of(count)):
         left //= radix
         distance = distance + ((group // left) % radix << shift)
     return distance
@@ -457,7 +457,7 @@
         if number == 1:
             second = second_part(more, weight, bias, held[0])
 
-    back = stages
+    back = stages[::-1]
     d_preact, rim, *chunks = after(
         me.reshape(1),
         ids,

time: 35.2 us -> 33.1 us (0.940)
  waiting for transfers between devices: 5.82 us -> 3.37 us
  starting transfers between devices: 13.9 us -> 14.3 us
    ppermute x1, waiting for transfers between devices: 2.09 us -> 0.55 us  [on_device(): lax.ppermute(rim, 'band', [(i, (i + 1) % count) for i in range(count)])]
    ppermute x12, waiting for transfers between devices: 3.73 us -> 2.82 us  [swap(): return lax.ppermute(block, 'band', [(i, i ^ mask) for i in range(count)])]
  transfers between devices with their start and end apart: 13 -> 13, of which waited for: 5 -> 5; matrix products, arithmetic and copies ran while one was open for 0% -> 0% of each run, Pallas kernels for 29% -> 31%
where the time goes in v14:
time: 33.1 us; the launch traced here: 32.9 us
  Pallas kernels  14.5 us (44%)
  starting transfers between devices  14.3 us (43%)
  waiting for transfers between devices  3.37 us (10%)
  between operations  0.75 us (2%)
    ppermute x12, starting transfers between devices, swap(): return lax.ppermute(block, 'band', [(i, i ^ mask) for i in range(count)])  13.9 us
    pallas_call x1, Pallas kernels, after(): pl.pallas_call(functools.partial(after_kernel, len(parts), chunks, owned,...  3.37 us
    pallas_call x1, Pallas kernels, first_part(): pl.pallas_call(functools.partial(first_kernel, block, copies), in_specs=[...  3.15 us
    pallas_call x1, Pallas kernels, second_part(): pl.pallas_call(functools.partial(second_kernel, block), in_specs=[VMEM, V...  3.1 us
    ppermute x12, waiting for transfers between devices, swap(): return lax.ppermute(block, 'band', [(i, i ^ mask) for i in range(count)])  2.82 us
    pallas_call x1, Pallas kernels, grid_rows(): pl.pallas_call(functools.partial(grid_kernel, block), in_specs=[VMEM] * 3...  2.12 us
    pallas_call x1, Pallas kernels, segments(): pl.pallas_call(functools.partial(segments_kernel, block), in_specs=[SMEM]...  1.77 us
    pallas_call x1, Pallas kernels, mesh_rows(): pl.pallas_call(functools.partial(mesh_kernel, len(pieces)), in_specs=[VME...  0.99 us
  transfers between devices with their start and end apart: 13, of which 5 were waited for; matrix products, arithmetic and copies ran while one was open for 0% of the time, Pallas kernels for 31%

profile of v14, /device:TPU:0, one launch (start us, length us, event | category | flops | bytes accessed | tf_op | source)
XLA Modules:
  0.0 32.9 jit_solution(2396571167597673634)
XLA Ops:
  0.6 3.1 %collective-permute-start = (bf16[16,512]{1,0:T(8,128)(2,1)}, bf16[16,512]{1,0:T(8,128)(2,1)S(1)}, u32[]{:S(2)}, u32[]{:S(2)}) collective-permute-start(bf16[16,512]{1,0:T(8,128)(2,1)} %refs_5_.1), channel_id=1, source_target_pairs={{0,4},{1,5},{2,6},{3,7},{4,0},{5,1},{6,2},{7,3},{8,12},{9,13},{10,... | collective-permute-start | bytes 49160 | tf_op jit(solution)/shard_map/ppermute | solution.py:46
  3.7 2.5 %collective-permute-start.2 = (bf16[16,512]{1,0:T(8,128)(2,1)}, bf16[16,512]{1,0:T(8,128)(2,1)S(1)}, u32[]{:S(2)}, u32[]{:S(2)}) collective-permute-start(bf16[16,512]{1,0:T(8,128)(2,1)} %refs_5_.1), channel_id=1, source_target_pairs={{0,12},{1,13},{2,14},{3,15},{4,8},{5,9},{6,10},{7,11},{8,4},{9,5},... | collective-permute-start | bytes 49160 | tf_op jit(solution)/shard_map/ppermute | solution.py:46
  6.2 0.1 collective-permute-start.1
  6.3 3.1 %first_part.1 = (bf16[512,512]{1,0:T(8,128)(2,1)S(1)}, f32[1,512]{1,0:T(1,128)S(1)}, bf16[512,512]{1,0:T(8,128)(2,1)S(1)}, bf16[512,512]{1,0:T(8,128)(2,1)S(1)},...) custom-call(bf16[3072,512]{1,0:T(8,128)(2,1)} %pre_hbm.1, ...), custom_call_target="tpu_custom_call" | custom-call | flops 1610612736 | bytes 5242880 | tf_op jit(solution)/shard_map/first_part/pallas_call | solution.py:162
  9.5 0.0 collective-permute-done.refs_1_
  9.5 0.2 collective-permute-done.2.refs_3_
  9.7 1.4 %collective-permute-done.1.refs_2_ = bf16[16,512]{1,0:T(8,128)(2,1)S(1)} collective-permute-done((bf16[16,512]{1,0:T(8,128)(2,1)}, bf16[16,512]{1,0:T(8,128)(2,1)S(1)}, u32[]{:S(2)}, u32[]{:S(2)}) %collective-permute-start.1) | collective-permute-done | bytes 16416 | tf_op jit(solution)/shard_map/ppermute | solution.py:46
  11.1 1.6 %collective-permute-start.4 = (bf16[64,512]{1,0:T(8,128)(2,1)S(1)}, bf16[64,512]{1,0:T(8,128)(2,1)S(1)}, u32[]{:S(2)}, u32[]{:S(2)}) collective-permute-start(bf16[64,512]{1,0:T(8,128)(2,1)S(1)} %join.1.after_ref.refs_6_), channel_id=1, source_target_pairs={{0,2},{1,3},{2,0},{3,1},{4,6},{5,7},{6,4},{7,5},{8,10},{9,11},{10,... | collective-permute-start | bytes 196616 | tf_op jit(solution)/shard_map/ppermute | solution.py:46
  12.6 0.3 collective-permute-start.3
  12.9 3.1 %second_part.1 = (bf16[2048,512]{1,0:T(8,128)(2,1)S(1)}, bf16[2048,512]{1,0:T(8,128)(2,1)S(1)}, f32[2048,512]{1,0:T(8,128)S(1)}) custom-call(bf16[2048,512]{1,0:T(8,128)(2,1)S(1)} %get-tuple-element.32.pre_ref, bf16[512,512]{1,0:T(8,128)(2,1)S(1)} %get-tuple-element.27.weight_ref, f32[1,512]{1,0:T(1,128)S(1)} %get-tuple-element.33.bias_ref, ...), custom_call_target="tpu_custom_call" | custom-call | flops 3221225472 | bytes 10485760 | tf_op jit(solution)/shard_map/second_part/pallas_call | solution.py:188
  16.0 0.8 %collective-permute-done.4.refs_8_ = bf16[64,512]{1,0:T(8,128)(2,1)S(1)} collective-permute-done((bf16[64,512]{1,0:T(8,128)(2,1)S(1)}, bf16[64,512]{1,0:T(8,128)(2,1)S(1)}, u32[]{:S(2)}, u32[]{:S(2)}) %collective-permute-start.4) | collective-permute-done | bytes 65568 | tf_op jit(solution)/shard_map/ppermute | solution.py:46
  16.9 3.4 %after.1 = (bf16[3072,512]{1,0:T(8,128)(2,1)S(1)}, bf16[128,512]{1,0:T(8,128)(2,1)S(1)}, bf16[16,384]{1,0:T(8,128)(2,1)S(1)}, bf16[16,384]{1,0:T(8,128)(2,1)S(1)...) custom-call(s32[1]{0:T(128)} %bitcast.1.refs_6_.me_ref, f32[32,128]{1,0:T(8,128)S(1)} %get-tuple-element.26.ids_ref, ...), custom_call_target="tpu_custom_call" | custom-call | flops 4831838208 | bytes 12582912 | tf_op jit(solution)/shard_map/after/pallas_call | solution.py:304
  20.2 0.1 collective-permute-start.7
  20.4 0.7 %collective-permute-start.8 = (bf16[16,384]{1,0:T(8,128)(2,1)S(1)}, bf16[16,384]{1,0:T(8,128)(2,1)S(1)}, u32[]{:S(2)}, u32[]{:S(2)}) collective-permute-start(bf16[16,384]{1,0:T(8,128)(2,1)S(1)} %get-tuple-element.43), channel_id=1, source_target_pairs={{0,2},{1,3},{2,0},{3,1},{4,6},{5,7},{6,4},{7,5},{8,10},{9,11},{10,... | collective-permute-start | bytes 36872 | tf_op jit(solution)/shard_map/ppermute | solution.py:46
  21.1 1.1 %collective-permute-start.9 = (bf16[16,384]{1,0:T(8,128)(2,1)S(1)}, bf16[16,384]{1,0:T(8,128)(2,1)S(1)}, u32[]{:S(2)}, u32[]{:S(2)}) collective-permute-start(bf16[16,384]{1,0:T(8,128)(2,1)S(1)} %get-tuple-element.44), channel_id=1, source_target_pairs={{0,3},{1,2},{2,1},{3,0},{4,7},{5,6},{6,5},{7,4},{8,11},{9,10},{10,... | collective-permute-start | bytes 36872 | tf_op jit(solution)/shard_map/ppermute | solution.py:46
  22.2 0.3 %collective-permute-start.6 = (bf16[128,512]{1,0:T(8,128)(2,1)S(1)}, bf16[128,512]{1,0:T(8,128)(2,1)S(1)}, u32[]{:S(2)}, u32[]{:S(2)}) collective-permute-start(bf16[128,512]{1,0:T(8,128)(2,1)S(1)} %get-tuple-element.39), channel_id=1, source_target_pairs={{0,1},{1,2},{2,3},{3,4},{4,5},{5,6},{6,7},{7,8},{8,9},{9,10},{10,1... | collective-permute-start | bytes 393224 | tf_op jit(solution)/shard_map/ppermute | solution.py:476
  22.5 1.8 %segments.1.total_ref.refs_4_ = f32[2448,512]{1,0:T(8,128)S(1)} custom-call(s32[3072]{0:T(1024)S(1)} %copy-done.1, s32[1,3072]{1,0:T(1,128)S(1)} %bitcast.8, bf16[3072,512]{1,0:T(8,128)(2,1)S(1)} %get-tuple-element.38.d_ref), custom_call_target="tpu_custom_call" | custom-call | flops 3221225472 | bytes 6291456 | tf_op jit(solution)/shard_map/segments/pallas_call | solution.py:330
  24.4 0.8 %collective-permute-start.10 = (bf16[16,384]{1,0:T(8,128)(2,1)S(1)}, bf16[16,384]{1,0:T(8,128)(2,1)S(1)}, u32[]{:S(2)}, u32[]{:S(2)}) collective-permute-start(bf16[16,384]{1,0:T(8,128)(2,1)S(1)} %get-tuple-element.46), channel_id=1, source_target_pairs={{0,4},{1,5},{2,6},{3,7},{4,0},{5,1},{6,2},{7,3},{8,12},{9,13},{10,... | collective-permute-start | bytes 36872 | tf_op jit(solution)/shard_map/ppermute | solution.py:46
  25.2 1.3 %collective-permute-start.11 = (bf16[16,384]{1,0:T(8,128)(2,1)S(1)}, bf16[16,384]{1,0:T(8,128)(2,1)S(1)}, u32[]{:S(2)}, u32[]{:S(2)}) collective-permute-start(bf16[16,384]{1,0:T(8,128)(2,1)S(1)} %get-tuple-element.47), channel_id=1, source_target_pairs={{0,8},{1,9},{2,10},{3,11},{4,12},{5,13},{6,14},{7,15},{8,0},{9,1},... | collective-permute-start | bytes 36872 | tf_op jit(solution)/shard_map/ppermute | solution.py:46
  26.4 2.4 %collective-permute-start.12 = (bf16[16,384]{1,0:T(8,128)(2,1)S(1)}, bf16[16,384]{1,0:T(8,128)(2,1)S(1)}, u32[]{:S(2)}, u32[]{:S(2)}) collective-permute-start(bf16[16,384]{1,0:T(8,128)(2,1)S(1)} %get-tuple-element.48), channel_id=1, source_target_pairs={{0,12},{1,13},{2,14},{3,15},{4,8},{5,9},{6,10},{7,11},{8,4},{9,5},... | collective-permute-start | bytes 36872 | tf_op jit(solution)/shard_map/ppermute | solution.py:46
  28.8 0.6 %collective-permute-done.6.carried_ref = bf16[128,512]{1,0:T(8,128)(2,1)S(1)} collective-permute-done((bf16[128,512]{1,0:T(8,128)(2,1)S(1)}, bf16[128,512]{1,0:T(8,128)(2,1)S(1)}, u32[]{:S(2)}, u32[]{:S(2)}) %collective-permute-start.6) | collective-permute-done | bytes 131104 | tf_op jit(solution)/shard_map/ppermute | solution.py:476
  29.4 2.1 %grid_rows.1.refs_5_ = bf16[2048,512]{1,0:T(8,128)(2,1)} custom-call(f32[2448,512]{1,0:T(8,128)S(1)} %segments.1.total_ref.refs_4_, bf16[128,512]{1,0:T(8,128)(2,1)S(1)} %collective-permute-done.6.carried_ref, bf16[512,512]{1,0:T(8,128)(2,1)S(1)} %get-tuple-element.40.weight_ref), custom_call_target="tpu_custom_call" | custom-call | flops 1073741824 | bytes 6291456 | tf_op jit(solution)/shard_map/grid_rows/pallas_call | solution.py:359
  31.5 0.4 %collective-permute-done.12.refs_3_ = bf16[16,384]{1,0:T(8,128)(2,1)S(1)} collective-permute-done((bf16[16,384]{1,0:T(8,128)(2,1)S(1)}, bf16[16,384]{1,0:T(8,128)(2,1)S(1)}, u32[]{:S(2)}, u32[]{:S(2)}) %collective-permute-start.12) | collective-permute-done | bytes 12320 | tf_op jit(solution)/shard_map/ppermute | solution.py:46
  31.9 1.0 %mesh_rows.1 = bf16[16,512]{1,0:T(8,128)(2,1)} custom-call(bf16[16,384]{1,0:T(8,128)(2,1)S(1)} %get-tuple-element.45.refs_0_, bf16[16,384]{1,0:T(8,128)(2,1)S(1)} %collective-permute-done.10.refs_1_, bf16[16,384]{1,0:T(8,128)(2,1)S(1)} %collective-permute-done.11.refs_2_, bf16[16,384]{1,0:T(8,128)(2,1)S(1)} %collective-permute-done.12.refs_3_, ...), custom_call_target="tpu_custom_call" | custom-call | flops 8388608 | bytes 524288 | tf_op jit(solution)/shard_map/mesh_rows/pallas_call | solution.py:409
  (14 shorter events, 0.1 us)
Async XLA Ops:
  0.6 8.8 %collective-permute-start = (bf16[16,512]{1,0:T(8,128)(2,1)}, bf16[16,512]{1,0:T(8,128)(2,1)S(1)}, u32[]{:S(2)}, u32[]{:S(2)}) collective-permute-start(bf16[16,512]{1,0:T(8,128)(2,1)} %refs_5_.1), channel_id=1, source_target_pairs={{0,4},{1,5},{2,6},{3,7},{4,0},{5,1},{6,2},{7,3},{8,12},{9,13},{10,... | collective-permute-start | bytes 49160 | tf_op jit(solution)/shard_map/ppermute | solution.py:46
  3.7 6.0 %collective-permute-start.2 = (bf16[16,512]{1,0:T(8,128)(2,1)}, bf16[16,512]{1,0:T(8,128)(2,1)S(1)}, u32[]{:S(2)}, u32[]{:S(2)}) collective-permute-start(bf16[16,512]{1,0:T(8,128)(2,1)} %refs_5_.1), channel_id=1, source_target_pairs={{0,12},{1,13},{2,14},{3,15},{4,8},{5,9},{6,10},{7,11},{8,4},{9,5},... | collective-permute-start | bytes 49160 | tf_op jit(solution)/shard_map/ppermute | solution.py:46
  6.2 4.9 %collective-permute-start.1 = (bf16[16,512]{1,0:T(8,128)(2,1)}, bf16[16,512]{1,0:T(8,128)(2,1)S(1)}, u32[]{:S(2)}, u32[]{:S(2)}) collective-permute-start(bf16[16,512]{1,0:T(8,128)(2,1)} %refs_5_.1), channel_id=1, source_target_pairs={{0,8},{1,9},{2,10},{3,11},{4,12},{5,13},{6,14},{7,15},{8,0},{9,1},... | collective-permute-start | bytes 49160 | tf_op jit(solution)/shard_map/ppermute | solution.py:46
  11.1 5.0 %collective-permute-start.5 = (bf16[64,512]{1,0:T(8,128)(2,1)S(1)}, bf16[64,512]{1,0:T(8,128)(2,1)S(1)}, u32[]{:S(2)}, u32[]{:S(2)}) collective-permute-start(bf16[64,512]{1,0:T(8,128)(2,1)S(1)} %join.1.after_ref.refs_6_), channel_id=1, source_target_pairs={{0,3},{1,2},{2,1},{3,0},{4,7},{5,6},{6,5},{7,4},{8,11},{9,10},{10,... | collective-permute-start | bytes 196616 | tf_op jit(solution)/shard_map/ppermute | solution.py:46
  11.1 5.8 %collective-permute-start.4 = (bf16[64,512]{1,0:T(8,128)(2,1)S(1)}, bf16[64,512]{1,0:T(8,128)(2,1)S(1)}, u32[]{:S(2)}, u32[]{:S(2)}) collective-permute-start(bf16[64,512]{1,0:T(8,128)(2,1)S(1)} %join.1.after_ref.refs_6_), channel_id=1, source_target_pairs={{0,2},{1,3},{2,0},{3,1},{4,6},{5,7},{6,4},{7,5},{8,10},{9,11},{10,... | collective-permute-start | bytes 196616 | tf_op jit(solution)/shard_map/ppermute | solution.py:46
  12.6 4.2 %collective-permute-start.3 = (bf16[64,512]{1,0:T(8,128)(2,1)S(1)}, bf16[64,512]{1,0:T(8,128)(2,1)S(1)}, u32[]{:S(2)}, u32[]{:S(2)}) collective-permute-start(bf16[64,512]{1,0:T(8,128)(2,1)S(1)} %join.1.after_ref.refs_6_), channel_id=1, source_target_pairs={{0,1},{1,0},{2,3},{3,2},{4,5},{5,4},{6,7},{7,6},{8,9},{9,8},{10,11... | collective-permute-start | bytes 196616 | tf_op jit(solution)/shard_map/ppermute | solution.py:46
  12.9 3.9 %copy-start = (s32[3072]{0:T(1024)S(1)}, s32[3072]{0:T(1024)}, u32[]{:S(2)}) copy-start(s32[3072]{0:T(1024)} %param.12) | copy-start | bytes 36868
  12.9 3.9 %copy-start.1 = (s32[3072]{0:T(1024)S(1)}, s32[3072]{0:T(1024)}, u32[]{:S(2)}) copy-start(s32[3072]{0:T(1024)} %starts_ref.1) | copy-start | bytes 36868
  20.2 4.1 %collective-permute-start.7 = (bf16[16,384]{1,0:T(8,128)(2,1)S(1)}, bf16[16,384]{1,0:T(8,128)(2,1)S(1)}, u32[]{:S(2)}, u32[]{:S(2)}) collective-permute-start(bf16[16,384]{1,0:T(8,128)(2,1)S(1)} %get-tuple-element.42), channel_id=1, source_target_pairs={{0,1},{1,0},{2,3},{3,2},{4,5},{5,4},{6,7},{7,6},{8,9},{9,8},{10,11... | collective-permute-start | bytes 36872 | tf_op jit(solution)/shard_map/ppermute | solution.py:46
  20.4 3.9 %collective-permute-start.8 = (bf16[16,384]{1,0:T(8,128)(2,1)S(1)}, bf16[16,384]{1,0:T(8,128)(2,1)S(1)}, u32[]{:S(2)}, u32[]{:S(2)}) collective-permute-start(bf16[16,384]{1,0:T(8,128)(2,1)S(1)} %get-tuple-element.43), channel_id=1, source_target_pairs={{0,2},{1,3},{2,0},{3,1},{4,6},{5,7},{6,4},{7,5},{8,10},{9,11},{10,... | collective-permute-start | bytes 36872 | tf_op jit(solution)/shard_map/ppermute | solution.py:46
  21.1 3.2 %collective-permute-start.9 = (bf16[16,384]{1,0:T(8,128)(2,1)S(1)}, bf16[16,384]{1,0:T(8,128)(2,1)S(1)}, u32[]{:S(2)}, u32[]{:S(2)}) collective-permute-start(bf16[16,384]{1,0:T(8,128)(2,1)S(1)} %get-tuple-element.44), channel_id=1, source_target_pairs={{0,3},{1,2},{2,1},{3,0},{4,7},{5,6},{6,5},{7,4},{8,11},{9,10},{10,... | collective-permute-start | bytes 36872 | tf_op jit(solution)/shard_map/ppermute | solution.py:46
  22.2 7.2 %collective-permute-start.6 = (bf16[128,512]{1,0:T(8,128)(2,1)S(1)}, bf16[128,512]{1,0:T(8,128)(2,1)S(1)}, u32[]{:S(2)}, u32[]{:S(2)}) collective-permute-start(bf16[128,512]{1,0:T(8,128)(2,1)S(1)} %get-tuple-element.39), channel_id=1, source_target_pairs={{0,1},{1,2},{2,3},{3,4},{4,5},{5,6},{6,7},{7,8},{8,9},{9,10},{10,1... | collective-permute-start | bytes 393224 | tf_op jit(solution)/shard_map/ppermute | solution.py:476
  24.4 7.1 %collective-permute-start.10 = (bf16[16,384]{1,0:T(8,128)(2,1)S(1)}, bf16[16,384]{1,0:T(8,128)(2,1)S(1)}, u32[]{:S(2)}, u32[]{:S(2)}) collective-permute-start(bf16[16,384]{1,0:T(8,128)(2,1)S(1)} %get-tuple-element.46), channel_id=1, source_target_pairs={{0,4},{1,5},{2,6},{3,7},{4,0},{5,1},{6,2},{7,3},{8,12},{9,13},{10,... | collective-permute-start | bytes 36872 | tf_op jit(solution)/shard_map/ppermute | solution.py:46
  25.2 6.4 %collective-permute-start.11 = (bf16[16,384]{1,0:T(8,128)(2,1)S(1)}, bf16[16,384]{1,0:T(8,128)(2,1)S(1)}, u32[]{:S(2)}, u32[]{:S(2)}) collective-permute-start(bf16[16,384]{1,0:T(8,128)(2,1)S(1)} %get-tuple-element.47), channel_id=1, source_target_pairs={{0,8},{1,9},{2,10},{3,11},{4,12},{5,13},{6,14},{7,15},{8,0},{9,1},... | collective-permute-start | bytes 36872 | tf_op jit(solution)/shard_map/ppermute | solution.py:46
  26.4 5.5 %collective-permute-start.12 = (bf16[16,384]{1,0:T(8,128)(2,1)S(1)}, bf16[16,384]{1,0:T(8,128)(2,1)S(1)}, u32[]{:S(2)}, u32[]{:S(2)}) collective-permute-start(bf16[16,384]{1,0:T(8,128)(2,1)S(1)} %get-tuple-element.48), channel_id=1, source_target_pairs={{0,12},{1,13},{2,14},{3,15},{4,8},{5,9},{6,10},{7,11},{8,4},{9,5},... | collective-permute-start | bytes 36872 | tf_op jit(solution)/shard_map/ppermute | solution.py:46

commit v15 on v14

--- a/solution.py
+++ b/solution.py
@@ -397,9 +397,10 @@
     owned, width = out_ref.shape
     loaded = [unpack(piece) for piece in pieces]
     rows = jnp.concatenate([sums for sums, _ in loaded], axis=0)
-    ids = jnp.concatenate([ids for _, ids in loaded], axis=0).T[:owned].astype(jnp.int32)
-    pick = (lax.broadcasted_iota(jnp.int32, ids.shape, 0) == ids).astype(F32)
-    total = dot(pick.astype(BF16), rows.astype(BF16))
+    ids = jnp.concatenate([ids for _, ids in loaded], axis=0).astype(jnp.int32)
+    pick = (lax.broadcasted_iota(jnp.int32, ids.shape, 1) == ids).astype(F32).astype(BF16)
+    total = lax.dot_general(pick, rows.astype(BF16), (((0,), (0,)), ((), ())), preferred_element_type=F32)
+    total = total[:owned]
     both = dot_t(jnp.concatenate(split(total), axis=0), weight_ref[...])
     out_ref[...] = (both[:owned] + both[owned:]).astype(BF16)
 

time: 33.1 us -> 33.1 us (level)
  no operation moved by 1% of the time
where the time goes in v15:
time: 33.1 us; the launch traced here: 32.9 us
  Pallas kernels  14.5 us (44%)
  starting transfers between devices  14.3 us (43%)
  waiting for transfers between devices  3.37 us (10%)
  between operations  0.75 us (2%)
    ppermute x12, starting transfers between devices, swap(): return lax.ppermute(block, 'band', [(i, i ^ mask) for i in range(count)])  13.9 us
    pallas_call x1, Pallas kernels, after(): pl.pallas_call(functools.partial(after_kernel, len(parts), chunks, owned,...  3.37 us
    pallas_call x1, Pallas kernels, first_part(): pl.pallas_call(functools.partial(first_kernel, block, copies), in_specs=[...  3.15 us
    pallas_call x1, Pallas kernels, second_part(): pl.pallas_call(functools.partial(second_kernel, block), in_specs=[VMEM, V...  3.1 us
    ppermute x12, waiting for transfers between devices, swap(): return lax.ppermute(block, 'band', [(i, i ^ mask) for i in range(count)])  2.82 us
    pallas_call x1, Pallas kernels, grid_rows(): pl.pallas_call(functools.partial(grid_kernel, block), in_specs=[VMEM] * 3...  2.12 us
    pallas_call x1, Pallas kernels, segments(): pl.pallas_call(functools.partial(segments_kernel, block), in_specs=[SMEM]...  1.77 us
    pallas_call x1, Pallas kernels, mesh_rows(): pl.pallas_call(functools.partial(mesh_kernel, len(pieces)), in_specs=[VME...  0.99 us
  transfers between devices with their start and end apart: 13, of which 5 were waited for; matrix products, arithmetic and copies ran while one was open for 0% of the time, Pallas kernels for 31%

profile of v15, /device:TPU:0, one launch (start us, length us, event | category | flops | bytes accessed | tf_op | source)
XLA Modules:
  0.0 32.9 jit_solution(12579520436857144063)
XLA Ops:
  0.6 3.1 %collective-permute-start = (bf16[16,512]{1,0:T(8,128)(2,1)}, bf16[16,512]{1,0:T(8,128)(2,1)S(1)}, u32[]{:S(2)}, u32[]{:S(2)}) collective-permute-start(bf16[16,512]{1,0:T(8,128)(2,1)} %refs_5_.1), channel_id=1, source_target_pairs={{0,4},{1,5},{2,6},{3,7},{4,0},{5,1},{6,2},{7,3},{8,12},{9,13},{10,... | collective-permute-start | bytes 49160 | tf_op jit(solution)/shard_map/ppermute | solution.py:46
  3.7 2.5 %collective-permute-start.2 = (bf16[16,512]{1,0:T(8,128)(2,1)}, bf16[16,512]{1,0:T(8,128)(2,1)S(1)}, u32[]{:S(2)}, u32[]{:S(2)}) collective-permute-start(bf16[16,512]{1,0:T(8,128)(2,1)} %refs_5_.1), channel_id=1, source_target_pairs={{0,12},{1,13},{2,14},{3,15},{4,8},{5,9},{6,10},{7,11},{8,4},{9,5},... | collective-permute-start | bytes 49160 | tf_op jit(solution)/shard_map/ppermute | solution.py:46
  6.2 0.1 collective-permute-start.1
  6.3 3.1 %first_part.1 = (bf16[512,512]{1,0:T(8,128)(2,1)S(1)}, f32[1,512]{1,0:T(1,128)S(1)}, bf16[512,512]{1,0:T(8,128)(2,1)S(1)}, bf16[512,512]{1,0:T(8,128)(2,1)S(1)},...) custom-call(bf16[3072,512]{1,0:T(8,128)(2,1)} %pre_hbm.1, ...), custom_call_target="tpu_custom_call" | custom-call | flops 1610612736 | bytes 5242880 | tf_op jit(solution)/shard_map/first_part/pallas_call | solution.py:162
  9.5 0.2 collective-permute-done.2.refs_3_
  9.7 1.4 %collective-permute-done.1.refs_2_ = bf16[16,512]{1,0:T(8,128)(2,1)S(1)} collective-permute-done((bf16[16,512]{1,0:T(8,128)(2,1)}, bf16[16,512]{1,0:T(8,128)(2,1)S(1)}, u32[]{:S(2)}, u32[]{:S(2)}) %collective-permute-start.1) | collective-permute-done | bytes 16416 | tf_op jit(solution)/shard_map/ppermute | solution.py:46
  11.1 1.6 %collective-permute-start.4 = (bf16[64,512]{1,0:T(8,128)(2,1)S(1)}, bf16[64,512]{1,0:T(8,128)(2,1)S(1)}, u32[]{:S(2)}, u32[]{:S(2)}) collective-permute-start(bf16[64,512]{1,0:T(8,128)(2,1)S(1)} %join.1.after_ref.refs_6_), channel_id=1, source_target_pairs={{0,2},{1,3},{2,0},{3,1},{4,6},{5,7},{6,4},{7,5},{8,10},{9,11},{10,... | collective-permute-start | bytes 196616 | tf_op jit(solution)/shard_map/ppermute | solution.py:46
  12.6 0.3 collective-permute-start.3
  12.9 3.1 %second_part.1 = (bf16[2048,512]{1,0:T(8,128)(2,1)S(1)}, bf16[2048,512]{1,0:T(8,128)(2,1)S(1)}, f32[2048,512]{1,0:T(8,128)S(1)}) custom-call(bf16[2048,512]{1,0:T(8,128)(2,1)S(1)} %get-tuple-element.32.pre_ref, bf16[512,512]{1,0:T(8,128)(2,1)S(1)} %get-tuple-element.27.weight_ref, f32[1,512]{1,0:T(1,128)S(1)} %get-tuple-element.33.bias_ref, ...), custom_call_target="tpu_custom_call" | custom-call | flops 3221225472 | bytes 10485760 | tf_op jit(solution)/shard_map/second_part/pallas_call | solution.py:188
  16.0 0.0 collective-permute-done.5.refs_9_
  16.0 0.8 %collective-permute-done.4.refs_8_ = bf16[64,512]{1,0:T(8,128)(2,1)S(1)} collective-permute-done((bf16[64,512]{1,0:T(8,128)(2,1)S(1)}, bf16[64,512]{1,0:T(8,128)(2,1)S(1)}, u32[]{:S(2)}, u32[]{:S(2)}) %collective-permute-start.4) | collective-permute-done | bytes 65568 | tf_op jit(solution)/shard_map/ppermute | solution.py:46
  16.9 3.4 %after.1 = (bf16[3072,512]{1,0:T(8,128)(2,1)S(1)}, bf16[128,512]{1,0:T(8,128)(2,1)S(1)}, bf16[16,384]{1,0:T(8,128)(2,1)S(1)}, bf16[16,384]{1,0:T(8,128)(2,1)S(1)...) custom-call(s32[1]{0:T(128)} %bitcast.1.refs_6_.me_ref, f32[32,128]{1,0:T(8,128)S(1)} %get-tuple-element.26.ids_ref, ...), custom_call_target="tpu_custom_call" | custom-call | flops 4831838208 | bytes 12582912 | tf_op jit(solution)/shard_map/after/pallas_call | solution.py:304
  20.2 0.1 collective-permute-start.7
  20.4 0.7 %collective-permute-start.8 = (bf16[16,384]{1,0:T(8,128)(2,1)S(1)}, bf16[16,384]{1,0:T(8,128)(2,1)S(1)}, u32[]{:S(2)}, u32[]{:S(2)}) collective-permute-start(bf16[16,384]{1,0:T(8,128)(2,1)S(1)} %get-tuple-element.43), channel_id=1, source_target_pairs={{0,2},{1,3},{2,0},{3,1},{4,6},{5,7},{6,4},{7,5},{8,10},{9,11},{10,... | collective-permute-start | bytes 36872 | tf_op jit(solution)/shard_map/ppermute | solution.py:46
  21.1 1.1 %collective-permute-start.9 = (bf16[16,384]{1,0:T(8,128)(2,1)S(1)}, bf16[16,384]{1,0:T(8,128)(2,1)S(1)}, u32[]{:S(2)}, u32[]{:S(2)}) collective-permute-start(bf16[16,384]{1,0:T(8,128)(2,1)S(1)} %get-tuple-element.44), channel_id=1, source_target_pairs={{0,3},{1,2},{2,1},{3,0},{4,7},{5,6},{6,5},{7,4},{8,11},{9,10},{10,... | collective-permute-start | bytes 36872 | tf_op jit(solution)/shard_map/ppermute | solution.py:46
  22.2 0.3 %collective-permute-start.6 = (bf16[128,512]{1,0:T(8,128)(2,1)S(1)}, bf16[128,512]{1,0:T(8,128)(2,1)S(1)}, u32[]{:S(2)}, u32[]{:S(2)}) collective-permute-start(bf16[128,512]{1,0:T(8,128)(2,1)S(1)} %get-tuple-element.39), channel_id=1, source_target_pairs={{0,1},{1,2},{2,3},{3,4},{4,5},{5,6},{6,7},{7,8},{8,9},{9,10},{10,1... | collective-permute-start | bytes 393224 | tf_op jit(solution)/shard_map/ppermute | solution.py:477
  22.5 1.8 %segments.1.total_ref.refs_4_ = f32[2448,512]{1,0:T(8,128)S(1)} custom-call(s32[3072]{0:T(1024)S(1)} %copy-done.1, s32[1,3072]{1,0:T(1,128)S(1)} %bitcast.8, bf16[3072,512]{1,0:T(8,128)(2,1)S(1)} %get-tuple-element.38.d_ref), custom_call_target="tpu_custom_call" | custom-call | flops 3221225472 | bytes 6291456 | tf_op jit(solution)/shard_map/segments/pallas_call | solution.py:330
  24.4 0.8 %collective-permute-start.10 = (bf16[16,384]{1,0:T(8,128)(2,1)S(1)}, bf16[16,384]{1,0:T(8,128)(2,1)S(1)}, u32[]{:S(2)}, u32[]{:S(2)}) collective-permute-start(bf16[16,384]{1,0:T(8,128)(2,1)S(1)} %get-tuple-element.46), channel_id=1, source_target_pairs={{0,4},{1,5},{2,6},{3,7},{4,0},{5,1},{6,2},{7,3},{8,12},{9,13},{10,... | collective-permute-start | bytes 36872 | tf_op jit(solution)/shard_map/ppermute | solution.py:46
  25.2 1.3 %collective-permute-start.11 = (bf16[16,384]{1,0:T(8,128)(2,1)S(1)}, bf16[16,384]{1,0:T(8,128)(2,1)S(1)}, u32[]{:S(2)}, u32[]{:S(2)}) collective-permute-start(bf16[16,384]{1,0:T(8,128)(2,1)S(1)} %get-tuple-element.47), channel_id=1, source_target_pairs={{0,8},{1,9},{2,10},{3,11},{4,12},{5,13},{6,14},{7,15},{8,0},{9,1},... | collective-permute-start | bytes 36872 | tf_op jit(solution)/shard_map/ppermute | solution.py:46
  26.4 2.4 %collective-permute-start.12 = (bf16[16,384]{1,0:T(8,128)(2,1)S(1)}, bf16[16,384]{1,0:T(8,128)(2,1)S(1)}, u32[]{:S(2)}, u32[]{:S(2)}) collective-permute-start(bf16[16,384]{1,0:T(8,128)(2,1)S(1)} %get-tuple-element.48), channel_id=1, source_target_pairs={{0,12},{1,13},{2,14},{3,15},{4,8},{5,9},{6,10},{7,11},{8,4},{9,5},... | collective-permute-start | bytes 36872 | tf_op jit(solution)/shard_map/ppermute | solution.py:46
  28.8 0.6 %collective-permute-done.6.carried_ref = bf16[128,512]{1,0:T(8,128)(2,1)S(1)} collective-permute-done((bf16[128,512]{1,0:T(8,128)(2,1)S(1)}, bf16[128,512]{1,0:T(8,128)(2,1)S(1)}, u32[]{:S(2)}, u32[]{:S(2)}) %collective-permute-start.6) | collective-permute-done | bytes 131104 | tf_op jit(solution)/shard_map/ppermute | solution.py:477
  29.4 2.1 %grid_rows.1.refs_5_ = bf16[2048,512]{1,0:T(8,128)(2,1)} custom-call(f32[2448,512]{1,0:T(8,128)S(1)} %segments.1.total_ref.refs_4_, bf16[128,512]{1,0:T(8,128)(2,1)S(1)} %collective-permute-done.6.carried_ref, bf16[512,512]{1,0:T(8,128)(2,1)S(1)} %get-tuple-element.40.weight_ref), custom_call_target="tpu_custom_call" | custom-call | flops 1073741824 | bytes 6291456 | tf_op jit(solution)/shard_map/grid_rows/pallas_call | solution.py:359
  31.5 0.4 %collective-permute-done.12.refs_3_ = bf16[16,384]{1,0:T(8,128)(2,1)S(1)} collective-permute-done((bf16[16,384]{1,0:T(8,128)(2,1)S(1)}, bf16[16,384]{1,0:T(8,128)(2,1)S(1)}, u32[]{:S(2)}, u32[]{:S(2)}) %collective-permute-start.12) | collective-permute-done | bytes 12320 | tf_op jit(solution)/shard_map/ppermute | solution.py:46
  31.9 1.0 %mesh_rows.1 = bf16[16,512]{1,0:T(8,128)(2,1)} custom-call(bf16[16,384]{1,0:T(8,128)(2,1)S(1)} %get-tuple-element.45.refs_0_, bf16[16,384]{1,0:T(8,128)(2,1)S(1)} %collective-permute-done.10.refs_1_, bf16[16,384]{1,0:T(8,128)(2,1)S(1)} %collective-permute-done.11.refs_2_, bf16[16,384]{1,0:T(8,128)(2,1)S(1)} %collective-permute-done.12.refs_3_, ...), custom_call_target="tpu_custom_call" | custom-call | flops 8388608 | bytes 524288 | tf_op jit(solution)/shard_map/mesh_rows/pallas_call | solution.py:410
  (14 shorter events, 0.1 us)
Async XLA Ops:
  0.6 8.8 %collective-permute-start = (bf16[16,512]{1,0:T(8,128)(2,1)}, bf16[16,512]{1,0:T(8,128)(2,1)S(1)}, u32[]{:S(2)}, u32[]{:S(2)}) collective-permute-start(bf16[16,512]{1,0:T(8,128)(2,1)} %refs_5_.1), channel_id=1, source_target_pairs={{0,4},{1,5},{2,6},{3,7},{4,0},{5,1},{6,2},{7,3},{8,12},{9,13},{10,... | collective-permute-start | bytes 49160 | tf_op jit(solution)/shard_map/ppermute | solution.py:46
  3.7 6.0 %collective-permute-start.2 = (bf16[16,512]{1,0:T(8,128)(2,1)}, bf16[16,512]{1,0:T(8,128)(2,1)S(1)}, u32[]{:S(2)}, u32[]{:S(2)}) collective-permute-start(bf16[16,512]{1,0:T(8,128)(2,1)} %refs_5_.1), channel_id=1, source_target_pairs={{0,12},{1,13},{2,14},{3,15},{4,8},{5,9},{6,10},{7,11},{8,4},{9,5},... | collective-permute-start | bytes 49160 | tf_op jit(solution)/shard_map/ppermute | solution.py:46
  6.2 4.9 %collective-permute-start.1 = (bf16[16,512]{1,0:T(8,128)(2,1)}, bf16[16,512]{1,0:T(8,128)(2,1)S(1)}, u32[]{:S(2)}, u32[]{:S(2)}) collective-permute-start(bf16[16,512]{1,0:T(8,128)(2,1)} %refs_5_.1), channel_id=1, source_target_pairs={{0,8},{1,9},{2,10},{3,11},{4,12},{5,13},{6,14},{7,15},{8,0},{9,1},... | collective-permute-start | bytes 49160 | tf_op jit(solution)/shard_map/ppermute | solution.py:46
  11.1 5.0 %collective-permute-start.5 = (bf16[64,512]{1,0:T(8,128)(2,1)S(1)}, bf16[64,512]{1,0:T(8,128)(2,1)S(1)}, u32[]{:S(2)}, u32[]{:S(2)}) collective-permute-start(bf16[64,512]{1,0:T(8,128)(2,1)S(1)} %join.1.after_ref.refs_6_), channel_id=1, source_target_pairs={{0,3},{1,2},{2,1},{3,0},{4,7},{5,6},{6,5},{7,4},{8,11},{9,10},{10,... | collective-permute-start | bytes 196616 | tf_op jit(solution)/shard_map/ppermute | solution.py:46
  11.1 5.8 %collective-permute-start.4 = (bf16[64,512]{1,0:T(8,128)(2,1)S(1)}, bf16[64,512]{1,0:T(8,128)(2,1)S(1)}, u32[]{:S(2)}, u32[]{:S(2)}) collective-permute-start(bf16[64,512]{1,0:T(8,128)(2,1)S(1)} %join.1.after_ref.refs_6_), channel_id=1, source_target_pairs={{0,2},{1,3},{2,0},{3,1},{4,6},{5,7},{6,4},{7,5},{8,10},{9,11},{10,... | collective-permute-start | bytes 196616 | tf_op jit(solution)/shard_map/ppermute | solution.py:46
  12.6 4.2 %collective-permute-start.3 = (bf16[64,512]{1,0:T(8,128)(2,1)S(1)}, bf16[64,512]{1,0:T(8,128)(2,1)S(1)}, u32[]{:S(2)}, u32[]{:S(2)}) collective-permute-start(bf16[64,512]{1,0:T(8,128)(2,1)S(1)} %join.1.after_ref.refs_6_), channel_id=1, source_target_pairs={{0,1},{1,0},{2,3},{3,2},{4,5},{5,4},{6,7},{7,6},{8,9},{9,8},{10,11... | collective-permute-start | bytes 196616 | tf_op jit(solution)/shard_map/ppermute | solution.py:46
  12.9 3.9 %copy-start = (s32[3072]{0:T(1024)S(1)}, s32[3072]{0:T(1024)}, u32[]{:S(2)}) copy-start(s32[3072]{0:T(1024)} %param.12) | copy-start | bytes 36868
  12.9 3.9 %copy-start.1 = (s32[3072]{0:T(1024)S(1)}, s32[3072]{0:T(1024)}, u32[]{:S(2)}) copy-start(s32[3072]{0:T(1024)} %starts_ref.1) | copy-start | bytes 36868
  20.2 4.1 %collective-permute-start.7 = (bf16[16,384]{1,0:T(8,128)(2,1)S(1)}, bf16[16,384]{1,0:T(8,128)(2,1)S(1)}, u32[]{:S(2)}, u32[]{:S(2)}) collective-permute-start(bf16[16,384]{1,0:T(8,128)(2,1)S(1)} %get-tuple-element.42), channel_id=1, source_target_pairs={{0,1},{1,0},{2,3},{3,2},{4,5},{5,4},{6,7},{7,6},{8,9},{9,8},{10,11... | collective-permute-start | bytes 36872 | tf_op jit(solution)/shard_map/ppermute | solution.py:46
  20.4 3.9 %collective-permute-start.8 = (bf16[16,384]{1,0:T(8,128)(2,1)S(1)}, bf16[16,384]{1,0:T(8,128)(2,1)S(1)}, u32[]{:S(2)}, u32[]{:S(2)}) collective-permute-start(bf16[16,384]{1,0:T(8,128)(2,1)S(1)} %get-tuple-element.43), channel_id=1, source_target_pairs={{0,2},{1,3},{2,0},{3,1},{4,6},{5,7},{6,4},{7,5},{8,10},{9,11},{10,... | collective-permute-start | bytes 36872 | tf_op jit(solution)/shard_map/ppermute | solution.py:46
  21.1 3.2 %collective-permute-start.9 = (bf16[16,384]{1,0:T(8,128)(2,1)S(1)}, bf16[16,384]{1,0:T(8,128)(2,1)S(1)}, u32[]{:S(2)}, u32[]{:S(2)}) collective-permute-start(bf16[16,384]{1,0:T(8,128)(2,1)S(1)} %get-tuple-element.44), channel_id=1, source_target_pairs={{0,3},{1,2},{2,1},{3,0},{4,7},{5,6},{6,5},{7,4},{8,11},{9,10},{10,... | collective-permute-start | bytes 36872 | tf_op jit(solution)/shard_map/ppermute | solution.py:46
  22.2 7.2 %collective-permute-start.6 = (bf16[128,512]{1,0:T(8,128)(2,1)S(1)}, bf16[128,512]{1,0:T(8,128)(2,1)S(1)}, u32[]{:S(2)}, u32[]{:S(2)}) collective-permute-start(bf16[128,512]{1,0:T(8,128)(2,1)S(1)} %get-tuple-element.39), channel_id=1, source_target_pairs={{0,1},{1,2},{2,3},{3,4},{4,5},{5,6},{6,7},{7,8},{8,9},{9,10},{10,1... | collective-permute-start | bytes 393224 | tf_op jit(solution)/shard_map/ppermute | solution.py:477
  24.4 7.1 %collective-permute-start.10 = (bf16[16,384]{1,0:T(8,128)(2,1)S(1)}, bf16[16,384]{1,0:T(8,128)(2,1)S(1)}, u32[]{:S(2)}, u32[]{:S(2)}) collective-permute-start(bf16[16,384]{1,0:T(8,128)(2,1)S(1)} %get-tuple-element.46), channel_id=1, source_target_pairs={{0,4},{1,5},{2,6},{3,7},{4,0},{5,1},{6,2},{7,3},{8,12},{9,13},{10,... | collective-permute-start | bytes 36872 | tf_op jit(solution)/shard_map/ppermute | solution.py:46
  25.2 6.4 %collective-permute-start.11 = (bf16[16,384]{1,0:T(8,128)(2,1)S(1)}, bf16[16,384]{1,0:T(8,128)(2,1)S(1)}, u32[]{:S(2)}, u32[]{:S(2)}) collective-permute-start(bf16[16,384]{1,0:T(8,128)(2,1)S(1)} %get-tuple-element.47), channel_id=1, source_target_pairs={{0,8},{1,9},{2,10},{3,11},{4,12},{5,13},{6,14},{7,15},{8,0},{9,1},... | collective-permute-start | bytes 36872 | tf_op jit(solution)/shard_map/ppermute | solution.py:46
  26.4 5.5 %collective-permute-start.12 = (bf16[16,384]{1,0:T(8,128)(2,1)S(1)}, bf16[16,384]{1,0:T(8,128)(2,1)S(1)}, u32[]{:S(2)}, u32[]{:S(2)}) collective-permute-start(bf16[16,384]{1,0:T(8,128)(2,1)S(1)} %get-tuple-element.48), channel_id=1, source_target_pairs={{0,12},{1,13},{2,14},{3,15},{4,8},{5,9},{6,10},{7,11},{8,4},{9,5},... | collective-permute-start | bytes 36872 | tf_op jit(solution)/shard_map/ppermute | solution.py:46
